TPU v7x, 128 devices: a whole 4x4x4 slice. The times are simulated.
128 devices in a mesh: grp: 4 (over z_lo, core), dev: 32 (over y, x, z_hi).
Axes of the slice: x: 4, y: 4, z: 4 (z_hi: 2, z_lo: 2; z = z_hi * 2 + z_lo), core: 2. Of those that a mesh axis runs over, the one named last changes fastest.
Arguments:
- embeds: bfloat16 [32768, 512], P(('grp', 'dev')), may hold values from -0.19921875 to 0.19921875
- partner: int32 [32768], P(('grp', 'dev')), may hold values from 0 to 32767, as said below
Outputs:
- loss: float32 [], replicated
- grad: float32 [32768, 512], P(('grp', 'dev'))
Inputs may be any that keep to these rules, and one draw needn't show every extreme that they name: partner pairs the views: partner[partner[i]] == i and partner[i] != i for every view i, and partner[i] lies in the same aligned block of 256 views as i.
All inputs are finite; a program needn't handle non-finite values.
Results may differ from a plain program's by a relative error of at most 0.0031.
Values may be sent and summed in bfloat16 or wider, within the bound.
No kernel may reach another device: no remote copies, remote signals or barrier semaphores. Data moves between devices by JAX's collectives and lax.ppermute only.
A program may use at most 128 MiB of HBM per device.

v0:
```python
import math

import jax
import jax.numpy as jnp
from jax import lax
from jax.sharding import PartitionSpec as P

INV_TAU = 10.0


def per_device(embeds, partner):
    rows = embeds.shape[0]
    devices = lax.axis_size("grp") * lax.axis_size("dev")
    total_views = rows * devices
    zf = embeds.astype(jnp.float32)
    recip = lax.rsqrt(jnp.sum(zf * zf, axis=1, keepdims=True) + 1e-06)
    unit = zf * recip
    unit_b = unit.astype(jnp.bfloat16)
    first = lax.axis_index(("grp", "dev")) * rows
    row_ids = first + jnp.arange(rows, dtype=jnp.int32)

    def scores(piece, start):
        s = jnp.dot(unit_b, piece.T, preferred_element_type=jnp.float32) * INV_TAU
        cols = start + jnp.arange(piece.shape[0], dtype=jnp.int32)
        off = cols[None, :] != row_ids[:, None]
        return (s, cols, off)

    whole = lax.all_gather(unit_b, ("grp", "dev"), axis=0, tiled=True)
    block = math.gcd(total_views, 2048)
    count = total_views // block
    empty_rows = jnp.zeros((rows,), jnp.float32)
    empty_acc = jnp.zeros((rows, embeds.shape[1]), jnp.float32)

    def forward_step(index, carry):
        total, positive = carry
        start = index * block
        piece = lax.dynamic_slice_in_dim(whole, start, block, 0)
        s, cols, off = scores(piece, start)
        total = total + jnp.sum(jnp.where(off, jnp.exp(s - INV_TAU), 0.0), axis=1)
        positive = positive + jnp.sum(jnp.where(cols[None, :] == partner[:, None], s, 0.0), axis=1)
        return (total, positive)

    total, positive = lax.fori_loop(0, count, forward_step, (empty_rows, empty_rows))
    lse = INV_TAU + jnp.log(total)
    lse_all = lax.all_gather(lse, ("grp", "dev"), axis=0, tiled=True)

    def backward_step(index, acc):
        start = index * block
        piece = lax.dynamic_slice_in_dim(whole, start, block, 0)
        col_lse = lax.dynamic_slice_in_dim(lse_all, start, block, 0)
        s, cols, off = scores(piece, start)
        w = jnp.where(off, jnp.exp(s - lse[:, None]) + jnp.exp(s - col_lse[None, :]), 0.0).astype(
            jnp.bfloat16
        )
        return acc + jnp.dot(w, piece, preferred_element_type=jnp.float32)

    acc = lax.fori_loop(0, count, backward_step, empty_acc)
    acc = acc - 2.0 * whole[partner].astype(jnp.float32)
    loss = lax.psum(jnp.sum(lse - positive), ("grp", "dev")) / total_views
    grad_unit = INV_TAU * acc
    grad = recip * (grad_unit - unit * jnp.sum(unit * grad_unit, axis=1, keepdims=True))
    return (loss, grad)


def solution(mesh):
    return jax.shard_map(
        per_device,
        mesh=mesh,
        in_specs=(P(("grp", "dev"), None), P(("grp", "dev"))),
        out_specs=(P(), P(("grp", "dev"), None)),
        check_vma=False,
    )
```

profile of v0, /device:TPU:0, one launch (start us, length us, event | category | flops | bytes accessed | tf_op | source)
XLA Modules:
  0.0 884.2 jit_solution(521857558617035673)
XLA Ops:
  10.8 350.4 %all-gather.3.cloned.1.call-done = bf16[32768,512]{1,0:T(8,128)(2,1)} async-done(((bf16[256,512]{1,0:T(8,128)(2,1)}), bf16[32768,512]{1,0:T(8,128)(2,1)}) %all-gather.3.cloned.1.call-update) | async-done | bytes 33554448 | tf_op jit(solution)/shard_map/all_gather | solution.py:28
  361.2 43.5 %while.32 = (s32[]{:T(128)}, f32[256]{0:T(256)S(1)}, f32[256]{0:T(256)S(1)}, bf16[32768,512]{1,0:T(8,128)(2,1)}, bf16[256,512]{1,0:T(8,128)(2,1)}, /*index=5*/s3...) while((s32[]{:T(128)}, f32[256]{0:T(256)S(1)}, ...), condition=%wide.region_4.5_spmd.clone, body=%wide.region_1.4_spmd.clone.sunk | while | flops 541068032 | bytes 2387129 | solution.py:43
  366.6 2.7 select_reduce_fusion.3
  369.4 2.6 select_reduce_fusion.3
  372.1 2.6 select_reduce_fusion.3
  374.8 2.6 select_reduce_fusion.3
  377.5 2.6 select_reduce_fusion.3
  380.3 2.6 select_reduce_fusion.3
  383.0 2.6 select_reduce_fusion.3
  385.7 2.6 select_reduce_fusion.3
  388.4 2.6 select_reduce_fusion.3
  391.1 2.6 select_reduce_fusion.3
  405.3 66.5 %psum.7 = f32[]{:T(128)} all-reduce(f32[]{:T(128)} %get-tuple-element.393), channel_id=1, replica_groups=mesh['grp'=4,'dev'=32] {'grp','dev'}, use_global_device_ids=true, to_apply=%region_6.7 | all-reduce | flops 1 | bytes 8 | tf_op jit(solution)/shard_map/psum | solution.py:59
  471.8 322.0 %all-gather = f32[128,1,256]{2,1,0:T(1,128)S(1)} all-gather(f32[1,1,256]{2,1,0:T(1,128)S(1)} %bitcast.19), channel_id=1, replica_groups=mesh['grp'=4,'dev'=32] {'grp','dev'}, dimensions={0}, use_global_device_ids=true | all-gather | bytes 132096 | tf_op jit(solution)/shard_map/all_gather | solution.py:45
  793.7 77.9 %while.33 = (s32[]{:T(128)}, f32[256,512]{1,0:T(8,128)S(1)}, bf16[32768,512]{1,0:T(8,128)(2,1)}, bf16[256,512]{1,0:T(8,128)(2,1)}, f32[256]{0:T(256)S(1)}, /*ind...) while((s32[]{:T(128)}, f32[256,512]{1,0:T(8,128)S(1)}, ...), condition=%wide.region_8.9_spmd.clone, body=%wide.region_7.8_spmd.clone.sunk | while | flops 1077676288 | bytes 5550776 | solution.py:57
  793.7 4.8 fusion.38
  798.6 4.8 fusion.38
  803.5 4.8 fusion.38
  808.3 4.8 fusion.38
  813.2 4.8 fusion.38
  818.1 4.8 fusion.38
  823.0 4.8 fusion.38
  827.8 4.8 fusion.38
  832.7 4.8 fusion.38
  837.6 4.8 fusion.38
  842.4 4.8 fusion.38
  847.3 4.8 fusion.38
  852.2 4.8 fusion.38
  857.1 4.8 fusion.38
  861.9 4.8 fusion.38
  866.8 4.8 fusion.38
  871.6 2.7 gather_fusion
  (117 shorter events, 22.0 us)
Async XLA Ops:
  7.2 354.0 %all-gather.3.cloned.1.call-start = ((), (), s32[]{:S(2)}) async-start(), calls=%async_computation | async-start | bytes 33816576 | tf_op jit(solution)/shard_map/all_gather | solution.py:28
  871.6 2.7 copy-start
Sparse Core Ops, SparseCore 0:
  10.3 350.8 all-gather.2
where the time goes:
time: 886 us; the launch traced here: 884 us
  blocking collectives  388 us (44%)
  waiting for transfers between devices  350 us (40%)
  matrix products  119 us (13%)
  between operations  15.9 us (2%)
    all_gather x1, waiting for transfers between devices, per_device(): whole = lax.all_gather(unit_b, ('grp', 'dev'), axis=0, tiled=True)  350 us
    all_gather x1, blocking collectives, per_device(): lse_all = lax.all_gather(lse, ('grp', 'dev'), axis=0, tiled=True)  322 us
    dot_general x16, matrix products, backward_step(): return acc + jnp.dot(w, piece, preferred_element_type=jnp.float32)  76.7 us
    psum x1, blocking collectives, per_device(): loss = lax.psum(jnp.sum(lse - positive), ('grp', 'dev')) / total_views  66.5 us
    dot_general x16, matrix products, scores(): s = jnp.dot(unit_b, piece.T, preferred_element_type=jnp.float32) * INV_TAU  42.4 us
  transfers between devices with their start and end apart: 1, of which 1 were waited for; matrix products, arithmetic and copies ran while one was open for 0% of the time, Pallas kernels for 0%

commit v1 on v0

v1 whole, which is shorter than its diff:
```python
import functools
import math

import jax
import jax.numpy as jnp
from jax import lax
from jax.experimental import pallas as pl
from jax.experimental.pallas import tpu as pltpu
from jax.sharding import Mesh, PartitionSpec as P

INV_TAU = 10.0
EXP_SCALE = INV_TAU * math.log2(math.e)
AXES = ("zlo", "core", "y", "x", "zhi")
SIZES = (2, 2, 4, 4, 2)
OFFSETS = (0, -1, 1, 2)
Z_OFFSETS = (0, 1, 3, 2)
NT = (((1,), (1,)), ((), ()))
NN = (((1,), (0,)), ((), ()))
ROWS = 256
ALL_ROWS = 2048
COLS = 4096
TILE = 512
NEAR_ROWS = 768
MIB = 1024 * 1024
E = 512
BF16 = jnp.bfloat16
F32 = jnp.float32


def place(x, y, z, core):
    return ((((z % 2) * 2 + core) * 4 + y) * 4 + x) * 2 + z // 2


def get(value, z=0, core=0, first=0, second=0, z_own=0):
    pairs = []
    for px in range(4):
        for py in range(4):
            for pz in range(4):
                for pc in range(2):
                    x, y = (first, second) if pc == 0 else (second, first)
                    away = z + (z_own if pc == 0 else -z_own)
                    source = place((px + x) % 4, (py + y) % 4, (pz + away) % 4, pc ^ core)
                    pairs.append((source, place(px, py, pz, pc)))
    return lax.ppermute(value, AXES, pairs)


def ring_sum(own, before, after, far):
    return (own + far) + (before + after)


def after(value, *others):
    return lax.optimization_barrier((value, *others))[0]


def vmem():
    return pl.BlockSpec(memory_space=pltpu.VMEM)


def smem():
    return pl.BlockSpec(memory_space=pltpu.SMEM)


def hbm():
    return pl.BlockSpec(memory_space=pltpu.HBM)


def params(mib):
    return pltpu.CompilerParams(vmem_limit_bytes=mib * MIB)


def block_of(z, core):
    return ((z & 1) * 2 + core) * 2 + lax.shift_right_logical(z, 1)


def unit_kernel(z_ref, unit_ref):
    zf = z_ref[...].astype(F32)
    recip = lax.rsqrt(jnp.sum(zf * zf, axis=1, keepdims=True) + 1e-06)
    unit_ref[...] = (zf * recip).astype(BF16)


def make_unit(embeds):
    return pl.pallas_call(
        unit_kernel,
        out_shape=jax.ShapeDtypeStruct((ROWS, E), BF16),
        in_specs=[vmem()],
        out_specs=vmem(),
        compiler_params=params(4),
        name="unit",
    )(embeds)


def mates_kernel(unit_ref, partner_ref, mates_ref, positive_ref):
    unit = unit_ref[...]
    ids = lax.broadcasted_iota(jnp.int32, (ROWS, ROWS), 0)
    pick = (ids == (partner_ref[...] & (ROWS - 1))).astype(F32).astype(BF16)
    mates = lax.dot_general(pick, unit, NN, preferred_element_type=F32)
    mates_ref[...] = mates.astype(BF16)
    products = jnp.sum(unit.astype(F32) * mates, axis=0, keepdims=True)
    total = jnp.sum(products, axis=1, keepdims=True) * INV_TAU
    positive_ref[...] = jnp.broadcast_to(total, (1, 128))


def make_mates(unit, partner):
    return pl.pallas_call(
        mates_kernel,
        out_shape=(
            jax.ShapeDtypeStruct((ROWS, E), BF16),
            jax.ShapeDtypeStruct((1, 128), F32),
        ),
        in_specs=[vmem(), vmem()],
        out_specs=(vmem(), vmem()),
        compiler_params=params(4),
        name="mates",
    )(unit, partner.reshape(1, ROWS))


def exps_kernel(places, olds, first, last, *refs):
    count = len(places)
    near, far = ((0, NEAR_ROWS), (1024, 1024 + NEAR_ROWS)), ((NEAR_ROWS, 1024), (1024 + NEAR_ROWS, 2048))
    info_ref, refs = refs[0], refs[1:]
    row_refs, refs = (refs[:2], refs[2:]) if first else (refs[:4], refs[4:])
    col_refs, refs = refs[:count], refs[count:]
    if not first:
        before_ref, refs = refs[0], refs[3:]
    if last:
        positive_ref, refs = refs[0], refs[1:]
    sums_ref, exps_ref, unit_ref, rows, sums, line = refs
    for ref, (start, stop) in zip(row_refs, near + far):
        rows[start:stop] = ref[...]
    sums[...] = jnp.zeros_like(sums) if first else before_ref[...]
    for n, col_ref in enumerate(col_refs):
        if n in olds:
            ranges = far
        else:
            ranges = near if first else ((0, 1024), (1024, 2048))
            start = places[n] * TILE
            unit_ref[start : start + col_ref.shape[0]] = col_ref[...]

        @pl.loop(0, col_ref.shape[0] // ROWS)
        def _(m):
            here = pl.ds(pl.multiple_of(places[n] * TILE + m * ROWS, ROWS), ROWS)
            cols = col_ref[pl.ds(pl.multiple_of(m * ROWS, ROWS), ROWS), :]
            for start, stop in ranges:
                s = lax.dot_general(rows[start:stop], cols, NT, preferred_element_type=F32)
                e = jnp.exp2(s * EXP_SCALE)
                if first and start == 0:
                    i = lax.broadcasted_iota(jnp.int32, (ROWS, ROWS), 0)
                    j = lax.broadcasted_iota(jnp.int32, (ROWS, ROWS), 1)
                    own = jnp.where(i == j + m * ROWS, 0.0, e[:ROWS])
                    e = jnp.concatenate([own, e[ROWS:]], axis=0)
                exps_ref[start:stop, here] = e.astype(BF16)
                sums[start:stop] += e[:, :128] + e[:, 128:]

    if last:
        totals = jnp.sum(sums[...].T, axis=0, keepdims=True)
        line[...] = jnp.zeros_like(line)
        for c in range(2):
            for k in range(4):
                n = c * 4 + k
                at = block_of((info_ref[2] + Z_OFFSETS[k]) & 3, info_ref[3] ^ c)
                line[pl.ds(at, 1), :] = totals[:, n * ROWS : (n + 1) * ROWS]
        line[8:9, 0:128] = positive_ref[...]
        sums_ref[...] = line[...]
    else:
        sums_ref[...] = sums[...]


def make_exps(info, rows, cols, places, olds, chain, positive, name):
    first, last = chain is None, positive is not None
    count = len(cols)
    tiles = sum(c.shape[0] for c in cols) // TILE
    sums_shape = (16, ROWS) if last else (ALL_ROWS, 128)
    operands = [info, *rows, *cols] + ([] if first else list(chain)) + ([positive] if last else [])
    return pl.pallas_call(
        functools.partial(exps_kernel, places, olds, first, last),
        out_shape=(
            jax.ShapeDtypeStruct(sums_shape, F32),
            pltpu.VMEM((ALL_ROWS, COLS), BF16),
            pltpu.VMEM((COLS, E), BF16),
        ),
        in_specs=[smem()] + [vmem()] * (len(operands) - 1),
        out_specs=(vmem(), vmem(), vmem()),
        input_output_aliases={} if first else {6 + count: 1, 7 + count: 2},
        scratch_shapes=[
            pltpu.VMEM((ALL_ROWS, E), BF16),
            pltpu.VMEM((ALL_ROWS, 128), F32),
            pltpu.VMEM((16, ROWS), F32),
        ],
        compiler_params=params(12),
        cost_estimate=pl.CostEstimate(
            flops=2 * ALL_ROWS * tiles * TILE * E,
            bytes_accessed=tiles * TILE * E * 2,
            transcendentals=ALL_ROWS * tiles * TILE,
        ),
        name=name,
    )(*operands)


def totals_kernel(info_ref, own_ref, before_ref, after_ref, far_ref, arow_ref, message_ref, recips):
    both = ring_sum(own_ref[...], before_ref[...], after_ref[...], far_ref[...])
    total = both[:8]
    recips[...] = 1.0 / total
    logs = jnp.sum(jnp.sum(jnp.log(total), axis=0, keepdims=True), axis=1, keepdims=True)
    loss = jnp.broadcast_to(logs, (1, 128)) - both[8:9, :128]
    for c in range(2):
        for k in range(4):
            n = c * 4 + k
            at = block_of((info_ref[2] + Z_OFFSETS[k]) & 3, info_ref[3] ^ c)
            line = recips[pl.ds(at, 1), :]
            arow_ref[n * ROWS : (n + 1) * ROWS] = jnp.broadcast_to(line, (128, ROWS)).T.astype(BF16)
    own = recips[pl.ds(block_of(info_ref[2], info_ref[3]), 1), :]
    zeros = jnp.zeros((5, 128), F32)
    message_ref[...] = jnp.concatenate([own[:, :128], own[:, 128:], loss, zeros], axis=0)


def make_totals(info, own, before, after, far):
    return pl.pallas_call(
        totals_kernel,
        out_shape=(
            jax.ShapeDtypeStruct((ALL_ROWS, 128), BF16),
            jax.ShapeDtypeStruct((8, 128), F32),
        ),
        in_specs=[smem()] + [vmem()] * 4,
        out_specs=(vmem(), vmem()),
        scratch_shapes=[pltpu.VMEM((8, ROWS), F32)],
        compiler_params=params(4),
        name="totals",
    )(info, own, before, after, far)


def grads_kernel(first, count, adds, info_ref, plane_ref, arow_ref, exps_ref, unit_ref, *refs):
    if adds:
        add_ref, refs = refs[0], refs[1:]
    (out_ref,) = refs
    size = min(count, 512)
    cols = [plane_ref[8 * (g // 2) + g % 2 : 8 * (g // 2) + g % 2 + 1].astype(BF16) for g in range(COLS // 128)]

    @pl.loop(0, count // size)
    def _(r):
        here = pl.ds(pl.multiple_of(first + r * size, ROWS), size)
        a = arow_ref[here]
        w = exps_ref[here] * jnp.concatenate([a + col for col in cols], axis=1)
        product = lax.dot_general(w, unit_ref[...], NN, preferred_element_type=F32)
        if adds:
            product += add_ref[here].astype(F32)
        out_ref[pl.ds(pl.multiple_of(r * size, size), size)] = product.astype(out_ref.dtype)


def make_grads(first, count, dtype, info, plane, arow, exps, unit, add, name):
    adds = add is not None
    exps = pltpu.with_memory_space_constraint(exps, pltpu.VMEM)
    unit = pltpu.with_memory_space_constraint(unit, pltpu.VMEM)
    return pl.pallas_call(
        functools.partial(grads_kernel, first, count, adds),
        out_shape=jax.ShapeDtypeStruct((count, E), dtype),
        in_specs=[smem()] + [vmem()] * (5 if adds else 4),
        out_specs=vmem(),
        compiler_params=params(16),
        cost_estimate=pl.CostEstimate(
            flops=2 * count * COLS * E,
            bytes_accessed=COLS * (count + E) * 2,
            transcendentals=0,
        ),
        name=name,
    )(info, plane, arow, exps, unit, *([add] if adds else []))


def far_kernel(raw_ref, core_ref, out_ref):
    out_ref[...] = (raw_ref[...] + core_ref[NEAR_ROWS:].astype(F32)).astype(BF16)


def make_far(raw, core):
    return pl.pallas_call(
        far_kernel,
        out_shape=jax.ShapeDtypeStruct((ROWS, E), BF16),
        in_specs=[vmem(), vmem()],
        out_specs=vmem(),
        compiler_params=params(4),
        name="far",
    )(raw, core)


def near_kernel(info_ref, raw_ref, far_ref, up_ref, down_ref):
    far = far_ref[...].astype(F32)
    zero = jnp.zeros_like(far)
    up_ref[...] = (raw_ref[:ROWS] + jnp.where(info_ref[3] == 0, far, zero)).astype(BF16)
    down_ref[...] = (raw_ref[ROWS:] + jnp.where(info_ref[3] == 0, zero, far)).astype(BF16)


def make_near(info, raw, far):
    return pl.pallas_call(
        near_kernel,
        out_shape=(jax.ShapeDtypeStruct((ROWS, E), BF16), jax.ShapeDtypeStruct((ROWS, E), BF16)),
        in_specs=[smem(), vmem(), vmem()],
        out_specs=(vmem(), vmem()),
        compiler_params=params(4),
        name="near",
    )(info, raw, far)


def final_kernel(info_ref, z_ref, mates_ref, own_ref, below_ref, above_ref, plane_ref, grad_ref, loss_ref):
    zf = z_ref[...].astype(F32)
    recip = lax.rsqrt(jnp.sum(zf * zf, axis=1, keepdims=True) + 1e-06)
    unit = zf * recip
    acc = own_ref[...] + below_ref[...].astype(F32) + above_ref[...].astype(F32)
    grad_unit = INV_TAU * (acc - 2.0 * mates_ref[...].astype(F32))
    along = jnp.sum(unit * grad_unit, axis=1, keepdims=True)
    grad_ref[...] = recip * (grad_unit - unit * along)
    parts = [[plane_ref[8 * n + 2 : 8 * n + 3] for n in range(4 * m, 4 * m + 4)] for m in range(4)]
    x_first = ring_sum(*[ring_sum(*line) for line in parts])
    y_first = ring_sum(*[ring_sum(*line) for line in zip(*parts)])
    loss = jnp.where(info_ref[3] == 0, x_first, y_first)
    loss_ref[...] = loss[:, :1] / (ROWS * 128)


def make_final(info, embeds, mates, own, below, above, plane):
    return pl.pallas_call(
        final_kernel,
        out_shape=(jax.ShapeDtypeStruct((ROWS, E), F32), jax.ShapeDtypeStruct((1, 1), F32)),
        in_specs=[smem()] + [vmem()] * 6,
        out_specs=(vmem(), vmem()),
        compiler_params=params(4),
        name="final",
    )(info, embeds, mates, own, below, above, plane)


def per_device(embeds, partner):
    unit = make_unit(embeds)
    core_id = lax.axis_index("core")
    z = lax.axis_index("zhi") * 2 + lax.axis_index("zlo")
    info = jnp.stack([lax.axis_index("x"), lax.axis_index("y"), z, core_id]).astype(jnp.int32)

    before, next_ = get(unit, first=-1), get(unit, first=1)
    z_before, z_after = get(unit, z=-1), get(unit, z=1)
    before, next_ = lax.optimization_barrier((before, next_))
    far = get(before, first=-1)
    line = jnp.concatenate([unit, before, next_, far], axis=0)
    line_before, line_after = get(line, second=-1), get(line, second=1)
    near = jnp.concatenate([after(unit, far), z_after, z_before], axis=0)
    near = [near, get(near, core=1)]
    z_far = get(jnp.where(core_id == 0, after(z_before, line), after(z_after, line)), z_own=-1)

    mates, positive = make_mates(unit, partner)
    chain = make_exps(info, near, [line], (0,), (), None, None, "exps0")
    far0 = get(after(line_before, line_after, chain[0])[: 2 * ROWS], second=-1)
    far1 = get(after(line_after, line_before, chain[0])[2 * ROWS :], second=1)
    rows = near + [z_far, get(after(z_far, chain[0]), core=1)]
    chain = make_exps(info, rows, [line, line_before, line_after], (0, 2, 4), (0,), chain, None, "exps1")
    sums, exps, units = make_exps(info, rows, [far0, far1], (6, 7), (), chain, positive, "exps2")

    sums = sums + get(sums, core=1)
    arow, plane = make_totals(info, sums, get(sums, z=-1), get(sums, z=1), get(sums, z=2))
    plane = jnp.concatenate([plane] + [get(plane, first=k) for k in OFFSETS[1:]], axis=0)
    plane = jnp.concatenate([plane] + [get(plane, second=k) for k in OFFSETS[1:]], axis=0)

    theirs = make_grads(1024, 1024, BF16, info, plane, arow, exps, units, None, "grads_core")
    core = get(theirs, core=1)
    raw = make_grads(NEAR_ROWS, ROWS, F32, after(info, theirs), plane, arow, exps, units, None, "grads_far")
    far = make_far(raw, core)
    passed = get(far, z_own=-1)
    raw = make_grads(ROWS, 2 * ROWS, F32, after(info, far), plane, arow, exps, units, core, "grads_near")
    up, down = make_near(info, raw, passed)
    below, above = get(up, z=-1), get(down, z=1)
    own = make_grads(0, ROWS, F32, after(info, up), plane, arow, exps, units, core, "grads_own")
    grad, loss = make_final(info, embeds, mates, own, below, above, plane)
    return (loss[0, 0], grad)


def solution(mesh):
    torus = Mesh(mesh.devices.reshape(SIZES), AXES)
    return jax.shard_map(
        per_device,
        mesh=torus,
        in_specs=(P(AXES, None), P(AXES)),
        out_specs=(P(), P(AXES, None)),
        check_vma=False,
    )
```

time: 886 us -> 113 us (0.13)
  blocking collectives: 388 us -> 0 us
  waiting for transfers between devices: 350 us -> 45.2 us
  matrix products: 119 us -> 0 us
  Pallas kernels: 0 us -> 32.1 us
  starting transfers between devices: 0.04 us -> 31 us
  between operations: 15.9 us -> 0.84 us
    all_gather x1 -> x0, waiting for transfers between devices: 350 us -> none  [per_device(): whole = lax.all_gather(unit_b, ('grp', 'dev'), axis=0, tiled=True)]
    all_gather x1 -> x0, blocking collectives: 322 us -> none  [per_device(): lse_all = lax.all_gather(lse, ('grp', 'dev'), axis=0, tiled=True)]
    dot_general x32 -> x0, matrix products: 119 us -> none  [the longest x16 76.7 us: backward_step(): return acc + jnp.dot(w, piece, preferred_element_type=jnp.float32)]
    psum x1 -> x0, blocking collectives: 66.5 us -> none  [per_device(): loss = lax.psum(jnp.sum(lse - positive), ('grp', 'dev')) / total_views]
    ppermute x0 -> x26, waiting for transfers between devices: none -> 45.2 us  [get(): return lax.ppermute(value, AXES, pairs)]
    pallas_call x0 -> x13, Pallas kernels: none -> 32.1 us  [the longest x3 16.9 us: make_exps(): pl.pallas_call(functools.partial(exps_kernel, places, olds, first, last),...]
    ppermute x0 -> x26, starting transfers between devices: none -> 31 us  [get(): return lax.ppermute(value, AXES, pairs)]
  transfers between devices with their start and end apart: 1 -> 26, of which waited for: 1 -> 19; matrix products, arithmetic and copies ran while one was open for 0% -> 2% of each run, Pallas kernels for 0% -> 17%
where the time goes in v1:
time: 113 us
  waiting for transfers between devices  45.2 us (40%)
  Pallas kernels  32.1 us (28%)
  starting transfers between devices  31 us (27%)
  local copies, waits for them, and re-layouts  3.17 us (3%)
    ppermute x26, waiting for transfers between devices, get(): return lax.ppermute(value, AXES, pairs)  45.2 us
    ppermute x26, starting transfers between devices, get(): return lax.ppermute(value, AXES, pairs)  31 us
    pallas_call x3, Pallas kernels, make_exps(): pl.pallas_call(functools.partial(exps_kernel, places, olds, first, last),...  16.9 us
    pallas_call x4, Pallas kernels, make_grads(): pl.pallas_call(functools.partial(grads_kernel, first, count, adds), out_s...  11.6 us
  transfers between devices with their start and end apart: 26, of which 19 were waited for; matrix products, arithmetic and copies ran while one was open for 2% of the time, Pallas kernels for 17%

profile of v1, /device:TPU:0, one launch (start us, length us, event | category | flops | bytes accessed | tf_op | source)
XLA Modules:
  0.0 112.6 jit_solution(2820975669982819969)
XLA Ops:
  1.7 1.6 %collective-permute-start = (bf16[256,512]{1,0:T(8,128)(2,1)S(1)}, bf16[256,512]{1,0:T(8,128)(2,1)S(1)}, u32[]{:S(2)}, u32[]{:S(2)}) collective-permute-start(bf16[256,512]{1,0:T(8,128)(2,1)S(1)} %unit.1.unit_ref), channel_id=1, source_target_pairs={{6,0},{56,32},{70,64},{120,96},{7,1},{57,33},{71,65},{121,97},{14,... | collective-permute-start | bytes 786440 | tf_op jit(solution)/shard_map/ppermute | solution.py:44
  3.4 1.7 %collective-permute-start.1 = (bf16[256,512]{1,0:T(8,128)(2,1)S(1)}, bf16[256,512]{1,0:T(8,128)(2,1)S(1)}, u32[]{:S(2)}, u32[]{:S(2)}) collective-permute-start(bf16[256,512]{1,0:T(8,128)(2,1)S(1)} %unit.1.unit_ref), channel_id=1, source_target_pairs={{2,0},{40,32},{66,64},{104,96},{3,1},{41,33},{67,65},{105,97},{10,... | collective-permute-start | bytes 786440 | tf_op jit(solution)/shard_map/ppermute | solution.py:44
  5.0 4.3 %collective-permute-done = bf16[256,512]{1,0:T(8,128)(2,1)S(1)} collective-permute-done((bf16[256,512]{1,0:T(8,128)(2,1)S(1)}, bf16[256,512]{1,0:T(8,128)(2,1)S(1)}, u32[]{:S(2)}, u32[]{:S(2)}) %collective-permute-start) | collective-permute-done | bytes 262176 | tf_op jit(solution)/shard_map/ppermute | solution.py:44
  11.2 4.0 %collective-permute-start.3 = (bf16[256,512]{1,0:T(8,128)(2,1)S(1)}, bf16[256,512]{1,0:T(8,128)(2,1)S(1)}, u32[]{:S(2)}, u32[]{:S(2)}) collective-permute-start(bf16[256,512]{1,0:T(8,128)(2,1)S(1)} %unit.1.unit_ref), channel_id=1, source_target_pairs={{64,0},{96,32},{1,64},{33,96},{65,1},{97,33},{0,65},{32,97},{72,8}... | collective-permute-start | bytes 786440 | tf_op jit(solution)/shard_map/ppermute | solution.py:44
  15.3 2.0 %collective-permute-done.2 = bf16[256,512]{1,0:T(8,128)(2,1)S(1)} collective-permute-done((bf16[256,512]{1,0:T(8,128)(2,1)S(1)}, bf16[256,512]{1,0:T(8,128)(2,1)S(1)}, u32[]{:S(2)}, u32[]{:S(2)}) %collective-permute-start.2) | collective-permute-done | bytes 262176 | tf_op jit(solution)/shard_map/ppermute | solution.py:44
  17.3 2.2 %collective-permute-done.3 = bf16[256,512]{1,0:T(8,128)(2,1)S(1)} collective-permute-done((bf16[256,512]{1,0:T(8,128)(2,1)S(1)}, bf16[256,512]{1,0:T(8,128)(2,1)S(1)}, u32[]{:S(2)}, u32[]{:S(2)}) %collective-permute-start.3) | collective-permute-done | bytes 262176 | tf_op jit(solution)/shard_map/ppermute | solution.py:44
  19.6 3.4 %collective-permute-done.4 = bf16[256,512]{1,0:T(8,128)(2,1)S(1)} collective-permute-done((bf16[256,512]{1,0:T(8,128)(2,1)S(1)}, bf16[256,512]{1,0:T(8,128)(2,1)S(1)}, u32[]{:S(2)}, u32[]{:S(2)}) %collective-permute-start.4) | collective-permute-done | bytes 262176 | tf_op jit(solution)/shard_map/ppermute | solution.py:44
  23.2 1.5 %collective-permute-start.8 = (bf16[1024,512]{1,0:T(8,128)(2,1)S(1)}, bf16[1024,512]{1,0:T(8,128)(2,1)}, u32[]{:S(2)}, u32[]{:S(2)}) collective-permute-start(bf16[1024,512]{1,0:T(8,128)(2,1)S(1)} %pad_maximum_fusion.refs_3_.refs_5_), channel_id=1, source_target_pairs={{24,0},{38,32},{88,64},{102,96},{25,1},{39,33},{89,65},{103,97},{0... | collective-permute-start | bytes 3145736 | tf_op jit(solution)/shard_map/ppermute | solution.py:44
  24.7 1.8 %collective-permute-start.9 = (bf16[1024,512]{1,0:T(8,128)(2,1)S(1)}, bf16[1024,512]{1,0:T(8,128)(2,1)}, u32[]{:S(2)}, u32[]{:S(2)}) collective-permute-start(bf16[1024,512]{1,0:T(8,128)(2,1)S(1)} %pad_maximum_fusion.refs_3_.refs_5_), channel_id=1, source_target_pairs={{8,0},{34,32},{72,64},{98,96},{9,1},{35,33},{73,65},{99,97},{16,8}... | collective-permute-start | bytes 3145736 | tf_op jit(solution)/shard_map/ppermute | solution.py:44
  26.7 3.4 %exps0.1 = (f32[2048,128]{1,0:T(8,128)S(1)}, bf16[2048,4096]{1,0:T(8,128)(2,1)S(1)}, bf16[4096,512]{1,0:T(8,128)(2,1)S(1)}) custom-call(s32[4]{0:T(128)S(1)} %pad_add_fusion.refs_0_.info_ref, bf16[768,512]{1,0:T(8,128)(2,1)S(1)} %constant_dynamic-update-slice_fusion.refs_1_, bf16[768,512]{1,0:T(8,128)(2,1)S(1)} %collective-permute-done.5.refs_2_, ...), custom_call_target="tpu_custom_call" | custom-call | flops 2147483648 | bytes 1048576 | tf_op jit(solution)/shard_map/exps0/pallas_call | solution.py:174
  30.1 4.1 %collective-permute-done.6.refs_3_ = bf16[256,512]{1,0:T(8,128)(2,1)S(1)} collective-permute-done((bf16[256,512]{1,0:T(8,128)(2,1)S(1)}, bf16[256,512]{1,0:T(8,128)(2,1)S(1)}, u32[]{:S(2)}, u32[]{:S(2)}) %collective-permute-start.6) | collective-permute-done | bytes 262176 | tf_op jit(solution)/shard_map/ppermute | solution.py:44
  34.5 4.9 %collective-permute-done.8.refs_6_ = bf16[1024,512]{1,0:T(8,128)(2,1)} collective-permute-done((bf16[1024,512]{1,0:T(8,128)(2,1)S(1)}, bf16[1024,512]{1,0:T(8,128)(2,1)}, u32[]{:S(2)}, u32[]{:S(2)}) %collective-permute-start.8) | collective-permute-done | bytes 1048608 | tf_op jit(solution)/shard_map/ppermute | solution.py:44
  40.7 3.1 %collective-permute-start.11 = (bf16[512,512]{1,0:T(8,128)(2,1)S(1)}, bf16[512,512]{1,0:T(8,128)(2,1)S(1)}, u32[]{:S(2)}, u32[]{:S(2)}) collective-permute-start(bf16[512,512]{1,0:T(8,128)(2,1)S(1)} %slice.7), channel_id=1, source_target_pairs={{8,0},{34,32},{72,64},{98,96},{9,1},{35,33},{73,65},{99,97},{16,8}... | collective-permute-start | bytes 1572872 | tf_op jit(solution)/shard_map/ppermute | solution.py:44
  44.9 9.3 %exps1.1 = (f32[2048,128]{1,0:T(8,128)S(1)}, bf16[2048,4096]{1,0:T(8,128)(2,1)S(1)}, bf16[4096,512]{1,0:T(8,128)(2,1)S(1)}) custom-call(s32[4]{0:T(128)S(1)} %pad_add_fusion.refs_0_.info_ref, bf16[768,512]{1,0:T(8,128)(2,1)S(1)} %constant_dynamic-update-slice_fusion.refs_1_, ...), custom_call_target="tpu_custom_call", output_to_operand_aliasing={{1}: (9, {}), {2}: (10, {})} | custom-call | flops 6442450944 | bytes 3145728 | tf_op jit(solution)/shard_map/exps1/pallas_call | solution.py:174
  55.3 4.2 %exps2.1 = (f32[16,256]{1,0:T(8,128)S(1)}, bf16[2048,4096]{1,0:T(8,128)(2,1)S(1)}, bf16[4096,512]{1,0:T(8,128)(2,1)S(1)}) custom-call(s32[4]{0:T(128)S(1)} %pad_add_fusion.refs_0_.info_ref, bf16[768,512]{1,0:T(8,128)(2,1)S(1)} %constant_dynamic-update-slice_fusion.refs_1_, ...), custom_call_target="tpu_custom_call", output_to_operand_aliasing={{1}: (8, {}), {2}: (9, {})} | custom-call | flops 2147483648 | bytes 1048576 | tf_op jit(solution)/shard_map/exps2/pallas_call | solution.py:174
  60.7 3.2 %collective-permute-start.14 = (f32[16,256]{1,0:T(8,128)S(1)}, f32[16,256]{1,0:T(8,128)S(1)}, u32[]{:S(2)}, u32[]{:S(2)}) collective-permute-start(f32[16,256]{1,0:T(8,128)S(1)} %add.7.own_ref), channel_id=1, source_target_pairs={{64,0},{96,32},{1,64},{33,96},{65,1},{97,33},{0,65},{32,97},{72,8}... | collective-permute-start | bytes 49160 | tf_op jit(solution)/shard_map/ppermute | solution.py:44
  64.0 1.7 %collective-permute-done.13.before_ref = f32[16,256]{1,0:T(8,128)S(1)} collective-permute-done((f32[16,256]{1,0:T(8,128)S(1)}, f32[16,256]{1,0:T(8,128)S(1)}, u32[]{:S(2)}, u32[]{:S(2)}) %collective-permute-start.13) | collective-permute-done | bytes 16416 | tf_op jit(solution)/shard_map/ppermute | solution.py:44
  65.7 3.5 %collective-permute-done.15.far_ref = f32[16,256]{1,0:T(8,128)S(1)} collective-permute-done((f32[16,256]{1,0:T(8,128)S(1)}, f32[16,256]{1,0:T(8,128)S(1)}, u32[]{:S(2)}, u32[]{:S(2)}) %collective-permute-start.15) | collective-permute-done | bytes 16416 | tf_op jit(solution)/shard_map/ppermute | solution.py:44
  70.0 1.6 %collective-permute-start.16 = (f32[8,128]{1,0:T(8,128)S(1)}, f32[8,128]{1,0:T(8,128)S(1)}, u32[]{:S(2)}, u32[]{:S(2)}) collective-permute-start(f32[8,128]{1,0:T(8,128)S(1)} %get-tuple-element.47), channel_id=1, source_target_pairs={{6,0},{56,32},{70,64},{120,96},{7,1},{57,33},{71,65},{121,97},{14,... | collective-permute-start | bytes 12296 | tf_op jit(solution)/shard_map/ppermute | solution.py:44
  71.6 1.7 %collective-permute-start.17 = (f32[8,128]{1,0:T(8,128)S(1)}, f32[8,128]{1,0:T(8,128)S(1)}, u32[]{:S(2)}, u32[]{:S(2)}) collective-permute-start(f32[8,128]{1,0:T(8,128)S(1)} %get-tuple-element.47), channel_id=1, source_target_pairs={{2,0},{40,32},{66,64},{104,96},{3,1},{41,33},{67,65},{105,97},{10,... | collective-permute-start | bytes 12296 | tf_op jit(solution)/shard_map/ppermute | solution.py:44
  73.3 1.8 %collective-permute-start.18 = (f32[8,128]{1,0:T(8,128)S(1)}, f32[8,128]{1,0:T(8,128)S(1)}, u32[]{:S(2)}, u32[]{:S(2)}) collective-permute-start(f32[8,128]{1,0:T(8,128)S(1)} %get-tuple-element.47), channel_id=1, source_target_pairs={{4,0},{48,32},{68,64},{112,96},{5,1},{49,33},{69,65},{113,97},{12,... | collective-permute-start | bytes 12296 | tf_op jit(solution)/shard_map/ppermute | solution.py:44
  75.2 3.2 %collective-permute-done.18 = f32[8,128]{1,0:T(8,128)S(1)} collective-permute-done((f32[8,128]{1,0:T(8,128)S(1)}, f32[8,128]{1,0:T(8,128)S(1)}, u32[]{:S(2)}, u32[]{:S(2)}) %collective-permute-start.18) | collective-permute-done | bytes 4128 | tf_op jit(solution)/shard_map/ppermute | solution.py:44
  78.4 3.2 %collective-permute-start.20 = (f32[32,128]{1,0:T(8,128)S(1)}, f32[32,128]{1,0:T(8,128)S(1)}, u32[]{:S(2)}, u32[]{:S(2)}) collective-permute-start(f32[32,128]{1,0:T(8,128)S(1)} %get-tuple-element.58), channel_id=1, source_target_pairs={{8,0},{34,32},{72,64},{98,96},{9,1},{35,33},{73,65},{99,97},{16,8}... | collective-permute-start | bytes 49160 | tf_op jit(solution)/shard_map/ppermute | solution.py:44
  83.4 3.5 %collective-permute-done.21 = f32[32,128]{1,0:T(8,128)S(1)} collective-permute-done((f32[32,128]{1,0:T(8,128)S(1)}, f32[32,128]{1,0:T(8,128)S(1)}, u32[]{:S(2)}, u32[]{:S(2)}) %collective-permute-start.21) | collective-permute-done | bytes 16416 | tf_op jit(solution)/shard_map/ppermute | solution.py:44
  86.9 5.2 %grads_core.1 = bf16[1024,512]{1,0:T(8,128)(2,1)S(1)} custom-call(s32[4]{0:T(128)S(1)} %pad_add_fusion.refs_0_.info_ref, f32[128,128]{1,0:T(8,128)S(1)} %constant_dynamic-update-slice_fusion.7.plane_ref, bf16[2048,128]{1,0:T(8,128)(2,1)S(1)} %get-tuple-element.48.arow_ref, bf16[2048,4096]{1,0:T(8,128)(2,1)S(1)} %get-tuple-element.49.exps_ref, ...), custom_call_target="tpu_custom_call" | custom-call | flops 4294967296 | bytes 12582912 | tf_op jit(solution)/shard_map/grads_core/pallas_call | solution.py:253
  92.2 1.8 %grads_far.1.raw_ref = f32[256,512]{1,0:T(8,128)S(1)} custom-call(s32[4]{0:T(128)S(1)} %pad_add_fusion.refs_0_.info_ref, f32[128,128]{1,0:T(8,128)S(1)} %constant_dynamic-update-slice_fusion.7.plane_ref, bf16[2048,128]{1,0:T(8,128)(2,1)S(1)} %get-tuple-element.48.arow_ref, bf16[2048,4096]{1,0:T(8,128)(2,1)S(1)} %get-tuple-element.49.exps_ref, ...), custom_call_target="tpu_custom_call" | custom-call | flops 1073741824 | bytes 6291456 | tf_op jit(solution)/shard_map/grads_far/pallas_call | solution.py:253
  95.0 2.9 %grads_near.1.raw_ref = f32[512,512]{1,0:T(8,128)S(1)} custom-call(s32[4]{0:T(128)S(1)} %pad_add_fusion.refs_0_.info_ref, f32[128,128]{1,0:T(8,128)S(1)} %constant_dynamic-update-slice_fusion.7.plane_ref, bf16[2048,128]{1,0:T(8,128)(2,1)S(1)} %get-tuple-element.48.arow_ref, bf16[2048,4096]{1,0:T(8,128)(2,1)S(1)} %get-tuple-element.49.exps_ref, ...), custom_call_target="tpu_custom_call" | custom-call | flops 2147483648 | bytes 8388608 | tf_op jit(solution)/shard_map/grads_near/pallas_call | solution.py:253
  97.9 4.7 %collective-permute-done.23.far_ref = bf16[256,512]{1,0:T(8,128)(2,1)S(1)} collective-permute-done((bf16[256,512]{1,0:T(8,128)(2,1)S(1)}, bf16[256,512]{1,0:T(8,128)(2,1)S(1)}, u32[]{:S(2)}, u32[]{:S(2)}) %collective-permute-start.23) | collective-permute-done | bytes 262176 | tf_op jit(solution)/shard_map/ppermute | solution.py:44
  103.3 3.2 %collective-permute-start.25 = (bf16[256,512]{1,0:T(8,128)(2,1)S(1)}, bf16[256,512]{1,0:T(8,128)(2,1)S(1)}, u32[]{:S(2)}, u32[]{:S(2)}) collective-permute-start(bf16[256,512]{1,0:T(8,128)(2,1)S(1)} %get-tuple-element.55), channel_id=1, source_target_pairs={{64,0},{96,32},{1,64},{33,96},{65,1},{97,33},{0,65},{32,97},{72,8}... | collective-permute-start | bytes 786440 | tf_op jit(solution)/shard_map/ppermute | solution.py:44
  106.5 1.8 %grads_own.1.own_ref = f32[256,512]{1,0:T(8,128)S(1)} custom-call(s32[4]{0:T(128)S(1)} %pad_add_fusion.refs_0_.info_ref, f32[128,128]{1,0:T(8,128)S(1)} %constant_dynamic-update-slice_fusion.7.plane_ref, bf16[2048,128]{1,0:T(8,128)(2,1)S(1)} %get-tuple-element.48.arow_ref, bf16[2048,4096]{1,0:T(8,128)(2,1)S(1)} %get-tuple-element.49.exps_ref, ...), custom_call_target="tpu_custom_call" | custom-call | flops 1073741824 | bytes 6291456 | tf_op jit(solution)/shard_map/grads_own/pallas_call | solution.py:253
  108.3 2.5 %collective-permute-done.24.below_ref = bf16[256,512]{1,0:T(8,128)(2,1)S(1)} collective-permute-done((bf16[256,512]{1,0:T(8,128)(2,1)S(1)}, bf16[256,512]{1,0:T(8,128)(2,1)S(1)}, u32[]{:S(2)}, u32[]{:S(2)}) %collective-permute-start.24) | collective-permute-done | bytes 262176 | tf_op jit(solution)/shard_map/ppermute | solution.py:44
  110.9 1.7 %final.1 = (f32[256,512]{1,0:T(8,128)}, f32[1,1]{1,0:T(1,128)}) custom-call(s32[4]{0:T(128)S(1)} %pad_add_fusion.refs_0_.info_ref, bf16[256,512]{1,0:T(8,128)(2,1)S(1)} %copy-done.1, bf16[256,512]{1,0:T(8,128)(2,1)S(1)} %get-tuple-element.30.mates_ref, f32[256,512]{1,0:T(8,128)S(1)} %grads_own.1.own_ref, ...), custom_call_target="tpu_custom_call" | custom-call | tf_op jit(solution)/shard_map/final/pallas_call | solution.py:317
  (55 shorter events, 12.8 us)
Async XLA Ops:
  0.6 1.0 copy-start
  1.7 7.7 %collective-permute-start = (bf16[256,512]{1,0:T(8,128)(2,1)S(1)}, bf16[256,512]{1,0:T(8,128)(2,1)S(1)}, u32[]{:S(2)}, u32[]{:S(2)}) collective-permute-start(bf16[256,512]{1,0:T(8,128)(2,1)S(1)} %unit.1.unit_ref), channel_id=1, source_target_pairs={{6,0},{56,32},{70,64},{120,96},{7,1},{57,33},{71,65},{121,97},{14,... | collective-permute-start | bytes 786440 | tf_op jit(solution)/shard_map/ppermute | solution.py:44
  3.4 6.4 %collective-permute-start.1 = (bf16[256,512]{1,0:T(8,128)(2,1)S(1)}, bf16[256,512]{1,0:T(8,128)(2,1)S(1)}, u32[]{:S(2)}, u32[]{:S(2)}) collective-permute-start(bf16[256,512]{1,0:T(8,128)(2,1)S(1)} %unit.1.unit_ref), channel_id=1, source_target_pairs={{2,0},{40,32},{66,64},{104,96},{3,1},{41,33},{67,65},{105,97},{10,... | collective-permute-start | bytes 786440 | tf_op jit(solution)/shard_map/ppermute | solution.py:44
  9.7 7.6 %collective-permute-start.2 = (bf16[256,512]{1,0:T(8,128)(2,1)S(1)}, bf16[256,512]{1,0:T(8,128)(2,1)S(1)}, u32[]{:S(2)}, u32[]{:S(2)}) collective-permute-start(bf16[256,512]{1,0:T(8,128)(2,1)S(1)} %collective-permute-done), channel_id=1, source_target_pairs={{6,0},{56,32},{70,64},{120,96},{7,1},{57,33},{71,65},{121,97},{14,... | collective-permute-start | bytes 786440 | tf_op jit(solution)/shard_map/ppermute | solution.py:44
  11.2 8.4 %collective-permute-start.3 = (bf16[256,512]{1,0:T(8,128)(2,1)S(1)}, bf16[256,512]{1,0:T(8,128)(2,1)S(1)}, u32[]{:S(2)}, u32[]{:S(2)}) collective-permute-start(bf16[256,512]{1,0:T(8,128)(2,1)S(1)} %unit.1.unit_ref), channel_id=1, source_target_pairs={{64,0},{96,32},{1,64},{33,96},{65,1},{97,33},{0,65},{32,97},{72,8}... | collective-permute-start | bytes 786440 | tf_op jit(solution)/shard_map/ppermute | solution.py:44
  15.3 7.7 %collective-permute-start.4 = (bf16[256,512]{1,0:T(8,128)(2,1)S(1)}, bf16[256,512]{1,0:T(8,128)(2,1)S(1)}, u32[]{:S(2)}, u32[]{:S(2)}) collective-permute-start(bf16[256,512]{1,0:T(8,128)(2,1)S(1)} %unit.1.unit_ref), channel_id=1, source_target_pairs={{65,0},{97,32},{0,64},{32,96},{64,1},{96,33},{1,65},{33,97},{73,8}... | collective-permute-start | bytes 786440 | tf_op jit(solution)/shard_map/ppermute | solution.py:44
  23.0 3.7 %collective-permute-start.5 = (bf16[768,512]{1,0:T(8,128)(2,1)S(1)}, bf16[768,512]{1,0:T(8,128)(2,1)S(1)}, u32[]{:S(2)}, u32[]{:S(2)}) collective-permute-start(bf16[768,512]{1,0:T(8,128)(2,1)S(1)} %constant_dynamic-update-slice_fusion.refs_1_), channel_id=1, source_target_pairs={{32,0},{0,32},{96,64},{64,96},{33,1},{1,33},{97,65},{65,97},{40,8}... | collective-permute-start | bytes 2359304 | tf_op jit(solution)/shard_map/ppermute | solution.py:44
  23.2 16.2 %collective-permute-start.8 = (bf16[1024,512]{1,0:T(8,128)(2,1)S(1)}, bf16[1024,512]{1,0:T(8,128)(2,1)}, u32[]{:S(2)}, u32[]{:S(2)}) collective-permute-start(bf16[1024,512]{1,0:T(8,128)(2,1)S(1)} %pad_maximum_fusion.refs_3_.refs_5_), channel_id=1, source_target_pairs={{24,0},{38,32},{88,64},{102,96},{25,1},{39,33},{89,65},{103,97},{0... | collective-permute-start | bytes 3145736 | tf_op jit(solution)/shard_map/ppermute | solution.py:44
  24.7 14.9 %collective-permute-start.9 = (bf16[1024,512]{1,0:T(8,128)(2,1)S(1)}, bf16[1024,512]{1,0:T(8,128)(2,1)}, u32[]{:S(2)}, u32[]{:S(2)}) collective-permute-start(bf16[1024,512]{1,0:T(8,128)(2,1)S(1)} %pad_maximum_fusion.refs_3_.refs_5_), channel_id=1, source_target_pairs={{8,0},{34,32},{72,64},{98,96},{9,1},{35,33},{73,65},{99,97},{16,8}... | collective-permute-start | bytes 3145736 | tf_op jit(solution)/shard_map/ppermute | solution.py:44
  26.5 7.7 %collective-permute-start.6 = (bf16[256,512]{1,0:T(8,128)(2,1)S(1)}, bf16[256,512]{1,0:T(8,128)(2,1)S(1)}, u32[]{:S(2)}, u32[]{:S(2)}) collective-permute-start(bf16[256,512]{1,0:T(8,128)(2,1)S(1)} %broadcast_select_fusion), channel_id=1, source_target_pairs={{65,0},{96,32},{0,64},{33,96},{64,1},{97,33},{1,65},{32,97},{73,8}... | collective-permute-start | bytes 786440 | tf_op jit(solution)/shard_map/ppermute | solution.py:44
  26.7 7.5 %copy-start.2 = (s32[256]{0:T(256)S(1)}, s32[256]{0:T(256)}, u32[]{:S(2)}) copy-start(s32[256]{0:T(256)} %param.3) | copy-start | bytes 3076
  34.2 10.7 %collective-permute-start.7 = (bf16[256,512]{1,0:T(8,128)(2,1)S(1)}, bf16[256,512]{1,0:T(8,128)(2,1)S(1)}, u32[]{:S(2)}, u32[]{:S(2)}) collective-permute-start(bf16[256,512]{1,0:T(8,128)(2,1)S(1)} %collective-permute-done.6.refs_3_), channel_id=1, source_target_pairs={{32,0},{0,32},{96,64},{64,96},{33,1},{1,33},{97,65},{65,97},{40,8}... | collective-permute-start | bytes 786440 | tf_op jit(solution)/shard_map/ppermute | solution.py:44
  40.7 13.6 %collective-permute-start.11 = (bf16[512,512]{1,0:T(8,128)(2,1)S(1)}, bf16[512,512]{1,0:T(8,128)(2,1)S(1)}, u32[]{:S(2)}, u32[]{:S(2)}) collective-permute-start(bf16[512,512]{1,0:T(8,128)(2,1)S(1)} %slice.7), channel_id=1, source_target_pairs={{8,0},{34,32},{72,64},{98,96},{9,1},{35,33},{73,65},{99,97},{16,8}... | collective-permute-start | bytes 1572872 | tf_op jit(solution)/shard_map/ppermute | solution.py:44
  44.8 10.5 %collective-permute-start.10 = (bf16[512,512]{1,0:T(8,128)(2,1)S(1)}, bf16[512,512]{1,0:T(8,128)(2,1)S(1)}, u32[]{:S(2)}, u32[]{:S(2)}) collective-permute-start(bf16[512,512]{1,0:T(8,128)(2,1)S(1)} %slice.6), channel_id=1, source_target_pairs={{24,0},{38,32},{88,64},{102,96},{25,1},{39,33},{89,65},{103,97},{0... | collective-permute-start | bytes 1572872 | tf_op jit(solution)/shard_map/ppermute | solution.py:44
  59.5 1.3 %collective-permute-start.12 = (f32[16,256]{1,0:T(8,128)S(1)}, f32[16,256]{1,0:T(8,128)S(1)}, u32[]{:S(2)}, u32[]{:S(2)}) collective-permute-start(f32[16,256]{1,0:T(8,128)S(1)} %get-tuple-element.46), channel_id=1, source_target_pairs={{32,0},{0,32},{96,64},{64,96},{33,1},{1,33},{97,65},{65,97},{40,8}... | collective-permute-start | bytes 49160 | tf_op jit(solution)/shard_map/ppermute | solution.py:44
  60.7 4.9 %collective-permute-start.13 = (f32[16,256]{1,0:T(8,128)S(1)}, f32[16,256]{1,0:T(8,128)S(1)}, u32[]{:S(2)}, u32[]{:S(2)}) collective-permute-start(f32[16,256]{1,0:T(8,128)S(1)} %add.7.own_ref), channel_id=1, source_target_pairs={{65,0},{97,32},{0,64},{32,96},{64,1},{96,33},{1,65},{33,97},{73,8}... | collective-permute-start | bytes 49160 | tf_op jit(solution)/shard_map/ppermute | solution.py:44
  60.7 4.9 %collective-permute-start.14 = (f32[16,256]{1,0:T(8,128)S(1)}, f32[16,256]{1,0:T(8,128)S(1)}, u32[]{:S(2)}, u32[]{:S(2)}) collective-permute-start(f32[16,256]{1,0:T(8,128)S(1)} %add.7.own_ref), channel_id=1, source_target_pairs={{64,0},{96,32},{1,64},{33,96},{65,1},{97,33},{0,65},{32,97},{72,8}... | collective-permute-start | bytes 49160 | tf_op jit(solution)/shard_map/ppermute | solution.py:44
  64.0 5.2 %collective-permute-start.15 = (f32[16,256]{1,0:T(8,128)S(1)}, f32[16,256]{1,0:T(8,128)S(1)}, u32[]{:S(2)}, u32[]{:S(2)}) collective-permute-start(f32[16,256]{1,0:T(8,128)S(1)} %add.7.own_ref), channel_id=1, source_target_pairs={{1,0},{33,32},{65,64},{97,96},{0,1},{32,33},{64,65},{96,97},{9,8},... | collective-permute-start | bytes 49160 | tf_op jit(solution)/shard_map/ppermute | solution.py:44
  70.0 5.1 %collective-permute-start.16 = (f32[8,128]{1,0:T(8,128)S(1)}, f32[8,128]{1,0:T(8,128)S(1)}, u32[]{:S(2)}, u32[]{:S(2)}) collective-permute-start(f32[8,128]{1,0:T(8,128)S(1)} %get-tuple-element.47), channel_id=1, source_target_pairs={{6,0},{56,32},{70,64},{120,96},{7,1},{57,33},{71,65},{121,97},{14,... | collective-permute-start | bytes 12296 | tf_op jit(solution)/shard_map/ppermute | solution.py:44
  71.6 3.6 %collective-permute-start.17 = (f32[8,128]{1,0:T(8,128)S(1)}, f32[8,128]{1,0:T(8,128)S(1)}, u32[]{:S(2)}, u32[]{:S(2)}) collective-permute-start(f32[8,128]{1,0:T(8,128)S(1)} %get-tuple-element.47), channel_id=1, source_target_pairs={{2,0},{40,32},{66,64},{104,96},{3,1},{41,33},{67,65},{105,97},{10,... | collective-permute-start | bytes 12296 | tf_op jit(solution)/shard_map/ppermute | solution.py:44
  73.3 5.1 %collective-permute-start.18 = (f32[8,128]{1,0:T(8,128)S(1)}, f32[8,128]{1,0:T(8,128)S(1)}, u32[]{:S(2)}, u32[]{:S(2)}) collective-permute-start(f32[8,128]{1,0:T(8,128)S(1)} %get-tuple-element.47), channel_id=1, source_target_pairs={{4,0},{48,32},{68,64},{112,96},{5,1},{49,33},{69,65},{113,97},{12,... | collective-permute-start | bytes 12296 | tf_op jit(solution)/shard_map/ppermute | solution.py:44
  78.4 4.9 %collective-permute-start.19 = (f32[32,128]{1,0:T(8,128)S(1)}, f32[32,128]{1,0:T(8,128)S(1)}, u32[]{:S(2)}, u32[]{:S(2)}) collective-permute-start(f32[32,128]{1,0:T(8,128)S(1)} %get-tuple-element.58), channel_id=1, source_target_pairs={{24,0},{38,32},{88,64},{102,96},{25,1},{39,33},{89,65},{103,97},{0... | collective-permute-start | bytes 49160 | tf_op jit(solution)/shard_map/ppermute | solution.py:44
  78.4 5.0 %collective-permute-start.20 = (f32[32,128]{1,0:T(8,128)S(1)}, f32[32,128]{1,0:T(8,128)S(1)}, u32[]{:S(2)}, u32[]{:S(2)}) collective-permute-start(f32[32,128]{1,0:T(8,128)S(1)} %get-tuple-element.58), channel_id=1, source_target_pairs={{8,0},{34,32},{72,64},{98,96},{9,1},{35,33},{73,65},{99,97},{16,8}... | collective-permute-start | bytes 49160 | tf_op jit(solution)/shard_map/ppermute | solution.py:44
  81.7 5.2 %collective-permute-start.21 = (f32[32,128]{1,0:T(8,128)S(1)}, f32[32,128]{1,0:T(8,128)S(1)}, u32[]{:S(2)}, u32[]{:S(2)}) collective-permute-start(f32[32,128]{1,0:T(8,128)S(1)} %get-tuple-element.58), channel_id=1, source_target_pairs={{16,0},{36,32},{80,64},{100,96},{17,1},{37,33},{81,65},{101,97},{2... | collective-permute-start | bytes 49160 | tf_op jit(solution)/shard_map/ppermute | solution.py:44
  92.1 2.7 %collective-permute-start.22 = (bf16[1024,512]{1,0:T(8,128)(2,1)S(1)}, bf16[1024,512]{1,0:T(8,128)(2,1)S(1)}, u32[]{:S(2)}, u32[]{:S(2)}) collective-permute-start(bf16[1024,512]{1,0:T(8,128)(2,1)S(1)} %grads_core.1), channel_id=1, source_target_pairs={{32,0},{0,32},{96,64},{64,96},{33,1},{1,33},{97,65},{65,97},{40,8}... | collective-permute-start | bytes 3145736 | tf_op jit(solution)/shard_map/ppermute | solution.py:44
  94.9 7.7 %collective-permute-start.23 = (bf16[256,512]{1,0:T(8,128)(2,1)S(1)}, bf16[256,512]{1,0:T(8,128)(2,1)S(1)}, u32[]{:S(2)}, u32[]{:S(2)}) collective-permute-start(bf16[256,512]{1,0:T(8,128)(2,1)S(1)} %far.1), channel_id=1, source_target_pairs={{65,0},{96,32},{0,64},{33,96},{64,1},{97,33},{1,65},{32,97},{73,8}... | collective-permute-start | bytes 786440 | tf_op jit(solution)/shard_map/ppermute | solution.py:44
  103.2 7.7 %collective-permute-start.24 = (bf16[256,512]{1,0:T(8,128)(2,1)S(1)}, bf16[256,512]{1,0:T(8,128)(2,1)S(1)}, u32[]{:S(2)}, u32[]{:S(2)}) collective-permute-start(bf16[256,512]{1,0:T(8,128)(2,1)S(1)} %get-tuple-element.53), channel_id=1, source_target_pairs={{65,0},{97,32},{0,64},{32,96},{64,1},{96,33},{1,65},{33,97},{73,8}... | collective-permute-start | bytes 786440 | tf_op jit(solution)/shard_map/ppermute | solution.py:44
  103.3 7.6 %copy-start.1 = (bf16[256,512]{1,0:T(8,128)(2,1)S(1)}, bf16[256,512]{1,0:T(8,128)(2,1)}, u32[]{:S(2)}) copy-start(bf16[256,512]{1,0:T(8,128)(2,1)} %z_ref.3) | copy-start | bytes 786436
  103.3 7.6 %collective-permute-start.25 = (bf16[256,512]{1,0:T(8,128)(2,1)S(1)}, bf16[256,512]{1,0:T(8,128)(2,1)S(1)}, u32[]{:S(2)}, u32[]{:S(2)}) collective-permute-start(bf16[256,512]{1,0:T(8,128)(2,1)S(1)} %get-tuple-element.55), channel_id=1, source_target_pairs={{64,0},{96,32},{1,64},{33,96},{65,1},{97,33},{0,65},{32,97},{72,8}... | collective-permute-start | bytes 786440 | tf_op jit(solution)/shard_map/ppermute | solution.py:44

commit v2 on v1

--- a/solution.py
+++ b/solution.py
@@ -143,7 +143,7 @@
             for start, stop in ranges:
                 s = lax.dot_general(rows[start:stop], cols, NT, preferred_element_type=F32)
                 e = jnp.exp2(s * EXP_SCALE)
-                if first and start == 0:
+                if first and n == 0 and start == 0:
                     i = lax.broadcasted_iota(jnp.int32, (ROWS, ROWS), 0)
                     j = lax.broadcasted_iota(jnp.int32, (ROWS, ROWS), 1)
                     own = jnp.where(i == j + m * ROWS, 0.0, e[:ROWS])
@@ -280,22 +280,36 @@
     )(raw, core)
 
 
-def near_kernel(info_ref, raw_ref, far_ref, up_ref, down_ref):
-    far = far_ref[...].astype(F32)
-    zero = jnp.zeros_like(far)
-    up_ref[...] = (raw_ref[:ROWS] + jnp.where(info_ref[3] == 0, far, zero)).astype(BF16)
-    down_ref[...] = (raw_ref[ROWS:] + jnp.where(info_ref[3] == 0, zero, far)).astype(BF16)
-
-
-def make_near(info, raw, far):
-    return pl.pallas_call(
-        near_kernel,
-        out_shape=(jax.ShapeDtypeStruct((ROWS, E), BF16), jax.ShapeDtypeStruct((ROWS, E), BF16)),
-        in_specs=[smem(), vmem(), vmem()],
+def pick_kernel(info_ref, raw_ref, free_ref, held_ref):
+    up, down = raw_ref[:ROWS], raw_ref[ROWS:]
+    free_ref[...] = jnp.where(info_ref[3] == 0, down, up).astype(BF16)
+    held_ref[...] = jnp.where(info_ref[3] == 0, up, down)
+
+
+def make_pick(info, raw):
+    return pl.pallas_call(
+        pick_kernel,
+        out_shape=(jax.ShapeDtypeStruct((ROWS, E), BF16), jax.ShapeDtypeStruct((ROWS, E), F32)),
+        in_specs=[smem(), vmem()],
         out_specs=(vmem(), vmem()),
         compiler_params=params(4),
-        name="near",
-    )(info, raw, far)
+        name="pick",
+    )(info, raw)
+
+
+def pass_kernel(held_ref, far_ref, out_ref):
+    out_ref[...] = (held_ref[...] + far_ref[...].astype(F32)).astype(BF16)
+
+
+def make_pass(held, far):
+    return pl.pallas_call(
+        pass_kernel,
+        out_shape=jax.ShapeDtypeStruct((ROWS, E), BF16),
+        in_specs=[vmem(), vmem()],
+        out_specs=vmem(),
+        compiler_params=params(4),
+        name="pass",
+    )(held, far)
 
 
 def final_kernel(info_ref, z_ref, mates_ref, own_ref, below_ref, above_ref, plane_ref, grad_ref, loss_ref):
@@ -334,18 +348,21 @@
     z_before, z_after = get(unit, z=-1), get(unit, z=1)
     before, next_ = lax.optimization_barrier((before, next_))
     far = get(before, first=-1)
-    line = jnp.concatenate([unit, before, next_, far], axis=0)
-    line_before, line_after = get(line, second=-1), get(line, second=1)
-    near = jnp.concatenate([after(unit, far), z_after, z_before], axis=0)
+    near = jnp.concatenate([unit, z_after, z_before], axis=0)
+    line0 = jnp.concatenate([after(unit, near), before], axis=0)
+    line1 = jnp.concatenate([after(next_, near), far], axis=0)
+    before0, after0 = get(line0, second=-1), get(line0, second=1)
+    before1, after1 = get(line1, second=-1), get(line1, second=1)
     near = [near, get(near, core=1)]
-    z_far = get(jnp.where(core_id == 0, after(z_before, line), after(z_after, line)), z_own=-1)
+    z_far = get(jnp.where(core_id == 0, after(z_before, line1), after(z_after, line1)), z_own=-1)
 
     mates, positive = make_mates(unit, partner)
-    chain = make_exps(info, near, [line], (0,), (), None, None, "exps0")
-    far0 = get(after(line_before, line_after, chain[0])[: 2 * ROWS], second=-1)
-    far1 = get(after(line_after, line_before, chain[0])[2 * ROWS :], second=1)
+    chain = make_exps(info, near, [line0, line1], (0, 1), (), None, None, "exps0")
+    far0 = get(after(before0, chain[0]), second=-1)
+    far1 = get(after(after1, chain[0]), second=1)
     rows = near + [z_far, get(after(z_far, chain[0]), core=1)]
-    chain = make_exps(info, rows, [line, line_before, line_after], (0, 2, 4), (0,), chain, None, "exps1")
+    cols = [line0, line1, before0, after0, before1, after1]
+    chain = make_exps(info, rows, cols, (0, 1, 2, 4, 3, 5), (0, 1), chain, None, "exps1")
     sums, exps, units = make_exps(info, rows, [far0, far1], (6, 7), (), chain, positive, "exps2")
 
     sums = sums + get(sums, core=1)
@@ -359,10 +376,12 @@
     far = make_far(raw, core)
     passed = get(far, z_own=-1)
     raw = make_grads(ROWS, 2 * ROWS, F32, after(info, far), plane, arow, exps, units, core, "grads_near")
-    up, down = make_near(info, raw, passed)
-    below, above = get(up, z=-1), get(down, z=1)
-    own = make_grads(0, ROWS, F32, after(info, up), plane, arow, exps, units, core, "grads_own")
-    grad, loss = make_final(info, embeds, mates, own, below, above, plane)
+    free, held = make_pick(info, raw)
+    one = get(free, z_own=1)
+    held = make_pass(held, passed)
+    other = get(held, z_own=-1)
+    own = make_grads(0, ROWS, F32, after(info, held), plane, arow, exps, units, core, "grads_own")
+    grad, loss = make_final(info, embeds, mates, own, one, other, plane)
     return (loss[0, 0], grad)
 
 

time: 113 us -> 107 us (0.947)
  waiting for transfers between devices: 45.2 us -> 40.1 us
  starting transfers between devices: 31 us -> 33.5 us
  local copies, waits for them, and re-layouts: 3.17 us -> 1.04 us
    ppermute x26 -> x28, waiting for transfers between devices: 45.2 us -> 40.1 us  [get(): return lax.ppermute(value, AXES, pairs)]
    ppermute x26 -> x28, starting transfers between devices: 31 us -> 33.5 us  [get(): return lax.ppermute(value, AXES, pairs)]
    slice x2 -> x0, local copies, waits for them, and re-layouts: 2.15 us -> none  [the longest x1 1.08 us: per_device(): far1 = get(after(line_after, line_before, chain[0])[2 * ROWS:], second=1)]
  transfers between devices with their start and end apart: 26 -> 28, of which waited for: 19 -> 16; matrix products, arithmetic and copies ran while one was open for 2% -> 0% of each run, Pallas kernels for 17% -> 18%
where the time goes in v2:
time: 107 us
  waiting for transfers between devices  40.1 us (37%)
  starting transfers between devices  33.5 us (31%)
  Pallas kernels  31.1 us (29%)
    ppermute x28, waiting for transfers between devices, get(): return lax.ppermute(value, AXES, pairs)  40.1 us
    ppermute x28, starting transfers between devices, get(): return lax.ppermute(value, AXES, pairs)  33.5 us
    pallas_call x3, Pallas kernels, make_exps(): pl.pallas_call(functools.partial(exps_kernel, places, olds, first, last),...  15.8 us
    pallas_call x4, Pallas kernels, make_grads(): pl.pallas_call(functools.partial(grads_kernel, first, count, adds), out_s...  11.6 us
  transfers between devices with their start and end apart: 28, of which 16 were waited for; matrix products, arithmetic and copies ran while one was open for 0% of the time, Pallas kernels for 18%

profile of v2, /device:TPU:0, one launch (start us, length us, event | category | flops | bytes accessed | tf_op | source)
XLA Modules:
  0.0 106.9 jit_solution(4451044916415413399)
XLA Ops:
  1.7 4.2 %collective-permute-start = (bf16[256,512]{1,0:T(8,128)(2,1)S(1)}, bf16[256,512]{1,0:T(8,128)(2,1)S(1)}, u32[]{:S(2)}, u32[]{:S(2)}) collective-permute-start(bf16[256,512]{1,0:T(8,128)(2,1)S(1)} %unit.1.unit_ref), channel_id=1, source_target_pairs={{64,0},{96,32},{1,64},{33,96},{65,1},{97,33},{0,65},{32,97},{72,8}... | collective-permute-start | bytes 786440 | tf_op jit(solution)/shard_map/ppermute | solution.py:44
  5.9 1.5 %collective-permute-start.3 = (bf16[256,512]{1,0:T(8,128)(2,1)S(1)}, bf16[256,512]{1,0:T(8,128)(2,1)S(1)}, u32[]{:S(2)}, u32[]{:S(2)}) collective-permute-start(bf16[256,512]{1,0:T(8,128)(2,1)S(1)} %unit.1.unit_ref), channel_id=1, source_target_pairs={{6,0},{56,32},{70,64},{120,96},{7,1},{57,33},{71,65},{121,97},{14,... | collective-permute-start | bytes 786440 | tf_op jit(solution)/shard_map/ppermute | solution.py:44
  7.4 1.7 %collective-permute-start.4 = (bf16[256,512]{1,0:T(8,128)(2,1)S(1)}, bf16[256,512]{1,0:T(8,128)(2,1)S(1)}, u32[]{:S(2)}, u32[]{:S(2)}) collective-permute-start(bf16[256,512]{1,0:T(8,128)(2,1)S(1)} %unit.1.unit_ref), channel_id=1, source_target_pairs={{2,0},{40,32},{66,64},{104,96},{3,1},{41,33},{67,65},{105,97},{10,... | collective-permute-start | bytes 786440 | tf_op jit(solution)/shard_map/ppermute | solution.py:44
  9.2 2.3 %collective-permute-done = bf16[256,512]{1,0:T(8,128)(2,1)S(1)} collective-permute-done((bf16[256,512]{1,0:T(8,128)(2,1)S(1)}, bf16[256,512]{1,0:T(8,128)(2,1)S(1)}, u32[]{:S(2)}, u32[]{:S(2)}) %collective-permute-start) | collective-permute-done | bytes 262176 | tf_op jit(solution)/shard_map/ppermute | solution.py:44
  11.5 3.4 %collective-permute-done.1 = bf16[256,512]{1,0:T(8,128)(2,1)S(1)} collective-permute-done((bf16[256,512]{1,0:T(8,128)(2,1)S(1)}, bf16[256,512]{1,0:T(8,128)(2,1)S(1)}, u32[]{:S(2)}, u32[]{:S(2)}) %collective-permute-start.1) | collective-permute-done | bytes 262176 | tf_op jit(solution)/shard_map/ppermute | solution.py:44
  15.1 1.6 %collective-permute-start.5 = (bf16[256,512]{1,0:T(8,128)(2,1)S(1)}, bf16[256,512]{1,0:T(8,128)(2,1)S(1)}, u32[]{:S(2)}, u32[]{:S(2)}) collective-permute-start(bf16[256,512]{1,0:T(8,128)(2,1)S(1)} %collective-permute-done.3), channel_id=1, source_target_pairs={{6,0},{56,32},{70,64},{120,96},{7,1},{57,33},{71,65},{121,97},{14,... | collective-permute-start | bytes 786440 | tf_op jit(solution)/shard_map/ppermute | solution.py:44
  16.7 1.6 %collective-permute-start.8 = (bf16[512,512]{1,0:T(8,128)(2,1)S(1)}, bf16[512,512]{1,0:T(8,128)(2,1)S(1)}, u32[]{:S(2)}, u32[]{:S(2)}) collective-permute-start(bf16[512,512]{1,0:T(8,128)(2,1)S(1)} %constant_dynamic-update-slice_fusion.2.refs_3_.refs_5_), channel_id=1, source_target_pairs={{24,0},{38,32},{88,64},{102,96},{25,1},{39,33},{89,65},{103,97},{0... | collective-permute-start | bytes 1572872 | tf_op jit(solution)/shard_map/ppermute | solution.py:44
  18.3 1.7 %collective-permute-start.12 = (bf16[512,512]{1,0:T(8,128)(2,1)S(1)}, bf16[512,512]{1,0:T(8,128)(2,1)S(1)}, u32[]{:S(2)}, u32[]{:S(2)}) collective-permute-start(bf16[512,512]{1,0:T(8,128)(2,1)S(1)} %constant_dynamic-update-slice_fusion.2.refs_3_.refs_5_), channel_id=1, source_target_pairs={{8,0},{34,32},{72,64},{98,96},{9,1},{35,33},{73,65},{99,97},{16,8}... | collective-permute-start | bytes 1572872 | tf_op jit(solution)/shard_map/ppermute | solution.py:44
  20.0 4.7 %collective-permute-done.5 = bf16[256,512]{1,0:T(8,128)(2,1)S(1)} collective-permute-done((bf16[256,512]{1,0:T(8,128)(2,1)S(1)}, bf16[256,512]{1,0:T(8,128)(2,1)S(1)}, u32[]{:S(2)}, u32[]{:S(2)}) %collective-permute-start.5) | collective-permute-done | bytes 262176 | tf_op jit(solution)/shard_map/ppermute | solution.py:44
  24.7 3.8 %collective-permute-start.10 = (bf16[512,512]{1,0:T(8,128)(2,1)S(1)}, bf16[512,512]{1,0:T(8,128)(2,1)S(1)}, u32[]{:S(2)}, u32[]{:S(2)}) collective-permute-start(bf16[512,512]{1,0:T(8,128)(2,1)S(1)} %constant_dynamic-update-slice_fusion.refs_4_.refs_6_), channel_id=1, source_target_pairs={{8,0},{34,32},{72,64},{98,96},{9,1},{35,33},{73,65},{99,97},{16,8}... | collective-permute-start | bytes 1572872 | tf_op jit(solution)/shard_map/ppermute | solution.py:44
  28.8 3.3 %exps0.1 = (f32[2048,128]{1,0:T(8,128)S(1)}, bf16[2048,4096]{1,0:T(8,128)(2,1)S(1)}, bf16[4096,512]{1,0:T(8,128)(2,1)S(1)}) custom-call(s32[4]{0:T(128)S(1)} %pad_add_fusion.refs_0_.info_ref, bf16[768,512]{1,0:T(8,128)(2,1)S(1)} %pad_maximum_fusion.refs_1_, bf16[768,512]{1,0:T(8,128)(2,1)S(1)} %collective-permute-done.2.refs_2_, ...), custom_call_target="tpu_custom_call" | custom-call | flops 2147483648 | bytes 1048576 | tf_op jit(solution)/shard_map/exps0/pallas_call | solution.py:174
  32.1 4.2 %collective-permute-done.6.refs_3_ = bf16[256,512]{1,0:T(8,128)(2,1)S(1)} collective-permute-done((bf16[256,512]{1,0:T(8,128)(2,1)S(1)}, bf16[256,512]{1,0:T(8,128)(2,1)S(1)}, u32[]{:S(2)}, u32[]{:S(2)}) %collective-permute-start.6) | collective-permute-done | bytes 262176 | tf_op jit(solution)/shard_map/ppermute | solution.py:44
  36.6 3.2 %collective-permute-start.11 = (bf16[512,512]{1,0:T(8,128)(2,1)S(1)}, bf16[512,512]{1,0:T(8,128)(2,1)S(1)}, u32[]{:S(2)}, u32[]{:S(2)}) collective-permute-start(bf16[512,512]{1,0:T(8,128)(2,1)S(1)} %collective-permute-done.10.refs_10_), channel_id=1, source_target_pairs={{8,0},{34,32},{72,64},{98,96},{9,1},{35,33},{73,65},{99,97},{16,8}... | collective-permute-start | bytes 1572872 | tf_op jit(solution)/shard_map/ppermute | solution.py:44
  39.9 8.3 %exps1.1 = (f32[2048,128]{1,0:T(8,128)S(1)}, bf16[2048,4096]{1,0:T(8,128)(2,1)S(1)}, bf16[4096,512]{1,0:T(8,128)(2,1)S(1)}) custom-call(s32[4]{0:T(128)S(1)} %pad_add_fusion.refs_0_.info_ref, bf16[768,512]{1,0:T(8,128)(2,1)S(1)} %pad_maximum_fusion.refs_1_, ...), custom_call_target="tpu_custom_call", output_to_operand_aliasing={{1}: (12, {}), {2}: (13, {})} | custom-call | flops 6442450944 | bytes 3145728 | tf_op jit(solution)/shard_map/exps1/pallas_call | solution.py:174
  48.2 2.0 %collective-permute-done.9.refs_5_ = bf16[512,512]{1,0:T(8,128)(2,1)S(1)} collective-permute-done((bf16[512,512]{1,0:T(8,128)(2,1)S(1)}, bf16[512,512]{1,0:T(8,128)(2,1)S(1)}, u32[]{:S(2)}, u32[]{:S(2)}) %collective-permute-start.9) | collective-permute-done | bytes 524320 | tf_op jit(solution)/shard_map/ppermute | solution.py:44
  50.2 4.1 %exps2.1 = (f32[16,256]{1,0:T(8,128)S(1)}, bf16[2048,4096]{1,0:T(8,128)(2,1)S(1)}, bf16[4096,512]{1,0:T(8,128)(2,1)S(1)}) custom-call(s32[4]{0:T(128)S(1)} %pad_add_fusion.refs_0_.info_ref, bf16[768,512]{1,0:T(8,128)(2,1)S(1)} %pad_maximum_fusion.refs_1_, ...), custom_call_target="tpu_custom_call", output_to_operand_aliasing={{1}: (8, {}), {2}: (9, {})} | custom-call | flops 2147483648 | bytes 1048576 | tf_op jit(solution)/shard_map/exps2/pallas_call | solution.py:174
  55.6 3.2 %collective-permute-start.16 = (f32[16,256]{1,0:T(8,128)S(1)}, f32[16,256]{1,0:T(8,128)S(1)}, u32[]{:S(2)}, u32[]{:S(2)}) collective-permute-start(f32[16,256]{1,0:T(8,128)S(1)} %add.7.own_ref), channel_id=1, source_target_pairs={{64,0},{96,32},{1,64},{33,96},{65,1},{97,33},{0,65},{32,97},{72,8}... | collective-permute-start | bytes 49160 | tf_op jit(solution)/shard_map/ppermute | solution.py:44
  58.9 1.7 %collective-permute-done.15.before_ref = f32[16,256]{1,0:T(8,128)S(1)} collective-permute-done((f32[16,256]{1,0:T(8,128)S(1)}, f32[16,256]{1,0:T(8,128)S(1)}, u32[]{:S(2)}, u32[]{:S(2)}) %collective-permute-start.15) | collective-permute-done | bytes 16416 | tf_op jit(solution)/shard_map/ppermute | solution.py:44
  60.6 3.5 %collective-permute-done.17.far_ref = f32[16,256]{1,0:T(8,128)S(1)} collective-permute-done((f32[16,256]{1,0:T(8,128)S(1)}, f32[16,256]{1,0:T(8,128)S(1)}, u32[]{:S(2)}, u32[]{:S(2)}) %collective-permute-start.17) | collective-permute-done | bytes 16416 | tf_op jit(solution)/shard_map/ppermute | solution.py:44
  65.3 2.9 %collective-permute-start.19 = (f32[8,128]{1,0:T(8,128)S(1)}, f32[8,128]{1,0:T(8,128)S(1)}, u32[]{:S(2)}, u32[]{:S(2)}) collective-permute-start(f32[8,128]{1,0:T(8,128)S(1)} %get-tuple-element.49), channel_id=1, source_target_pairs={{2,0},{40,32},{66,64},{104,96},{3,1},{41,33},{67,65},{105,97},{10,... | collective-permute-start | bytes 12296 | tf_op jit(solution)/shard_map/ppermute | solution.py:44
  69.8 3.5 %collective-permute-done.20 = f32[8,128]{1,0:T(8,128)S(1)} collective-permute-done((f32[8,128]{1,0:T(8,128)S(1)}, f32[8,128]{1,0:T(8,128)S(1)}, u32[]{:S(2)}, u32[]{:S(2)}) %collective-permute-start.20) | collective-permute-done | bytes 4128 | tf_op jit(solution)/shard_map/ppermute | solution.py:44
  73.3 3.2 %collective-permute-start.22 = (f32[32,128]{1,0:T(8,128)S(1)}, f32[32,128]{1,0:T(8,128)S(1)}, u32[]{:S(2)}, u32[]{:S(2)}) collective-permute-start(f32[32,128]{1,0:T(8,128)S(1)} %get-tuple-element.60), channel_id=1, source_target_pairs={{8,0},{34,32},{72,64},{98,96},{9,1},{35,33},{73,65},{99,97},{16,8}... | collective-permute-start | bytes 49160 | tf_op jit(solution)/shard_map/ppermute | solution.py:44
  76.6 1.7 %collective-permute-done.21 = f32[32,128]{1,0:T(8,128)S(1)} collective-permute-done((f32[32,128]{1,0:T(8,128)S(1)}, f32[32,128]{1,0:T(8,128)S(1)}, u32[]{:S(2)}, u32[]{:S(2)}) %collective-permute-start.21) | collective-permute-done | bytes 16416 | tf_op jit(solution)/shard_map/ppermute | solution.py:44
  78.3 3.5 %collective-permute-done.23 = f32[32,128]{1,0:T(8,128)S(1)} collective-permute-done((f32[32,128]{1,0:T(8,128)S(1)}, f32[32,128]{1,0:T(8,128)S(1)}, u32[]{:S(2)}, u32[]{:S(2)}) %collective-permute-start.23) | collective-permute-done | bytes 16416 | tf_op jit(solution)/shard_map/ppermute | solution.py:44
  81.8 5.2 %grads_core.1 = bf16[1024,512]{1,0:T(8,128)(2,1)S(1)} custom-call(s32[4]{0:T(128)S(1)} %pad_add_fusion.refs_0_.info_ref, f32[128,128]{1,0:T(8,128)S(1)} %constant_dynamic-update-slice_fusion.8.plane_ref, bf16[2048,128]{1,0:T(8,128)(2,1)S(1)} %get-tuple-element.50.arow_ref, bf16[2048,4096]{1,0:T(8,128)(2,1)S(1)} %get-tuple-element.51.exps_ref, ...), custom_call_target="tpu_custom_call" | custom-call | flops 4294967296 | bytes 12582912 | tf_op jit(solution)/shard_map/grads_core/pallas_call | solution.py:253
  87.1 1.8 %grads_far.1.raw_ref = f32[256,512]{1,0:T(8,128)S(1)} custom-call(s32[4]{0:T(128)S(1)} %pad_add_fusion.refs_0_.info_ref, f32[128,128]{1,0:T(8,128)S(1)} %constant_dynamic-update-slice_fusion.8.plane_ref, bf16[2048,128]{1,0:T(8,128)(2,1)S(1)} %get-tuple-element.50.arow_ref, bf16[2048,4096]{1,0:T(8,128)(2,1)S(1)} %get-tuple-element.51.exps_ref, ...), custom_call_target="tpu_custom_call" | custom-call | flops 1073741824 | bytes 6291456 | tf_op jit(solution)/shard_map/grads_far/pallas_call | solution.py:253
  89.9 2.9 %grads_near.1.raw_ref = f32[512,512]{1,0:T(8,128)S(1)} custom-call(s32[4]{0:T(128)S(1)} %pad_add_fusion.refs_0_.info_ref, f32[128,128]{1,0:T(8,128)S(1)} %constant_dynamic-update-slice_fusion.8.plane_ref, bf16[2048,128]{1,0:T(8,128)(2,1)S(1)} %get-tuple-element.50.arow_ref, bf16[2048,4096]{1,0:T(8,128)(2,1)S(1)} %get-tuple-element.51.exps_ref, ...), custom_call_target="tpu_custom_call" | custom-call | flops 2147483648 | bytes 8388608 | tf_op jit(solution)/shard_map/grads_near/pallas_call | solution.py:253
  93.4 3.3 %collective-permute-start.26 = (bf16[256,512]{1,0:T(8,128)(2,1)S(1)}, bf16[256,512]{1,0:T(8,128)(2,1)S(1)}, u32[]{:S(2)}, u32[]{:S(2)}) collective-permute-start(bf16[256,512]{1,0:T(8,128)(2,1)S(1)} %get-tuple-element.57), channel_id=1, source_target_pairs={{64,0},{97,32},{1,64},{32,96},{65,1},{96,33},{0,65},{33,97},{72,8}... | collective-permute-start | bytes 786440 | tf_op jit(solution)/shard_map/ppermute | solution.py:44
  97.6 1.8 %grads_own.1.own_ref = f32[256,512]{1,0:T(8,128)S(1)} custom-call(s32[4]{0:T(128)S(1)} %pad_add_fusion.refs_0_.info_ref, f32[128,128]{1,0:T(8,128)S(1)} %constant_dynamic-update-slice_fusion.8.plane_ref, bf16[2048,128]{1,0:T(8,128)(2,1)S(1)} %get-tuple-element.50.arow_ref, bf16[2048,4096]{1,0:T(8,128)(2,1)S(1)} %get-tuple-element.51.exps_ref, ...), custom_call_target="tpu_custom_call" | custom-call | flops 1073741824 | bytes 6291456 | tf_op jit(solution)/shard_map/grads_own/pallas_call | solution.py:253
  99.4 3.2 %collective-permute-done.26.below_ref = bf16[256,512]{1,0:T(8,128)(2,1)S(1)} collective-permute-done((bf16[256,512]{1,0:T(8,128)(2,1)S(1)}, bf16[256,512]{1,0:T(8,128)(2,1)S(1)}, u32[]{:S(2)}, u32[]{:S(2)}) %collective-permute-start.26) | collective-permute-done | bytes 262176 | tf_op jit(solution)/shard_map/ppermute | solution.py:44
  102.6 2.6 %collective-permute-done.27.above_ref = bf16[256,512]{1,0:T(8,128)(2,1)S(1)} collective-permute-done((bf16[256,512]{1,0:T(8,128)(2,1)S(1)}, bf16[256,512]{1,0:T(8,128)(2,1)S(1)}, u32[]{:S(2)}, u32[]{:S(2)}) %collective-permute-start.27) | collective-permute-done | bytes 262176 | tf_op jit(solution)/shard_map/ppermute | solution.py:44
  105.2 1.7 %final.1 = (f32[256,512]{1,0:T(8,128)}, f32[1,1]{1,0:T(1,128)}) custom-call(s32[4]{0:T(128)S(1)} %pad_add_fusion.refs_0_.info_ref, bf16[256,512]{1,0:T(8,128)(2,1)S(1)} %copy-done.1, bf16[256,512]{1,0:T(8,128)(2,1)S(1)} %get-tuple-element.31.mates_ref, f32[256,512]{1,0:T(8,128)S(1)} %grads_own.1.own_ref, ...), custom_call_target="tpu_custom_call" | custom-call | tf_op jit(solution)/shard_map/final/pallas_call | solution.py:331
  (59 shorter events, 8.4 us)
Async XLA Ops:
  0.6 1.0 copy-start
  1.7 9.8 %collective-permute-start = (bf16[256,512]{1,0:T(8,128)(2,1)S(1)}, bf16[256,512]{1,0:T(8,128)(2,1)S(1)}, u32[]{:S(2)}, u32[]{:S(2)}) collective-permute-start(bf16[256,512]{1,0:T(8,128)(2,1)S(1)} %unit.1.unit_ref), channel_id=1, source_target_pairs={{64,0},{96,32},{1,64},{33,96},{65,1},{97,33},{0,65},{32,97},{72,8}... | collective-permute-start | bytes 786440 | tf_op jit(solution)/shard_map/ppermute | solution.py:44
  5.9 9.0 %collective-permute-start.1 = (bf16[256,512]{1,0:T(8,128)(2,1)S(1)}, bf16[256,512]{1,0:T(8,128)(2,1)S(1)}, u32[]{:S(2)}, u32[]{:S(2)}) collective-permute-start(bf16[256,512]{1,0:T(8,128)(2,1)S(1)} %unit.1.unit_ref), channel_id=1, source_target_pairs={{65,0},{97,32},{0,64},{32,96},{64,1},{96,33},{1,65},{33,97},{73,8}... | collective-permute-start | bytes 786440 | tf_op jit(solution)/shard_map/ppermute | solution.py:44
  5.9 9.1 %collective-permute-start.3 = (bf16[256,512]{1,0:T(8,128)(2,1)S(1)}, bf16[256,512]{1,0:T(8,128)(2,1)S(1)}, u32[]{:S(2)}, u32[]{:S(2)}) collective-permute-start(bf16[256,512]{1,0:T(8,128)(2,1)S(1)} %unit.1.unit_ref), channel_id=1, source_target_pairs={{6,0},{56,32},{70,64},{120,96},{7,1},{57,33},{71,65},{121,97},{14,... | collective-permute-start | bytes 786440 | tf_op jit(solution)/shard_map/ppermute | solution.py:44
  7.4 7.7 %collective-permute-start.4 = (bf16[256,512]{1,0:T(8,128)(2,1)S(1)}, bf16[256,512]{1,0:T(8,128)(2,1)S(1)}, u32[]{:S(2)}, u32[]{:S(2)}) collective-permute-start(bf16[256,512]{1,0:T(8,128)(2,1)S(1)} %unit.1.unit_ref), channel_id=1, source_target_pairs={{2,0},{40,32},{66,64},{104,96},{3,1},{41,33},{67,65},{105,97},{10,... | collective-permute-start | bytes 786440 | tf_op jit(solution)/shard_map/ppermute | solution.py:44
  14.9 13.7 %collective-permute-start.2 = (bf16[768,512]{1,0:T(8,128)(2,1)S(1)}, bf16[768,512]{1,0:T(8,128)(2,1)S(1)}, u32[]{:S(2)}, u32[]{:S(2)}) collective-permute-start(bf16[768,512]{1,0:T(8,128)(2,1)S(1)} %pad_maximum_fusion.refs_1_), channel_id=1, source_target_pairs={{32,0},{0,32},{96,64},{64,96},{33,1},{1,33},{97,65},{65,97},{40,8}... | collective-permute-start | bytes 2359304 | tf_op jit(solution)/shard_map/ppermute | solution.py:44
  15.1 9.6 %collective-permute-start.5 = (bf16[256,512]{1,0:T(8,128)(2,1)S(1)}, bf16[256,512]{1,0:T(8,128)(2,1)S(1)}, u32[]{:S(2)}, u32[]{:S(2)}) collective-permute-start(bf16[256,512]{1,0:T(8,128)(2,1)S(1)} %collective-permute-done.3), channel_id=1, source_target_pairs={{6,0},{56,32},{70,64},{120,96},{7,1},{57,33},{71,65},{121,97},{14,... | collective-permute-start | bytes 786440 | tf_op jit(solution)/shard_map/ppermute | solution.py:44
  16.7 23.2 %collective-permute-start.8 = (bf16[512,512]{1,0:T(8,128)(2,1)S(1)}, bf16[512,512]{1,0:T(8,128)(2,1)S(1)}, u32[]{:S(2)}, u32[]{:S(2)}) collective-permute-start(bf16[512,512]{1,0:T(8,128)(2,1)S(1)} %constant_dynamic-update-slice_fusion.2.refs_3_.refs_5_), channel_id=1, source_target_pairs={{24,0},{38,32},{88,64},{102,96},{25,1},{39,33},{89,65},{103,97},{0... | collective-permute-start | bytes 1572872 | tf_op jit(solution)/shard_map/ppermute | solution.py:44
  18.3 21.5 %collective-permute-start.12 = (bf16[512,512]{1,0:T(8,128)(2,1)S(1)}, bf16[512,512]{1,0:T(8,128)(2,1)S(1)}, u32[]{:S(2)}, u32[]{:S(2)}) collective-permute-start(bf16[512,512]{1,0:T(8,128)(2,1)S(1)} %constant_dynamic-update-slice_fusion.2.refs_3_.refs_5_), channel_id=1, source_target_pairs={{8,0},{34,32},{72,64},{98,96},{9,1},{35,33},{73,65},{99,97},{16,8}... | collective-permute-start | bytes 1572872 | tf_op jit(solution)/shard_map/ppermute | solution.py:44
  24.7 11.5 %copy-start.2 = (s32[256]{0:T(256)S(1)}, s32[256]{0:T(256)}, u32[]{:S(2)}) copy-start(s32[256]{0:T(256)} %param.3) | copy-start | bytes 3076
  24.7 11.9 %collective-permute-start.10 = (bf16[512,512]{1,0:T(8,128)(2,1)S(1)}, bf16[512,512]{1,0:T(8,128)(2,1)S(1)}, u32[]{:S(2)}, u32[]{:S(2)}) collective-permute-start(bf16[512,512]{1,0:T(8,128)(2,1)S(1)} %constant_dynamic-update-slice_fusion.refs_4_.refs_6_), channel_id=1, source_target_pairs={{8,0},{34,32},{72,64},{98,96},{9,1},{35,33},{73,65},{99,97},{16,8}... | collective-permute-start | bytes 1572872 | tf_op jit(solution)/shard_map/ppermute | solution.py:44
  28.6 11.3 %collective-permute-start.13 = (bf16[512,512]{1,0:T(8,128)(2,1)S(1)}, bf16[512,512]{1,0:T(8,128)(2,1)S(1)}, u32[]{:S(2)}, u32[]{:S(2)}) collective-permute-start(bf16[512,512]{1,0:T(8,128)(2,1)S(1)} %constant_dynamic-update-slice_fusion.refs_4_.refs_6_), channel_id=1, source_target_pairs={{24,0},{38,32},{88,64},{102,96},{25,1},{39,33},{89,65},{103,97},{0... | collective-permute-start | bytes 1572872 | tf_op jit(solution)/shard_map/ppermute | solution.py:44
  28.6 7.7 %collective-permute-start.6 = (bf16[256,512]{1,0:T(8,128)(2,1)S(1)}, bf16[256,512]{1,0:T(8,128)(2,1)S(1)}, u32[]{:S(2)}, u32[]{:S(2)}) collective-permute-start(bf16[256,512]{1,0:T(8,128)(2,1)S(1)} %broadcast_select_fusion), channel_id=1, source_target_pairs={{65,0},{96,32},{0,64},{33,96},{64,1},{97,33},{1,65},{32,97},{73,8}... | collective-permute-start | bytes 786440 | tf_op jit(solution)/shard_map/ppermute | solution.py:44
  36.3 3.6 %collective-permute-start.7 = (bf16[256,512]{1,0:T(8,128)(2,1)S(1)}, bf16[256,512]{1,0:T(8,128)(2,1)S(1)}, u32[]{:S(2)}, u32[]{:S(2)}) collective-permute-start(bf16[256,512]{1,0:T(8,128)(2,1)S(1)} %collective-permute-done.6.refs_3_), channel_id=1, source_target_pairs={{32,0},{0,32},{96,64},{64,96},{33,1},{1,33},{97,65},{65,97},{40,8}... | collective-permute-start | bytes 786440 | tf_op jit(solution)/shard_map/ppermute | solution.py:44
  36.6 11.6 %collective-permute-start.11 = (bf16[512,512]{1,0:T(8,128)(2,1)S(1)}, bf16[512,512]{1,0:T(8,128)(2,1)S(1)}, u32[]{:S(2)}, u32[]{:S(2)}) collective-permute-start(bf16[512,512]{1,0:T(8,128)(2,1)S(1)} %collective-permute-done.10.refs_10_), channel_id=1, source_target_pairs={{8,0},{34,32},{72,64},{98,96},{9,1},{35,33},{73,65},{99,97},{16,8}... | collective-permute-start | bytes 1572872 | tf_op jit(solution)/shard_map/ppermute | solution.py:44
  39.8 10.4 %collective-permute-start.9 = (bf16[512,512]{1,0:T(8,128)(2,1)S(1)}, bf16[512,512]{1,0:T(8,128)(2,1)S(1)}, u32[]{:S(2)}, u32[]{:S(2)}) collective-permute-start(bf16[512,512]{1,0:T(8,128)(2,1)S(1)} %collective-permute-done.8.refs_7_), channel_id=1, source_target_pairs={{24,0},{38,32},{88,64},{102,96},{25,1},{39,33},{89,65},{103,97},{0... | collective-permute-start | bytes 1572872 | tf_op jit(solution)/shard_map/ppermute | solution.py:44
  54.4 1.3 %collective-permute-start.14 = (f32[16,256]{1,0:T(8,128)S(1)}, f32[16,256]{1,0:T(8,128)S(1)}, u32[]{:S(2)}, u32[]{:S(2)}) collective-permute-start(f32[16,256]{1,0:T(8,128)S(1)} %get-tuple-element.48), channel_id=1, source_target_pairs={{32,0},{0,32},{96,64},{64,96},{33,1},{1,33},{97,65},{65,97},{40,8}... | collective-permute-start | bytes 49160 | tf_op jit(solution)/shard_map/ppermute | solution.py:44
  55.6 4.9 %collective-permute-start.15 = (f32[16,256]{1,0:T(8,128)S(1)}, f32[16,256]{1,0:T(8,128)S(1)}, u32[]{:S(2)}, u32[]{:S(2)}) collective-permute-start(f32[16,256]{1,0:T(8,128)S(1)} %add.7.own_ref), channel_id=1, source_target_pairs={{65,0},{97,32},{0,64},{32,96},{64,1},{96,33},{1,65},{33,97},{73,8}... | collective-permute-start | bytes 49160 | tf_op jit(solution)/shard_map/ppermute | solution.py:44
  55.6 4.9 %collective-permute-start.16 = (f32[16,256]{1,0:T(8,128)S(1)}, f32[16,256]{1,0:T(8,128)S(1)}, u32[]{:S(2)}, u32[]{:S(2)}) collective-permute-start(f32[16,256]{1,0:T(8,128)S(1)} %add.7.own_ref), channel_id=1, source_target_pairs={{64,0},{96,32},{1,64},{33,96},{65,1},{97,33},{0,65},{32,97},{72,8}... | collective-permute-start | bytes 49160 | tf_op jit(solution)/shard_map/ppermute | solution.py:44
  58.9 5.2 %collective-permute-start.17 = (f32[16,256]{1,0:T(8,128)S(1)}, f32[16,256]{1,0:T(8,128)S(1)}, u32[]{:S(2)}, u32[]{:S(2)}) collective-permute-start(f32[16,256]{1,0:T(8,128)S(1)} %add.7.own_ref), channel_id=1, source_target_pairs={{1,0},{33,32},{65,64},{97,96},{0,1},{32,33},{64,65},{96,97},{9,8},... | collective-permute-start | bytes 49160 | tf_op jit(solution)/shard_map/ppermute | solution.py:44
  64.9 4.9 %collective-permute-start.18 = (f32[8,128]{1,0:T(8,128)S(1)}, f32[8,128]{1,0:T(8,128)S(1)}, u32[]{:S(2)}, u32[]{:S(2)}) collective-permute-start(f32[8,128]{1,0:T(8,128)S(1)} %get-tuple-element.49), channel_id=1, source_target_pairs={{6,0},{56,32},{70,64},{120,96},{7,1},{57,33},{71,65},{121,97},{14,... | collective-permute-start | bytes 12296 | tf_op jit(solution)/shard_map/ppermute | solution.py:44
  65.3 4.5 %collective-permute-start.19 = (f32[8,128]{1,0:T(8,128)S(1)}, f32[8,128]{1,0:T(8,128)S(1)}, u32[]{:S(2)}, u32[]{:S(2)}) collective-permute-start(f32[8,128]{1,0:T(8,128)S(1)} %get-tuple-element.49), channel_id=1, source_target_pairs={{2,0},{40,32},{66,64},{104,96},{3,1},{41,33},{67,65},{105,97},{10,... | collective-permute-start | bytes 12296 | tf_op jit(solution)/shard_map/ppermute | solution.py:44
  68.2 5.1 %collective-permute-start.20 = (f32[8,128]{1,0:T(8,128)S(1)}, f32[8,128]{1,0:T(8,128)S(1)}, u32[]{:S(2)}, u32[]{:S(2)}) collective-permute-start(f32[8,128]{1,0:T(8,128)S(1)} %get-tuple-element.49), channel_id=1, source_target_pairs={{4,0},{48,32},{68,64},{112,96},{5,1},{49,33},{69,65},{113,97},{12,... | collective-permute-start | bytes 12296 | tf_op jit(solution)/shard_map/ppermute | solution.py:44
  73.3 4.9 %collective-permute-start.21 = (f32[32,128]{1,0:T(8,128)S(1)}, f32[32,128]{1,0:T(8,128)S(1)}, u32[]{:S(2)}, u32[]{:S(2)}) collective-permute-start(f32[32,128]{1,0:T(8,128)S(1)} %get-tuple-element.60), channel_id=1, source_target_pairs={{24,0},{38,32},{88,64},{102,96},{25,1},{39,33},{89,65},{103,97},{0... | collective-permute-start | bytes 49160 | tf_op jit(solution)/shard_map/ppermute | solution.py:44
  73.3 5.0 %collective-permute-start.22 = (f32[32,128]{1,0:T(8,128)S(1)}, f32[32,128]{1,0:T(8,128)S(1)}, u32[]{:S(2)}, u32[]{:S(2)}) collective-permute-start(f32[32,128]{1,0:T(8,128)S(1)} %get-tuple-element.60), channel_id=1, source_target_pairs={{8,0},{34,32},{72,64},{98,96},{9,1},{35,33},{73,65},{99,97},{16,8}... | collective-permute-start | bytes 49160 | tf_op jit(solution)/shard_map/ppermute | solution.py:44
  76.6 5.2 %collective-permute-start.23 = (f32[32,128]{1,0:T(8,128)S(1)}, f32[32,128]{1,0:T(8,128)S(1)}, u32[]{:S(2)}, u32[]{:S(2)}) collective-permute-start(f32[32,128]{1,0:T(8,128)S(1)} %get-tuple-element.60), channel_id=1, source_target_pairs={{16,0},{36,32},{80,64},{100,96},{17,1},{37,33},{81,65},{101,97},{2... | collective-permute-start | bytes 49160 | tf_op jit(solution)/shard_map/ppermute | solution.py:44
  87.0 2.7 %collective-permute-start.24 = (bf16[1024,512]{1,0:T(8,128)(2,1)S(1)}, bf16[1024,512]{1,0:T(8,128)(2,1)S(1)}, u32[]{:S(2)}, u32[]{:S(2)}) collective-permute-start(bf16[1024,512]{1,0:T(8,128)(2,1)S(1)} %grads_core.1), channel_id=1, source_target_pairs={{32,0},{0,32},{96,64},{64,96},{33,1},{1,33},{97,65},{65,97},{40,8}... | collective-permute-start | bytes 3145736 | tf_op jit(solution)/shard_map/ppermute | solution.py:44
  89.8 7.7 %collective-permute-start.25 = (bf16[256,512]{1,0:T(8,128)(2,1)S(1)}, bf16[256,512]{1,0:T(8,128)(2,1)S(1)}, u32[]{:S(2)}, u32[]{:S(2)}) collective-permute-start(bf16[256,512]{1,0:T(8,128)(2,1)S(1)} %far.1), channel_id=1, source_target_pairs={{65,0},{96,32},{0,64},{33,96},{64,1},{97,33},{1,65},{32,97},{73,8}... | collective-permute-start | bytes 786440 | tf_op jit(solution)/shard_map/ppermute | solution.py:44
  93.4 9.2 %collective-permute-start.26 = (bf16[256,512]{1,0:T(8,128)(2,1)S(1)}, bf16[256,512]{1,0:T(8,128)(2,1)S(1)}, u32[]{:S(2)}, u32[]{:S(2)}) collective-permute-start(bf16[256,512]{1,0:T(8,128)(2,1)S(1)} %get-tuple-element.57), channel_id=1, source_target_pairs={{64,0},{97,32},{1,64},{32,96},{65,1},{96,33},{0,65},{33,97},{72,8}... | collective-permute-start | bytes 786440 | tf_op jit(solution)/shard_map/ppermute | solution.py:44
  97.5 7.7 %copy-start.1 = (bf16[256,512]{1,0:T(8,128)(2,1)S(1)}, bf16[256,512]{1,0:T(8,128)(2,1)}, u32[]{:S(2)}) copy-start(bf16[256,512]{1,0:T(8,128)(2,1)} %z_ref.3) | copy-start | bytes 786436
  97.5 7.7 %collective-permute-start.27 = (bf16[256,512]{1,0:T(8,128)(2,1)S(1)}, bf16[256,512]{1,0:T(8,128)(2,1)S(1)}, u32[]{:S(2)}, u32[]{:S(2)}) collective-permute-start(bf16[256,512]{1,0:T(8,128)(2,1)S(1)} %pass.1), channel_id=1, source_target_pairs={{65,0},{96,32},{0,64},{33,96},{64,1},{97,33},{1,65},{32,97},{73,8}... | collective-permute-start | bytes 786440 | tf_op jit(solution)/shard_map/ppermute | solution.py:44

commit v3 on v1

v3 whole, which is shorter than its diff:
```python
import functools
import math

import jax
import jax.numpy as jnp
from jax import lax
from jax.experimental import pallas as pl
from jax.experimental.pallas import tpu as pltpu
from jax.sharding import Mesh, PartitionSpec as P

INV_TAU = 10.0
EXP_SCALE = INV_TAU * math.log2(math.e)
AXES = ("zlo", "core", "y", "x", "zhi")
SIZES = (2, 2, 4, 4, 2)
OFFSETS = (0, -1, 1, 2)
NT = (((1,), (1,)), ((), ()))
NN = (((1,), (0,)), ((), ()))
ROWS = 256
ALL_ROWS = 2048
COLS = 4096
TILE = 512
MIB = 1024 * 1024
E = 512
BF16 = jnp.bfloat16
F32 = jnp.float32


def place(x, y, z, core):
    return ((((z % 2) * 2 + core) * 4 + y) * 4 + x) * 2 + z // 2


def get(value, z=0, core=0, first=0, second=0, z_own=0):
    pairs = []
    for px in range(4):
        for py in range(4):
            for pz in range(4):
                for pc in range(2):
                    x, y = (first, second) if pc == 0 else (second, first)
                    away = z + (z_own if pc == 0 else -z_own)
                    source = place((px + x) % 4, (py + y) % 4, (pz + away) % 4, pc ^ core)
                    pairs.append((source, place(px, py, pz, pc)))
    return lax.ppermute(value, AXES, pairs)


def ring_sum(own, before, after, far):
    return (own + far) + (before + after)


def after(value, *others):
    return lax.optimization_barrier((value, *others))[0]


def vmem():
    return pl.BlockSpec(memory_space=pltpu.VMEM)


def smem():
    return pl.BlockSpec(memory_space=pltpu.SMEM)


def hbm():
    return pl.BlockSpec(memory_space=pltpu.HBM)


def params(mib):
    return pltpu.CompilerParams(vmem_limit_bytes=mib * MIB)


def block_of(z, core):
    return ((z & 1) * 2 + core) * 2 + lax.shift_right_logical(z, 1)


def row_blocks(info_ref):
    for c in range(2):
        core = info_ref[3] ^ c
        up = 1 - 2 * core
        for k, away in enumerate((0, -up, up, 2)):
            yield (k // 2) * 1024 + c * 512 + (k % 2) * ROWS, block_of((info_ref[2] + away) & 3, core)


def unit_kernel(z_ref, unit_ref):
    zf = z_ref[...].astype(F32)
    recip = lax.rsqrt(jnp.sum(zf * zf, axis=1, keepdims=True) + 1e-06)
    unit_ref[...] = (zf * recip).astype(BF16)


def make_unit(embeds):
    return pl.pallas_call(
        unit_kernel,
        out_shape=jax.ShapeDtypeStruct((ROWS, E), BF16),
        in_specs=[vmem()],
        out_specs=vmem(),
        compiler_params=params(4),
        name="unit",
    )(embeds)


def mates_kernel(unit_ref, partner_ref, mates_ref, positive_ref):
    unit = unit_ref[...]
    ids = lax.broadcasted_iota(jnp.int32, (ROWS, ROWS), 0)
    pick = (ids == (partner_ref[...] & (ROWS - 1))).astype(F32).astype(BF16)
    mates = lax.dot_general(pick, unit, NN, preferred_element_type=F32)
    mates_ref[...] = mates.astype(BF16)
    products = jnp.sum(unit.astype(F32) * mates, axis=0, keepdims=True)
    total = jnp.sum(products, axis=1, keepdims=True) * INV_TAU
    positive_ref[...] = jnp.broadcast_to(total, (1, 128))


def make_mates(unit, partner):
    return pl.pallas_call(
        mates_kernel,
        out_shape=(
            jax.ShapeDtypeStruct((ROWS, E), BF16),
            jax.ShapeDtypeStruct((1, 128), F32),
        ),
        in_specs=[vmem(), vmem()],
        out_specs=(vmem(), vmem()),
        compiler_params=params(4),
        name="mates",
    )(unit, partner.reshape(1, ROWS))


def exps_kernel(places, rows_here, first, last, *refs):
    count = len(places)
    halves = len(rows_here)
    info_ref, refs = refs[0], refs[1:]
    row_refs, col_refs, refs = refs[: 2 * halves], refs[2 * halves : 2 * halves + count], refs[2 * halves + count :]
    if not first:
        before_ref, refs = refs[0], refs[3:]
    if last:
        positive_ref, refs = refs[0], refs[1:]
    sums_ref, exps_ref, unit_ref, rows, sums, line = refs
    for n, ref in enumerate(row_refs):
        start = rows_here[n // 2] * 1024 + (n % 2) * 512
        rows[start : start + 512] = ref[...]
    sums[...] = jnp.zeros_like(sums) if first else before_ref[...]
    part = slice(rows_here[0] * 1024, rows_here[-1] * 1024 + 1024)
    for n, col_ref in enumerate(col_refs):
        if 0 in rows_here:
            start = places[n] * TILE
            unit_ref[start : start + col_ref.shape[0]] = col_ref[...]

        @pl.loop(0, col_ref.shape[0] // ROWS)
        def _(m):
            here = pl.ds(pl.multiple_of(places[n] * TILE + m * ROWS, ROWS), ROWS)
            cols = col_ref[pl.ds(pl.multiple_of(m * ROWS, ROWS), ROWS), :]
            for start in range(part.start, part.stop, ROWS):
                piece = slice(start, start + ROWS)
                s = lax.dot_general(rows[piece], cols, NT, preferred_element_type=F32)
                e = jnp.exp2(s * EXP_SCALE)
                if first and n == 0 and start == 0:
                    i = lax.broadcasted_iota(jnp.int32, (ROWS, ROWS), 0)
                    j = lax.broadcasted_iota(jnp.int32, (ROWS, ROWS), 1)
                    e = jnp.where(i == j + m * ROWS, 0.0, e)
                exps_ref[piece, here] = e.astype(BF16)
                sums[piece] += e[:, :128] + e[:, 128:]

    if last:
        totals = jnp.sum(sums[...].T, axis=0, keepdims=True)
        line[...] = jnp.zeros_like(line)
        for start, at in row_blocks(info_ref):
            line[pl.ds(at, 1), :] = totals[:, start : start + ROWS]
        line[8:9, 0:128] = positive_ref[...]
        sums_ref[...] = line[...]
    else:
        sums_ref[...] = sums[...]


def make_exps(info, rows, rows_here, cols, places, chain, positive, name):
    first, last = chain is None, positive is not None
    count = len(cols)
    tiles = sum(c.shape[0] for c in cols) // TILE
    sums_shape = (16, ROWS) if last else (ALL_ROWS, 128)
    operands = [info, *rows, *cols] + ([] if first else list(chain)) + ([positive] if last else [])
    return pl.pallas_call(
        functools.partial(exps_kernel, places, rows_here, first, last),
        out_shape=(
            jax.ShapeDtypeStruct(sums_shape, F32),
            pltpu.VMEM((ALL_ROWS, COLS), BF16),
            pltpu.VMEM((COLS, E), BF16),
        ),
        in_specs=[smem()] + [vmem()] * (len(operands) - 1),
        out_specs=(vmem(), vmem(), vmem()),
        input_output_aliases={} if first else {2 + len(rows) + count: 1, 3 + len(rows) + count: 2},
        scratch_shapes=[
            pltpu.VMEM((ALL_ROWS, E), BF16),
            pltpu.VMEM((ALL_ROWS, 128), F32),
            pltpu.VMEM((16, ROWS), F32),
        ],
        compiler_params=params(12),
        cost_estimate=pl.CostEstimate(
            flops=2 * len(rows) * 512 * tiles * TILE * E * (8 if len(rows) == 2 else 4),
            bytes_accessed=tiles * TILE * E * 2,
            transcendentals=len(rows) * 512 * tiles * TILE,
        ),
        name=name,
    )(*operands)


def totals_kernel(info_ref, own_ref, before_ref, after_ref, far_ref, arow_ref, message_ref, recips):
    both = ring_sum(own_ref[...], before_ref[...], after_ref[...], far_ref[...])
    total = both[:8]
    recips[...] = 1.0 / total
    logs = jnp.sum(jnp.sum(jnp.log(total), axis=0, keepdims=True), axis=1, keepdims=True)
    loss = jnp.broadcast_to(logs, (1, 128)) - both[8:9, :128]
    for start, at in row_blocks(info_ref):
        line = recips[pl.ds(at, 1), :]
        arow_ref[start : start + ROWS] = jnp.broadcast_to(line, (128, ROWS)).T.astype(BF16)
    own = recips[pl.ds(block_of(info_ref[2], info_ref[3]), 1), :]
    zeros = jnp.zeros((5, 128), F32)
    message_ref[...] = jnp.concatenate([own[:, :128], own[:, 128:], loss, zeros], axis=0)


def make_totals(info, own, before, after, far):
    return pl.pallas_call(
        totals_kernel,
        out_shape=(
            jax.ShapeDtypeStruct((ALL_ROWS, 128), BF16),
            jax.ShapeDtypeStruct((8, 128), F32),
        ),
        in_specs=[smem()] + [vmem()] * 4,
        out_specs=(vmem(), vmem()),
        scratch_shapes=[pltpu.VMEM((8, ROWS), F32)],
        compiler_params=params(4),
        name="totals",
    )(info, own, before, after, far)


def grads_kernel(pieces, adds, info_ref, plane_ref, arow_ref, exps_ref, unit_ref, *refs):
    if adds is not None:
        add_ref, refs = refs[0], refs[1:]
    cols = [plane_ref[8 * (g // 2) + g % 2 : 8 * (g // 2) + g % 2 + 1].astype(BF16) for g in range(COLS // 128)]

    def weights(here):
        a = arow_ref[here]
        return exps_ref[here] * jnp.concatenate([a + col for col in cols], axis=1)

    if adds is None:
        size = pieces[0][1]
        step = pieces[-1][0] - pieces[0][0]

        @pl.loop(0, len(pieces))
        def _(n):
            w = weights(pl.ds(pl.multiple_of(pieces[0][0] + n * step, size), size))
            product = lax.dot_general(w, unit_ref[...], NN, preferred_element_type=F32)
            refs[0][pl.ds(pl.multiple_of(n * size, size), size)] = product.astype(refs[0].dtype)

    else:
        w = jnp.concatenate([weights(slice(start, start + size)) for start, size in pieces], axis=0)
        product = lax.dot_general(w, unit_ref[...], NN, preferred_element_type=F32)
        start = 0
        for (_, size), add, ref in zip(pieces, adds, refs):
            ref[...] = (product[start : start + size] + add_ref[add : add + size].astype(F32)).astype(ref.dtype)
            start += size


def make_grads(pieces, adds, dtypes, info, plane, arow, exps, unit, add, name):
    count = sum(size for _, size in pieces)
    sizes = [count] if adds is None else [size for _, size in pieces]
    exps = pltpu.with_memory_space_constraint(exps, pltpu.VMEM)
    unit = pltpu.with_memory_space_constraint(unit, pltpu.VMEM)
    return pl.pallas_call(
        functools.partial(grads_kernel, pieces, adds),
        out_shape=tuple(jax.ShapeDtypeStruct((size, E), dtype) for size, dtype in zip(sizes, dtypes)),
        in_specs=[smem()] + [vmem()] * (4 if adds is None else 5),
        out_specs=(vmem(),) * len(sizes),
        compiler_params=params(16),
        cost_estimate=pl.CostEstimate(
            flops=2 * count * COLS * E,
            bytes_accessed=COLS * (count + E) * 2,
            transcendentals=0,
        ),
        name=name,
    )(info, plane, arow, exps, unit, *([] if adds is None else [add]))


def pass_kernel(start, held_ref, far_ref, out_ref):
    out_ref[...] = (held_ref[...] + far_ref[start : start + ROWS].astype(F32)).astype(BF16)


def make_pass(held, far, start, name):
    return pl.pallas_call(
        functools.partial(pass_kernel, start),
        out_shape=jax.ShapeDtypeStruct((ROWS, E), BF16),
        in_specs=[vmem(), vmem()],
        out_specs=vmem(),
        compiler_params=params(4),
        name=name,
    )(held, far)


def final_kernel(info_ref, z_ref, mates_ref, own_ref, below_ref, above_ref, plane_ref, grad_ref, loss_ref):
    zf = z_ref[...].astype(F32)
    recip = lax.rsqrt(jnp.sum(zf * zf, axis=1, keepdims=True) + 1e-06)
    unit = zf * recip
    acc = own_ref[...] + below_ref[...].astype(F32) + above_ref[...].astype(F32)
    grad_unit = INV_TAU * (acc - 2.0 * mates_ref[...].astype(F32))
    along = jnp.sum(unit * grad_unit, axis=1, keepdims=True)
    grad_ref[...] = recip * (grad_unit - unit * along)
    parts = [[plane_ref[8 * n + 2 : 8 * n + 3] for n in range(4 * m, 4 * m + 4)] for m in range(4)]
    x_first = ring_sum(*[ring_sum(*line) for line in parts])
    y_first = ring_sum(*[ring_sum(*line) for line in zip(*parts)])
    loss = jnp.where(info_ref[3] == 0, x_first, y_first)
    loss_ref[...] = loss[:, :1] / (ROWS * 128)


def make_final(info, embeds, mates, own, below, above, plane):
    return pl.pallas_call(
        final_kernel,
        out_shape=(jax.ShapeDtypeStruct((ROWS, E), F32), jax.ShapeDtypeStruct((1, 1), F32)),
        in_specs=[smem()] + [vmem()] * 6,
        out_specs=(vmem(), vmem()),
        compiler_params=params(4),
        name="final",
    )(info, embeds, mates, own, below, above, plane)


def per_device(embeds, partner):
    unit = make_unit(embeds)
    core_id = lax.axis_index("core")
    z = lax.axis_index("zhi") * 2 + lax.axis_index("zlo")
    info = jnp.stack([lax.axis_index("x"), lax.axis_index("y"), z, core_id]).astype(jnp.int32)

    z_one = get(unit, z_own=-1)
    before, next_ = get(unit, first=-1), get(unit, first=1)
    before, next_ = lax.optimization_barrier((before, next_))
    far = get(unit, first=2)
    near = jnp.concatenate([unit, z_one], axis=0)
    line0 = jnp.concatenate([after(unit, near), before], axis=0)
    line1 = jnp.concatenate([next_, far], axis=0)
    before0, after0 = get(line0, second=-1), get(line0, second=1)
    before1, after1 = get(line1, second=-1), get(line1, second=1)
    z_two = get(unit, z_own=1)
    z_far = get(z_one, z_own=-1)
    near = [near, get(near, core=1)]

    mates, positive = make_mates(unit, partner)
    chain = make_exps(info, near, (0,), [line0, line1], (0, 1), None, None, "exps0")
    rest = jnp.concatenate([z_two, z_far], axis=0)
    rest = [rest, get(rest, core=1)]
    chain = make_exps(info, rest, (1,), [line0, line1], (0, 1), chain, None, "exps1")
    far0 = get(after(before0, after0, chain[0]), second=-1)
    far1 = get(after(after1, before1, chain[0]), second=1)
    rows = near + rest
    cols = [before0, after0, before1, after1]
    chain = make_exps(info, rows, (0, 1), cols, (2, 4, 3, 5), chain, None, "exps2")
    sums, exps, units = make_exps(info, rows, (0, 1), [far0, far1], (6, 7), chain, positive, "exps3")

    sums = sums + get(sums, core=1)
    arow, plane = make_totals(info, sums, get(sums, z=-1), get(sums, z=1), get(sums, z=2))
    plane = jnp.concatenate([plane] + [get(plane, first=k) for k in OFFSETS[1:]], axis=0)
    plane = jnp.concatenate([plane] + [get(plane, second=k) for k in OFFSETS[1:]], axis=0)

    (theirs,) = make_grads(((512, 512), (1536, 512)), None, (BF16,), info, plane, arow, exps, units, None, "grads_core")
    core = get(theirs, core=1)
    (far,) = make_grads(((1280, ROWS),), None, (F32,), after(info, theirs), plane, arow, exps, units, None, "grads_far")
    far = make_pass(far, core, 768, "pass_far")
    passed = get(far, z_own=-1)
    free, held = make_grads(
        ((256, ROWS), (1024, ROWS)), (256, 512), (BF16, F32), after(info, far), plane, arow, exps, units, core, "grads_near"
    )
    one = get(free, z_own=1)
    held = make_pass(held, passed, 0, "pass_two")
    two = get(held, z_own=-1)
    (own,) = make_grads(((0, ROWS),), (0,), (F32,), after(info, held), plane, arow, exps, units, core, "grads_own")
    grad, loss = make_final(info, embeds, mates, own, one, two, plane)
    return (loss[0, 0], grad)


def solution(mesh):
    torus = Mesh(mesh.devices.reshape(SIZES), AXES)
    return jax.shard_map(
        per_device,
        mesh=torus,
        in_specs=(P(AXES, None), P(AXES)),
        out_specs=(P(), P(AXES, None)),
        check_vma=False,
    )
```

time: 113 us -> 103 us (0.912)
  waiting for transfers between devices: 45.2 us -> 31.3 us
  starting transfers between devices: 31 us -> 37.9 us
  local copies, waits for them, and re-layouts: 3.17 us -> 1.75 us
    ppermute x26 -> x28, waiting for transfers between devices: 45.2 us -> 31.3 us  [get(): return lax.ppermute(value, AXES, pairs)]
    ppermute x26 -> x28, starting transfers between devices: 31 us -> 37.9 us  [get(): return lax.ppermute(value, AXES, pairs)]
    slice x2 -> x0, local copies, waits for them, and re-layouts: 2.15 us -> none  [the longest x1 1.08 us: per_device(): far1 = get(after(line_after, line_before, chain[0])[2 * ROWS:], second=1)]
    pallas_call x9 -> x10, Pallas kernels: 29.2 us -> 28.5 us  [the longest x4 16.8 us: make_exps(): pl.pallas_call(functools.partial(exps_kernel, places, rows_here, first, l...]
  transfers between devices with their start and end apart: 26 -> 28, of which waited for: 19 -> 16; matrix products, arithmetic and copies ran while one was open for 2% -> 0% of each run, Pallas kernels for 17% -> 19%
where the time goes in v3:
time: 103 us
  starting transfers between devices  37.9 us (37%)
  Pallas kernels  31.4 us (30%)
  waiting for transfers between devices  31.3 us (30%)
  local copies, waits for them, and re-layouts  1.75 us (2%)
    ppermute x28, starting transfers between devices, get(): return lax.ppermute(value, AXES, pairs)  37.9 us
    ppermute x28, waiting for transfers between devices, get(): return lax.ppermute(value, AXES, pairs)  31.3 us
    pallas_call x4, Pallas kernels, make_exps(): pl.pallas_call(functools.partial(exps_kernel, places, rows_here, first, l...  16.8 us
    pallas_call x4, Pallas kernels, make_grads(): pl.pallas_call(functools.partial(grads_kernel, pieces, adds), out_shape=t...  11.6 us
  transfers between devices with their start and end apart: 28, of which 16 were waited for; matrix products, arithmetic and copies ran while one was open for 0% of the time, Pallas kernels for 19%

profile of v3, /device:TPU:0, one launch (start us, length us, event | category | flops | bytes accessed | tf_op | source)
XLA Modules:
  0.0 103.3 jit_solution(13518114654475321915)
XLA Ops:
  1.7 2.1 %collective-permute-start = (bf16[256,512]{1,0:T(8,128)(2,1)S(1)}, bf16[256,512]{1,0:T(8,128)(2,1)S(1)}, u32[]{:S(2)}, u32[]{:S(2)}) collective-permute-start(bf16[256,512]{1,0:T(8,128)(2,1)S(1)} %unit.1.unit_ref), channel_id=1, source_target_pairs={{65,0},{96,32},{0,64},{33,96},{64,1},{97,33},{1,65},{32,97},{73,8}... | collective-permute-start | bytes 786440 | tf_op jit(solution)/shard_map/ppermute | solution.py:42
  5.3 1.7 %collective-permute-start.6 = (bf16[256,512]{1,0:T(8,128)(2,1)S(1)}, bf16[256,512]{1,0:T(8,128)(2,1)S(1)}, u32[]{:S(2)}, u32[]{:S(2)}) collective-permute-start(bf16[256,512]{1,0:T(8,128)(2,1)S(1)} %unit.1.unit_ref), channel_id=1, source_target_pairs={{2,0},{40,32},{66,64},{104,96},{3,1},{41,33},{67,65},{105,97},{10,... | collective-permute-start | bytes 786440 | tf_op jit(solution)/shard_map/ppermute | solution.py:42
  7.0 1.8 %collective-permute-start.9 = (bf16[256,512]{1,0:T(8,128)(2,1)S(1)}, bf16[256,512]{1,0:T(8,128)(2,1)S(1)}, u32[]{:S(2)}, u32[]{:S(2)}) collective-permute-start(bf16[256,512]{1,0:T(8,128)(2,1)S(1)} %unit.1.unit_ref), channel_id=1, source_target_pairs={{4,0},{48,32},{68,64},{112,96},{5,1},{49,33},{69,65},{113,97},{12,... | collective-permute-start | bytes 786440 | tf_op jit(solution)/shard_map/ppermute | solution.py:42
  8.8 2.2 %collective-permute-start.2 = (bf16[256,512]{1,0:T(8,128)(2,1)S(1)}, bf16[256,512]{1,0:T(8,128)(2,1)S(1)}, u32[]{:S(2)}, u32[]{:S(2)}) collective-permute-start(bf16[256,512]{1,0:T(8,128)(2,1)S(1)} %unit.1.unit_ref), channel_id=1, source_target_pairs={{64,0},{97,32},{1,64},{32,96},{65,1},{96,33},{0,65},{33,97},{72,8}... | collective-permute-start | bytes 786440 | tf_op jit(solution)/shard_map/ppermute | solution.py:42
  13.8 2.0 %collective-permute-start.3 = (bf16[256,512]{1,0:T(8,128)(2,1)S(1)}, bf16[256,512]{1,0:T(8,128)(2,1)S(1)}, u32[]{:S(2)}, u32[]{:S(2)}) collective-permute-start(bf16[256,512]{1,0:T(8,128)(2,1)S(1)} %collective-permute-done), channel_id=1, source_target_pairs={{65,0},{96,32},{0,64},{33,96},{64,1},{97,33},{1,65},{32,97},{73,8}... | collective-permute-start | bytes 786440 | tf_op jit(solution)/shard_map/ppermute | solution.py:42
  15.8 1.6 %collective-permute-start.7 = (bf16[512,512]{1,0:T(8,128)(2,1)S(1)}, bf16[512,512]{1,0:T(8,128)(2,1)S(1)}, u32[]{:S(2)}, u32[]{:S(2)}) collective-permute-start(bf16[512,512]{1,0:T(8,128)(2,1)S(1)} %constant_dynamic-update-slice_fusion.2.refs_3_), channel_id=1, source_target_pairs={{24,0},{38,32},{88,64},{102,96},{25,1},{39,33},{89,65},{103,97},{0... | collective-permute-start | bytes 1572872 | tf_op jit(solution)/shard_map/ppermute | solution.py:42
  17.4 1.7 %collective-permute-start.8 = (bf16[512,512]{1,0:T(8,128)(2,1)S(1)}, bf16[512,512]{1,0:T(8,128)(2,1)S(1)}, u32[]{:S(2)}, u32[]{:S(2)}) collective-permute-start(bf16[512,512]{1,0:T(8,128)(2,1)S(1)} %constant_dynamic-update-slice_fusion.2.refs_3_), channel_id=1, source_target_pairs={{8,0},{34,32},{72,64},{98,96},{9,1},{35,33},{73,65},{99,97},{16,8}... | collective-permute-start | bytes 1572872 | tf_op jit(solution)/shard_map/ppermute | solution.py:42
  19.1 1.9 %collective-permute-start.11 = (bf16[512,512]{1,0:T(8,128)(2,1)S(1)}, bf16[512,512]{1,0:T(8,128)(2,1)S(1)}, u32[]{:S(2)}, u32[]{:S(2)}) collective-permute-start(bf16[512,512]{1,0:T(8,128)(2,1)S(1)} %constant_dynamic-update-slice_fusion.4.refs_4_), channel_id=1, source_target_pairs={{8,0},{34,32},{72,64},{98,96},{9,1},{35,33},{73,65},{99,97},{16,8}... | collective-permute-start | bytes 1572872 | tf_op jit(solution)/shard_map/ppermute | solution.py:42
  23.1 2.8 %exps0.1 = (f32[2048,128]{1,0:T(8,128)S(1)}, bf16[2048,4096]{1,0:T(8,128)(2,1)S(1)}, bf16[4096,512]{1,0:T(8,128)(2,1)S(1)}) custom-call(s32[4]{0:T(128)S(1)} %pad_add_fusion.refs_0_.info_ref, bf16[512,512]{1,0:T(8,128)(2,1)S(1)} %pad_maximum_fusion.refs_1_, bf16[512,512]{1,0:T(8,128)(2,1)S(1)} %collective-permute-done.1.refs_2_, ...), custom_call_target="tpu_custom_call" | custom-call | flops 8589934592 | bytes 1048576 | tf_op jit(solution)/shard_map/exps0/pallas_call | solution.py:175
  25.9 2.7 %exps1.1 = (f32[2048,128]{1,0:T(8,128)S(1)}, bf16[2048,4096]{1,0:T(8,128)(2,1)S(1)}, bf16[4096,512]{1,0:T(8,128)(2,1)S(1)}) custom-call(s32[4]{0:T(128)S(1)} %pad_add_fusion.refs_0_.info_ref, bf16[512,512]{1,0:T(8,128)(2,1)S(1)} %constant_dynamic-update-slice_fusion.refs_1_.refs_3_, ...), custom_call_target="tpu_custom_call", output_to_operand_aliasing={{1}: (6, {}), {2}: (7, {})} | custom-call | flops 8589934592 | bytes 1048576 | tf_op jit(solution)/shard_map/exps1/pallas_call | solution.py:175
  28.6 3.6 %collective-permute-done.11.refs_8_ = bf16[512,512]{1,0:T(8,128)(2,1)S(1)} collective-permute-done((bf16[512,512]{1,0:T(8,128)(2,1)S(1)}, bf16[512,512]{1,0:T(8,128)(2,1)S(1)}, u32[]{:S(2)}, u32[]{:S(2)}) %collective-permute-start.11) | collective-permute-done | bytes 524320 | tf_op jit(solution)/shard_map/ppermute | solution.py:42
  32.2 2.9 %collective-permute-start.13 = (bf16[512,512]{1,0:T(8,128)(2,1)S(1)}, bf16[512,512]{1,0:T(8,128)(2,1)S(1)}, u32[]{:S(2)}, u32[]{:S(2)}) collective-permute-start(bf16[512,512]{1,0:T(8,128)(2,1)S(1)} %collective-permute-done.11.refs_8_), channel_id=1, source_target_pairs={{8,0},{34,32},{72,64},{98,96},{9,1},{35,33},{73,65},{99,97},{16,8}... | collective-permute-start | bytes 1572872 | tf_op jit(solution)/shard_map/ppermute | solution.py:42
  35.1 7.1 %exps2.1 = (f32[2048,128]{1,0:T(8,128)S(1)}, bf16[2048,4096]{1,0:T(8,128)(2,1)S(1)}, bf16[4096,512]{1,0:T(8,128)(2,1)S(1)}) custom-call(s32[4]{0:T(128)S(1)} %pad_add_fusion.refs_0_.info_ref, bf16[512,512]{1,0:T(8,128)(2,1)S(1)} %pad_maximum_fusion.refs_1_, ...), custom_call_target="tpu_custom_call", output_to_operand_aliasing={{1}: (10, {}), {2}: (11, {})} | custom-call | flops 17179869184 | bytes 2097152 | tf_op jit(solution)/shard_map/exps2/pallas_call | solution.py:175
  42.3 3.2 %collective-permute-done.10.refs_5_ = bf16[512,512]{1,0:T(8,128)(2,1)S(1)} collective-permute-done((bf16[512,512]{1,0:T(8,128)(2,1)S(1)}, bf16[512,512]{1,0:T(8,128)(2,1)S(1)}, u32[]{:S(2)}, u32[]{:S(2)}) %collective-permute-start.10) | collective-permute-done | bytes 524320 | tf_op jit(solution)/shard_map/ppermute | solution.py:42
  45.5 4.2 %exps3.1 = (f32[16,256]{1,0:T(8,128)S(1)}, bf16[2048,4096]{1,0:T(8,128)(2,1)S(1)}, bf16[4096,512]{1,0:T(8,128)(2,1)S(1)}) custom-call(s32[4]{0:T(128)S(1)} %pad_add_fusion.refs_0_.info_ref, bf16[512,512]{1,0:T(8,128)(2,1)S(1)} %pad_maximum_fusion.refs_1_, ...), custom_call_target="tpu_custom_call", output_to_operand_aliasing={{1}: (8, {}), {2}: (9, {})} | custom-call | flops 8589934592 | bytes 1048576 | tf_op jit(solution)/shard_map/exps3/pallas_call | solution.py:175
  51.0 1.6 %collective-permute-start.15 = (f32[16,256]{1,0:T(8,128)S(1)}, f32[16,256]{1,0:T(8,128)S(1)}, u32[]{:S(2)}, u32[]{:S(2)}) collective-permute-start(f32[16,256]{1,0:T(8,128)S(1)} %add.7.own_ref), channel_id=1, source_target_pairs={{65,0},{97,32},{0,64},{32,96},{64,1},{96,33},{1,65},{33,97},{73,8}... | collective-permute-start | bytes 49160 | tf_op jit(solution)/shard_map/ppermute | solution.py:42
  52.6 1.6 %collective-permute-start.16 = (f32[16,256]{1,0:T(8,128)S(1)}, f32[16,256]{1,0:T(8,128)S(1)}, u32[]{:S(2)}, u32[]{:S(2)}) collective-permute-start(f32[16,256]{1,0:T(8,128)S(1)} %add.7.own_ref), channel_id=1, source_target_pairs={{64,0},{96,32},{1,64},{33,96},{65,1},{97,33},{0,65},{32,97},{72,8}... | collective-permute-start | bytes 49160 | tf_op jit(solution)/shard_map/ppermute | solution.py:42
  56.4 3.1 %collective-permute-done.17.far_ref = f32[16,256]{1,0:T(8,128)S(1)} collective-permute-done((f32[16,256]{1,0:T(8,128)S(1)}, f32[16,256]{1,0:T(8,128)S(1)}, u32[]{:S(2)}, u32[]{:S(2)}) %collective-permute-start.17) | collective-permute-done | bytes 16416 | tf_op jit(solution)/shard_map/ppermute | solution.py:42
  60.9 3.2 %collective-permute-start.19 = (f32[8,128]{1,0:T(8,128)S(1)}, f32[8,128]{1,0:T(8,128)S(1)}, u32[]{:S(2)}, u32[]{:S(2)}) collective-permute-start(f32[8,128]{1,0:T(8,128)S(1)} %get-tuple-element.47), channel_id=1, source_target_pairs={{2,0},{40,32},{66,64},{104,96},{3,1},{41,33},{67,65},{105,97},{10,... | collective-permute-start | bytes 12296 | tf_op jit(solution)/shard_map/ppermute | solution.py:42
  65.6 3.6 %collective-permute-done.20 = f32[8,128]{1,0:T(8,128)S(1)} collective-permute-done((f32[8,128]{1,0:T(8,128)S(1)}, f32[8,128]{1,0:T(8,128)S(1)}, u32[]{:S(2)}, u32[]{:S(2)}) %collective-permute-start.20) | collective-permute-done | bytes 4128 | tf_op jit(solution)/shard_map/ppermute | solution.py:42
  69.2 3.2 %collective-permute-start.22 = (f32[32,128]{1,0:T(8,128)S(1)}, f32[32,128]{1,0:T(8,128)S(1)}, u32[]{:S(2)}, u32[]{:S(2)}) collective-permute-start(f32[32,128]{1,0:T(8,128)S(1)} %get-tuple-element.58), channel_id=1, source_target_pairs={{8,0},{34,32},{72,64},{98,96},{9,1},{35,33},{73,65},{99,97},{16,8}... | collective-permute-start | bytes 49160 | tf_op jit(solution)/shard_map/ppermute | solution.py:42
  72.5 1.7 %collective-permute-done.21 = f32[32,128]{1,0:T(8,128)S(1)} collective-permute-done((f32[32,128]{1,0:T(8,128)S(1)}, f32[32,128]{1,0:T(8,128)S(1)}, u32[]{:S(2)}, u32[]{:S(2)}) %collective-permute-start.21) | collective-permute-done | bytes 16416 | tf_op jit(solution)/shard_map/ppermute | solution.py:42
  74.2 3.5 %collective-permute-done.23 = f32[32,128]{1,0:T(8,128)S(1)} collective-permute-done((f32[32,128]{1,0:T(8,128)S(1)}, f32[32,128]{1,0:T(8,128)S(1)}, u32[]{:S(2)}, u32[]{:S(2)}) %collective-permute-start.23) | collective-permute-done | bytes 16416 | tf_op jit(solution)/shard_map/ppermute | solution.py:42
  77.7 5.2 %grads_core.1 = bf16[1024,512]{1,0:T(8,128)(2,1)S(1)} custom-call(s32[4]{0:T(128)S(1)} %pad_add_fusion.refs_0_.info_ref, f32[128,128]{1,0:T(8,128)S(1)} %constant_dynamic-update-slice_fusion.10.plane_ref, bf16[2048,128]{1,0:T(8,128)(2,1)S(1)} %get-tuple-element.48.arow_ref, bf16[2048,4096]{1,0:T(8,128)(2,1)S(1)} %get-tuple-element.49.exps_ref, ...), custom_call_target="tpu_custom_call" | custom-call | flops 4294967296 | bytes 12582912 | tf_op jit(solution)/shard_map/grads_core/pallas_call | solution.py:262
  83.0 1.8 %grads_far.1.held_ref = f32[256,512]{1,0:T(8,128)S(1)} custom-call(s32[4]{0:T(128)S(1)} %pad_add_fusion.refs_0_.info_ref, f32[128,128]{1,0:T(8,128)S(1)} %constant_dynamic-update-slice_fusion.10.plane_ref, bf16[2048,128]{1,0:T(8,128)(2,1)S(1)} %get-tuple-element.48.arow_ref, bf16[2048,4096]{1,0:T(8,128)(2,1)S(1)} %get-tuple-element.49.exps_ref, ...), custom_call_target="tpu_custom_call" | custom-call | flops 1073741824 | bytes 6291456 | tf_op jit(solution)/shard_map/grads_far/pallas_call | solution.py:262
  86.2 2.9 %grads_near.1 = (bf16[256,512]{1,0:T(8,128)(2,1)S(1)}, f32[256,512]{1,0:T(8,128)S(1)}) custom-call(s32[4]{0:T(128)S(1)} %pad_add_fusion.refs_0_.info_ref, f32[128,128]{1,0:T(8,128)S(1)} %constant_dynamic-update-slice_fusion.10.plane_ref, bf16[2048,128]{1,0:T(8,128)(2,1)S(1)} %get-tuple-element.48.arow_ref, ...), custom_call_target="tpu_custom_call" | custom-call | flops 2147483648 | bytes 8388608 | tf_op jit(solution)/shard_map/grads_near/pallas_call | solution.py:262
  89.1 2.9 %collective-permute-start.26 = (bf16[256,512]{1,0:T(8,128)(2,1)S(1)}, bf16[256,512]{1,0:T(8,128)(2,1)S(1)}, u32[]{:S(2)}, u32[]{:S(2)}) collective-permute-start(bf16[256,512]{1,0:T(8,128)(2,1)S(1)} %get-tuple-element.55), channel_id=1, source_target_pairs={{64,0},{97,32},{1,64},{32,96},{65,1},{96,33},{0,65},{33,97},{72,8}... | collective-permute-start | bytes 786440 | tf_op jit(solution)/shard_map/ppermute | solution.py:42
  92.0 2.0 %collective-permute-done.25.far_ref = bf16[256,512]{1,0:T(8,128)(2,1)S(1)} collective-permute-done((bf16[256,512]{1,0:T(8,128)(2,1)S(1)}, bf16[256,512]{1,0:T(8,128)(2,1)S(1)}, u32[]{:S(2)}, u32[]{:S(2)}) %collective-permute-start.25) | collective-permute-done | bytes 262176 | tf_op jit(solution)/shard_map/ppermute | solution.py:42
  94.1 1.8 %grads_own.1.own_ref = f32[256,512]{1,0:T(8,128)S(1)} custom-call(s32[4]{0:T(128)S(1)} %pad_add_fusion.refs_0_.info_ref, f32[128,128]{1,0:T(8,128)S(1)} %constant_dynamic-update-slice_fusion.10.plane_ref, bf16[2048,128]{1,0:T(8,128)(2,1)S(1)} %get-tuple-element.48.arow_ref, bf16[2048,4096]{1,0:T(8,128)(2,1)S(1)} %get-tuple-element.49.exps_ref, ...), custom_call_target="tpu_custom_call" | custom-call | flops 1073741824 | bytes 6291456 | tf_op jit(solution)/shard_map/grads_own/pallas_call | solution.py:262
  95.9 2.6 %collective-permute-done.26.below_ref = bf16[256,512]{1,0:T(8,128)(2,1)S(1)} collective-permute-done((bf16[256,512]{1,0:T(8,128)(2,1)S(1)}, bf16[256,512]{1,0:T(8,128)(2,1)S(1)}, u32[]{:S(2)}, u32[]{:S(2)}) %collective-permute-start.26) | collective-permute-done | bytes 262176 | tf_op jit(solution)/shard_map/ppermute | solution.py:42
  98.5 3.2 %collective-permute-done.27.above_ref = bf16[256,512]{1,0:T(8,128)(2,1)S(1)} collective-permute-done((bf16[256,512]{1,0:T(8,128)(2,1)S(1)}, bf16[256,512]{1,0:T(8,128)(2,1)S(1)}, u32[]{:S(2)}, u32[]{:S(2)}) %collective-permute-start.27) | collective-permute-done | bytes 262176 | tf_op jit(solution)/shard_map/ppermute | solution.py:42
  101.7 1.7 %final.1 = (f32[256,512]{1,0:T(8,128)}, f32[1,1]{1,0:T(1,128)}) custom-call(s32[4]{0:T(128)S(1)} %pad_add_fusion.refs_0_.info_ref, bf16[256,512]{1,0:T(8,128)(2,1)S(1)} %copy-done.1, bf16[256,512]{1,0:T(8,128)(2,1)S(1)} %get-tuple-element.30.mates_ref, f32[256,512]{1,0:T(8,128)S(1)} %grads_own.1.own_ref, ...), custom_call_target="tpu_custom_call" | custom-call | tf_op jit(solution)/shard_map/final/pallas_call | solution.py:308
  (60 shorter events, 15.3 us)
Async XLA Ops:
  0.6 1.0 copy-start
  1.7 10.4 %collective-permute-start = (bf16[256,512]{1,0:T(8,128)(2,1)S(1)}, bf16[256,512]{1,0:T(8,128)(2,1)S(1)}, u32[]{:S(2)}, u32[]{:S(2)}) collective-permute-start(bf16[256,512]{1,0:T(8,128)(2,1)S(1)} %unit.1.unit_ref), channel_id=1, source_target_pairs={{65,0},{96,32},{0,64},{33,96},{64,1},{97,33},{1,65},{32,97},{73,8}... | collective-permute-start | bytes 786440 | tf_op jit(solution)/shard_map/ppermute | solution.py:42
  3.8 8.5 %collective-permute-start.5 = (bf16[256,512]{1,0:T(8,128)(2,1)S(1)}, bf16[256,512]{1,0:T(8,128)(2,1)S(1)}, u32[]{:S(2)}, u32[]{:S(2)}) collective-permute-start(bf16[256,512]{1,0:T(8,128)(2,1)S(1)} %unit.1.unit_ref), channel_id=1, source_target_pairs={{6,0},{56,32},{70,64},{120,96},{7,1},{57,33},{71,65},{121,97},{14,... | collective-permute-start | bytes 786440 | tf_op jit(solution)/shard_map/ppermute | solution.py:42
  5.3 8.5 %collective-permute-start.6 = (bf16[256,512]{1,0:T(8,128)(2,1)S(1)}, bf16[256,512]{1,0:T(8,128)(2,1)S(1)}, u32[]{:S(2)}, u32[]{:S(2)}) collective-permute-start(bf16[256,512]{1,0:T(8,128)(2,1)S(1)} %unit.1.unit_ref), channel_id=1, source_target_pairs={{2,0},{40,32},{66,64},{104,96},{3,1},{41,33},{67,65},{105,97},{10,... | collective-permute-start | bytes 786440 | tf_op jit(solution)/shard_map/ppermute | solution.py:42
  7.0 10.4 %collective-permute-start.9 = (bf16[256,512]{1,0:T(8,128)(2,1)S(1)}, bf16[256,512]{1,0:T(8,128)(2,1)S(1)}, u32[]{:S(2)}, u32[]{:S(2)}) collective-permute-start(bf16[256,512]{1,0:T(8,128)(2,1)S(1)} %unit.1.unit_ref), channel_id=1, source_target_pairs={{4,0},{48,32},{68,64},{112,96},{5,1},{49,33},{69,65},{113,97},{12,... | collective-permute-start | bytes 786440 | tf_op jit(solution)/shard_map/ppermute | solution.py:42
  8.8 10.3 %collective-permute-start.2 = (bf16[256,512]{1,0:T(8,128)(2,1)S(1)}, bf16[256,512]{1,0:T(8,128)(2,1)S(1)}, u32[]{:S(2)}, u32[]{:S(2)}) collective-permute-start(bf16[256,512]{1,0:T(8,128)(2,1)S(1)} %unit.1.unit_ref), channel_id=1, source_target_pairs={{64,0},{97,32},{1,64},{32,96},{65,1},{96,33},{0,65},{33,97},{72,8}... | collective-permute-start | bytes 786440 | tf_op jit(solution)/shard_map/ppermute | solution.py:42
  11.1 0.7 copy-start.2
  12.2 10.9 %collective-permute-start.1 = (bf16[512,512]{1,0:T(8,128)(2,1)S(1)}, bf16[512,512]{1,0:T(8,128)(2,1)S(1)}, u32[]{:S(2)}, u32[]{:S(2)}) collective-permute-start(bf16[512,512]{1,0:T(8,128)(2,1)S(1)} %pad_maximum_fusion.refs_1_), channel_id=1, source_target_pairs={{32,0},{0,32},{96,64},{64,96},{33,1},{1,33},{97,65},{65,97},{40,8}... | collective-permute-start | bytes 1572872 | tf_op jit(solution)/shard_map/ppermute | solution.py:42
  13.8 7.7 %collective-permute-start.3 = (bf16[256,512]{1,0:T(8,128)(2,1)S(1)}, bf16[256,512]{1,0:T(8,128)(2,1)S(1)}, u32[]{:S(2)}, u32[]{:S(2)}) collective-permute-start(bf16[256,512]{1,0:T(8,128)(2,1)S(1)} %collective-permute-done), channel_id=1, source_target_pairs={{65,0},{96,32},{0,64},{33,96},{64,1},{97,33},{1,65},{32,97},{73,8}... | collective-permute-start | bytes 786440 | tf_op jit(solution)/shard_map/ppermute | solution.py:42
  15.8 19.3 %collective-permute-start.7 = (bf16[512,512]{1,0:T(8,128)(2,1)S(1)}, bf16[512,512]{1,0:T(8,128)(2,1)S(1)}, u32[]{:S(2)}, u32[]{:S(2)}) collective-permute-start(bf16[512,512]{1,0:T(8,128)(2,1)S(1)} %constant_dynamic-update-slice_fusion.2.refs_3_), channel_id=1, source_target_pairs={{24,0},{38,32},{88,64},{102,96},{25,1},{39,33},{89,65},{103,97},{0... | collective-permute-start | bytes 1572872 | tf_op jit(solution)/shard_map/ppermute | solution.py:42
  17.4 17.7 %collective-permute-start.8 = (bf16[512,512]{1,0:T(8,128)(2,1)S(1)}, bf16[512,512]{1,0:T(8,128)(2,1)S(1)}, u32[]{:S(2)}, u32[]{:S(2)}) collective-permute-start(bf16[512,512]{1,0:T(8,128)(2,1)S(1)} %constant_dynamic-update-slice_fusion.2.refs_3_), channel_id=1, source_target_pairs={{8,0},{34,32},{72,64},{98,96},{9,1},{35,33},{73,65},{99,97},{16,8}... | collective-permute-start | bytes 1572872 | tf_op jit(solution)/shard_map/ppermute | solution.py:42
  19.1 13.1 %collective-permute-start.11 = (bf16[512,512]{1,0:T(8,128)(2,1)S(1)}, bf16[512,512]{1,0:T(8,128)(2,1)S(1)}, u32[]{:S(2)}, u32[]{:S(2)}) collective-permute-start(bf16[512,512]{1,0:T(8,128)(2,1)S(1)} %constant_dynamic-update-slice_fusion.4.refs_4_), channel_id=1, source_target_pairs={{8,0},{34,32},{72,64},{98,96},{9,1},{35,33},{73,65},{99,97},{16,8}... | collective-permute-start | bytes 1572872 | tf_op jit(solution)/shard_map/ppermute | solution.py:42
  21.4 10.8 %collective-permute-start.12 = (bf16[512,512]{1,0:T(8,128)(2,1)S(1)}, bf16[512,512]{1,0:T(8,128)(2,1)S(1)}, u32[]{:S(2)}, u32[]{:S(2)}) collective-permute-start(bf16[512,512]{1,0:T(8,128)(2,1)S(1)} %constant_dynamic-update-slice_fusion.4.refs_4_), channel_id=1, source_target_pairs={{24,0},{38,32},{88,64},{102,96},{25,1},{39,33},{89,65},{103,97},{0... | collective-permute-start | bytes 1572872 | tf_op jit(solution)/shard_map/ppermute | solution.py:42
  23.0 2.9 %collective-permute-start.4 = (bf16[512,512]{1,0:T(8,128)(2,1)S(1)}, bf16[512,512]{1,0:T(8,128)(2,1)S(1)}, u32[]{:S(2)}, u32[]{:S(2)}) collective-permute-start(bf16[512,512]{1,0:T(8,128)(2,1)S(1)} %constant_dynamic-update-slice_fusion.refs_1_.refs_3_), channel_id=1, source_target_pairs={{32,0},{0,32},{96,64},{64,96},{33,1},{1,33},{97,65},{65,97},{40,8}... | collective-permute-start | bytes 1572872 | tf_op jit(solution)/shard_map/ppermute | solution.py:42
  32.2 10.0 %collective-permute-start.13 = (bf16[512,512]{1,0:T(8,128)(2,1)S(1)}, bf16[512,512]{1,0:T(8,128)(2,1)S(1)}, u32[]{:S(2)}, u32[]{:S(2)}) collective-permute-start(bf16[512,512]{1,0:T(8,128)(2,1)S(1)} %collective-permute-done.11.refs_8_), channel_id=1, source_target_pairs={{8,0},{34,32},{72,64},{98,96},{9,1},{35,33},{73,65},{99,97},{16,8}... | collective-permute-start | bytes 1572872 | tf_op jit(solution)/shard_map/ppermute | solution.py:42
  35.1 10.4 %collective-permute-start.10 = (bf16[512,512]{1,0:T(8,128)(2,1)S(1)}, bf16[512,512]{1,0:T(8,128)(2,1)S(1)}, u32[]{:S(2)}, u32[]{:S(2)}) collective-permute-start(bf16[512,512]{1,0:T(8,128)(2,1)S(1)} %collective-permute-done.7.refs_5_), channel_id=1, source_target_pairs={{24,0},{38,32},{88,64},{102,96},{25,1},{39,33},{89,65},{103,97},{0... | collective-permute-start | bytes 1572872 | tf_op jit(solution)/shard_map/ppermute | solution.py:42
  49.7 1.3 %collective-permute-start.14 = (f32[16,256]{1,0:T(8,128)S(1)}, f32[16,256]{1,0:T(8,128)S(1)}, u32[]{:S(2)}, u32[]{:S(2)}) collective-permute-start(f32[16,256]{1,0:T(8,128)S(1)} %get-tuple-element.46), channel_id=1, source_target_pairs={{32,0},{0,32},{96,64},{64,96},{33,1},{1,33},{97,65},{65,97},{40,8}... | collective-permute-start | bytes 49160 | tf_op jit(solution)/shard_map/ppermute | solution.py:42
  51.0 5.0 %collective-permute-start.15 = (f32[16,256]{1,0:T(8,128)S(1)}, f32[16,256]{1,0:T(8,128)S(1)}, u32[]{:S(2)}, u32[]{:S(2)}) collective-permute-start(f32[16,256]{1,0:T(8,128)S(1)} %add.7.own_ref), channel_id=1, source_target_pairs={{65,0},{97,32},{0,64},{32,96},{64,1},{96,33},{1,65},{33,97},{73,8}... | collective-permute-start | bytes 49160 | tf_op jit(solution)/shard_map/ppermute | solution.py:42
  52.6 3.7 %collective-permute-start.16 = (f32[16,256]{1,0:T(8,128)S(1)}, f32[16,256]{1,0:T(8,128)S(1)}, u32[]{:S(2)}, u32[]{:S(2)}) collective-permute-start(f32[16,256]{1,0:T(8,128)S(1)} %add.7.own_ref), channel_id=1, source_target_pairs={{64,0},{96,32},{1,64},{33,96},{65,1},{97,33},{0,65},{32,97},{72,8}... | collective-permute-start | bytes 49160 | tf_op jit(solution)/shard_map/ppermute | solution.py:42
  54.2 5.2 %collective-permute-start.17 = (f32[16,256]{1,0:T(8,128)S(1)}, f32[16,256]{1,0:T(8,128)S(1)}, u32[]{:S(2)}, u32[]{:S(2)}) collective-permute-start(f32[16,256]{1,0:T(8,128)S(1)} %add.7.own_ref), channel_id=1, source_target_pairs={{1,0},{33,32},{65,64},{97,96},{0,1},{32,33},{64,65},{96,97},{9,8},... | collective-permute-start | bytes 49160 | tf_op jit(solution)/shard_map/ppermute | solution.py:42
  60.3 5.3 %collective-permute-start.18 = (f32[8,128]{1,0:T(8,128)S(1)}, f32[8,128]{1,0:T(8,128)S(1)}, u32[]{:S(2)}, u32[]{:S(2)}) collective-permute-start(f32[8,128]{1,0:T(8,128)S(1)} %get-tuple-element.47), channel_id=1, source_target_pairs={{6,0},{56,32},{70,64},{120,96},{7,1},{57,33},{71,65},{121,97},{14,... | collective-permute-start | bytes 12296 | tf_op jit(solution)/shard_map/ppermute | solution.py:42
  60.9 4.7 %collective-permute-start.19 = (f32[8,128]{1,0:T(8,128)S(1)}, f32[8,128]{1,0:T(8,128)S(1)}, u32[]{:S(2)}, u32[]{:S(2)}) collective-permute-start(f32[8,128]{1,0:T(8,128)S(1)} %get-tuple-element.47), channel_id=1, source_target_pairs={{2,0},{40,32},{66,64},{104,96},{3,1},{41,33},{67,65},{105,97},{10,... | collective-permute-start | bytes 12296 | tf_op jit(solution)/shard_map/ppermute | solution.py:42
  64.1 5.1 %collective-permute-start.20 = (f32[8,128]{1,0:T(8,128)S(1)}, f32[8,128]{1,0:T(8,128)S(1)}, u32[]{:S(2)}, u32[]{:S(2)}) collective-permute-start(f32[8,128]{1,0:T(8,128)S(1)} %get-tuple-element.47), channel_id=1, source_target_pairs={{4,0},{48,32},{68,64},{112,96},{5,1},{49,33},{69,65},{113,97},{12,... | collective-permute-start | bytes 12296 | tf_op jit(solution)/shard_map/ppermute | solution.py:42
  69.2 4.9 %collective-permute-start.21 = (f32[32,128]{1,0:T(8,128)S(1)}, f32[32,128]{1,0:T(8,128)S(1)}, u32[]{:S(2)}, u32[]{:S(2)}) collective-permute-start(f32[32,128]{1,0:T(8,128)S(1)} %get-tuple-element.58), channel_id=1, source_target_pairs={{24,0},{38,32},{88,64},{102,96},{25,1},{39,33},{89,65},{103,97},{0... | collective-permute-start | bytes 49160 | tf_op jit(solution)/shard_map/ppermute | solution.py:42
  69.2 5.0 %collective-permute-start.22 = (f32[32,128]{1,0:T(8,128)S(1)}, f32[32,128]{1,0:T(8,128)S(1)}, u32[]{:S(2)}, u32[]{:S(2)}) collective-permute-start(f32[32,128]{1,0:T(8,128)S(1)} %get-tuple-element.58), channel_id=1, source_target_pairs={{8,0},{34,32},{72,64},{98,96},{9,1},{35,33},{73,65},{99,97},{16,8}... | collective-permute-start | bytes 49160 | tf_op jit(solution)/shard_map/ppermute | solution.py:42
  72.4 5.2 %collective-permute-start.23 = (f32[32,128]{1,0:T(8,128)S(1)}, f32[32,128]{1,0:T(8,128)S(1)}, u32[]{:S(2)}, u32[]{:S(2)}) collective-permute-start(f32[32,128]{1,0:T(8,128)S(1)} %get-tuple-element.58), channel_id=1, source_target_pairs={{16,0},{36,32},{80,64},{100,96},{17,1},{37,33},{81,65},{101,97},{2... | collective-permute-start | bytes 49160 | tf_op jit(solution)/shard_map/ppermute | solution.py:42
  82.9 2.7 %collective-permute-start.24 = (bf16[1024,512]{1,0:T(8,128)(2,1)S(1)}, bf16[1024,512]{1,0:T(8,128)(2,1)S(1)}, u32[]{:S(2)}, u32[]{:S(2)}) collective-permute-start(bf16[1024,512]{1,0:T(8,128)(2,1)S(1)} %grads_core.1), channel_id=1, source_target_pairs={{32,0},{0,32},{96,64},{64,96},{33,1},{1,33},{97,65},{65,97},{40,8}... | collective-permute-start | bytes 3145736 | tf_op jit(solution)/shard_map/ppermute | solution.py:42
  85.7 8.2 %collective-permute-start.25 = (bf16[256,512]{1,0:T(8,128)(2,1)S(1)}, bf16[256,512]{1,0:T(8,128)(2,1)S(1)}, u32[]{:S(2)}, u32[]{:S(2)}) collective-permute-start(bf16[256,512]{1,0:T(8,128)(2,1)S(1)} %pass_far.1), channel_id=1, source_target_pairs={{65,0},{96,32},{0,64},{33,96},{64,1},{97,33},{1,65},{32,97},{73,8}... | collective-permute-start | bytes 786440 | tf_op jit(solution)/shard_map/ppermute | solution.py:42
  89.1 12.6 %copy-start.1 = (bf16[256,512]{1,0:T(8,128)(2,1)S(1)}, bf16[256,512]{1,0:T(8,128)(2,1)}, u32[]{:S(2)}) copy-start(bf16[256,512]{1,0:T(8,128)(2,1)} %z_ref.3) | copy-start | bytes 786436
  89.1 9.4 %collective-permute-start.26 = (bf16[256,512]{1,0:T(8,128)(2,1)S(1)}, bf16[256,512]{1,0:T(8,128)(2,1)S(1)}, u32[]{:S(2)}, u32[]{:S(2)}) collective-permute-start(bf16[256,512]{1,0:T(8,128)(2,1)S(1)} %get-tuple-element.55), channel_id=1, source_target_pairs={{64,0},{97,32},{1,64},{32,96},{65,1},{96,33},{0,65},{33,97},{72,8}... | collective-permute-start | bytes 786440 | tf_op jit(solution)/shard_map/ppermute | solution.py:42
  94.0 7.7 %collective-permute-start.27 = (bf16[256,512]{1,0:T(8,128)(2,1)S(1)}, bf16[256,512]{1,0:T(8,128)(2,1)S(1)}, u32[]{:S(2)}, u32[]{:S(2)}) collective-permute-start(bf16[256,512]{1,0:T(8,128)(2,1)S(1)} %pass_two.1), channel_id=1, source_target_pairs={{65,0},{96,32},{0,64},{33,96},{64,1},{97,33},{1,65},{32,97},{73,8}... | collective-permute-start | bytes 786440 | tf_op jit(solution)/shard_map/ppermute | solution.py:42

commit v4 on v3

--- a/solution.py
+++ b/solution.py
@@ -78,6 +78,28 @@
             yield (k // 2) * 1024 + c * 512 + (k % 2) * ROWS, block_of((info_ref[2] + away) & 3, core)
 
 
+def col_blocks(info_ref):
+    for two in OFFSETS:
+        for one in OFFSETS:
+            x = info_ref[0] + jnp.where(info_ref[3] == 0, one, two)
+            y = info_ref[1] + jnp.where(info_ref[3] == 0, two, one)
+            yield (y & 3) * 4 + (x & 3)
+
+
+def in_parts(value):
+    high = value.astype(BF16)
+    rest = value - high.astype(F32)
+    middle = rest.astype(BF16)
+    low = (rest - middle.astype(F32)).astype(BF16)
+    rows = [high.astype(F32), middle.astype(F32), low.astype(F32), jnp.zeros((13, value.shape[1]), F32)]
+    return jnp.concatenate(rows, axis=0).astype(BF16)
+
+
+def of_parts(block):
+    rows = block.astype(F32)
+    return rows[0:1] + (rows[1:2] + rows[2:3])
+
+
 def unit_kernel(z_ref, unit_ref):
     zf = z_ref[...].astype(F32)
     recip = lax.rsqrt(jnp.sum(zf * zf, axis=1, keepdims=True) + 1e-06)
@@ -126,14 +148,15 @@
     info_ref, refs = refs[0], refs[1:]
     row_refs, col_refs, refs = refs[: 2 * halves], refs[2 * halves : 2 * halves + count], refs[2 * halves + count :]
     if not first:
-        before_ref, refs = refs[0], refs[3:]
+        before_ref, col_before_ref, refs = refs[0], refs[1], refs[4:]
     if last:
         positive_ref, refs = refs[0], refs[1:]
-    sums_ref, exps_ref, unit_ref, rows, sums, line = refs
+    sums_ref, col_sums_ref, exps_ref, unit_ref, rows, sums, col_sums, line, col_line = refs
     for n, ref in enumerate(row_refs):
         start = rows_here[n // 2] * 1024 + (n % 2) * 512
         rows[start : start + 512] = ref[...]
     sums[...] = jnp.zeros_like(sums) if first else before_ref[...]
+    col_sums[...] = jnp.zeros_like(col_sums) if first else col_before_ref[...]
     part = slice(rows_here[0] * 1024, rows_here[-1] * 1024 + 1024)
     for n, col_ref in enumerate(col_refs):
         if 0 in rows_here:
@@ -144,48 +167,57 @@
         def _(m):
             here = pl.ds(pl.multiple_of(places[n] * TILE + m * ROWS, ROWS), ROWS)
             cols = col_ref[pl.ds(pl.multiple_of(m * ROWS, ROWS), ROWS), :]
-            for start in range(part.start, part.stop, ROWS):
-                piece = slice(start, start + ROWS)
-                s = lax.dot_general(rows[piece], cols, NT, preferred_element_type=F32)
-                e = jnp.exp2(s * EXP_SCALE)
-                if first and n == 0 and start == 0:
-                    i = lax.broadcasted_iota(jnp.int32, (ROWS, ROWS), 0)
-                    j = lax.broadcasted_iota(jnp.int32, (ROWS, ROWS), 1)
-                    e = jnp.where(i == j + m * ROWS, 0.0, e)
-                exps_ref[piece, here] = e.astype(BF16)
-                sums[piece] += e[:, :128] + e[:, 128:]
+            s = lax.dot_general(rows[part], cols, NT, preferred_element_type=F32)
+            e = jnp.exp2(s * EXP_SCALE)
+            if first and n == 0:
+                i = lax.broadcasted_iota(jnp.int32, (ROWS, ROWS), 0)
+                j = lax.broadcasted_iota(jnp.int32, (ROWS, ROWS), 1)
+                own = jnp.where(i == j + m * ROWS, 0.0, e[:ROWS])
+                e = jnp.concatenate([own, e[ROWS:]], axis=0)
+            exps_ref[part, here] = e.astype(BF16)
+            sums[part] += e[:, :128] + e[:, 128:]
+            col_sums[:, here] += jnp.sum(e.reshape(-1, 8, ROWS), axis=0)
 
     if last:
         totals = jnp.sum(sums[...].T, axis=0, keepdims=True)
-        line[...] = jnp.zeros_like(line)
         for start, at in row_blocks(info_ref):
             line[pl.ds(at, 1), :] = totals[:, start : start + ROWS]
-        line[8:9, 0:128] = positive_ref[...]
         sums_ref[...] = line[...]
+        totals = jnp.sum(col_sums[...], axis=0, keepdims=True)
+        col_line[...] = jnp.zeros_like(col_line)
+        for n, at in enumerate(col_blocks(info_ref)):
+            col_line[pl.ds(at, 1), :] = totals[:, n * ROWS : (n + 1) * ROWS]
+        col_line[16:17, 0:128] = positive_ref[...]
+        col_sums_ref[...] = col_line[...]
     else:
         sums_ref[...] = sums[...]
+        col_sums_ref[...] = col_sums[...]
 
 
 def make_exps(info, rows, rows_here, cols, places, chain, positive, name):
     first, last = chain is None, positive is not None
     count = len(cols)
     tiles = sum(c.shape[0] for c in cols) // TILE
-    sums_shape = (16, ROWS) if last else (ALL_ROWS, 128)
+    sums_shape = (8, ROWS) if last else (ALL_ROWS, 128)
+    col_sums_shape = (24, ROWS) if last else (8, COLS)
     operands = [info, *rows, *cols] + ([] if first else list(chain)) + ([positive] if last else [])
     return pl.pallas_call(
         functools.partial(exps_kernel, places, rows_here, first, last),
         out_shape=(
             jax.ShapeDtypeStruct(sums_shape, F32),
+            jax.ShapeDtypeStruct(col_sums_shape, F32),
             pltpu.VMEM((ALL_ROWS, COLS), BF16),
             pltpu.VMEM((COLS, E), BF16),
         ),
         in_specs=[smem()] + [vmem()] * (len(operands) - 1),
-        out_specs=(vmem(), vmem(), vmem()),
-        input_output_aliases={} if first else {2 + len(rows) + count: 1, 3 + len(rows) + count: 2},
+        out_specs=(vmem(), vmem(), vmem(), vmem()),
+        input_output_aliases={} if first else {3 + len(rows) + count: 2, 4 + len(rows) + count: 3},
         scratch_shapes=[
             pltpu.VMEM((ALL_ROWS, E), BF16),
             pltpu.VMEM((ALL_ROWS, 128), F32),
-            pltpu.VMEM((16, ROWS), F32),
+            pltpu.VMEM((8, COLS), F32),
+            pltpu.VMEM((8, ROWS), F32),
+            pltpu.VMEM((24, ROWS), F32),
         ],
         compiler_params=params(12),
         cost_estimate=pl.CostEstimate(
@@ -197,39 +229,48 @@
     )(*operands)
 
 
-def totals_kernel(info_ref, own_ref, before_ref, after_ref, far_ref, arow_ref, message_ref, recips):
-    both = ring_sum(own_ref[...], before_ref[...], after_ref[...], far_ref[...])
-    total = both[:8]
-    recips[...] = 1.0 / total
-    logs = jnp.sum(jnp.sum(jnp.log(total), axis=0, keepdims=True), axis=1, keepdims=True)
-    loss = jnp.broadcast_to(logs, (1, 128)) - both[8:9, :128]
+def totals_kernel(info_ref, *refs):
+    row_refs, col_refs, (arow_ref, acol_ref, loss_ref, recips, col_recips) = refs[:4], refs[4:8], refs[8:]
+    recips[...] = 1.0 / ring_sum(*[ref[...] for ref in row_refs])
+    both = ring_sum(*[ref[...] for ref in col_refs])
+    totals = both[:16]
+    col_recips[...] = 1.0 / totals
+    logs = jnp.sum(jnp.sum(jnp.log(totals), axis=0, keepdims=True), axis=1, keepdims=True)
+    loss = jnp.broadcast_to(logs, (1, 128)) - both[16:17, :128]
+    loss_ref[...] = in_parts(jnp.concatenate([loss] * (E // 128), axis=1))
     for start, at in row_blocks(info_ref):
         line = recips[pl.ds(at, 1), :]
         arow_ref[start : start + ROWS] = jnp.broadcast_to(line, (128, ROWS)).T.astype(BF16)
-    own = recips[pl.ds(block_of(info_ref[2], info_ref[3]), 1), :]
-    zeros = jnp.zeros((5, 128), F32)
-    message_ref[...] = jnp.concatenate([own[:, :128], own[:, 128:], loss, zeros], axis=0)
-
-
-def make_totals(info, own, before, after, far):
+    for n, at in enumerate(col_blocks(info_ref)):
+        line = col_recips[pl.ds(at, 1), :]
+        acol_ref[2 * n : 2 * n + 1] = line[:, :128]
+        acol_ref[2 * n + 1 : 2 * n + 2] = line[:, 128:]
+
+
+def make_totals(info, by_row, by_col):
     return pl.pallas_call(
         totals_kernel,
         out_shape=(
             jax.ShapeDtypeStruct((ALL_ROWS, 128), BF16),
-            jax.ShapeDtypeStruct((8, 128), F32),
+            jax.ShapeDtypeStruct((32, 128), F32),
+            jax.ShapeDtypeStruct((16, E), BF16),
         ),
-        in_specs=[smem()] + [vmem()] * 4,
-        out_specs=(vmem(), vmem()),
-        scratch_shapes=[pltpu.VMEM((8, ROWS), F32)],
+        in_specs=[smem()] + [vmem()] * 8,
+        out_specs=(vmem(), vmem(), vmem()),
+        scratch_shapes=[pltpu.VMEM((8, ROWS), F32), pltpu.VMEM((16, ROWS), F32)],
         compiler_params=params(4),
         name="totals",
-    )(info, own, before, after, far)
-
-
-def grads_kernel(pieces, adds, info_ref, plane_ref, arow_ref, exps_ref, unit_ref, *refs):
+    )(info, *by_row, *by_col)
+
+
+def grads_kernel(pieces, adds, carries, acol_ref, arow_ref, exps_ref, unit_ref, *refs):
     if adds is not None:
         add_ref, refs = refs[0], refs[1:]
-    cols = [plane_ref[8 * (g // 2) + g % 2 : 8 * (g // 2) + g % 2 + 1].astype(BF16) for g in range(COLS // 128)]
+    if carries:
+        carry_ref, refs = refs[0], refs[1:]
+        end = refs[0].shape[0]
+        refs[0][end - 16 : end] = carry_ref[carry_ref.shape[0] - 16 : carry_ref.shape[0]]
+    cols = [acol_ref[g : g + 1].astype(BF16) for g in range(COLS // 128)]
 
     def weights(here):
         a = arow_ref[here]
@@ -250,19 +291,24 @@
         product = lax.dot_general(w, unit_ref[...], NN, preferred_element_type=F32)
         start = 0
         for (_, size), add, ref in zip(pieces, adds, refs):
-            ref[...] = (product[start : start + size] + add_ref[add : add + size].astype(F32)).astype(ref.dtype)
+            ref[:size] = (product[start : start + size] + add_ref[add : add + size].astype(F32)).astype(ref.dtype)
             start += size
 
 
-def make_grads(pieces, adds, dtypes, info, plane, arow, exps, unit, add, name):
+def make_grads(pieces, adds, dtypes, token, acol, arow, exps, unit, add, carry, name):
     count = sum(size for _, size in pieces)
     sizes = [count] if adds is None else [size for _, size in pieces]
+    if carry is not None:
+        sizes[0] += 16
     exps = pltpu.with_memory_space_constraint(exps, pltpu.VMEM)
     unit = pltpu.with_memory_space_constraint(unit, pltpu.VMEM)
-    return pl.pallas_call(
-        functools.partial(grads_kernel, pieces, adds),
+    operands = [after(acol, token), arow, exps, unit]
+    operands += [] if adds is None else [add]
+    operands += [] if carry is None else [carry]
+    return pl.pallas_call(
+        functools.partial(grads_kernel, pieces, adds, carry is not None),
         out_shape=tuple(jax.ShapeDtypeStruct((size, E), dtype) for size, dtype in zip(sizes, dtypes)),
-        in_specs=[smem()] + [vmem()] * (4 if adds is None else 5),
+        in_specs=[vmem()] * len(operands),
         out_specs=(vmem(),) * len(sizes),
         compiler_params=params(16),
         cost_estimate=pl.CostEstimate(
@@ -271,48 +317,51 @@
             transcendentals=0,
         ),
         name=name,
-    )(info, plane, arow, exps, unit, *([] if adds is None else [add]))
-
-
-def pass_kernel(start, held_ref, far_ref, out_ref):
-    out_ref[...] = (held_ref[...] + far_ref[start : start + ROWS].astype(F32)).astype(BF16)
-
-
-def make_pass(held, far, start, name):
-    return pl.pallas_call(
-        functools.partial(pass_kernel, start),
-        out_shape=jax.ShapeDtypeStruct((ROWS, E), BF16),
-        in_specs=[vmem(), vmem()],
+    )(*operands)
+
+
+def far_kernel(raw_ref, core_ref, loss_ref, out_ref):
+    out_ref[:ROWS] = (raw_ref[...] + core_ref[768:1024].astype(F32)).astype(BF16)
+    out_ref[ROWS:] = in_parts(of_parts(loss_ref[...]) + of_parts(core_ref[1024:]))
+
+
+def two_kernel(held_ref, far_ref, out_ref):
+    out_ref[:ROWS] = (held_ref[...] + far_ref[:ROWS].astype(F32)).astype(BF16)
+    out_ref[ROWS:] = far_ref[ROWS:]
+
+
+def make_sum(kernel, operands, name):
+    return pl.pallas_call(
+        kernel,
+        out_shape=jax.ShapeDtypeStruct((ROWS + 16, E), BF16),
+        in_specs=[vmem()] * len(operands),
         out_specs=vmem(),
         compiler_params=params(4),
         name=name,
-    )(held, far)
-
-
-def final_kernel(info_ref, z_ref, mates_ref, own_ref, below_ref, above_ref, plane_ref, grad_ref, loss_ref):
+    )(*operands)
+
+
+def final_kernel(z_ref, mates_ref, own_ref, one_ref, two_ref, here_ref, passed_ref, grad_ref, loss_ref):
     zf = z_ref[...].astype(F32)
     recip = lax.rsqrt(jnp.sum(zf * zf, axis=1, keepdims=True) + 1e-06)
     unit = zf * recip
-    acc = own_ref[...] + below_ref[...].astype(F32) + above_ref[...].astype(F32)
+    acc = own_ref[...] + one_ref[:ROWS].astype(F32) + two_ref[:ROWS].astype(F32)
     grad_unit = INV_TAU * (acc - 2.0 * mates_ref[...].astype(F32))
     along = jnp.sum(unit * grad_unit, axis=1, keepdims=True)
     grad_ref[...] = recip * (grad_unit - unit * along)
-    parts = [[plane_ref[8 * n + 2 : 8 * n + 3] for n in range(4 * m, 4 * m + 4)] for m in range(4)]
-    x_first = ring_sum(*[ring_sum(*line) for line in parts])
-    y_first = ring_sum(*[ring_sum(*line) for line in zip(*parts)])
-    loss = jnp.where(info_ref[3] == 0, x_first, y_first)
+    loss = ring_sum(*[of_parts(ref[ROWS:]) for ref in (here_ref, passed_ref, one_ref, two_ref)])
     loss_ref[...] = loss[:, :1] / (ROWS * 128)
 
 
-def make_final(info, embeds, mates, own, below, above, plane):
+def make_final(operands):
     return pl.pallas_call(
         final_kernel,
         out_shape=(jax.ShapeDtypeStruct((ROWS, E), F32), jax.ShapeDtypeStruct((1, 1), F32)),
-        in_specs=[smem()] + [vmem()] * 6,
+        in_specs=[vmem()] * len(operands),
         out_specs=(vmem(), vmem()),
         compiler_params=params(4),
         name="final",
-    )(info, embeds, mates, own, below, above, plane)
+    )(*operands)
 
 
 def per_device(embeds, partner):
@@ -344,26 +393,29 @@
     rows = near + rest
     cols = [before0, after0, before1, after1]
     chain = make_exps(info, rows, (0, 1), cols, (2, 4, 3, 5), chain, None, "exps2")
-    sums, exps, units = make_exps(info, rows, (0, 1), [far0, far1], (6, 7), chain, positive, "exps3")
-
-    sums = sums + get(sums, core=1)
-    arow, plane = make_totals(info, sums, get(sums, z=-1), get(sums, z=1), get(sums, z=2))
-    plane = jnp.concatenate([plane] + [get(plane, first=k) for k in OFFSETS[1:]], axis=0)
-    plane = jnp.concatenate([plane] + [get(plane, second=k) for k in OFFSETS[1:]], axis=0)
-
-    (theirs,) = make_grads(((512, 512), (1536, 512)), None, (BF16,), info, plane, arow, exps, units, None, "grads_core")
+    sums, col_sums, exps, units = make_exps(info, rows, (0, 1), [far0, far1], (6, 7), chain, positive, "exps3")
+
+    by_row = sums + get(sums, core=1)
+    by_row = [by_row] + [get(by_row, z=k) for k in OFFSETS[1:]]
+    by_col = ring_sum(col_sums, *[get(col_sums, first=k) for k in OFFSETS[1:]])
+    by_col = [by_col] + [get(by_col, second=k) for k in OFFSETS[1:]]
+    arow, acol, loss = make_totals(info, by_row, by_col)
+
+    given = (acol, arow, exps, units)
+    (theirs,) = make_grads(((512, 512), (1536, 512)), None, (BF16,), info, *given, None, loss, "grads_core")
     core = get(theirs, core=1)
-    (far,) = make_grads(((1280, ROWS),), None, (F32,), after(info, theirs), plane, arow, exps, units, None, "grads_far")
-    far = make_pass(far, core, 768, "pass_far")
+    (far,) = make_grads(((1280, ROWS),), None, (F32,), theirs, *given, None, None, "grads_far")
+    far = make_sum(far_kernel, (far, core, loss), "sum_far")
     passed = get(far, z_own=-1)
     free, held = make_grads(
-        ((256, ROWS), (1024, ROWS)), (256, 512), (BF16, F32), after(info, far), plane, arow, exps, units, core, "grads_near"
+        ((256, ROWS), (1024, ROWS)), (256, 512), (BF16, F32), info, *given, core, far, "grads_near"
     )
     one = get(free, z_own=1)
-    held = make_pass(held, passed, 0, "pass_two")
-    two = get(held, z_own=-1)
-    (own,) = make_grads(((0, ROWS),), (0,), (F32,), after(info, held), plane, arow, exps, units, core, "grads_own")
-    grad, loss = make_final(info, embeds, mates, own, one, two, plane)
+    two = make_sum(two_kernel, (held, passed), "sum_two")
+    own_token = two
+    two = get(two, z_own=-1)
+    (own,) = make_grads(((0, ROWS),), (0,), (F32,), own_token, *given, core, None, "grads_own")
+    grad, loss = make_final((embeds, mates, own, one, two, far, passed))
     return (loss[0, 0], grad)
 
 

time: 103 us -> 98.6 us (0.957)
  Pallas kernels: 31.4 us -> 28.5 us
  starting transfers between devices: 37.9 us -> 36.6 us
    pallas_call x6, Pallas kernels: 11.7 us -> 9.6 us  [the longest x4 9.49 us: make_grads(): pl.pallas_call(functools.partial(grads_kernel, pieces, adds, carry is not...]
    ppermute x28, starting transfers between devices: 37.9 us -> 36.6 us  [get(): return lax.ppermute(value, AXES, pairs)]
  transfers between devices with their start and end apart: 28 -> 28, of which waited for: 16 -> 13; matrix products, arithmetic and copies ran while one was open for 0% -> 0% of each run, Pallas kernels for 19% -> 18%
where the time goes in v4:
time: 98.6 us; the launch traced here: 98.2 us
  starting transfers between devices  36.6 us (37%)
  waiting for transfers between devices  30.5 us (31%)
  Pallas kernels  28.5 us (29%)
  local copies, waits for them, and re-layouts  1.74 us (2%)
    ppermute x28, starting transfers between devices, get(): return lax.ppermute(value, AXES, pairs)  36.6 us
    ppermute x28, waiting for transfers between devices, get(): return lax.ppermute(value, AXES, pairs)  30.5 us
    pallas_call x4, Pallas kernels, make_exps(): pl.pallas_call(functools.partial(exps_kernel, places, rows_here, first, l...  16.5 us
    pallas_call x4, Pallas kernels, make_grads(): pl.pallas_call(functools.partial(grads_kernel, pieces, adds, carry is not...  9.49 us
  transfers between devices with their start and end apart: 28, of which 13 were waited for; matrix products, arithmetic and copies ran while one was open for 0% of the time, Pallas kernels for 18%

profile of v4, /device:TPU:0, one launch (start us, length us, event | category | flops | bytes accessed | tf_op | source)
XLA Modules:
  0.0 98.2 jit_solution(12831355292128143919)
XLA Ops:
  1.7 2.1 %collective-permute-start = (bf16[256,512]{1,0:T(8,128)(2,1)S(1)}, bf16[256,512]{1,0:T(8,128)(2,1)S(1)}, u32[]{:S(2)}, u32[]{:S(2)}) collective-permute-start(bf16[256,512]{1,0:T(8,128)(2,1)S(1)} %unit.1.unit_ref), channel_id=1, source_target_pairs={{65,0},{96,32},{0,64},{33,96},{64,1},{97,33},{1,65},{32,97},{73,8}... | collective-permute-start | bytes 786440 | tf_op jit(solution)/shard_map/ppermute | solution.py:42
  3.8 1.5 %collective-permute-start.5 = (bf16[256,512]{1,0:T(8,128)(2,1)S(1)}, bf16[256,512]{1,0:T(8,128)(2,1)S(1)}, u32[]{:S(2)}, u32[]{:S(2)}) collective-permute-start(bf16[256,512]{1,0:T(8,128)(2,1)S(1)} %unit.1.unit_ref), channel_id=1, source_target_pairs={{6,0},{56,32},{70,64},{120,96},{7,1},{57,33},{71,65},{121,97},{14,... | collective-permute-start | bytes 786440 | tf_op jit(solution)/shard_map/ppermute | solution.py:42
  5.3 1.7 %collective-permute-start.6 = (bf16[256,512]{1,0:T(8,128)(2,1)S(1)}, bf16[256,512]{1,0:T(8,128)(2,1)S(1)}, u32[]{:S(2)}, u32[]{:S(2)}) collective-permute-start(bf16[256,512]{1,0:T(8,128)(2,1)S(1)} %unit.1.unit_ref), channel_id=1, source_target_pairs={{2,0},{40,32},{66,64},{104,96},{3,1},{41,33},{67,65},{105,97},{10,... | collective-permute-start | bytes 786440 | tf_op jit(solution)/shard_map/ppermute | solution.py:42
  7.0 1.8 %collective-permute-start.9 = (bf16[256,512]{1,0:T(8,128)(2,1)S(1)}, bf16[256,512]{1,0:T(8,128)(2,1)S(1)}, u32[]{:S(2)}, u32[]{:S(2)}) collective-permute-start(bf16[256,512]{1,0:T(8,128)(2,1)S(1)} %unit.1.unit_ref), channel_id=1, source_target_pairs={{4,0},{48,32},{68,64},{112,96},{5,1},{49,33},{69,65},{113,97},{12,... | collective-permute-start | bytes 786440 | tf_op jit(solution)/shard_map/ppermute | solution.py:42
  8.8 2.2 %collective-permute-start.2 = (bf16[256,512]{1,0:T(8,128)(2,1)S(1)}, bf16[256,512]{1,0:T(8,128)(2,1)S(1)}, u32[]{:S(2)}, u32[]{:S(2)}) collective-permute-start(bf16[256,512]{1,0:T(8,128)(2,1)S(1)} %unit.1.unit_ref), channel_id=1, source_target_pairs={{64,0},{97,32},{1,64},{32,96},{65,1},{96,33},{0,65},{33,97},{72,8}... | collective-permute-start | bytes 786440 | tf_op jit(solution)/shard_map/ppermute | solution.py:42
  12.3 1.5 %collective-permute-done.6 = bf16[256,512]{1,0:T(8,128)(2,1)S(1)} collective-permute-done((bf16[256,512]{1,0:T(8,128)(2,1)S(1)}, bf16[256,512]{1,0:T(8,128)(2,1)S(1)}, u32[]{:S(2)}, u32[]{:S(2)}) %collective-permute-start.6) | collective-permute-done | bytes 262176 | tf_op jit(solution)/shard_map/ppermute | solution.py:42
  13.8 2.0 %collective-permute-start.3 = (bf16[256,512]{1,0:T(8,128)(2,1)S(1)}, bf16[256,512]{1,0:T(8,128)(2,1)S(1)}, u32[]{:S(2)}, u32[]{:S(2)}) collective-permute-start(bf16[256,512]{1,0:T(8,128)(2,1)S(1)} %collective-permute-done), channel_id=1, source_target_pairs={{65,0},{96,32},{0,64},{33,96},{64,1},{97,33},{1,65},{32,97},{73,8}... | collective-permute-start | bytes 786440 | tf_op jit(solution)/shard_map/ppermute | solution.py:42
  15.8 1.6 %collective-permute-start.7 = (bf16[512,512]{1,0:T(8,128)(2,1)S(1)}, bf16[512,512]{1,0:T(8,128)(2,1)S(1)}, u32[]{:S(2)}, u32[]{:S(2)}) collective-permute-start(bf16[512,512]{1,0:T(8,128)(2,1)S(1)} %constant_dynamic-update-slice_fusion.2.refs_3_), channel_id=1, source_target_pairs={{24,0},{38,32},{88,64},{102,96},{25,1},{39,33},{89,65},{103,97},{0... | collective-permute-start | bytes 1572872 | tf_op jit(solution)/shard_map/ppermute | solution.py:42
  17.4 1.7 %collective-permute-start.8 = (bf16[512,512]{1,0:T(8,128)(2,1)S(1)}, bf16[512,512]{1,0:T(8,128)(2,1)S(1)}, u32[]{:S(2)}, u32[]{:S(2)}) collective-permute-start(bf16[512,512]{1,0:T(8,128)(2,1)S(1)} %constant_dynamic-update-slice_fusion.2.refs_3_), channel_id=1, source_target_pairs={{8,0},{34,32},{72,64},{98,96},{9,1},{35,33},{73,65},{99,97},{16,8}... | collective-permute-start | bytes 1572872 | tf_op jit(solution)/shard_map/ppermute | solution.py:42
  19.1 1.9 %collective-permute-start.11 = (bf16[512,512]{1,0:T(8,128)(2,1)S(1)}, bf16[512,512]{1,0:T(8,128)(2,1)S(1)}, u32[]{:S(2)}, u32[]{:S(2)}) collective-permute-start(bf16[512,512]{1,0:T(8,128)(2,1)S(1)} %constant_dynamic-update-slice_fusion.4.refs_4_), channel_id=1, source_target_pairs={{8,0},{34,32},{72,64},{98,96},{9,1},{35,33},{73,65},{99,97},{16,8}... | collective-permute-start | bytes 1572872 | tf_op jit(solution)/shard_map/ppermute | solution.py:42
  21.4 1.6 %collective-permute-start.12 = (bf16[512,512]{1,0:T(8,128)(2,1)S(1)}, bf16[512,512]{1,0:T(8,128)(2,1)S(1)}, u32[]{:S(2)}, u32[]{:S(2)}) collective-permute-start(bf16[512,512]{1,0:T(8,128)(2,1)S(1)} %constant_dynamic-update-slice_fusion.4.refs_4_), channel_id=1, source_target_pairs={{24,0},{38,32},{88,64},{102,96},{25,1},{39,33},{89,65},{103,97},{0... | collective-permute-start | bytes 1572872 | tf_op jit(solution)/shard_map/ppermute | solution.py:42
  23.1 2.7 %exps0.1 = (f32[2048,128]{1,0:T(8,128)S(1)}, f32[8,4096]{1,0:T(8,128)S(1)}, bf16[2048,4096]{1,0:T(8,128)(2,1)S(1)}, bf16[4096,512]{1,0:T(8,128)(2,1)S(1)}) custom-call(s32[4]{0:T(128)S(1)} %pad_add_fusion.refs_0_.info_ref, bf16[512,512]{1,0:T(8,128)(2,1)S(1)} %pad_maximum_fusion.refs_1_, bf16[512,512]{1,0:T(8,128)(2,1)S(1)} %collective-permute-done.1.refs_2_, ...), custom_call_target="tpu_custom_call" | custom-call | flops 8589934592 | bytes 1048576 | tf_op jit(solution)/shard_map/exps0/pallas_call | solution.py:204
  25.9 2.7 %exps1.1 = (f32[2048,128]{1,0:T(8,128)S(1)}, f32[8,4096]{1,0:T(8,128)S(1)}, bf16[2048,4096]{1,0:T(8,128)(2,1)S(1)}, bf16[4096,512]{1,0:T(8,128)(2,1)S(1)}) custom-call(s32[4]{0:T(128)S(1)} %pad_add_fusion.refs_0_.info_ref, bf16[512,512]{1,0:T(8,128)(2,1)S(1)} %constant_dynamic-update-slice_fusion.refs_1_.refs_3_, ...), custom_call_target="tpu_custom_call", output_to_operand_aliasing={{2}: (7, {}), {3}: (8, {})} | custom-call | flops 8589934592 | bytes 1048576 | tf_op jit(solution)/shard_map/exps1/pallas_call | solution.py:204
  28.5 3.7 %collective-permute-done.11.refs_8_ = bf16[512,512]{1,0:T(8,128)(2,1)S(1)} collective-permute-done((bf16[512,512]{1,0:T(8,128)(2,1)S(1)}, bf16[512,512]{1,0:T(8,128)(2,1)S(1)}, u32[]{:S(2)}, u32[]{:S(2)}) %collective-permute-start.11) | collective-permute-done | bytes 524320 | tf_op jit(solution)/shard_map/ppermute | solution.py:42
  32.2 2.9 %collective-permute-start.13 = (bf16[512,512]{1,0:T(8,128)(2,1)S(1)}, bf16[512,512]{1,0:T(8,128)(2,1)S(1)}, u32[]{:S(2)}, u32[]{:S(2)}) collective-permute-start(bf16[512,512]{1,0:T(8,128)(2,1)S(1)} %collective-permute-done.11.refs_8_), channel_id=1, source_target_pairs={{8,0},{34,32},{72,64},{98,96},{9,1},{35,33},{73,65},{99,97},{16,8}... | collective-permute-start | bytes 1572872 | tf_op jit(solution)/shard_map/ppermute | solution.py:42
  35.1 6.9 %exps2.1 = (f32[2048,128]{1,0:T(8,128)S(1)}, f32[8,4096]{1,0:T(8,128)S(1)}, bf16[2048,4096]{1,0:T(8,128)(2,1)S(1)}, bf16[4096,512]{1,0:T(8,128)(2,1)S(1)}) custom-call(s32[4]{0:T(128)S(1)} %pad_add_fusion.refs_0_.info_ref, bf16[512,512]{1,0:T(8,128)(2,1)S(1)} %pad_maximum_fusion.refs_1_, ...), custom_call_target="tpu_custom_call", output_to_operand_aliasing={{2}: (11, {}), {3}: (12, {})} | custom-call | flops 17179869184 | bytes 2097152 | tf_op jit(solution)/shard_map/exps2/pallas_call | solution.py:204
  42.1 3.4 %collective-permute-done.10.refs_5_ = bf16[512,512]{1,0:T(8,128)(2,1)S(1)} collective-permute-done((bf16[512,512]{1,0:T(8,128)(2,1)S(1)}, bf16[512,512]{1,0:T(8,128)(2,1)S(1)}, u32[]{:S(2)}, u32[]{:S(2)}) %collective-permute-start.10) | collective-permute-done | bytes 524320 | tf_op jit(solution)/shard_map/ppermute | solution.py:42
  45.5 4.1 %exps3.1 = (f32[8,256]{1,0:T(8,128)S(1)}, f32[24,256]{1,0:T(8,128)S(1)}, bf16[2048,4096]{1,0:T(8,128)(2,1)S(1)}, bf16[4096,512]{1,0:T(8,128)(2,1)S(1)}) custom-call(s32[4]{0:T(128)S(1)} %pad_add_fusion.refs_0_.info_ref, bf16[512,512]{1,0:T(8,128)(2,1)S(1)} %pad_maximum_fusion.refs_1_, ...), custom_call_target="tpu_custom_call", output_to_operand_aliasing={{2}: (9, {}), {3}: (10, {})} | custom-call | flops 8589934592 | bytes 1048576 | tf_op jit(solution)/shard_map/exps3/pallas_call | solution.py:204
  50.4 3.9 %collective-permute-start.19 = (f32[24,256]{1,0:T(8,128)S(1)}, f32[24,256]{1,0:T(8,128)S(1)}, u32[]{:S(2)}, u32[]{:S(2)}) collective-permute-start(f32[24,256]{1,0:T(8,128)S(1)} %get-tuple-element.55), channel_id=1, source_target_pairs={{6,0},{56,32},{70,64},{120,96},{7,1},{57,33},{71,65},{121,97},{14,... | collective-permute-start | bytes 73736 | tf_op jit(solution)/shard_map/ppermute | solution.py:42
  55.8 2.3 %collective-permute-done.20 = f32[24,256]{1,0:T(8,128)S(1)} collective-permute-done((f32[24,256]{1,0:T(8,128)S(1)}, f32[24,256]{1,0:T(8,128)S(1)}, u32[]{:S(2)}, u32[]{:S(2)}) %collective-permute-start.20) | collective-permute-done | bytes 24608 | tf_op jit(solution)/shard_map/ppermute | solution.py:42
  58.2 3.2 %collective-permute-start.22 = (f32[24,256]{1,0:T(8,128)S(1)}, f32[24,256]{1,0:T(8,128)S(1)}, u32[]{:S(2)}, u32[]{:S(2)}) collective-permute-start(f32[24,256]{1,0:T(8,128)S(1)} %add_add_fusion.refs_4_), channel_id=1, source_target_pairs={{8,0},{34,32},{72,64},{98,96},{9,1},{35,33},{73,65},{99,97},{16,8}... | collective-permute-start | bytes 73736 | tf_op jit(solution)/shard_map/ppermute | solution.py:42
  61.4 1.7 %collective-permute-start.15 = (f32[8,256]{1,0:T(8,128)S(1)}, f32[8,256]{1,0:T(8,128)S(1)}, u32[]{:S(2)}, u32[]{:S(2)}) collective-permute-start(f32[8,256]{1,0:T(8,128)S(1)} %add.16.refs_0_), channel_id=1, source_target_pairs={{65,0},{97,32},{0,64},{32,96},{64,1},{96,33},{1,65},{33,97},{73,8}... | collective-permute-start | bytes 24584 | tf_op jit(solution)/shard_map/ppermute | solution.py:42
  63.1 1.6 %collective-permute-start.16 = (f32[8,256]{1,0:T(8,128)S(1)}, f32[8,256]{1,0:T(8,128)S(1)}, u32[]{:S(2)}, u32[]{:S(2)}) collective-permute-start(f32[8,256]{1,0:T(8,128)S(1)} %add.16.refs_0_), channel_id=1, source_target_pairs={{64,0},{96,32},{1,64},{33,96},{65,1},{97,33},{0,65},{32,97},{72,8}... | collective-permute-start | bytes 24584 | tf_op jit(solution)/shard_map/ppermute | solution.py:42
  64.7 1.6 %collective-permute-done.15.refs_1_ = f32[8,256]{1,0:T(8,128)S(1)} collective-permute-done((f32[8,256]{1,0:T(8,128)S(1)}, f32[8,256]{1,0:T(8,128)S(1)}, u32[]{:S(2)}, u32[]{:S(2)}) %collective-permute-start.15) | collective-permute-done | bytes 8224 | tf_op jit(solution)/shard_map/ppermute | solution.py:42
  66.9 4.6 %collective-permute-done.17.refs_3_ = f32[8,256]{1,0:T(8,128)S(1)} collective-permute-done((f32[8,256]{1,0:T(8,128)S(1)}, f32[8,256]{1,0:T(8,128)S(1)}, u32[]{:S(2)}, u32[]{:S(2)}) %collective-permute-start.17) | collective-permute-done | bytes 8224 | tf_op jit(solution)/shard_map/ppermute | solution.py:42
  72.3 4.7 %grads_core.1 = bf16[1040,512]{1,0:T(8,128)(2,1)S(1)} custom-call(f32[32,128]{1,0:T(8,128)S(1)} %get-tuple-element.64.acol_ref, bf16[2048,128]{1,0:T(8,128)(2,1)S(1)} %get-tuple-element.58.arow_ref, bf16[2048,4096]{1,0:T(8,128)(2,1)S(1)} %get-tuple-element.59.exps_ref, bf16[4096,512]{1,0:T(8,128)(2,1)S(1)} %get-tuple-element.60.unit_ref, ...), custom_call_target="tpu_custom_call" | custom-call | flops 4294967296 | bytes 12582912 | tf_op jit(solution)/shard_map/grads_core/pallas_call | solution.py:308
  78.4 1.4 %collective-permute-done.24.core_ref.refs_0_ = bf16[1040,512]{1,0:T(8,128)(2,1)S(1)} collective-permute-done((bf16[1040,512]{1,0:T(8,128)(2,1)S(1)}, bf16[1040,512]{1,0:T(8,128)(2,1)S(1)}, u32[]{:S(2)}, u32[]{:S(2)}) %collective-permute-start.24) | collective-permute-done | bytes 1064992 | tf_op jit(solution)/shard_map/ppermute | solution.py:42
  80.5 2.3 %grads_near.1 = (bf16[272,512]{1,0:T(8,128)(2,1)S(1)}, f32[256,512]{1,0:T(8,128)S(1)}) custom-call(f32[32,128]{1,0:T(8,128)S(1)} %get-tuple-element.64.acol_ref, bf16[2048,128]{1,0:T(8,128)(2,1)S(1)} %get-tuple-element.58.arow_ref, bf16[2048,4096]{1,0:T(8,128)(2,1)S(1)} %get-tuple-element.59.exps_ref, bf16[4096,512]{1,0:T(8,128)(2,1)S(1)} %get-tuple-element.60.unit_ref, ...), custom_call_target="tpu_custom_call" | custom-call | flops 2147483648 | bytes 8388608 | tf_op jit(solution)/shard_map/grads_near/pallas_call | solution.py:308
  82.9 2.9 %collective-permute-start.26 = (bf16[272,512]{1,0:T(8,128)(2,1)S(1)}, bf16[272,512]{1,0:T(8,128)(2,1)S(1)}, u32[]{:S(2)}, u32[]{:S(2)}) collective-permute-start(bf16[272,512]{1,0:T(8,128)(2,1)S(1)} %get-tuple-element.65), channel_id=1, source_target_pairs={{64,0},{97,32},{1,64},{32,96},{65,1},{96,33},{0,65},{33,97},{72,8}... | collective-permute-start | bytes 835592 | tf_op jit(solution)/shard_map/ppermute | solution.py:42
  85.8 3.5 %collective-permute-done.25.far_ref.passed_ref = bf16[272,512]{1,0:T(8,128)(2,1)S(1)} collective-permute-done((bf16[272,512]{1,0:T(8,128)(2,1)S(1)}, bf16[272,512]{1,0:T(8,128)(2,1)S(1)}, u32[]{:S(2)}, u32[]{:S(2)}) %collective-permute-start.25) | collective-permute-done | bytes 278560 | tf_op jit(solution)/shard_map/ppermute | solution.py:42
  90.6 1.7 %collective-permute-done.26.one_ref = bf16[272,512]{1,0:T(8,128)(2,1)S(1)} collective-permute-done((bf16[272,512]{1,0:T(8,128)(2,1)S(1)}, bf16[272,512]{1,0:T(8,128)(2,1)S(1)}, u32[]{:S(2)}, u32[]{:S(2)}) %collective-permute-start.26) | collective-permute-done | bytes 278560 | tf_op jit(solution)/shard_map/ppermute | solution.py:42
  92.3 4.8 %collective-permute-done.27.two_ref = bf16[272,512]{1,0:T(8,128)(2,1)S(1)} collective-permute-done((bf16[272,512]{1,0:T(8,128)(2,1)S(1)}, bf16[272,512]{1,0:T(8,128)(2,1)S(1)}, u32[]{:S(2)}, u32[]{:S(2)}) %collective-permute-start.27) | collective-permute-done | bytes 278560 | tf_op jit(solution)/shard_map/ppermute | solution.py:42
  (54 shorter events, 11.2 us)
Async XLA Ops:
  0.6 1.0 copy-start
  1.7 10.4 %collective-permute-start = (bf16[256,512]{1,0:T(8,128)(2,1)S(1)}, bf16[256,512]{1,0:T(8,128)(2,1)S(1)}, u32[]{:S(2)}, u32[]{:S(2)}) collective-permute-start(bf16[256,512]{1,0:T(8,128)(2,1)S(1)} %unit.1.unit_ref), channel_id=1, source_target_pairs={{65,0},{96,32},{0,64},{33,96},{64,1},{97,33},{1,65},{32,97},{73,8}... | collective-permute-start | bytes 786440 | tf_op jit(solution)/shard_map/ppermute | solution.py:42
  3.8 8.5 %collective-permute-start.5 = (bf16[256,512]{1,0:T(8,128)(2,1)S(1)}, bf16[256,512]{1,0:T(8,128)(2,1)S(1)}, u32[]{:S(2)}, u32[]{:S(2)}) collective-permute-start(bf16[256,512]{1,0:T(8,128)(2,1)S(1)} %unit.1.unit_ref), channel_id=1, source_target_pairs={{6,0},{56,32},{70,64},{120,96},{7,1},{57,33},{71,65},{121,97},{14,... | collective-permute-start | bytes 786440 | tf_op jit(solution)/shard_map/ppermute | solution.py:42
  5.3 8.5 %collective-permute-start.6 = (bf16[256,512]{1,0:T(8,128)(2,1)S(1)}, bf16[256,512]{1,0:T(8,128)(2,1)S(1)}, u32[]{:S(2)}, u32[]{:S(2)}) collective-permute-start(bf16[256,512]{1,0:T(8,128)(2,1)S(1)} %unit.1.unit_ref), channel_id=1, source_target_pairs={{2,0},{40,32},{66,64},{104,96},{3,1},{41,33},{67,65},{105,97},{10,... | collective-permute-start | bytes 786440 | tf_op jit(solution)/shard_map/ppermute | solution.py:42
  7.0 10.4 %collective-permute-start.9 = (bf16[256,512]{1,0:T(8,128)(2,1)S(1)}, bf16[256,512]{1,0:T(8,128)(2,1)S(1)}, u32[]{:S(2)}, u32[]{:S(2)}) collective-permute-start(bf16[256,512]{1,0:T(8,128)(2,1)S(1)} %unit.1.unit_ref), channel_id=1, source_target_pairs={{4,0},{48,32},{68,64},{112,96},{5,1},{49,33},{69,65},{113,97},{12,... | collective-permute-start | bytes 786440 | tf_op jit(solution)/shard_map/ppermute | solution.py:42
  8.8 10.3 %collective-permute-start.2 = (bf16[256,512]{1,0:T(8,128)(2,1)S(1)}, bf16[256,512]{1,0:T(8,128)(2,1)S(1)}, u32[]{:S(2)}, u32[]{:S(2)}) collective-permute-start(bf16[256,512]{1,0:T(8,128)(2,1)S(1)} %unit.1.unit_ref), channel_id=1, source_target_pairs={{64,0},{97,32},{1,64},{32,96},{65,1},{96,33},{0,65},{33,97},{72,8}... | collective-permute-start | bytes 786440 | tf_op jit(solution)/shard_map/ppermute | solution.py:42
  11.1 0.7 copy-start.2
  12.2 10.9 %collective-permute-start.1 = (bf16[512,512]{1,0:T(8,128)(2,1)S(1)}, bf16[512,512]{1,0:T(8,128)(2,1)S(1)}, u32[]{:S(2)}, u32[]{:S(2)}) collective-permute-start(bf16[512,512]{1,0:T(8,128)(2,1)S(1)} %pad_maximum_fusion.refs_1_), channel_id=1, source_target_pairs={{32,0},{0,32},{96,64},{64,96},{33,1},{1,33},{97,65},{65,97},{40,8}... | collective-permute-start | bytes 1572872 | tf_op jit(solution)/shard_map/ppermute | solution.py:42
  13.8 7.7 %collective-permute-start.3 = (bf16[256,512]{1,0:T(8,128)(2,1)S(1)}, bf16[256,512]{1,0:T(8,128)(2,1)S(1)}, u32[]{:S(2)}, u32[]{:S(2)}) collective-permute-start(bf16[256,512]{1,0:T(8,128)(2,1)S(1)} %collective-permute-done), channel_id=1, source_target_pairs={{65,0},{96,32},{0,64},{33,96},{64,1},{97,33},{1,65},{32,97},{73,8}... | collective-permute-start | bytes 786440 | tf_op jit(solution)/shard_map/ppermute | solution.py:42
  15.8 19.3 %collective-permute-start.7 = (bf16[512,512]{1,0:T(8,128)(2,1)S(1)}, bf16[512,512]{1,0:T(8,128)(2,1)S(1)}, u32[]{:S(2)}, u32[]{:S(2)}) collective-permute-start(bf16[512,512]{1,0:T(8,128)(2,1)S(1)} %constant_dynamic-update-slice_fusion.2.refs_3_), channel_id=1, source_target_pairs={{24,0},{38,32},{88,64},{102,96},{25,1},{39,33},{89,65},{103,97},{0... | collective-permute-start | bytes 1572872 | tf_op jit(solution)/shard_map/ppermute | solution.py:42
  17.4 17.7 %collective-permute-start.8 = (bf16[512,512]{1,0:T(8,128)(2,1)S(1)}, bf16[512,512]{1,0:T(8,128)(2,1)S(1)}, u32[]{:S(2)}, u32[]{:S(2)}) collective-permute-start(bf16[512,512]{1,0:T(8,128)(2,1)S(1)} %constant_dynamic-update-slice_fusion.2.refs_3_), channel_id=1, source_target_pairs={{8,0},{34,32},{72,64},{98,96},{9,1},{35,33},{73,65},{99,97},{16,8}... | collective-permute-start | bytes 1572872 | tf_op jit(solution)/shard_map/ppermute | solution.py:42
  19.1 13.1 %collective-permute-start.11 = (bf16[512,512]{1,0:T(8,128)(2,1)S(1)}, bf16[512,512]{1,0:T(8,128)(2,1)S(1)}, u32[]{:S(2)}, u32[]{:S(2)}) collective-permute-start(bf16[512,512]{1,0:T(8,128)(2,1)S(1)} %constant_dynamic-update-slice_fusion.4.refs_4_), channel_id=1, source_target_pairs={{8,0},{34,32},{72,64},{98,96},{9,1},{35,33},{73,65},{99,97},{16,8}... | collective-permute-start | bytes 1572872 | tf_op jit(solution)/shard_map/ppermute | solution.py:42
  21.4 10.8 %collective-permute-start.12 = (bf16[512,512]{1,0:T(8,128)(2,1)S(1)}, bf16[512,512]{1,0:T(8,128)(2,1)S(1)}, u32[]{:S(2)}, u32[]{:S(2)}) collective-permute-start(bf16[512,512]{1,0:T(8,128)(2,1)S(1)} %constant_dynamic-update-slice_fusion.4.refs_4_), channel_id=1, source_target_pairs={{24,0},{38,32},{88,64},{102,96},{25,1},{39,33},{89,65},{103,97},{0... | collective-permute-start | bytes 1572872 | tf_op jit(solution)/shard_map/ppermute | solution.py:42
  23.0 2.8 %collective-permute-start.4 = (bf16[512,512]{1,0:T(8,128)(2,1)S(1)}, bf16[512,512]{1,0:T(8,128)(2,1)S(1)}, u32[]{:S(2)}, u32[]{:S(2)}) collective-permute-start(bf16[512,512]{1,0:T(8,128)(2,1)S(1)} %constant_dynamic-update-slice_fusion.refs_1_.refs_3_), channel_id=1, source_target_pairs={{32,0},{0,32},{96,64},{64,96},{33,1},{1,33},{97,65},{65,97},{40,8}... | collective-permute-start | bytes 1572872 | tf_op jit(solution)/shard_map/ppermute | solution.py:42
  32.2 9.8 %collective-permute-start.13 = (bf16[512,512]{1,0:T(8,128)(2,1)S(1)}, bf16[512,512]{1,0:T(8,128)(2,1)S(1)}, u32[]{:S(2)}, u32[]{:S(2)}) collective-permute-start(bf16[512,512]{1,0:T(8,128)(2,1)S(1)} %collective-permute-done.11.refs_8_), channel_id=1, source_target_pairs={{8,0},{34,32},{72,64},{98,96},{9,1},{35,33},{73,65},{99,97},{16,8}... | collective-permute-start | bytes 1572872 | tf_op jit(solution)/shard_map/ppermute | solution.py:42
  35.1 10.4 %collective-permute-start.10 = (bf16[512,512]{1,0:T(8,128)(2,1)S(1)}, bf16[512,512]{1,0:T(8,128)(2,1)S(1)}, u32[]{:S(2)}, u32[]{:S(2)}) collective-permute-start(bf16[512,512]{1,0:T(8,128)(2,1)S(1)} %collective-permute-done.7.refs_5_), channel_id=1, source_target_pairs={{24,0},{38,32},{88,64},{102,96},{25,1},{39,33},{89,65},{103,97},{0... | collective-permute-start | bytes 1572872 | tf_op jit(solution)/shard_map/ppermute | solution.py:42
  49.7 5.4 %collective-permute-start.18 = (f32[24,256]{1,0:T(8,128)S(1)}, f32[24,256]{1,0:T(8,128)S(1)}, u32[]{:S(2)}, u32[]{:S(2)}) collective-permute-start(f32[24,256]{1,0:T(8,128)S(1)} %get-tuple-element.55), channel_id=1, source_target_pairs={{4,0},{48,32},{68,64},{112,96},{5,1},{49,33},{69,65},{113,97},{12,... | collective-permute-start | bytes 73736 | tf_op jit(solution)/shard_map/ppermute | solution.py:42
  50.4 5.4 %collective-permute-start.19 = (f32[24,256]{1,0:T(8,128)S(1)}, f32[24,256]{1,0:T(8,128)S(1)}, u32[]{:S(2)}, u32[]{:S(2)}) collective-permute-start(f32[24,256]{1,0:T(8,128)S(1)} %get-tuple-element.55), channel_id=1, source_target_pairs={{6,0},{56,32},{70,64},{120,96},{7,1},{57,33},{71,65},{121,97},{14,... | collective-permute-start | bytes 73736 | tf_op jit(solution)/shard_map/ppermute | solution.py:42
  54.3 3.8 %collective-permute-start.20 = (f32[24,256]{1,0:T(8,128)S(1)}, f32[24,256]{1,0:T(8,128)S(1)}, u32[]{:S(2)}, u32[]{:S(2)}) collective-permute-start(f32[24,256]{1,0:T(8,128)S(1)} %get-tuple-element.55), channel_id=1, source_target_pairs={{2,0},{40,32},{66,64},{104,96},{3,1},{41,33},{67,65},{105,97},{10,... | collective-permute-start | bytes 73736 | tf_op jit(solution)/shard_map/ppermute | solution.py:42
  54.3 7.1 %collective-permute-start.14 = (f32[8,256]{1,0:T(8,128)S(1)}, f32[8,256]{1,0:T(8,128)S(1)}, u32[]{:S(2)}, u32[]{:S(2)}) collective-permute-start(f32[8,256]{1,0:T(8,128)S(1)} %get-tuple-element.54), channel_id=1, source_target_pairs={{32,0},{0,32},{96,64},{64,96},{33,1},{1,33},{97,65},{65,97},{40,8}... | collective-permute-start | bytes 24584 | tf_op jit(solution)/shard_map/ppermute | solution.py:42
  58.1 13.4 %collective-permute-start.21 = (f32[24,256]{1,0:T(8,128)S(1)}, f32[24,256]{1,0:T(8,128)S(1)}, u32[]{:S(2)}, u32[]{:S(2)}) collective-permute-start(f32[24,256]{1,0:T(8,128)S(1)} %add_add_fusion.refs_4_), channel_id=1, source_target_pairs={{24,0},{38,32},{88,64},{102,96},{25,1},{39,33},{89,65},{103,97},{0... | collective-permute-start | bytes 73736 | tf_op jit(solution)/shard_map/ppermute | solution.py:42
  58.2 13.3 %collective-permute-start.22 = (f32[24,256]{1,0:T(8,128)S(1)}, f32[24,256]{1,0:T(8,128)S(1)}, u32[]{:S(2)}, u32[]{:S(2)}) collective-permute-start(f32[24,256]{1,0:T(8,128)S(1)} %add_add_fusion.refs_4_), channel_id=1, source_target_pairs={{8,0},{34,32},{72,64},{98,96},{9,1},{35,33},{73,65},{99,97},{16,8}... | collective-permute-start | bytes 73736 | tf_op jit(solution)/shard_map/ppermute | solution.py:42
  61.4 10.1 %collective-permute-start.23 = (f32[24,256]{1,0:T(8,128)S(1)}, f32[24,256]{1,0:T(8,128)S(1)}, u32[]{:S(2)}, u32[]{:S(2)}) collective-permute-start(f32[24,256]{1,0:T(8,128)S(1)} %add_add_fusion.refs_4_), channel_id=1, source_target_pairs={{16,0},{36,32},{80,64},{100,96},{17,1},{37,33},{81,65},{101,97},{2... | collective-permute-start | bytes 73736 | tf_op jit(solution)/shard_map/ppermute | solution.py:42
  61.4 4.9 %collective-permute-start.15 = (f32[8,256]{1,0:T(8,128)S(1)}, f32[8,256]{1,0:T(8,128)S(1)}, u32[]{:S(2)}, u32[]{:S(2)}) collective-permute-start(f32[8,256]{1,0:T(8,128)S(1)} %add.16.refs_0_), channel_id=1, source_target_pairs={{65,0},{97,32},{0,64},{32,96},{64,1},{96,33},{1,65},{33,97},{73,8}... | collective-permute-start | bytes 24584 | tf_op jit(solution)/shard_map/ppermute | solution.py:42
  63.1 3.8 %collective-permute-start.16 = (f32[8,256]{1,0:T(8,128)S(1)}, f32[8,256]{1,0:T(8,128)S(1)}, u32[]{:S(2)}, u32[]{:S(2)}) collective-permute-start(f32[8,256]{1,0:T(8,128)S(1)} %add.16.refs_0_), channel_id=1, source_target_pairs={{64,0},{96,32},{1,64},{33,96},{65,1},{97,33},{0,65},{32,97},{72,8}... | collective-permute-start | bytes 24584 | tf_op jit(solution)/shard_map/ppermute | solution.py:42
  66.4 5.2 %collective-permute-start.17 = (f32[8,256]{1,0:T(8,128)S(1)}, f32[8,256]{1,0:T(8,128)S(1)}, u32[]{:S(2)}, u32[]{:S(2)}) collective-permute-start(f32[8,256]{1,0:T(8,128)S(1)} %add.16.refs_0_), channel_id=1, source_target_pairs={{1,0},{33,32},{65,64},{97,96},{0,1},{32,33},{64,65},{96,97},{9,8},... | collective-permute-start | bytes 24584 | tf_op jit(solution)/shard_map/ppermute | solution.py:42
  77.0 2.8 %collective-permute-start.24 = (bf16[1040,512]{1,0:T(8,128)(2,1)S(1)}, bf16[1040,512]{1,0:T(8,128)(2,1)S(1)}, u32[]{:S(2)}, u32[]{:S(2)}) collective-permute-start(bf16[1040,512]{1,0:T(8,128)(2,1)S(1)} %grads_core.1), channel_id=1, source_target_pairs={{32,0},{0,32},{96,64},{64,96},{33,1},{1,33},{97,65},{65,97},{40,8}... | collective-permute-start | bytes 3194888 | tf_op jit(solution)/shard_map/ppermute | solution.py:42
  79.8 9.4 %collective-permute-start.25 = (bf16[272,512]{1,0:T(8,128)(2,1)S(1)}, bf16[272,512]{1,0:T(8,128)(2,1)S(1)}, u32[]{:S(2)}, u32[]{:S(2)}) collective-permute-start(bf16[272,512]{1,0:T(8,128)(2,1)S(1)} %sum_far.1.refs_1_.here_ref), channel_id=1, source_target_pairs={{65,0},{96,32},{0,64},{33,96},{64,1},{97,33},{1,65},{32,97},{73,8}... | collective-permute-start | bytes 835592 | tf_op jit(solution)/shard_map/ppermute | solution.py:42
  82.9 9.5 %collective-permute-start.26 = (bf16[272,512]{1,0:T(8,128)(2,1)S(1)}, bf16[272,512]{1,0:T(8,128)(2,1)S(1)}, u32[]{:S(2)}, u32[]{:S(2)}) collective-permute-start(bf16[272,512]{1,0:T(8,128)(2,1)S(1)} %get-tuple-element.65), channel_id=1, source_target_pairs={{64,0},{97,32},{1,64},{32,96},{65,1},{96,33},{0,65},{33,97},{72,8}... | collective-permute-start | bytes 835592 | tf_op jit(solution)/shard_map/ppermute | solution.py:42
  89.3 7.8 %copy-start.1 = (bf16[256,512]{1,0:T(8,128)(2,1)S(1)}, bf16[256,512]{1,0:T(8,128)(2,1)}, u32[]{:S(2)}) copy-start(bf16[256,512]{1,0:T(8,128)(2,1)} %z_ref.3) | copy-start | bytes 786436
  89.3 7.8 %collective-permute-start.27 = (bf16[272,512]{1,0:T(8,128)(2,1)S(1)}, bf16[272,512]{1,0:T(8,128)(2,1)S(1)}, u32[]{:S(2)}, u32[]{:S(2)}) collective-permute-start(bf16[272,512]{1,0:T(8,128)(2,1)S(1)} %sum_two.1), channel_id=1, source_target_pairs={{65,0},{96,32},{0,64},{33,96},{64,1},{97,33},{1,65},{32,97},{73,8}... | collective-permute-start | bytes 835592 | tf_op jit(solution)/shard_map/ppermute | solution.py:42

commit v5 on v4

--- a/solution.py
+++ b/solution.py
@@ -39,6 +39,19 @@
                     away = z + (z_own if pc == 0 else -z_own)
                     source = place((px + x) % 4, (py + y) % 4, (pz + away) % 4, pc ^ core)
                     pairs.append((source, place(px, py, pz, pc)))
+    return lax.ppermute(value, AXES, pairs)
+
+
+def swap(value, way, step):
+    pairs = []
+    for px in range(4):
+        for py in range(4):
+            for pz in range(4):
+                for pc in range(2):
+                    at = [px, py, pz]
+                    axis = {"z": 2, "first": pc, "second": 1 - pc}[way]
+                    at[axis] = at[axis] ^ 1 if step == 0 else 3 - at[axis]
+                    pairs.append((place(*at, pc), place(px, py, pz, pc)))
     return lax.ppermute(value, AXES, pairs)
 
 
@@ -230,9 +243,9 @@
 
 
 def totals_kernel(info_ref, *refs):
-    row_refs, col_refs, (arow_ref, acol_ref, loss_ref, recips, col_recips) = refs[:4], refs[4:8], refs[8:]
-    recips[...] = 1.0 / ring_sum(*[ref[...] for ref in row_refs])
-    both = ring_sum(*[ref[...] for ref in col_refs])
+    row_refs, col_refs, (arow_ref, acol_ref, loss_ref, recips, col_recips) = refs[:2], refs[2:4], refs[4:]
+    recips[...] = 1.0 / (row_refs[0][...] + row_refs[1][...])
+    both = col_refs[0][...] + col_refs[1][...]
     totals = both[:16]
     col_recips[...] = 1.0 / totals
     logs = jnp.sum(jnp.sum(jnp.log(totals), axis=0, keepdims=True), axis=1, keepdims=True)
@@ -255,7 +268,7 @@
             jax.ShapeDtypeStruct((32, 128), F32),
             jax.ShapeDtypeStruct((16, E), BF16),
         ),
-        in_specs=[smem()] + [vmem()] * 8,
+        in_specs=[smem()] + [vmem()] * 4,
         out_specs=(vmem(), vmem(), vmem()),
         scratch_shapes=[pltpu.VMEM((8, ROWS), F32), pltpu.VMEM((16, ROWS), F32)],
         compiler_params=params(4),
@@ -389,16 +402,20 @@
     rest = [rest, get(rest, core=1)]
     chain = make_exps(info, rest, (1,), [line0, line1], (0, 1), chain, None, "exps1")
     far0 = get(after(before0, after0, chain[0]), second=-1)
+    rows = near + rest
+    chain = make_exps(info, rows, (0, 1), [before0, after0], (2, 4), chain, None, "exps2")
     far1 = get(after(after1, before1, chain[0]), second=1)
-    rows = near + rest
-    cols = [before0, after0, before1, after1]
-    chain = make_exps(info, rows, (0, 1), cols, (2, 4, 3, 5), chain, None, "exps2")
-    sums, col_sums, exps, units = make_exps(info, rows, (0, 1), [far0, far1], (6, 7), chain, positive, "exps3")
+    chain = make_exps(info, rows, (0, 1), [before1, after1, far0], (3, 5, 6), chain, None, "exps3")
+    sums, col_sums, exps, units = make_exps(info, rows, (0, 1), [far1], (7,), chain, positive, "exps4")
 
     by_row = sums + get(sums, core=1)
-    by_row = [by_row] + [get(by_row, z=k) for k in OFFSETS[1:]]
-    by_col = ring_sum(col_sums, *[get(col_sums, first=k) for k in OFFSETS[1:]])
-    by_col = [by_col] + [get(by_col, second=k) for k in OFFSETS[1:]]
+    by_col = col_sums + swap(col_sums, "first", 0)
+    by_col = by_col + swap(after(by_col, by_row), "first", 1)
+    by_row = by_row + swap(by_row, "z", 0)
+    by_col = by_col + swap(by_col, "second", 0)
+    by_col = after(by_col, by_row)
+    by_row = [by_row, swap(by_row, "z", 1)]
+    by_col = [by_col, swap(by_col, "second", 1)]
     arow, acol, loss = make_totals(info, by_row, by_col)
 
     given = (acol, arow, exps, units)

time: 98.6 us -> 93.6 us (0.949)
  waiting for transfers between devices: 30.5 us -> 26.6 us
  starting transfers between devices: 36.6 us -> 34.5 us
    ppermute x28 -> x19, waiting for transfers between devices: 30.5 us -> 16.4 us  [get(): return lax.ppermute(value, AXES, pairs)]
    ppermute x0 -> x6, waiting for transfers between devices: none -> 10.2 us  [swap(): return lax.ppermute(value, AXES, pairs)]
    ppermute x28 -> x19, starting transfers between devices: 36.6 us -> 26.6 us  [get(): return lax.ppermute(value, AXES, pairs)]
    ppermute x0 -> x6, starting transfers between devices: none -> 7.83 us  [swap(): return lax.ppermute(value, AXES, pairs)]
    pallas_call x4 -> x5, Pallas kernels: 16.5 us -> 17.3 us  [make_exps(): pl.pallas_call(functools.partial(exps_kernel, places, rows_here, first, l...]
  transfers between devices with their start and end apart: 28 -> 25, of which waited for: 13 -> 12; matrix products, arithmetic and copies ran while one was open for 0% -> 0% of each run, Pallas kernels for 18% -> 21%
where the time goes in v5:
time: 93.6 us; the launch traced here: 93.1 us
  starting transfers between devices  34.5 us (37%)
  Pallas kernels  29.3 us (31%)
  waiting for transfers between devices  26.6 us (28%)
  local copies, waits for them, and re-layouts  1.74 us (2%)
    ppermute x19, starting transfers between devices, get(): return lax.ppermute(value, AXES, pairs)  26.6 us
    pallas_call x5, Pallas kernels, make_exps(): pl.pallas_call(functools.partial(exps_kernel, places, rows_here, first, l...  17.3 us
    ppermute x19, waiting for transfers between devices, get(): return lax.ppermute(value, AXES, pairs)  16.4 us
    ppermute x6, waiting for transfers between devices, swap(): return lax.ppermute(value, AXES, pairs)  10.2 us
    pallas_call x4, Pallas kernels, make_grads(): pl.pallas_call(functools.partial(grads_kernel, pieces, adds, carry is not...  9.49 us
    ppermute x6, starting transfers between devices, swap(): return lax.ppermute(value, AXES, pairs)  7.83 us
  transfers between devices with their start and end apart: 25, of which 12 were waited for; matrix products, arithmetic and copies ran while one was open for 0% of the time, Pallas kernels for 21%

profile of v5, /device:TPU:0, one launch (start us, length us, event | category | flops | bytes accessed | tf_op | source)
XLA Modules:
  0.0 93.1 jit_solution(13117790869501497317)
XLA Ops:
  1.7 2.1 %collective-permute-start = (bf16[256,512]{1,0:T(8,128)(2,1)S(1)}, bf16[256,512]{1,0:T(8,128)(2,1)S(1)}, u32[]{:S(2)}, u32[]{:S(2)}) collective-permute-start(bf16[256,512]{1,0:T(8,128)(2,1)S(1)} %unit.1.unit_ref), channel_id=1, source_target_pairs={{65,0},{96,32},{0,64},{33,96},{64,1},{97,33},{1,65},{32,97},{73,8}... | collective-permute-start | bytes 786440 | tf_op jit(solution)/shard_map/ppermute | solution.py:42
  3.8 1.5 %collective-permute-start.5 = (bf16[256,512]{1,0:T(8,128)(2,1)S(1)}, bf16[256,512]{1,0:T(8,128)(2,1)S(1)}, u32[]{:S(2)}, u32[]{:S(2)}) collective-permute-start(bf16[256,512]{1,0:T(8,128)(2,1)S(1)} %unit.1.unit_ref), channel_id=1, source_target_pairs={{6,0},{56,32},{70,64},{120,96},{7,1},{57,33},{71,65},{121,97},{14,... | collective-permute-start | bytes 786440 | tf_op jit(solution)/shard_map/ppermute | solution.py:42
  5.3 1.7 %collective-permute-start.6 = (bf16[256,512]{1,0:T(8,128)(2,1)S(1)}, bf16[256,512]{1,0:T(8,128)(2,1)S(1)}, u32[]{:S(2)}, u32[]{:S(2)}) collective-permute-start(bf16[256,512]{1,0:T(8,128)(2,1)S(1)} %unit.1.unit_ref), channel_id=1, source_target_pairs={{2,0},{40,32},{66,64},{104,96},{3,1},{41,33},{67,65},{105,97},{10,... | collective-permute-start | bytes 786440 | tf_op jit(solution)/shard_map/ppermute | solution.py:42
  7.0 1.8 %collective-permute-start.7 = (bf16[256,512]{1,0:T(8,128)(2,1)S(1)}, bf16[256,512]{1,0:T(8,128)(2,1)S(1)}, u32[]{:S(2)}, u32[]{:S(2)}) collective-permute-start(bf16[256,512]{1,0:T(8,128)(2,1)S(1)} %unit.1.unit_ref), channel_id=1, source_target_pairs={{4,0},{48,32},{68,64},{112,96},{5,1},{49,33},{69,65},{113,97},{12,... | collective-permute-start | bytes 786440 | tf_op jit(solution)/shard_map/ppermute | solution.py:42
  8.8 2.2 %collective-permute-start.2 = (bf16[256,512]{1,0:T(8,128)(2,1)S(1)}, bf16[256,512]{1,0:T(8,128)(2,1)S(1)}, u32[]{:S(2)}, u32[]{:S(2)}) collective-permute-start(bf16[256,512]{1,0:T(8,128)(2,1)S(1)} %unit.1.unit_ref), channel_id=1, source_target_pairs={{64,0},{97,32},{1,64},{32,96},{65,1},{96,33},{0,65},{33,97},{72,8}... | collective-permute-start | bytes 786440 | tf_op jit(solution)/shard_map/ppermute | solution.py:42
  12.3 1.5 %collective-permute-done.6 = bf16[256,512]{1,0:T(8,128)(2,1)S(1)} collective-permute-done((bf16[256,512]{1,0:T(8,128)(2,1)S(1)}, bf16[256,512]{1,0:T(8,128)(2,1)S(1)}, u32[]{:S(2)}, u32[]{:S(2)}) %collective-permute-start.6) | collective-permute-done | bytes 262176 | tf_op jit(solution)/shard_map/ppermute | solution.py:42
  13.8 2.0 %collective-permute-start.3 = (bf16[256,512]{1,0:T(8,128)(2,1)S(1)}, bf16[256,512]{1,0:T(8,128)(2,1)S(1)}, u32[]{:S(2)}, u32[]{:S(2)}) collective-permute-start(bf16[256,512]{1,0:T(8,128)(2,1)S(1)} %collective-permute-done), channel_id=1, source_target_pairs={{65,0},{96,32},{0,64},{33,96},{64,1},{97,33},{1,65},{32,97},{73,8}... | collective-permute-start | bytes 786440 | tf_op jit(solution)/shard_map/ppermute | solution.py:42
  15.8 1.6 %collective-permute-start.10 = (bf16[512,512]{1,0:T(8,128)(2,1)S(1)}, bf16[512,512]{1,0:T(8,128)(2,1)S(1)}, u32[]{:S(2)}, u32[]{:S(2)}) collective-permute-start(bf16[512,512]{1,0:T(8,128)(2,1)S(1)} %constant_dynamic-update-slice_fusion.4.refs_3_), channel_id=1, source_target_pairs={{24,0},{38,32},{88,64},{102,96},{25,1},{39,33},{89,65},{103,97},{0... | collective-permute-start | bytes 1572872 | tf_op jit(solution)/shard_map/ppermute | solution.py:42
  17.4 1.7 %collective-permute-start.11 = (bf16[512,512]{1,0:T(8,128)(2,1)S(1)}, bf16[512,512]{1,0:T(8,128)(2,1)S(1)}, u32[]{:S(2)}, u32[]{:S(2)}) collective-permute-start(bf16[512,512]{1,0:T(8,128)(2,1)S(1)} %constant_dynamic-update-slice_fusion.4.refs_3_), channel_id=1, source_target_pairs={{8,0},{34,32},{72,64},{98,96},{9,1},{35,33},{73,65},{99,97},{16,8}... | collective-permute-start | bytes 1572872 | tf_op jit(solution)/shard_map/ppermute | solution.py:42
  19.1 1.9 %collective-permute-start.8 = (bf16[512,512]{1,0:T(8,128)(2,1)S(1)}, bf16[512,512]{1,0:T(8,128)(2,1)S(1)}, u32[]{:S(2)}, u32[]{:S(2)}) collective-permute-start(bf16[512,512]{1,0:T(8,128)(2,1)S(1)} %constant_dynamic-update-slice_fusion.2.refs_4_), channel_id=1, source_target_pairs={{8,0},{34,32},{72,64},{98,96},{9,1},{35,33},{73,65},{99,97},{16,8}... | collective-permute-start | bytes 1572872 | tf_op jit(solution)/shard_map/ppermute | solution.py:42
  21.4 1.6 %collective-permute-start.9 = (bf16[512,512]{1,0:T(8,128)(2,1)S(1)}, bf16[512,512]{1,0:T(8,128)(2,1)S(1)}, u32[]{:S(2)}, u32[]{:S(2)}) collective-permute-start(bf16[512,512]{1,0:T(8,128)(2,1)S(1)} %constant_dynamic-update-slice_fusion.2.refs_4_), channel_id=1, source_target_pairs={{24,0},{38,32},{88,64},{102,96},{25,1},{39,33},{89,65},{103,97},{0... | collective-permute-start | bytes 1572872 | tf_op jit(solution)/shard_map/ppermute | solution.py:42
  23.1 2.7 %exps0.1 = (f32[2048,128]{1,0:T(8,128)S(1)}, f32[8,4096]{1,0:T(8,128)S(1)}, bf16[2048,4096]{1,0:T(8,128)(2,1)S(1)}, bf16[4096,512]{1,0:T(8,128)(2,1)S(1)}) custom-call(s32[4]{0:T(128)S(1)} %pad_add_fusion.refs_0_.info_ref, bf16[512,512]{1,0:T(8,128)(2,1)S(1)} %pad_maximum_fusion.refs_1_, bf16[512,512]{1,0:T(8,128)(2,1)S(1)} %collective-permute-done.1.refs_2_, ...), custom_call_target="tpu_custom_call" | custom-call | flops 8589934592 | bytes 1048576 | tf_op jit(solution)/shard_map/exps0/pallas_call | solution.py:217
  25.9 2.7 %exps1.1 = (f32[2048,128]{1,0:T(8,128)S(1)}, f32[8,4096]{1,0:T(8,128)S(1)}, bf16[2048,4096]{1,0:T(8,128)(2,1)S(1)}, bf16[4096,512]{1,0:T(8,128)(2,1)S(1)}) custom-call(s32[4]{0:T(128)S(1)} %pad_add_fusion.refs_0_.info_ref, bf16[512,512]{1,0:T(8,128)(2,1)S(1)} %constant_dynamic-update-slice_fusion.refs_1_.refs_3_, ...), custom_call_target="tpu_custom_call", output_to_operand_aliasing={{2}: (7, {}), {3}: (8, {})} | custom-call | flops 8589934592 | bytes 1048576 | tf_op jit(solution)/shard_map/exps1/pallas_call | solution.py:217
  28.6 1.7 %collective-permute-start.13 = (bf16[512,512]{1,0:T(8,128)(2,1)S(1)}, bf16[512,512]{1,0:T(8,128)(2,1)S(1)}, u32[]{:S(2)}, u32[]{:S(2)}) collective-permute-start(bf16[512,512]{1,0:T(8,128)(2,1)S(1)} %collective-permute-done.10.refs_5_), channel_id=1, source_target_pairs={{24,0},{38,32},{88,64},{102,96},{25,1},{39,33},{89,65},{103,97},{0... | collective-permute-start | bytes 1572872 | tf_op jit(solution)/shard_map/ppermute | solution.py:42
  30.2 3.9 %exps2.1 = (f32[2048,128]{1,0:T(8,128)S(1)}, f32[8,4096]{1,0:T(8,128)S(1)}, bf16[2048,4096]{1,0:T(8,128)(2,1)S(1)}, bf16[4096,512]{1,0:T(8,128)(2,1)S(1)}) custom-call(s32[4]{0:T(128)S(1)} %pad_add_fusion.refs_0_.info_ref, bf16[512,512]{1,0:T(8,128)(2,1)S(1)} %pad_maximum_fusion.refs_1_, ...), custom_call_target="tpu_custom_call", output_to_operand_aliasing={{2}: (9, {}), {3}: (10, {})} | custom-call | flops 8589934592 | bytes 1048576 | tf_op jit(solution)/shard_map/exps2/pallas_call | solution.py:217
  34.1 1.9 %collective-permute-start.12 = (bf16[512,512]{1,0:T(8,128)(2,1)S(1)}, bf16[512,512]{1,0:T(8,128)(2,1)S(1)}, u32[]{:S(2)}, u32[]{:S(2)}) collective-permute-start(bf16[512,512]{1,0:T(8,128)(2,1)S(1)} %collective-permute-done.8.refs_6_), channel_id=1, source_target_pairs={{8,0},{34,32},{72,64},{98,96},{9,1},{35,33},{73,65},{99,97},{16,8}... | collective-permute-start | bytes 1572872 | tf_op jit(solution)/shard_map/ppermute | solution.py:42
  36.0 3.0 %collective-permute-done.13.refs_7_ = bf16[512,512]{1,0:T(8,128)(2,1)S(1)} collective-permute-done((bf16[512,512]{1,0:T(8,128)(2,1)S(1)}, bf16[512,512]{1,0:T(8,128)(2,1)S(1)}, u32[]{:S(2)}, u32[]{:S(2)}) %collective-permute-start.13) | collective-permute-done | bytes 524320 | tf_op jit(solution)/shard_map/ppermute | solution.py:42
  39.0 5.4 %exps3.1 = (f32[2048,128]{1,0:T(8,128)S(1)}, f32[8,4096]{1,0:T(8,128)S(1)}, bf16[2048,4096]{1,0:T(8,128)(2,1)S(1)}, bf16[4096,512]{1,0:T(8,128)(2,1)S(1)}) custom-call(s32[4]{0:T(128)S(1)} %pad_add_fusion.refs_0_.info_ref, bf16[512,512]{1,0:T(8,128)(2,1)S(1)} %pad_maximum_fusion.refs_1_, ...), custom_call_target="tpu_custom_call", output_to_operand_aliasing={{2}: (10, {}), {3}: (11, {})} | custom-call | flops 12884901888 | bytes 1572864 | tf_op jit(solution)/shard_map/exps3/pallas_call | solution.py:217
  44.4 2.6 %exps4.1 = (f32[8,256]{1,0:T(8,128)S(1)}, f32[24,256]{1,0:T(8,128)S(1)}, bf16[2048,4096]{1,0:T(8,128)(2,1)S(1)}, bf16[4096,512]{1,0:T(8,128)(2,1)S(1)}) custom-call(s32[4]{0:T(128)S(1)} %pad_add_fusion.refs_0_.info_ref, bf16[512,512]{1,0:T(8,128)(2,1)S(1)} %pad_maximum_fusion.refs_1_, ...), custom_call_target="tpu_custom_call", output_to_operand_aliasing={{2}: (8, {}), {3}: (9, {})} | custom-call | flops 4294967296 | bytes 524288 | tf_op jit(solution)/shard_map/exps4/pallas_call | solution.py:217
  49.3 1.6 %collective-permute-done.17 = f32[24,256]{1,0:T(8,128)S(1)} collective-permute-done((f32[24,256]{1,0:T(8,128)S(1)}, f32[24,256]{1,0:T(8,128)S(1)}, u32[]{:S(2)}, u32[]{:S(2)}) %collective-permute-start.17) | collective-permute-done | bytes 24608 | tf_op jit(solution)/shard_map/ppermute | solution.py:55
  51.0 3.7 %collective-permute-start.18 = (f32[24,256]{1,0:T(8,128)S(1)}, f32[24,256]{1,0:T(8,128)S(1)}, u32[]{:S(2)}, u32[]{:S(2)}) collective-permute-start(f32[24,256]{1,0:T(8,128)S(1)} %add.21), channel_id=1, source_target_pairs={{6,0},{56,32},{70,64},{120,96},{7,1},{57,33},{71,65},{121,97},{14,... | collective-permute-start | bytes 73736 | tf_op jit(solution)/shard_map/ppermute | solution.py:55
  54.7 1.8 %collective-permute-done.18 = f32[24,256]{1,0:T(8,128)S(1)} collective-permute-done((f32[24,256]{1,0:T(8,128)S(1)}, f32[24,256]{1,0:T(8,128)S(1)}, u32[]{:S(2)}, u32[]{:S(2)}) %collective-permute-start.18) | collective-permute-done | bytes 24608 | tf_op jit(solution)/shard_map/ppermute | solution.py:55
  57.6 2.9 %collective-permute-done.15 = f32[8,256]{1,0:T(8,128)S(1)} collective-permute-done((f32[8,256]{1,0:T(8,128)S(1)}, f32[8,256]{1,0:T(8,128)S(1)}, u32[]{:S(2)}, u32[]{:S(2)}) %collective-permute-start.15) | collective-permute-done | bytes 8224 | tf_op jit(solution)/shard_map/ppermute | solution.py:55
  60.5 1.9 %collective-permute-start.20 = (f32[24,256]{1,0:T(8,128)S(1)}, f32[24,256]{1,0:T(8,128)S(1)}, u32[]{:S(2)}, u32[]{:S(2)}) collective-permute-start(f32[24,256]{1,0:T(8,128)S(1)} %add.23.refs_2_), channel_id=1, source_target_pairs={{24,0},{38,32},{88,64},{102,96},{25,1},{39,33},{89,65},{103,97},{1... | collective-permute-start | bytes 73736 | tf_op jit(solution)/shard_map/ppermute | solution.py:55
  63.5 3.8 %collective-permute-done.16.refs_1_ = f32[8,256]{1,0:T(8,128)S(1)} collective-permute-done((f32[8,256]{1,0:T(8,128)S(1)}, f32[8,256]{1,0:T(8,128)S(1)}, u32[]{:S(2)}, u32[]{:S(2)}) %collective-permute-start.16) | collective-permute-done | bytes 8224 | tf_op jit(solution)/shard_map/ppermute | solution.py:55
  68.1 4.7 %grads_core.1 = bf16[1040,512]{1,0:T(8,128)(2,1)S(1)} custom-call(f32[32,128]{1,0:T(8,128)S(1)} %get-tuple-element.76.acol_ref, bf16[2048,128]{1,0:T(8,128)(2,1)S(1)} %get-tuple-element.70.arow_ref, bf16[2048,4096]{1,0:T(8,128)(2,1)S(1)} %get-tuple-element.71.exps_ref, bf16[4096,512]{1,0:T(8,128)(2,1)S(1)} %get-tuple-element.72.unit_ref, ...), custom_call_target="tpu_custom_call" | custom-call | flops 4294967296 | bytes 12582912 | tf_op jit(solution)/shard_map/grads_core/pallas_call | solution.py:321
  74.1 1.4 %collective-permute-done.21.core_ref.refs_0_ = bf16[1040,512]{1,0:T(8,128)(2,1)S(1)} collective-permute-done((bf16[1040,512]{1,0:T(8,128)(2,1)S(1)}, bf16[1040,512]{1,0:T(8,128)(2,1)S(1)}, u32[]{:S(2)}, u32[]{:S(2)}) %collective-permute-start.21) | collective-permute-done | bytes 1064992 | tf_op jit(solution)/shard_map/ppermute | solution.py:42
  75.7 2.3 %grads_near.1 = (bf16[272,512]{1,0:T(8,128)(2,1)S(1)}, f32[256,512]{1,0:T(8,128)S(1)}) custom-call(f32[32,128]{1,0:T(8,128)S(1)} %get-tuple-element.76.acol_ref, bf16[2048,128]{1,0:T(8,128)(2,1)S(1)} %get-tuple-element.70.arow_ref, bf16[2048,4096]{1,0:T(8,128)(2,1)S(1)} %get-tuple-element.71.exps_ref, bf16[4096,512]{1,0:T(8,128)(2,1)S(1)} %get-tuple-element.72.unit_ref, ...), custom_call_target="tpu_custom_call" | custom-call | flops 2147483648 | bytes 8388608 | tf_op jit(solution)/shard_map/grads_near/pallas_call | solution.py:321
  78.0 3.3 %collective-permute-start.23 = (bf16[272,512]{1,0:T(8,128)(2,1)S(1)}, bf16[272,512]{1,0:T(8,128)(2,1)S(1)}, u32[]{:S(2)}, u32[]{:S(2)}) collective-permute-start(bf16[272,512]{1,0:T(8,128)(2,1)S(1)} %get-tuple-element.77), channel_id=1, source_target_pairs={{64,0},{97,32},{1,64},{32,96},{65,1},{96,33},{0,65},{33,97},{72,8}... | collective-permute-start | bytes 835592 | tf_op jit(solution)/shard_map/ppermute | solution.py:42
  81.3 2.7 %collective-permute-done.22.far_ref.passed_ref = bf16[272,512]{1,0:T(8,128)(2,1)S(1)} collective-permute-done((bf16[272,512]{1,0:T(8,128)(2,1)S(1)}, bf16[272,512]{1,0:T(8,128)(2,1)S(1)}, u32[]{:S(2)}, u32[]{:S(2)}) %collective-permute-start.22) | collective-permute-done | bytes 278560 | tf_op jit(solution)/shard_map/ppermute | solution.py:42
  85.5 1.6 %collective-permute-done.23.one_ref = bf16[272,512]{1,0:T(8,128)(2,1)S(1)} collective-permute-done((bf16[272,512]{1,0:T(8,128)(2,1)S(1)}, bf16[272,512]{1,0:T(8,128)(2,1)S(1)}, u32[]{:S(2)}, u32[]{:S(2)}) %collective-permute-start.23) | collective-permute-done | bytes 278560 | tf_op jit(solution)/shard_map/ppermute | solution.py:42
  87.0 4.9 %collective-permute-done.24.two_ref = bf16[272,512]{1,0:T(8,128)(2,1)S(1)} collective-permute-done((bf16[272,512]{1,0:T(8,128)(2,1)S(1)}, bf16[272,512]{1,0:T(8,128)(2,1)S(1)}, u32[]{:S(2)}, u32[]{:S(2)}) %collective-permute-start.24) | collective-permute-done | bytes 278560 | tf_op jit(solution)/shard_map/ppermute | solution.py:42
  (52 shorter events, 12.1 us)
Async XLA Ops:
  0.6 1.0 %copy-start = (bf16[256,512]{1,0:T(8,128)(2,1)S(1)}, bf16[256,512]{1,0:T(8,128)(2,1)}, u32[]{:S(2)}) copy-start(bf16[256,512]{1,0:T(8,128)(2,1)} %z_ref.3) | copy-start | bytes 786436
  1.7 10.4 %collective-permute-start = (bf16[256,512]{1,0:T(8,128)(2,1)S(1)}, bf16[256,512]{1,0:T(8,128)(2,1)S(1)}, u32[]{:S(2)}, u32[]{:S(2)}) collective-permute-start(bf16[256,512]{1,0:T(8,128)(2,1)S(1)} %unit.1.unit_ref), channel_id=1, source_target_pairs={{65,0},{96,32},{0,64},{33,96},{64,1},{97,33},{1,65},{32,97},{73,8}... | collective-permute-start | bytes 786440 | tf_op jit(solution)/shard_map/ppermute | solution.py:42
  3.8 8.5 %collective-permute-start.5 = (bf16[256,512]{1,0:T(8,128)(2,1)S(1)}, bf16[256,512]{1,0:T(8,128)(2,1)S(1)}, u32[]{:S(2)}, u32[]{:S(2)}) collective-permute-start(bf16[256,512]{1,0:T(8,128)(2,1)S(1)} %unit.1.unit_ref), channel_id=1, source_target_pairs={{6,0},{56,32},{70,64},{120,96},{7,1},{57,33},{71,65},{121,97},{14,... | collective-permute-start | bytes 786440 | tf_op jit(solution)/shard_map/ppermute | solution.py:42
  5.3 8.5 %collective-permute-start.6 = (bf16[256,512]{1,0:T(8,128)(2,1)S(1)}, bf16[256,512]{1,0:T(8,128)(2,1)S(1)}, u32[]{:S(2)}, u32[]{:S(2)}) collective-permute-start(bf16[256,512]{1,0:T(8,128)(2,1)S(1)} %unit.1.unit_ref), channel_id=1, source_target_pairs={{2,0},{40,32},{66,64},{104,96},{3,1},{41,33},{67,65},{105,97},{10,... | collective-permute-start | bytes 786440 | tf_op jit(solution)/shard_map/ppermute | solution.py:42
  7.0 10.4 %collective-permute-start.7 = (bf16[256,512]{1,0:T(8,128)(2,1)S(1)}, bf16[256,512]{1,0:T(8,128)(2,1)S(1)}, u32[]{:S(2)}, u32[]{:S(2)}) collective-permute-start(bf16[256,512]{1,0:T(8,128)(2,1)S(1)} %unit.1.unit_ref), channel_id=1, source_target_pairs={{4,0},{48,32},{68,64},{112,96},{5,1},{49,33},{69,65},{113,97},{12,... | collective-permute-start | bytes 786440 | tf_op jit(solution)/shard_map/ppermute | solution.py:42
  8.8 10.3 %collective-permute-start.2 = (bf16[256,512]{1,0:T(8,128)(2,1)S(1)}, bf16[256,512]{1,0:T(8,128)(2,1)S(1)}, u32[]{:S(2)}, u32[]{:S(2)}) collective-permute-start(bf16[256,512]{1,0:T(8,128)(2,1)S(1)} %unit.1.unit_ref), channel_id=1, source_target_pairs={{64,0},{97,32},{1,64},{32,96},{65,1},{96,33},{0,65},{33,97},{72,8}... | collective-permute-start | bytes 786440 | tf_op jit(solution)/shard_map/ppermute | solution.py:42
  11.1 0.7 copy-start.2
  12.2 10.9 %collective-permute-start.1 = (bf16[512,512]{1,0:T(8,128)(2,1)S(1)}, bf16[512,512]{1,0:T(8,128)(2,1)S(1)}, u32[]{:S(2)}, u32[]{:S(2)}) collective-permute-start(bf16[512,512]{1,0:T(8,128)(2,1)S(1)} %pad_maximum_fusion.refs_1_), channel_id=1, source_target_pairs={{32,0},{0,32},{96,64},{64,96},{33,1},{1,33},{97,65},{65,97},{40,8}... | collective-permute-start | bytes 1572872 | tf_op jit(solution)/shard_map/ppermute | solution.py:42
  13.8 7.7 %collective-permute-start.3 = (bf16[256,512]{1,0:T(8,128)(2,1)S(1)}, bf16[256,512]{1,0:T(8,128)(2,1)S(1)}, u32[]{:S(2)}, u32[]{:S(2)}) collective-permute-start(bf16[256,512]{1,0:T(8,128)(2,1)S(1)} %collective-permute-done), channel_id=1, source_target_pairs={{65,0},{96,32},{0,64},{33,96},{64,1},{97,33},{1,65},{32,97},{73,8}... | collective-permute-start | bytes 786440 | tf_op jit(solution)/shard_map/ppermute | solution.py:42
  15.8 12.8 %collective-permute-start.10 = (bf16[512,512]{1,0:T(8,128)(2,1)S(1)}, bf16[512,512]{1,0:T(8,128)(2,1)S(1)}, u32[]{:S(2)}, u32[]{:S(2)}) collective-permute-start(bf16[512,512]{1,0:T(8,128)(2,1)S(1)} %constant_dynamic-update-slice_fusion.4.refs_3_), channel_id=1, source_target_pairs={{24,0},{38,32},{88,64},{102,96},{25,1},{39,33},{89,65},{103,97},{0... | collective-permute-start | bytes 1572872 | tf_op jit(solution)/shard_map/ppermute | solution.py:42
  17.4 11.1 %collective-permute-start.11 = (bf16[512,512]{1,0:T(8,128)(2,1)S(1)}, bf16[512,512]{1,0:T(8,128)(2,1)S(1)}, u32[]{:S(2)}, u32[]{:S(2)}) collective-permute-start(bf16[512,512]{1,0:T(8,128)(2,1)S(1)} %constant_dynamic-update-slice_fusion.4.refs_3_), channel_id=1, source_target_pairs={{8,0},{34,32},{72,64},{98,96},{9,1},{35,33},{73,65},{99,97},{16,8}... | collective-permute-start | bytes 1572872 | tf_op jit(solution)/shard_map/ppermute | solution.py:42
  19.1 15.0 %collective-permute-start.8 = (bf16[512,512]{1,0:T(8,128)(2,1)S(1)}, bf16[512,512]{1,0:T(8,128)(2,1)S(1)}, u32[]{:S(2)}, u32[]{:S(2)}) collective-permute-start(bf16[512,512]{1,0:T(8,128)(2,1)S(1)} %constant_dynamic-update-slice_fusion.2.refs_4_), channel_id=1, source_target_pairs={{8,0},{34,32},{72,64},{98,96},{9,1},{35,33},{73,65},{99,97},{16,8}... | collective-permute-start | bytes 1572872 | tf_op jit(solution)/shard_map/ppermute | solution.py:42
  21.4 12.7 %collective-permute-start.9 = (bf16[512,512]{1,0:T(8,128)(2,1)S(1)}, bf16[512,512]{1,0:T(8,128)(2,1)S(1)}, u32[]{:S(2)}, u32[]{:S(2)}) collective-permute-start(bf16[512,512]{1,0:T(8,128)(2,1)S(1)} %constant_dynamic-update-slice_fusion.2.refs_4_), channel_id=1, source_target_pairs={{24,0},{38,32},{88,64},{102,96},{25,1},{39,33},{89,65},{103,97},{0... | collective-permute-start | bytes 1572872 | tf_op jit(solution)/shard_map/ppermute | solution.py:42
  23.0 2.8 %collective-permute-start.4 = (bf16[512,512]{1,0:T(8,128)(2,1)S(1)}, bf16[512,512]{1,0:T(8,128)(2,1)S(1)}, u32[]{:S(2)}, u32[]{:S(2)}) collective-permute-start(bf16[512,512]{1,0:T(8,128)(2,1)S(1)} %constant_dynamic-update-slice_fusion.refs_1_.refs_3_), channel_id=1, source_target_pairs={{32,0},{0,32},{96,64},{64,96},{33,1},{1,33},{97,65},{65,97},{40,8}... | collective-permute-start | bytes 1572872 | tf_op jit(solution)/shard_map/ppermute | solution.py:42
  28.6 10.5 %collective-permute-start.13 = (bf16[512,512]{1,0:T(8,128)(2,1)S(1)}, bf16[512,512]{1,0:T(8,128)(2,1)S(1)}, u32[]{:S(2)}, u32[]{:S(2)}) collective-permute-start(bf16[512,512]{1,0:T(8,128)(2,1)S(1)} %collective-permute-done.10.refs_5_), channel_id=1, source_target_pairs={{24,0},{38,32},{88,64},{102,96},{25,1},{39,33},{89,65},{103,97},{0... | collective-permute-start | bytes 1572872 | tf_op jit(solution)/shard_map/ppermute | solution.py:42
  34.1 10.3 %collective-permute-start.12 = (bf16[512,512]{1,0:T(8,128)(2,1)S(1)}, bf16[512,512]{1,0:T(8,128)(2,1)S(1)}, u32[]{:S(2)}, u32[]{:S(2)}) collective-permute-start(bf16[512,512]{1,0:T(8,128)(2,1)S(1)} %collective-permute-done.8.refs_6_), channel_id=1, source_target_pairs={{8,0},{34,32},{72,64},{98,96},{9,1},{35,33},{73,65},{99,97},{16,8}... | collective-permute-start | bytes 1572872 | tf_op jit(solution)/shard_map/ppermute | solution.py:42
  47.1 3.9 %collective-permute-start.17 = (f32[24,256]{1,0:T(8,128)S(1)}, f32[24,256]{1,0:T(8,128)S(1)}, u32[]{:S(2)}, u32[]{:S(2)}) collective-permute-start(f32[24,256]{1,0:T(8,128)S(1)} %get-tuple-element.65), channel_id=1, source_target_pairs={{2,0},{40,32},{66,64},{104,96},{3,1},{41,33},{67,65},{105,97},{10,... | collective-permute-start | bytes 73736 | tf_op jit(solution)/shard_map/ppermute | solution.py:55
  47.2 2.2 %collective-permute-start.14 = (f32[8,256]{1,0:T(8,128)S(1)}, f32[8,256]{1,0:T(8,128)S(1)}, u32[]{:S(2)}, u32[]{:S(2)}) collective-permute-start(f32[8,256]{1,0:T(8,128)S(1)} %get-tuple-element.64), channel_id=1, source_target_pairs={{32,0},{0,32},{96,64},{64,96},{33,1},{1,33},{97,65},{65,97},{40,8}... | collective-permute-start | bytes 24584 | tf_op jit(solution)/shard_map/ppermute | solution.py:42
  51.0 5.5 %collective-permute-start.18 = (f32[24,256]{1,0:T(8,128)S(1)}, f32[24,256]{1,0:T(8,128)S(1)}, u32[]{:S(2)}, u32[]{:S(2)}) collective-permute-start(f32[24,256]{1,0:T(8,128)S(1)} %add.21), channel_id=1, source_target_pairs={{6,0},{56,32},{70,64},{120,96},{7,1},{57,33},{71,65},{121,97},{14,... | collective-permute-start | bytes 73736 | tf_op jit(solution)/shard_map/ppermute | solution.py:55
  56.5 4.0 %collective-permute-start.19 = (f32[24,256]{1,0:T(8,128)S(1)}, f32[24,256]{1,0:T(8,128)S(1)}, u32[]{:S(2)}, u32[]{:S(2)}) collective-permute-start(f32[24,256]{1,0:T(8,128)S(1)} %add.22), channel_id=1, source_target_pairs={{8,0},{34,32},{72,64},{98,96},{9,1},{35,33},{73,65},{99,97},{0,8},... | collective-permute-start | bytes 73736 | tf_op jit(solution)/shard_map/ppermute | solution.py:55
  56.8 3.7 %collective-permute-start.15 = (f32[8,256]{1,0:T(8,128)S(1)}, f32[8,256]{1,0:T(8,128)S(1)}, u32[]{:S(2)}, u32[]{:S(2)}) collective-permute-start(f32[8,256]{1,0:T(8,128)S(1)} %add.19), channel_id=1, source_target_pairs={{64,0},{96,32},{0,64},{32,96},{65,1},{97,33},{1,65},{33,97},{72,8}... | collective-permute-start | bytes 24584 | tf_op jit(solution)/shard_map/ppermute | solution.py:55
  60.5 6.8 %collective-permute-start.20 = (f32[24,256]{1,0:T(8,128)S(1)}, f32[24,256]{1,0:T(8,128)S(1)}, u32[]{:S(2)}, u32[]{:S(2)}) collective-permute-start(f32[24,256]{1,0:T(8,128)S(1)} %add.23.refs_2_), channel_id=1, source_target_pairs={{24,0},{38,32},{88,64},{102,96},{25,1},{39,33},{89,65},{103,97},{1... | collective-permute-start | bytes 73736 | tf_op jit(solution)/shard_map/ppermute | solution.py:55
  62.4 4.9 %collective-permute-start.16 = (f32[8,256]{1,0:T(8,128)S(1)}, f32[8,256]{1,0:T(8,128)S(1)}, u32[]{:S(2)}, u32[]{:S(2)}) collective-permute-start(f32[8,256]{1,0:T(8,128)S(1)} %add.20.refs_0_), channel_id=1, source_target_pairs={{65,0},{97,32},{1,64},{33,96},{64,1},{96,33},{0,65},{32,97},{73,8}... | collective-permute-start | bytes 24584 | tf_op jit(solution)/shard_map/ppermute | solution.py:55
  72.8 2.8 %collective-permute-start.21 = (bf16[1040,512]{1,0:T(8,128)(2,1)S(1)}, bf16[1040,512]{1,0:T(8,128)(2,1)S(1)}, u32[]{:S(2)}, u32[]{:S(2)}) collective-permute-start(bf16[1040,512]{1,0:T(8,128)(2,1)S(1)} %grads_core.1), channel_id=1, source_target_pairs={{32,0},{0,32},{96,64},{64,96},{33,1},{1,33},{97,65},{65,97},{40,8}... | collective-permute-start | bytes 3194888 | tf_op jit(solution)/shard_map/ppermute | solution.py:42
  75.6 8.4 %collective-permute-start.22 = (bf16[272,512]{1,0:T(8,128)(2,1)S(1)}, bf16[272,512]{1,0:T(8,128)(2,1)S(1)}, u32[]{:S(2)}, u32[]{:S(2)}) collective-permute-start(bf16[272,512]{1,0:T(8,128)(2,1)S(1)} %sum_far.1.refs_1_.here_ref), channel_id=1, source_target_pairs={{65,0},{96,32},{0,64},{33,96},{64,1},{97,33},{1,65},{32,97},{73,8}... | collective-permute-start | bytes 835592 | tf_op jit(solution)/shard_map/ppermute | solution.py:42
  78.0 9.0 %collective-permute-start.23 = (bf16[272,512]{1,0:T(8,128)(2,1)S(1)}, bf16[272,512]{1,0:T(8,128)(2,1)S(1)}, u32[]{:S(2)}, u32[]{:S(2)}) collective-permute-start(bf16[272,512]{1,0:T(8,128)(2,1)S(1)} %get-tuple-element.77), channel_id=1, source_target_pairs={{64,0},{97,32},{1,64},{32,96},{65,1},{96,33},{0,65},{33,97},{72,8}... | collective-permute-start | bytes 835592 | tf_op jit(solution)/shard_map/ppermute | solution.py:42
  84.1 7.8 %copy-start.1 = (bf16[256,512]{1,0:T(8,128)(2,1)S(1)}, bf16[256,512]{1,0:T(8,128)(2,1)}, u32[]{:S(2)}) copy-start(bf16[256,512]{1,0:T(8,128)(2,1)} %z_ref.3) | copy-start | bytes 786436
  84.1 7.8 %collective-permute-start.24 = (bf16[272,512]{1,0:T(8,128)(2,1)S(1)}, bf16[272,512]{1,0:T(8,128)(2,1)S(1)}, u32[]{:S(2)}, u32[]{:S(2)}) collective-permute-start(bf16[272,512]{1,0:T(8,128)(2,1)S(1)} %sum_two.1), channel_id=1, source_target_pairs={{65,0},{96,32},{0,64},{33,96},{64,1},{97,33},{1,65},{32,97},{73,8}... | collective-permute-start | bytes 835592 | tf_op jit(solution)/shard_map/ppermute | solution.py:42

commit v6 on v5

--- a/solution.py
+++ b/solution.py
@@ -157,20 +157,17 @@
 
 def exps_kernel(places, rows_here, first, last, *refs):
     count = len(places)
-    halves = len(rows_here)
     info_ref, refs = refs[0], refs[1:]
-    row_refs, col_refs, refs = refs[: 2 * halves], refs[2 * halves : 2 * halves + count], refs[2 * halves + count :]
+    row_refs, refs = refs[: 2 * len(rows_here)], refs[2 * len(rows_here) :]
+    col_refs, refs = refs[:count], refs[count:]
     if not first:
-        before_ref, col_before_ref, refs = refs[0], refs[1], refs[4:]
+        refs = refs[4:]
     if last:
         positive_ref, refs = refs[0], refs[1:]
-    sums_ref, col_sums_ref, exps_ref, unit_ref, rows, sums, col_sums, line, col_line = refs
-    for n, ref in enumerate(row_refs):
-        start = rows_here[n // 2] * 1024 + (n % 2) * 512
-        rows[start : start + 512] = ref[...]
-    sums[...] = jnp.zeros_like(sums) if first else before_ref[...]
-    col_sums[...] = jnp.zeros_like(col_sums) if first else col_before_ref[...]
-    part = slice(rows_here[0] * 1024, rows_here[-1] * 1024 + 1024)
+    sums_ref, col_sums_ref, exps_ref, unit_ref = refs[:4]
+    if first:
+        sums_ref[...] = jnp.zeros_like(sums_ref)
+        col_sums_ref[...] = jnp.zeros_like(col_sums_ref)
     for n, col_ref in enumerate(col_refs):
         if 0 in rows_here:
             start = places[n] * TILE
@@ -180,58 +177,54 @@
         def _(m):
             here = pl.ds(pl.multiple_of(places[n] * TILE + m * ROWS, ROWS), ROWS)
             cols = col_ref[pl.ds(pl.multiple_of(m * ROWS, ROWS), ROWS), :]
-            s = lax.dot_general(rows[part], cols, NT, preferred_element_type=F32)
-            e = jnp.exp2(s * EXP_SCALE)
-            if first and n == 0:
-                i = lax.broadcasted_iota(jnp.int32, (ROWS, ROWS), 0)
-                j = lax.broadcasted_iota(jnp.int32, (ROWS, ROWS), 1)
-                own = jnp.where(i == j + m * ROWS, 0.0, e[:ROWS])
-                e = jnp.concatenate([own, e[ROWS:]], axis=0)
-            exps_ref[part, here] = e.astype(BF16)
-            sums[part] += e[:, :128] + e[:, 128:]
-            col_sums[:, here] += jnp.sum(e.reshape(-1, 8, ROWS), axis=0)
+            by_col = col_sums_ref[:, here]
+            for k, ref in enumerate(row_refs):
+                start = rows_here[k // 2] * 1024 + (k % 2) * 512
+                part = slice(start, start + 512)
+                s = lax.dot_general(ref[...], cols, NT, preferred_element_type=F32)
+                e = jnp.exp2(s * EXP_SCALE)
+                if first and n == 0 and k == 0:
+                    i = lax.broadcasted_iota(jnp.int32, (ROWS, ROWS), 0)
+                    j = lax.broadcasted_iota(jnp.int32, (ROWS, ROWS), 1)
+                    own = jnp.where(i == j + m * ROWS, 0.0, e[:ROWS])
+                    e = jnp.concatenate([own, e[ROWS:]], axis=0)
+                exps_ref[part, here] = e.astype(BF16)
+                sums_ref[part] += e[:, :128] + e[:, 128:]
+                by_col += jnp.sum(e.reshape(-1, 8, ROWS), axis=0)
+            col_sums_ref[:, here] = by_col
 
     if last:
-        totals = jnp.sum(sums[...].T, axis=0, keepdims=True)
+        line_ref, col_line_ref = refs[4:]
+        totals = jnp.sum(sums_ref[...].T, axis=0, keepdims=True)
         for start, at in row_blocks(info_ref):
-            line[pl.ds(at, 1), :] = totals[:, start : start + ROWS]
-        sums_ref[...] = line[...]
-        totals = jnp.sum(col_sums[...], axis=0, keepdims=True)
-        col_line[...] = jnp.zeros_like(col_line)
+            line_ref[pl.ds(at, 1), :] = totals[:, start : start + ROWS]
+        totals = jnp.sum(col_sums_ref[...], axis=0, keepdims=True)
+        col_line_ref[...] = jnp.zeros_like(col_line_ref)
         for n, at in enumerate(col_blocks(info_ref)):
-            col_line[pl.ds(at, 1), :] = totals[:, n * ROWS : (n + 1) * ROWS]
-        col_line[16:17, 0:128] = positive_ref[...]
-        col_sums_ref[...] = col_line[...]
-    else:
-        sums_ref[...] = sums[...]
-        col_sums_ref[...] = col_sums[...]
+            col_line_ref[pl.ds(at, 1), :] = totals[:, n * ROWS : (n + 1) * ROWS]
+        col_line_ref[16:17, 0:128] = positive_ref[...]
 
 
 def make_exps(info, rows, rows_here, cols, places, chain, positive, name):
     first, last = chain is None, positive is not None
     count = len(cols)
     tiles = sum(c.shape[0] for c in cols) // TILE
-    sums_shape = (8, ROWS) if last else (ALL_ROWS, 128)
-    col_sums_shape = (24, ROWS) if last else (8, COLS)
-    operands = [info, *rows, *cols] + ([] if first else list(chain)) + ([positive] if last else [])
+    operands = [info, *rows, *cols] + ([] if first else list(chain[:4])) + ([positive] if last else [])
+    out_shape = (
+        pltpu.VMEM((ALL_ROWS, 128), F32),
+        pltpu.VMEM((8, COLS), F32),
+        pltpu.VMEM((ALL_ROWS, COLS), BF16),
+        pltpu.VMEM((COLS, E), BF16),
+    )
+    if last:
+        out_shape += (jax.ShapeDtypeStruct((8, ROWS), F32), jax.ShapeDtypeStruct((24, ROWS), F32))
+    start = 1 + len(rows) + count
     return pl.pallas_call(
         functools.partial(exps_kernel, places, rows_here, first, last),
-        out_shape=(
-            jax.ShapeDtypeStruct(sums_shape, F32),
-            jax.ShapeDtypeStruct(col_sums_shape, F32),
-            pltpu.VMEM((ALL_ROWS, COLS), BF16),
-            pltpu.VMEM((COLS, E), BF16),
-        ),
+        out_shape=out_shape,
         in_specs=[smem()] + [vmem()] * (len(operands) - 1),
-        out_specs=(vmem(), vmem(), vmem(), vmem()),
-        input_output_aliases={} if first else {3 + len(rows) + count: 2, 4 + len(rows) + count: 3},
-        scratch_shapes=[
-            pltpu.VMEM((ALL_ROWS, E), BF16),
-            pltpu.VMEM((ALL_ROWS, 128), F32),
-            pltpu.VMEM((8, COLS), F32),
-            pltpu.VMEM((8, ROWS), F32),
-            pltpu.VMEM((24, ROWS), F32),
-        ],
+        out_specs=(vmem(),) * len(out_shape),
+        input_output_aliases={} if first else {start + n: n for n in range(4)},
         compiler_params=params(12),
         cost_estimate=pl.CostEstimate(
             flops=2 * len(rows) * 512 * tiles * TILE * E * (8 if len(rows) == 2 else 4),
@@ -290,14 +283,12 @@
         return exps_ref[here] * jnp.concatenate([a + col for col in cols], axis=1)
 
     if adds is None:
-        size = pieces[0][1]
-        step = pieces[-1][0] - pieces[0][0]
-
-        @pl.loop(0, len(pieces))
-        def _(n):
-            w = weights(pl.ds(pl.multiple_of(pieces[0][0] + n * step, size), size))
+        to = 0
+        for start, size in pieces:
+            w = weights(slice(start, start + size))
             product = lax.dot_general(w, unit_ref[...], NN, preferred_element_type=F32)
-            refs[0][pl.ds(pl.multiple_of(n * size, size), size)] = product.astype(refs[0].dtype)
+            refs[0][to : to + size] = product.astype(refs[0].dtype)
+            to += size
 
     else:
         w = jnp.concatenate([weights(slice(start, start + size)) for start, size in pieces], axis=0)
@@ -334,8 +325,8 @@
 
 
 def far_kernel(raw_ref, core_ref, loss_ref, out_ref):
-    out_ref[:ROWS] = (raw_ref[...] + core_ref[768:1024].astype(F32)).astype(BF16)
-    out_ref[ROWS:] = in_parts(of_parts(loss_ref[...]) + of_parts(core_ref[1024:]))
+    out_ref[:ROWS] = (raw_ref[...] + core_ref[256:512].astype(F32)).astype(BF16)
+    out_ref[ROWS:] = in_parts(of_parts(loss_ref[...]) + of_parts(core_ref[768:]))
 
 
 def two_kernel(held_ref, far_ref, out_ref):
@@ -406,7 +397,8 @@
     chain = make_exps(info, rows, (0, 1), [before0, after0], (2, 4), chain, None, "exps2")
     far1 = get(after(after1, before1, chain[0]), second=1)
     chain = make_exps(info, rows, (0, 1), [before1, after1, far0], (3, 5, 6), chain, None, "exps3")
-    sums, col_sums, exps, units = make_exps(info, rows, (0, 1), [far1], (7,), chain, positive, "exps4")
+    chain = make_exps(info, rows, (0, 1), [far1], (7,), chain, positive, "exps4")
+    _, _, exps, units, sums, col_sums = chain
 
     by_row = sums + get(sums, core=1)
     by_col = col_sums + swap(col_sums, "first", 0)
@@ -419,19 +411,21 @@
     arow, acol, loss = make_totals(info, by_row, by_col)
 
     given = (acol, arow, exps, units)
-    (theirs,) = make_grads(((512, 512), (1536, 512)), None, (BF16,), info, *given, None, loss, "grads_core")
+    (theirs,) = make_grads(((1536, 512), (768, ROWS)), None, (BF16,), info, *given, None, loss, "grads_core")
     core = get(theirs, core=1)
     (far,) = make_grads(((1280, ROWS),), None, (F32,), theirs, *given, None, None, "grads_far")
     far = make_sum(far_kernel, (far, core, loss), "sum_far")
     passed = get(far, z_own=-1)
     free, held = make_grads(
-        ((256, ROWS), (1024, ROWS)), (256, 512), (BF16, F32), info, *given, core, far, "grads_near"
+        ((256, ROWS), (1024, ROWS)), (512, 0), (BF16, F32), info, *given, core, far, "grads_near"
     )
     one = get(free, z_own=1)
+    (theirs,) = make_grads(((512, ROWS),), None, (BF16,), held, *given, None, None, "grads_core_own")
+    core = get(theirs, core=1)
     two = make_sum(two_kernel, (held, passed), "sum_two")
-    own_token = two
+    token = two
     two = get(two, z_own=-1)
-    (own,) = make_grads(((0, ROWS),), (0,), (F32,), own_token, *given, core, None, "grads_own")
+    (own,) = make_grads(((0, ROWS),), (0,), (F32,), token, *given, core, None, "grads_own")
     grad, loss = make_final((embeds, mates, own, one, two, far, passed))
     return (loss[0, 0], grad)
 

time: 93.6 us -> 91 us (0.972)
  waiting for transfers between devices: 26.6 us -> 24.6 us
    ppermute x19 -> x20, waiting for transfers between devices: 16.4 us -> 14.3 us  [get(): return lax.ppermute(value, AXES, pairs)]
    ppermute x19 -> x20, starting transfers between devices: 26.6 us -> 26.5 us  [get(): return lax.ppermute(value, AXES, pairs)]
    pallas_call x4 -> x5, Pallas kernels: 9.49 us -> 9.47 us  [make_grads(): pl.pallas_call(functools.partial(grads_kernel, pieces, adds, carry is not...]
  transfers between devices with their start and end apart: 25 -> 26, of which waited for: 12 -> 12; matrix products, arithmetic and copies ran while one was open for 0% -> 0% of each run, Pallas kernels for 21% -> 23%
where the time goes in v6:
time: 91 us; the launch traced here: 90.5 us
  starting transfers between devices  34.4 us (38%)
  Pallas kernels  28.8 us (32%)
  waiting for transfers between devices  24.6 us (27%)
  local copies, waits for them, and re-layouts  1.74 us (2%)
  between operations  0.92 us (1%)
    ppermute x20, starting transfers between devices, get(): return lax.ppermute(value, AXES, pairs)  26.5 us
    pallas_call x5, Pallas kernels, make_exps(): pl.pallas_call(functools.partial(exps_kernel, places, rows_here, first, l...  16.8 us
    ppermute x20, waiting for transfers between devices, get(): return lax.ppermute(value, AXES, pairs)  14.3 us
    ppermute x6, waiting for transfers between devices, swap(): return lax.ppermute(value, AXES, pairs)  10.2 us
    pallas_call x5, Pallas kernels, make_grads(): pl.pallas_call(functools.partial(grads_kernel, pieces, adds, carry is not...  9.47 us
    ppermute x6, starting transfers between devices, swap(): return lax.ppermute(value, AXES, pairs)  7.82 us
  transfers between devices with their start and end apart: 26, of which 12 were waited for; matrix products, arithmetic and copies ran while one was open for 0% of the time, Pallas kernels for 23%

profile of v6, /device:TPU:0, one launch (start us, length us, event | category | flops | bytes accessed | tf_op | source)
XLA Modules:
  0.0 90.5 jit_solution(15546642627428951989)
XLA Ops:
  1.7 2.1 %collective-permute-start = (bf16[256,512]{1,0:T(8,128)(2,1)S(1)}, bf16[256,512]{1,0:T(8,128)(2,1)S(1)}, u32[]{:S(2)}, u32[]{:S(2)}) collective-permute-start(bf16[256,512]{1,0:T(8,128)(2,1)S(1)} %unit.1.unit_ref), channel_id=1, source_target_pairs={{65,0},{96,32},{0,64},{33,96},{64,1},{97,33},{1,65},{32,97},{73,8}... | collective-permute-start | bytes 786440 | tf_op jit(solution)/shard_map/ppermute | solution.py:42
  3.8 1.5 %collective-permute-start.5 = (bf16[256,512]{1,0:T(8,128)(2,1)S(1)}, bf16[256,512]{1,0:T(8,128)(2,1)S(1)}, u32[]{:S(2)}, u32[]{:S(2)}) collective-permute-start(bf16[256,512]{1,0:T(8,128)(2,1)S(1)} %unit.1.unit_ref), channel_id=1, source_target_pairs={{6,0},{56,32},{70,64},{120,96},{7,1},{57,33},{71,65},{121,97},{14,... | collective-permute-start | bytes 786440 | tf_op jit(solution)/shard_map/ppermute | solution.py:42
  5.3 1.7 %collective-permute-start.6 = (bf16[256,512]{1,0:T(8,128)(2,1)S(1)}, bf16[256,512]{1,0:T(8,128)(2,1)S(1)}, u32[]{:S(2)}, u32[]{:S(2)}) collective-permute-start(bf16[256,512]{1,0:T(8,128)(2,1)S(1)} %unit.1.unit_ref), channel_id=1, source_target_pairs={{2,0},{40,32},{66,64},{104,96},{3,1},{41,33},{67,65},{105,97},{10,... | collective-permute-start | bytes 786440 | tf_op jit(solution)/shard_map/ppermute | solution.py:42
  7.0 1.8 %collective-permute-start.7 = (bf16[256,512]{1,0:T(8,128)(2,1)S(1)}, bf16[256,512]{1,0:T(8,128)(2,1)S(1)}, u32[]{:S(2)}, u32[]{:S(2)}) collective-permute-start(bf16[256,512]{1,0:T(8,128)(2,1)S(1)} %unit.1.unit_ref), channel_id=1, source_target_pairs={{4,0},{48,32},{68,64},{112,96},{5,1},{49,33},{69,65},{113,97},{12,... | collective-permute-start | bytes 786440 | tf_op jit(solution)/shard_map/ppermute | solution.py:42
  8.8 2.2 %collective-permute-start.2 = (bf16[256,512]{1,0:T(8,128)(2,1)S(1)}, bf16[256,512]{1,0:T(8,128)(2,1)S(1)}, u32[]{:S(2)}, u32[]{:S(2)}) collective-permute-start(bf16[256,512]{1,0:T(8,128)(2,1)S(1)} %unit.1.unit_ref), channel_id=1, source_target_pairs={{64,0},{97,32},{1,64},{32,96},{65,1},{96,33},{0,65},{33,97},{72,8}... | collective-permute-start | bytes 786440 | tf_op jit(solution)/shard_map/ppermute | solution.py:42
  12.3 1.5 %collective-permute-done.6 = bf16[256,512]{1,0:T(8,128)(2,1)S(1)} collective-permute-done((bf16[256,512]{1,0:T(8,128)(2,1)S(1)}, bf16[256,512]{1,0:T(8,128)(2,1)S(1)}, u32[]{:S(2)}, u32[]{:S(2)}) %collective-permute-start.6) | collective-permute-done | bytes 262176 | tf_op jit(solution)/shard_map/ppermute | solution.py:42
  13.8 2.0 %collective-permute-start.3 = (bf16[256,512]{1,0:T(8,128)(2,1)S(1)}, bf16[256,512]{1,0:T(8,128)(2,1)S(1)}, u32[]{:S(2)}, u32[]{:S(2)}) collective-permute-start(bf16[256,512]{1,0:T(8,128)(2,1)S(1)} %collective-permute-done), channel_id=1, source_target_pairs={{65,0},{96,32},{0,64},{33,96},{64,1},{97,33},{1,65},{32,97},{73,8}... | collective-permute-start | bytes 786440 | tf_op jit(solution)/shard_map/ppermute | solution.py:42
  15.8 1.6 %collective-permute-start.10 = (bf16[512,512]{1,0:T(8,128)(2,1)S(1)}, bf16[512,512]{1,0:T(8,128)(2,1)S(1)}, u32[]{:S(2)}, u32[]{:S(2)}) collective-permute-start(bf16[512,512]{1,0:T(8,128)(2,1)S(1)} %constant_dynamic-update-slice_fusion.4.refs_3_), channel_id=1, source_target_pairs={{24,0},{38,32},{88,64},{102,96},{25,1},{39,33},{89,65},{103,97},{0... | collective-permute-start | bytes 1572872 | tf_op jit(solution)/shard_map/ppermute | solution.py:42
  17.4 1.7 %collective-permute-start.11 = (bf16[512,512]{1,0:T(8,128)(2,1)S(1)}, bf16[512,512]{1,0:T(8,128)(2,1)S(1)}, u32[]{:S(2)}, u32[]{:S(2)}) collective-permute-start(bf16[512,512]{1,0:T(8,128)(2,1)S(1)} %constant_dynamic-update-slice_fusion.4.refs_3_), channel_id=1, source_target_pairs={{8,0},{34,32},{72,64},{98,96},{9,1},{35,33},{73,65},{99,97},{16,8}... | collective-permute-start | bytes 1572872 | tf_op jit(solution)/shard_map/ppermute | solution.py:42
  19.1 1.9 %collective-permute-start.8 = (bf16[512,512]{1,0:T(8,128)(2,1)S(1)}, bf16[512,512]{1,0:T(8,128)(2,1)S(1)}, u32[]{:S(2)}, u32[]{:S(2)}) collective-permute-start(bf16[512,512]{1,0:T(8,128)(2,1)S(1)} %constant_dynamic-update-slice_fusion.2.refs_4_), channel_id=1, source_target_pairs={{8,0},{34,32},{72,64},{98,96},{9,1},{35,33},{73,65},{99,97},{16,8}... | collective-permute-start | bytes 1572872 | tf_op jit(solution)/shard_map/ppermute | solution.py:42
  21.4 1.6 %collective-permute-start.9 = (bf16[512,512]{1,0:T(8,128)(2,1)S(1)}, bf16[512,512]{1,0:T(8,128)(2,1)S(1)}, u32[]{:S(2)}, u32[]{:S(2)}) collective-permute-start(bf16[512,512]{1,0:T(8,128)(2,1)S(1)} %constant_dynamic-update-slice_fusion.2.refs_4_), channel_id=1, source_target_pairs={{24,0},{38,32},{88,64},{102,96},{25,1},{39,33},{89,65},{103,97},{0... | collective-permute-start | bytes 1572872 | tf_op jit(solution)/shard_map/ppermute | solution.py:42
  23.1 2.7 %exps0.1 = (f32[2048,128]{1,0:T(8,128)S(1)}, f32[8,4096]{1,0:T(8,128)S(1)}, bf16[2048,4096]{1,0:T(8,128)(2,1)S(1)}, bf16[4096,512]{1,0:T(8,128)(2,1)S(1)}) custom-call(s32[4]{0:T(128)S(1)} %pad_add_fusion.refs_0_.info_ref, bf16[512,512]{1,0:T(8,128)(2,1)S(1)} %pad_maximum_fusion.refs_1_, bf16[512,512]{1,0:T(8,128)(2,1)S(1)} %collective-permute-done.1.refs_2_, ...), custom_call_target="tpu_custom_call" | custom-call | flops 8589934592 | bytes 1048576 | tf_op jit(solution)/shard_map/exps0/pallas_call | solution.py:222
  25.9 2.5 %exps1.1 = (f32[2048,128]{1,0:T(8,128)S(1)}, f32[8,4096]{1,0:T(8,128)S(1)}, bf16[2048,4096]{1,0:T(8,128)(2,1)S(1)}, bf16[4096,512]{1,0:T(8,128)(2,1)S(1)}) custom-call(s32[4]{0:T(128)S(1)} %pad_add_fusion.refs_0_.info_ref, ...), custom_call_target="tpu_custom_call", output_to_operand_aliasing={{0}: (5, {}), {1}: (6, {}), {2}: (7, {}), {3}: (8, {})} | custom-call | flops 8589934592 | bytes 1048576 | tf_op jit(solution)/shard_map/exps1/pallas_call | solution.py:222
  28.4 1.7 %collective-permute-start.13 = (bf16[512,512]{1,0:T(8,128)(2,1)S(1)}, bf16[512,512]{1,0:T(8,128)(2,1)S(1)}, u32[]{:S(2)}, u32[]{:S(2)}) collective-permute-start(bf16[512,512]{1,0:T(8,128)(2,1)S(1)} %collective-permute-done.10.refs_5_), channel_id=1, source_target_pairs={{24,0},{38,32},{88,64},{102,96},{25,1},{39,33},{89,65},{103,97},{0... | collective-permute-start | bytes 1572872 | tf_op jit(solution)/shard_map/ppermute | solution.py:42
  30.1 3.7 %exps2.1 = (f32[2048,128]{1,0:T(8,128)S(1)}, f32[8,4096]{1,0:T(8,128)S(1)}, bf16[2048,4096]{1,0:T(8,128)(2,1)S(1)}, bf16[4096,512]{1,0:T(8,128)(2,1)S(1)}) custom-call(s32[4]{0:T(128)S(1)} %pad_add_fusion.refs_0_.info_ref, bf16[512,512]{1,0:T(8,128)(2,1)S(1)} %pad_maximum_fusion.refs_1_, ...), custom_call_target="tpu_custom_call", output_to_operand_aliasing={{0}: (7, {}), {1}: (8, {}), {2}: (9, {}), {3}: (10, {})} | custom-call | flops 8589934592 | bytes 1048576 | tf_op jit(solution)/shard_map/exps2/pallas_call | solution.py:222
  33.9 1.7 %collective-permute-start.12 = (bf16[512,512]{1,0:T(8,128)(2,1)S(1)}, bf16[512,512]{1,0:T(8,128)(2,1)S(1)}, u32[]{:S(2)}, u32[]{:S(2)}) collective-permute-start(bf16[512,512]{1,0:T(8,128)(2,1)S(1)} %collective-permute-done.8.refs_6_), channel_id=1, source_target_pairs={{8,0},{34,32},{72,64},{98,96},{9,1},{35,33},{73,65},{99,97},{16,8}... | collective-permute-start | bytes 1572872 | tf_op jit(solution)/shard_map/ppermute | solution.py:42
  35.6 3.3 %collective-permute-done.13.refs_7_ = bf16[512,512]{1,0:T(8,128)(2,1)S(1)} collective-permute-done((bf16[512,512]{1,0:T(8,128)(2,1)S(1)}, bf16[512,512]{1,0:T(8,128)(2,1)S(1)}, u32[]{:S(2)}, u32[]{:S(2)}) %collective-permute-start.13) | collective-permute-done | bytes 524320 | tf_op jit(solution)/shard_map/ppermute | solution.py:42
  38.9 5.3 %exps3.1 = (f32[2048,128]{1,0:T(8,128)S(1)}, f32[8,4096]{1,0:T(8,128)S(1)}, bf16[2048,4096]{1,0:T(8,128)(2,1)S(1)}, bf16[4096,512]{1,0:T(8,128)(2,1)S(1)}) custom-call(s32[4]{0:T(128)S(1)} %pad_add_fusion.refs_0_.info_ref, bf16[512,512]{1,0:T(8,128)(2,1)S(1)} %pad_maximum_fusion.refs_1_, ...), custom_call_target="tpu_custom_call", output_to_operand_aliasing={{0}: (8, {}), {1}: (9, {}), {2}: (10, {}), {3}: (11, {})} | custom-call | flops 12884901888 | bytes 1572864 | tf_op jit(solution)/shard_map/exps3/pallas_call | solution.py:222
  44.2 2.5 %exps4.1 = (f32[2048,128]{1,0:T(8,128)S(1)}, f32[8,4096]{1,0:T(8,128)S(1)}, bf16[2048,4096]{1,0:T(8,128)(2,1)S(1)}, bf16[4096,512]{1,0:T(8,128)(2,1)S(1)}, f32[8,256]{1,0:T(8,128)S(1)}, /*index=5*/f32[24,256]{1,0:T(8,128)S(1)}) custom-call(s32[4]{0:T(128)S(1)} %pad_add_fusion.refs_0_.info_ref, ...), custom_call_target="tpu_custom_call", output_to_operand_aliasing={{0}: (6, {}), {1}: (7, {}), {2}: (8, {}), {3}: (9, {})} | custom-call | flops 4294967296 | bytes 524288 | tf_op jit(solution)/shard_map/exps4/pallas_call | solution.py:222
  46.8 1.3 %collective-permute-start.14 = (f32[8,256]{1,0:T(8,128)S(1)}, f32[8,256]{1,0:T(8,128)S(1)}, u32[]{:S(2)}, u32[]{:S(2)}) collective-permute-start(f32[8,256]{1,0:T(8,128)S(1)} %get-tuple-element.65), channel_id=1, source_target_pairs={{32,0},{0,32},{96,64},{64,96},{33,1},{1,33},{97,65},{65,97},{40,8}... | collective-permute-start | bytes 24584 | tf_op jit(solution)/shard_map/ppermute | solution.py:42
  49.0 1.7 %collective-permute-done.17 = f32[24,256]{1,0:T(8,128)S(1)} collective-permute-done((f32[24,256]{1,0:T(8,128)S(1)}, f32[24,256]{1,0:T(8,128)S(1)}, u32[]{:S(2)}, u32[]{:S(2)}) %collective-permute-start.17) | collective-permute-done | bytes 24608 | tf_op jit(solution)/shard_map/ppermute | solution.py:55
  50.6 3.7 %collective-permute-start.18 = (f32[24,256]{1,0:T(8,128)S(1)}, f32[24,256]{1,0:T(8,128)S(1)}, u32[]{:S(2)}, u32[]{:S(2)}) collective-permute-start(f32[24,256]{1,0:T(8,128)S(1)} %add.21), channel_id=1, source_target_pairs={{6,0},{56,32},{70,64},{120,96},{7,1},{57,33},{71,65},{121,97},{14,... | collective-permute-start | bytes 73736 | tf_op jit(solution)/shard_map/ppermute | solution.py:55
  54.3 1.8 %collective-permute-done.18 = f32[24,256]{1,0:T(8,128)S(1)} collective-permute-done((f32[24,256]{1,0:T(8,128)S(1)}, f32[24,256]{1,0:T(8,128)S(1)}, u32[]{:S(2)}, u32[]{:S(2)}) %collective-permute-start.18) | collective-permute-done | bytes 24608 | tf_op jit(solution)/shard_map/ppermute | solution.py:55
  57.2 2.9 %collective-permute-done.15 = f32[8,256]{1,0:T(8,128)S(1)} collective-permute-done((f32[8,256]{1,0:T(8,128)S(1)}, f32[8,256]{1,0:T(8,128)S(1)}, u32[]{:S(2)}, u32[]{:S(2)}) %collective-permute-start.15) | collective-permute-done | bytes 8224 | tf_op jit(solution)/shard_map/ppermute | solution.py:55
  60.1 2.0 %collective-permute-start.20 = (f32[24,256]{1,0:T(8,128)S(1)}, f32[24,256]{1,0:T(8,128)S(1)}, u32[]{:S(2)}, u32[]{:S(2)}) collective-permute-start(f32[24,256]{1,0:T(8,128)S(1)} %add.23.refs_2_), channel_id=1, source_target_pairs={{24,0},{38,32},{88,64},{102,96},{25,1},{39,33},{89,65},{103,97},{1... | collective-permute-start | bytes 73736 | tf_op jit(solution)/shard_map/ppermute | solution.py:55
  63.1 3.8 %collective-permute-done.16.refs_1_ = f32[8,256]{1,0:T(8,128)S(1)} collective-permute-done((f32[8,256]{1,0:T(8,128)S(1)}, f32[8,256]{1,0:T(8,128)S(1)}, u32[]{:S(2)}, u32[]{:S(2)}) %collective-permute-start.16) | collective-permute-done | bytes 8224 | tf_op jit(solution)/shard_map/ppermute | solution.py:55
  67.8 3.4 %grads_core.1 = bf16[784,512]{1,0:T(8,128)(2,1)S(1)} custom-call(f32[32,128]{1,0:T(8,128)S(1)} %get-tuple-element.78.acol_ref, bf16[2048,128]{1,0:T(8,128)(2,1)S(1)} %get-tuple-element.71.arow_ref, bf16[2048,4096]{1,0:T(8,128)(2,1)S(1)} %get-tuple-element.72.exps_ref, bf16[4096,512]{1,0:T(8,128)(2,1)S(1)} %get-tuple-element.73.unit_ref, ...), custom_call_target="tpu_custom_call" | custom-call | flops 3221225472 | bytes 10485760 | tf_op jit(solution)/shard_map/grads_core/pallas_call | solution.py:312
  73.7 2.3 %grads_near.1 = (bf16[272,512]{1,0:T(8,128)(2,1)S(1)}, f32[256,512]{1,0:T(8,128)S(1)}) custom-call(f32[32,128]{1,0:T(8,128)S(1)} %get-tuple-element.78.acol_ref, bf16[2048,128]{1,0:T(8,128)(2,1)S(1)} %get-tuple-element.71.arow_ref, bf16[2048,4096]{1,0:T(8,128)(2,1)S(1)} %get-tuple-element.72.exps_ref, bf16[4096,512]{1,0:T(8,128)(2,1)S(1)} %get-tuple-element.73.unit_ref, ...), custom_call_target="tpu_custom_call" | custom-call | flops 2147483648 | bytes 8388608 | tf_op jit(solution)/shard_map/grads_near/pallas_call | solution.py:312
  76.1 1.3 %grads_core_own.1 = bf16[256,512]{1,0:T(8,128)(2,1)S(1)} custom-call(f32[32,128]{1,0:T(8,128)S(1)} %get-tuple-element.78.acol_ref, bf16[2048,128]{1,0:T(8,128)(2,1)S(1)} %get-tuple-element.71.arow_ref, bf16[2048,4096]{1,0:T(8,128)(2,1)S(1)} %get-tuple-element.72.exps_ref, bf16[4096,512]{1,0:T(8,128)(2,1)S(1)} %get-tuple-element.73.unit_ref), custom_call_target="tpu_custom_call" | custom-call | flops 1073741824 | bytes 6291456 | tf_op jit(solution)/shard_map/grads_core_own/pallas_call | solution.py:312
  78.3 2.5 %collective-permute-start.24 = (bf16[272,512]{1,0:T(8,128)(2,1)S(1)}, bf16[272,512]{1,0:T(8,128)(2,1)S(1)}, u32[]{:S(2)}, u32[]{:S(2)}) collective-permute-start(bf16[272,512]{1,0:T(8,128)(2,1)S(1)} %get-tuple-element.79), channel_id=1, source_target_pairs={{64,0},{97,32},{1,64},{32,96},{65,1},{96,33},{0,65},{33,97},{72,8}... | collective-permute-start | bytes 835592 | tf_op jit(solution)/shard_map/ppermute | solution.py:42
  82.9 4.8 %collective-permute-done.24.one_ref = bf16[272,512]{1,0:T(8,128)(2,1)S(1)} collective-permute-done((bf16[272,512]{1,0:T(8,128)(2,1)S(1)}, bf16[272,512]{1,0:T(8,128)(2,1)S(1)}, u32[]{:S(2)}, u32[]{:S(2)}) %collective-permute-start.24) | collective-permute-done | bytes 278560 | tf_op jit(solution)/shard_map/ppermute | solution.py:42
  87.7 1.7 %collective-permute-done.25.two_ref = bf16[272,512]{1,0:T(8,128)(2,1)S(1)} collective-permute-done((bf16[272,512]{1,0:T(8,128)(2,1)S(1)}, bf16[272,512]{1,0:T(8,128)(2,1)S(1)}, u32[]{:S(2)}, u32[]{:S(2)}) %collective-permute-start.25) | collective-permute-done | bytes 278560 | tf_op jit(solution)/shard_map/ppermute | solution.py:42
  (55 shorter events, 13.5 us)
Async XLA Ops:
  0.6 1.0 %copy-start = (bf16[256,512]{1,0:T(8,128)(2,1)S(1)}, bf16[256,512]{1,0:T(8,128)(2,1)}, u32[]{:S(2)}) copy-start(bf16[256,512]{1,0:T(8,128)(2,1)} %z_ref.3) | copy-start | bytes 786436
  1.7 10.4 %collective-permute-start = (bf16[256,512]{1,0:T(8,128)(2,1)S(1)}, bf16[256,512]{1,0:T(8,128)(2,1)S(1)}, u32[]{:S(2)}, u32[]{:S(2)}) collective-permute-start(bf16[256,512]{1,0:T(8,128)(2,1)S(1)} %unit.1.unit_ref), channel_id=1, source_target_pairs={{65,0},{96,32},{0,64},{33,96},{64,1},{97,33},{1,65},{32,97},{73,8}... | collective-permute-start | bytes 786440 | tf_op jit(solution)/shard_map/ppermute | solution.py:42
  3.8 8.5 %collective-permute-start.5 = (bf16[256,512]{1,0:T(8,128)(2,1)S(1)}, bf16[256,512]{1,0:T(8,128)(2,1)S(1)}, u32[]{:S(2)}, u32[]{:S(2)}) collective-permute-start(bf16[256,512]{1,0:T(8,128)(2,1)S(1)} %unit.1.unit_ref), channel_id=1, source_target_pairs={{6,0},{56,32},{70,64},{120,96},{7,1},{57,33},{71,65},{121,97},{14,... | collective-permute-start | bytes 786440 | tf_op jit(solution)/shard_map/ppermute | solution.py:42
  5.3 8.5 %collective-permute-start.6 = (bf16[256,512]{1,0:T(8,128)(2,1)S(1)}, bf16[256,512]{1,0:T(8,128)(2,1)S(1)}, u32[]{:S(2)}, u32[]{:S(2)}) collective-permute-start(bf16[256,512]{1,0:T(8,128)(2,1)S(1)} %unit.1.unit_ref), channel_id=1, source_target_pairs={{2,0},{40,32},{66,64},{104,96},{3,1},{41,33},{67,65},{105,97},{10,... | collective-permute-start | bytes 786440 | tf_op jit(solution)/shard_map/ppermute | solution.py:42
  7.0 10.4 %collective-permute-start.7 = (bf16[256,512]{1,0:T(8,128)(2,1)S(1)}, bf16[256,512]{1,0:T(8,128)(2,1)S(1)}, u32[]{:S(2)}, u32[]{:S(2)}) collective-permute-start(bf16[256,512]{1,0:T(8,128)(2,1)S(1)} %unit.1.unit_ref), channel_id=1, source_target_pairs={{4,0},{48,32},{68,64},{112,96},{5,1},{49,33},{69,65},{113,97},{12,... | collective-permute-start | bytes 786440 | tf_op jit(solution)/shard_map/ppermute | solution.py:42
  8.8 10.3 %collective-permute-start.2 = (bf16[256,512]{1,0:T(8,128)(2,1)S(1)}, bf16[256,512]{1,0:T(8,128)(2,1)S(1)}, u32[]{:S(2)}, u32[]{:S(2)}) collective-permute-start(bf16[256,512]{1,0:T(8,128)(2,1)S(1)} %unit.1.unit_ref), channel_id=1, source_target_pairs={{64,0},{97,32},{1,64},{32,96},{65,1},{96,33},{0,65},{33,97},{72,8}... | collective-permute-start | bytes 786440 | tf_op jit(solution)/shard_map/ppermute | solution.py:42
  11.1 0.7 copy-start.2
  12.2 10.9 %collective-permute-start.1 = (bf16[512,512]{1,0:T(8,128)(2,1)S(1)}, bf16[512,512]{1,0:T(8,128)(2,1)S(1)}, u32[]{:S(2)}, u32[]{:S(2)}) collective-permute-start(bf16[512,512]{1,0:T(8,128)(2,1)S(1)} %pad_maximum_fusion.refs_1_), channel_id=1, source_target_pairs={{32,0},{0,32},{96,64},{64,96},{33,1},{1,33},{97,65},{65,97},{40,8}... | collective-permute-start | bytes 1572872 | tf_op jit(solution)/shard_map/ppermute | solution.py:42
  13.8 7.7 %collective-permute-start.3 = (bf16[256,512]{1,0:T(8,128)(2,1)S(1)}, bf16[256,512]{1,0:T(8,128)(2,1)S(1)}, u32[]{:S(2)}, u32[]{:S(2)}) collective-permute-start(bf16[256,512]{1,0:T(8,128)(2,1)S(1)} %collective-permute-done), channel_id=1, source_target_pairs={{65,0},{96,32},{0,64},{33,96},{64,1},{97,33},{1,65},{32,97},{73,8}... | collective-permute-start | bytes 786440 | tf_op jit(solution)/shard_map/ppermute | solution.py:42
  15.8 12.6 %collective-permute-start.10 = (bf16[512,512]{1,0:T(8,128)(2,1)S(1)}, bf16[512,512]{1,0:T(8,128)(2,1)S(1)}, u32[]{:S(2)}, u32[]{:S(2)}) collective-permute-start(bf16[512,512]{1,0:T(8,128)(2,1)S(1)} %constant_dynamic-update-slice_fusion.4.refs_3_), channel_id=1, source_target_pairs={{24,0},{38,32},{88,64},{102,96},{25,1},{39,33},{89,65},{103,97},{0... | collective-permute-start | bytes 1572872 | tf_op jit(solution)/shard_map/ppermute | solution.py:42
  17.4 11.0 %collective-permute-start.11 = (bf16[512,512]{1,0:T(8,128)(2,1)S(1)}, bf16[512,512]{1,0:T(8,128)(2,1)S(1)}, u32[]{:S(2)}, u32[]{:S(2)}) collective-permute-start(bf16[512,512]{1,0:T(8,128)(2,1)S(1)} %constant_dynamic-update-slice_fusion.4.refs_3_), channel_id=1, source_target_pairs={{8,0},{34,32},{72,64},{98,96},{9,1},{35,33},{73,65},{99,97},{16,8}... | collective-permute-start | bytes 1572872 | tf_op jit(solution)/shard_map/ppermute | solution.py:42
  19.1 14.7 %collective-permute-start.8 = (bf16[512,512]{1,0:T(8,128)(2,1)S(1)}, bf16[512,512]{1,0:T(8,128)(2,1)S(1)}, u32[]{:S(2)}, u32[]{:S(2)}) collective-permute-start(bf16[512,512]{1,0:T(8,128)(2,1)S(1)} %constant_dynamic-update-slice_fusion.2.refs_4_), channel_id=1, source_target_pairs={{8,0},{34,32},{72,64},{98,96},{9,1},{35,33},{73,65},{99,97},{16,8}... | collective-permute-start | bytes 1572872 | tf_op jit(solution)/shard_map/ppermute | solution.py:42
  21.4 12.4 %collective-permute-start.9 = (bf16[512,512]{1,0:T(8,128)(2,1)S(1)}, bf16[512,512]{1,0:T(8,128)(2,1)S(1)}, u32[]{:S(2)}, u32[]{:S(2)}) collective-permute-start(bf16[512,512]{1,0:T(8,128)(2,1)S(1)} %constant_dynamic-update-slice_fusion.2.refs_4_), channel_id=1, source_target_pairs={{24,0},{38,32},{88,64},{102,96},{25,1},{39,33},{89,65},{103,97},{0... | collective-permute-start | bytes 1572872 | tf_op jit(solution)/shard_map/ppermute | solution.py:42
  23.0 2.8 %collective-permute-start.4 = (bf16[512,512]{1,0:T(8,128)(2,1)S(1)}, bf16[512,512]{1,0:T(8,128)(2,1)S(1)}, u32[]{:S(2)}, u32[]{:S(2)}) collective-permute-start(bf16[512,512]{1,0:T(8,128)(2,1)S(1)} %constant_dynamic-update-slice_fusion.refs_1_.refs_3_), channel_id=1, source_target_pairs={{32,0},{0,32},{96,64},{64,96},{33,1},{1,33},{97,65},{65,97},{40,8}... | collective-permute-start | bytes 1572872 | tf_op jit(solution)/shard_map/ppermute | solution.py:42
  28.4 10.5 %collective-permute-start.13 = (bf16[512,512]{1,0:T(8,128)(2,1)S(1)}, bf16[512,512]{1,0:T(8,128)(2,1)S(1)}, u32[]{:S(2)}, u32[]{:S(2)}) collective-permute-start(bf16[512,512]{1,0:T(8,128)(2,1)S(1)} %collective-permute-done.10.refs_5_), channel_id=1, source_target_pairs={{24,0},{38,32},{88,64},{102,96},{25,1},{39,33},{89,65},{103,97},{0... | collective-permute-start | bytes 1572872 | tf_op jit(solution)/shard_map/ppermute | solution.py:42
  33.9 10.4 %collective-permute-start.12 = (bf16[512,512]{1,0:T(8,128)(2,1)S(1)}, bf16[512,512]{1,0:T(8,128)(2,1)S(1)}, u32[]{:S(2)}, u32[]{:S(2)}) collective-permute-start(bf16[512,512]{1,0:T(8,128)(2,1)S(1)} %collective-permute-done.8.refs_6_), channel_id=1, source_target_pairs={{8,0},{34,32},{72,64},{98,96},{9,1},{35,33},{73,65},{99,97},{16,8}... | collective-permute-start | bytes 1572872 | tf_op jit(solution)/shard_map/ppermute | solution.py:42
  46.7 3.9 %collective-permute-start.17 = (f32[24,256]{1,0:T(8,128)S(1)}, f32[24,256]{1,0:T(8,128)S(1)}, u32[]{:S(2)}, u32[]{:S(2)}) collective-permute-start(f32[24,256]{1,0:T(8,128)S(1)} %get-tuple-element.66), channel_id=1, source_target_pairs={{2,0},{40,32},{66,64},{104,96},{3,1},{41,33},{67,65},{105,97},{10,... | collective-permute-start | bytes 73736 | tf_op jit(solution)/shard_map/ppermute | solution.py:55
  46.8 2.2 %collective-permute-start.14 = (f32[8,256]{1,0:T(8,128)S(1)}, f32[8,256]{1,0:T(8,128)S(1)}, u32[]{:S(2)}, u32[]{:S(2)}) collective-permute-start(f32[8,256]{1,0:T(8,128)S(1)} %get-tuple-element.65), channel_id=1, source_target_pairs={{32,0},{0,32},{96,64},{64,96},{33,1},{1,33},{97,65},{65,97},{40,8}... | collective-permute-start | bytes 24584 | tf_op jit(solution)/shard_map/ppermute | solution.py:42
  50.6 5.5 %collective-permute-start.18 = (f32[24,256]{1,0:T(8,128)S(1)}, f32[24,256]{1,0:T(8,128)S(1)}, u32[]{:S(2)}, u32[]{:S(2)}) collective-permute-start(f32[24,256]{1,0:T(8,128)S(1)} %add.21), channel_id=1, source_target_pairs={{6,0},{56,32},{70,64},{120,96},{7,1},{57,33},{71,65},{121,97},{14,... | collective-permute-start | bytes 73736 | tf_op jit(solution)/shard_map/ppermute | solution.py:55
  56.1 4.0 %collective-permute-start.19 = (f32[24,256]{1,0:T(8,128)S(1)}, f32[24,256]{1,0:T(8,128)S(1)}, u32[]{:S(2)}, u32[]{:S(2)}) collective-permute-start(f32[24,256]{1,0:T(8,128)S(1)} %add.22), channel_id=1, source_target_pairs={{8,0},{34,32},{72,64},{98,96},{9,1},{35,33},{73,65},{99,97},{0,8},... | collective-permute-start | bytes 73736 | tf_op jit(solution)/shard_map/ppermute | solution.py:55
  56.5 3.7 %collective-permute-start.15 = (f32[8,256]{1,0:T(8,128)S(1)}, f32[8,256]{1,0:T(8,128)S(1)}, u32[]{:S(2)}, u32[]{:S(2)}) collective-permute-start(f32[8,256]{1,0:T(8,128)S(1)} %add.19), channel_id=1, source_target_pairs={{64,0},{96,32},{0,64},{32,96},{65,1},{97,33},{1,65},{33,97},{72,8}... | collective-permute-start | bytes 24584 | tf_op jit(solution)/shard_map/ppermute | solution.py:55
  60.1 6.8 %collective-permute-start.20 = (f32[24,256]{1,0:T(8,128)S(1)}, f32[24,256]{1,0:T(8,128)S(1)}, u32[]{:S(2)}, u32[]{:S(2)}) collective-permute-start(f32[24,256]{1,0:T(8,128)S(1)} %add.23.refs_2_), channel_id=1, source_target_pairs={{24,0},{38,32},{88,64},{102,96},{25,1},{39,33},{89,65},{103,97},{1... | collective-permute-start | bytes 73736 | tf_op jit(solution)/shard_map/ppermute | solution.py:55
  62.1 4.9 %collective-permute-start.16 = (f32[8,256]{1,0:T(8,128)S(1)}, f32[8,256]{1,0:T(8,128)S(1)}, u32[]{:S(2)}, u32[]{:S(2)}) collective-permute-start(f32[8,256]{1,0:T(8,128)S(1)} %add.20.refs_0_), channel_id=1, source_target_pairs={{65,0},{97,32},{1,64},{33,96},{64,1},{96,33},{0,65},{32,97},{73,8}... | collective-permute-start | bytes 24584 | tf_op jit(solution)/shard_map/ppermute | solution.py:55
  71.2 2.4 %collective-permute-start.21 = (bf16[784,512]{1,0:T(8,128)(2,1)S(1)}, bf16[784,512]{1,0:T(8,128)(2,1)S(1)}, u32[]{:S(2)}, u32[]{:S(2)}) collective-permute-start(bf16[784,512]{1,0:T(8,128)(2,1)S(1)} %grads_core.1), channel_id=1, source_target_pairs={{32,0},{0,32},{96,64},{64,96},{33,1},{1,33},{97,65},{65,97},{40,8}... | collective-permute-start | bytes 2408456 | tf_op jit(solution)/shard_map/ppermute | solution.py:42
  73.7 7.8 %collective-permute-start.22 = (bf16[272,512]{1,0:T(8,128)(2,1)S(1)}, bf16[272,512]{1,0:T(8,128)(2,1)S(1)}, u32[]{:S(2)}, u32[]{:S(2)}) collective-permute-start(bf16[272,512]{1,0:T(8,128)(2,1)S(1)} %sum_far.1.refs_1_.here_ref), channel_id=1, source_target_pairs={{65,0},{96,32},{0,64},{33,96},{64,1},{97,33},{1,65},{32,97},{73,8}... | collective-permute-start | bytes 835592 | tf_op jit(solution)/shard_map/ppermute | solution.py:42
  77.3 12.0 %copy-start.1 = (bf16[256,512]{1,0:T(8,128)(2,1)S(1)}, bf16[256,512]{1,0:T(8,128)(2,1)}, u32[]{:S(2)}) copy-start(bf16[256,512]{1,0:T(8,128)(2,1)} %z_ref.3) | copy-start | bytes 786436
  77.3 4.3 %collective-permute-start.23 = (bf16[256,512]{1,0:T(8,128)(2,1)S(1)}, bf16[256,512]{1,0:T(8,128)(2,1)S(1)}, u32[]{:S(2)}, u32[]{:S(2)}) collective-permute-start(bf16[256,512]{1,0:T(8,128)(2,1)S(1)} %grads_core_own.1), channel_id=1, source_target_pairs={{32,0},{0,32},{96,64},{64,96},{33,1},{1,33},{97,65},{65,97},{40,8}... | collective-permute-start | bytes 786440 | tf_op jit(solution)/shard_map/ppermute | solution.py:42
  78.3 9.4 %collective-permute-start.24 = (bf16[272,512]{1,0:T(8,128)(2,1)S(1)}, bf16[272,512]{1,0:T(8,128)(2,1)S(1)}, u32[]{:S(2)}, u32[]{:S(2)}) collective-permute-start(bf16[272,512]{1,0:T(8,128)(2,1)S(1)} %get-tuple-element.79), channel_id=1, source_target_pairs={{64,0},{97,32},{1,64},{32,96},{65,1},{96,33},{0,65},{33,97},{72,8}... | collective-permute-start | bytes 835592 | tf_op jit(solution)/shard_map/ppermute | solution.py:42
  81.5 7.8 %collective-permute-start.25 = (bf16[272,512]{1,0:T(8,128)(2,1)S(1)}, bf16[272,512]{1,0:T(8,128)(2,1)S(1)}, u32[]{:S(2)}, u32[]{:S(2)}) collective-permute-start(bf16[272,512]{1,0:T(8,128)(2,1)S(1)} %sum_two.1), channel_id=1, source_target_pairs={{65,0},{96,32},{0,64},{33,96},{64,1},{97,33},{1,65},{32,97},{73,8}... | collective-permute-start | bytes 835592 | tf_op jit(solution)/shard_map/ppermute | solution.py:42

commit v7 on v6

--- a/solution.py
+++ b/solution.py
@@ -205,7 +205,7 @@
         col_line_ref[16:17, 0:128] = positive_ref[...]
 
 
-def make_exps(info, rows, rows_here, cols, places, chain, positive, name):
+def make_exps(info, rows, rows_here, cols, places, chain, positive, weight, name):
     first, last = chain is None, positive is not None
     count = len(cols)
     tiles = sum(c.shape[0] for c in cols) // TILE
@@ -227,9 +227,9 @@
         input_output_aliases={} if first else {start + n: n for n in range(4)},
         compiler_params=params(12),
         cost_estimate=pl.CostEstimate(
-            flops=2 * len(rows) * 512 * tiles * TILE * E * (8 if len(rows) == 2 else 4),
-            bytes_accessed=tiles * TILE * E * 2,
-            transcendentals=len(rows) * 512 * tiles * TILE,
+            flops=2 * len(rows) * 512 * tiles * TILE * E * weight,
+            bytes_accessed=tiles * TILE * E * 2 * weight,
+            transcendentals=len(rows) * 512 * tiles * TILE * weight,
         ),
         name=name,
     )(*operands)
@@ -388,16 +388,17 @@
     near = [near, get(near, core=1)]
 
     mates, positive = make_mates(unit, partner)
-    chain = make_exps(info, near, (0,), [line0, line1], (0, 1), None, None, "exps0")
+    chain = make_exps(info, near, (0,), [line0, line1], (0, 1), None, None, 8, "exps0")
     rest = jnp.concatenate([z_two, z_far], axis=0)
     rest = [rest, get(rest, core=1)]
-    chain = make_exps(info, rest, (1,), [line0, line1], (0, 1), chain, None, "exps1")
+    chain = make_exps(info, rest, (1,), [line0, line1], (0, 1), chain, None, 8, "exps1")
     far0 = get(after(before0, after0, chain[0]), second=-1)
     rows = near + rest
-    chain = make_exps(info, rows, (0, 1), [before0, after0], (2, 4), chain, None, "exps2")
+    chain = make_exps(info, rows, (0, 1), [before0], (2,), chain, None, 4, "exps2")
     far1 = get(after(after1, before1, chain[0]), second=1)
-    chain = make_exps(info, rows, (0, 1), [before1, after1, far0], (3, 5, 6), chain, None, "exps3")
-    chain = make_exps(info, rows, (0, 1), [far1], (7,), chain, positive, "exps4")
+    chain = make_exps(info, rows, (0, 1), [after0, before1, after1], (4, 3, 5), chain, None, 0, "exps3")
+    chain = make_exps(info, rows, (0, 1), [far0], (6,), chain, None, 0, "exps4")
+    chain = make_exps(info, rows, (0, 1), [far1], (7,), chain, positive, 0, "exps5")
     _, _, exps, units, sums, col_sums = chain
 
     by_row = sums + get(sums, core=1)

time: 91 us -> 90.3 us (level)
  waiting for transfers between devices: 24.6 us -> 21.5 us
  starting transfers between devices: 34.4 us -> 36.8 us
    ppermute x20, waiting for transfers between devices: 14.3 us -> 12 us  [get(): return lax.ppermute(value, AXES, pairs)]
    ppermute x6, starting transfers between devices: 7.82 us -> 10.1 us  [swap(): return lax.ppermute(value, AXES, pairs)]
    pallas_call x5 -> x6, Pallas kernels: 16.8 us -> 17.4 us  [make_exps(): pl.pallas_call(functools.partial(exps_kernel, places, rows_here, first, l...]
  transfers between devices with their start and end apart: 26 -> 26, of which waited for: 12 -> 12; matrix products, arithmetic and copies ran while one was open for 0% -> 0% of each run, Pallas kernels for 23% -> 24%
where the time goes in v7:
time: 90.3 us; the launch traced here: 89.8 us
  starting transfers between devices  36.8 us (41%)
  Pallas kernels  29.3 us (32%)
  waiting for transfers between devices  21.5 us (24%)
  local copies, waits for them, and re-layouts  1.07 us (1%)
  between operations  0.92 us (1%)
    ppermute x20, starting transfers between devices, get(): return lax.ppermute(value, AXES, pairs)  26.7 us
    pallas_call x6, Pallas kernels, make_exps(): pl.pallas_call(functools.partial(exps_kernel, places, rows_here, first, l...  17.4 us
    ppermute x20, waiting for transfers between devices, get(): return lax.ppermute(value, AXES, pairs)  12 us
    ppermute x6, starting transfers between devices, swap(): return lax.ppermute(value, AXES, pairs)  10.1 us
    ppermute x6, waiting for transfers between devices, swap(): return lax.ppermute(value, AXES, pairs)  9.52 us
    pallas_call x5, Pallas kernels, make_grads(): pl.pallas_call(functools.partial(grads_kernel, pieces, adds, carry is not...  9.47 us
  transfers between devices with their start and end apart: 26, of which 12 were waited for; matrix products, arithmetic and copies ran while one was open for 0% of the time, Pallas kernels for 24%

profile of v7, /device:TPU:0, one launch (start us, length us, event | category | flops | bytes accessed | tf_op | source)
XLA Modules:
  0.0 89.8 jit_solution(6976431031548094555)
XLA Ops:
  1.7 2.1 %collective-permute-start = (bf16[256,512]{1,0:T(8,128)(2,1)S(1)}, bf16[256,512]{1,0:T(8,128)(2,1)S(1)}, u32[]{:S(2)}, u32[]{:S(2)}) collective-permute-start(bf16[256,512]{1,0:T(8,128)(2,1)S(1)} %unit.1.unit_ref), channel_id=1, source_target_pairs={{65,0},{96,32},{0,64},{33,96},{64,1},{97,33},{1,65},{32,97},{73,8}... | collective-permute-start | bytes 786440 | tf_op jit(solution)/shard_map/ppermute | solution.py:42
  3.8 1.5 %collective-permute-start.5 = (bf16[256,512]{1,0:T(8,128)(2,1)S(1)}, bf16[256,512]{1,0:T(8,128)(2,1)S(1)}, u32[]{:S(2)}, u32[]{:S(2)}) collective-permute-start(bf16[256,512]{1,0:T(8,128)(2,1)S(1)} %unit.1.unit_ref), channel_id=1, source_target_pairs={{6,0},{56,32},{70,64},{120,96},{7,1},{57,33},{71,65},{121,97},{14,... | collective-permute-start | bytes 786440 | tf_op jit(solution)/shard_map/ppermute | solution.py:42
  5.3 1.7 %collective-permute-start.6 = (bf16[256,512]{1,0:T(8,128)(2,1)S(1)}, bf16[256,512]{1,0:T(8,128)(2,1)S(1)}, u32[]{:S(2)}, u32[]{:S(2)}) collective-permute-start(bf16[256,512]{1,0:T(8,128)(2,1)S(1)} %unit.1.unit_ref), channel_id=1, source_target_pairs={{2,0},{40,32},{66,64},{104,96},{3,1},{41,33},{67,65},{105,97},{10,... | collective-permute-start | bytes 786440 | tf_op jit(solution)/shard_map/ppermute | solution.py:42
  7.0 1.8 %collective-permute-start.7 = (bf16[256,512]{1,0:T(8,128)(2,1)S(1)}, bf16[256,512]{1,0:T(8,128)(2,1)S(1)}, u32[]{:S(2)}, u32[]{:S(2)}) collective-permute-start(bf16[256,512]{1,0:T(8,128)(2,1)S(1)} %unit.1.unit_ref), channel_id=1, source_target_pairs={{4,0},{48,32},{68,64},{112,96},{5,1},{49,33},{69,65},{113,97},{12,... | collective-permute-start | bytes 786440 | tf_op jit(solution)/shard_map/ppermute | solution.py:42
  8.8 2.2 %collective-permute-start.2 = (bf16[256,512]{1,0:T(8,128)(2,1)S(1)}, bf16[256,512]{1,0:T(8,128)(2,1)S(1)}, u32[]{:S(2)}, u32[]{:S(2)}) collective-permute-start(bf16[256,512]{1,0:T(8,128)(2,1)S(1)} %unit.1.unit_ref), channel_id=1, source_target_pairs={{64,0},{97,32},{1,64},{32,96},{65,1},{96,33},{0,65},{33,97},{72,8}... | collective-permute-start | bytes 786440 | tf_op jit(solution)/shard_map/ppermute | solution.py:42
  11.4 2.4 %collective-permute-done.6 = bf16[256,512]{1,0:T(8,128)(2,1)S(1)} collective-permute-done((bf16[256,512]{1,0:T(8,128)(2,1)S(1)}, bf16[256,512]{1,0:T(8,128)(2,1)S(1)}, u32[]{:S(2)}, u32[]{:S(2)}) %collective-permute-start.6) | collective-permute-done | bytes 262176 | tf_op jit(solution)/shard_map/ppermute | solution.py:42
  13.8 2.0 %collective-permute-start.3 = (bf16[256,512]{1,0:T(8,128)(2,1)S(1)}, bf16[256,512]{1,0:T(8,128)(2,1)S(1)}, u32[]{:S(2)}, u32[]{:S(2)}) collective-permute-start(bf16[256,512]{1,0:T(8,128)(2,1)S(1)} %collective-permute-done), channel_id=1, source_target_pairs={{65,0},{96,32},{0,64},{33,96},{64,1},{97,33},{1,65},{32,97},{73,8}... | collective-permute-start | bytes 786440 | tf_op jit(solution)/shard_map/ppermute | solution.py:42
  15.8 1.6 %collective-permute-start.10 = (bf16[512,512]{1,0:T(8,128)(2,1)S(1)}, bf16[512,512]{1,0:T(8,128)(2,1)S(1)}, u32[]{:S(2)}, u32[]{:S(2)}) collective-permute-start(bf16[512,512]{1,0:T(8,128)(2,1)S(1)} %constant_dynamic-update-slice_fusion.4.refs_3_), channel_id=1, source_target_pairs={{24,0},{38,32},{88,64},{102,96},{25,1},{39,33},{89,65},{103,97},{0... | collective-permute-start | bytes 1572872 | tf_op jit(solution)/shard_map/ppermute | solution.py:42
  17.4 1.7 %collective-permute-start.12 = (bf16[512,512]{1,0:T(8,128)(2,1)S(1)}, bf16[512,512]{1,0:T(8,128)(2,1)S(1)}, u32[]{:S(2)}, u32[]{:S(2)}) collective-permute-start(bf16[512,512]{1,0:T(8,128)(2,1)S(1)} %constant_dynamic-update-slice_fusion.4.refs_3_), channel_id=1, source_target_pairs={{8,0},{34,32},{72,64},{98,96},{9,1},{35,33},{73,65},{99,97},{16,8}... | collective-permute-start | bytes 1572872 | tf_op jit(solution)/shard_map/ppermute | solution.py:42
  19.1 1.9 %collective-permute-start.8 = (bf16[512,512]{1,0:T(8,128)(2,1)S(1)}, bf16[512,512]{1,0:T(8,128)(2,1)S(1)}, u32[]{:S(2)}, u32[]{:S(2)}) collective-permute-start(bf16[512,512]{1,0:T(8,128)(2,1)S(1)} %constant_dynamic-update-slice_fusion.2.refs_4_), channel_id=1, source_target_pairs={{8,0},{34,32},{72,64},{98,96},{9,1},{35,33},{73,65},{99,97},{16,8}... | collective-permute-start | bytes 1572872 | tf_op jit(solution)/shard_map/ppermute | solution.py:42
  21.4 1.6 %collective-permute-start.9 = (bf16[512,512]{1,0:T(8,128)(2,1)S(1)}, bf16[512,512]{1,0:T(8,128)(2,1)S(1)}, u32[]{:S(2)}, u32[]{:S(2)}) collective-permute-start(bf16[512,512]{1,0:T(8,128)(2,1)S(1)} %constant_dynamic-update-slice_fusion.2.refs_4_), channel_id=1, source_target_pairs={{24,0},{38,32},{88,64},{102,96},{25,1},{39,33},{89,65},{103,97},{0... | collective-permute-start | bytes 1572872 | tf_op jit(solution)/shard_map/ppermute | solution.py:42
  23.1 2.7 %exps0.1 = (f32[2048,128]{1,0:T(8,128)S(1)}, f32[8,4096]{1,0:T(8,128)S(1)}, bf16[2048,4096]{1,0:T(8,128)(2,1)S(1)}, bf16[4096,512]{1,0:T(8,128)(2,1)S(1)}) custom-call(s32[4]{0:T(128)S(1)} %pad_add_fusion.refs_0_.info_ref, bf16[512,512]{1,0:T(8,128)(2,1)S(1)} %pad_maximum_fusion.refs_1_, bf16[512,512]{1,0:T(8,128)(2,1)S(1)} %collective-permute-done.1.refs_2_, ...), custom_call_target="tpu_custom_call" | custom-call | flops 8589934592 | bytes 8388608 | tf_op jit(solution)/shard_map/exps0/pallas_call | solution.py:222
  25.9 2.5 %exps1.1 = (f32[2048,128]{1,0:T(8,128)S(1)}, f32[8,4096]{1,0:T(8,128)S(1)}, bf16[2048,4096]{1,0:T(8,128)(2,1)S(1)}, bf16[4096,512]{1,0:T(8,128)(2,1)S(1)}) custom-call(s32[4]{0:T(128)S(1)} %pad_add_fusion.refs_0_.info_ref, ...), custom_call_target="tpu_custom_call", output_to_operand_aliasing={{0}: (5, {}), {1}: (6, {}), {2}: (7, {}), {3}: (8, {})} | custom-call | flops 8589934592 | bytes 8388608 | tf_op jit(solution)/shard_map/exps1/pallas_call | solution.py:222
  28.5 1.7 %collective-permute-start.13 = (bf16[512,512]{1,0:T(8,128)(2,1)S(1)}, bf16[512,512]{1,0:T(8,128)(2,1)S(1)}, u32[]{:S(2)}, u32[]{:S(2)}) collective-permute-start(bf16[512,512]{1,0:T(8,128)(2,1)S(1)} %collective-permute-done.10.refs_5_), channel_id=1, source_target_pairs={{24,0},{38,32},{88,64},{102,96},{25,1},{39,33},{89,65},{103,97},{0... | collective-permute-start | bytes 1572872 | tf_op jit(solution)/shard_map/ppermute | solution.py:42
  30.1 2.1 %exps2.1 = (f32[2048,128]{1,0:T(8,128)S(1)}, f32[8,4096]{1,0:T(8,128)S(1)}, bf16[2048,4096]{1,0:T(8,128)(2,1)S(1)}, bf16[4096,512]{1,0:T(8,128)(2,1)S(1)}) custom-call(s32[4]{0:T(128)S(1)} %pad_add_fusion.refs_0_.info_ref, bf16[512,512]{1,0:T(8,128)(2,1)S(1)} %pad_maximum_fusion.refs_1_, ...), custom_call_target="tpu_custom_call", output_to_operand_aliasing={{0}: (6, {}), {1}: (7, {}), {2}: (8, {}), {3}: (9, {})} | custom-call | flops 4294967296 | bytes 2097152 | tf_op jit(solution)/shard_map/exps2/pallas_call | solution.py:222
  32.3 2.8 %collective-permute-start.11 = (bf16[512,512]{1,0:T(8,128)(2,1)S(1)}, bf16[512,512]{1,0:T(8,128)(2,1)S(1)}, u32[]{:S(2)}, u32[]{:S(2)}) collective-permute-start(bf16[512,512]{1,0:T(8,128)(2,1)S(1)} %collective-permute-done.8.refs_7_), channel_id=1, source_target_pairs={{8,0},{34,32},{72,64},{98,96},{9,1},{35,33},{73,65},{99,97},{16,8}... | collective-permute-start | bytes 1572872 | tf_op jit(solution)/shard_map/ppermute | solution.py:42
  35.4 5.3 %exps3.1 = (f32[2048,128]{1,0:T(8,128)S(1)}, f32[8,4096]{1,0:T(8,128)S(1)}, bf16[2048,4096]{1,0:T(8,128)(2,1)S(1)}, bf16[4096,512]{1,0:T(8,128)(2,1)S(1)}) custom-call(s32[4]{0:T(128)S(1)} %pad_add_fusion.refs_0_.info_ref, bf16[512,512]{1,0:T(8,128)(2,1)S(1)} %pad_maximum_fusion.refs_1_, ...), custom_call_target="tpu_custom_call", output_to_operand_aliasing={{0}: (8, {}), {1}: (9, {}), {2}: (10, {}), {3}: (11, {})} | custom-call | tf_op jit(solution)/shard_map/exps3/pallas_call | solution.py:222
  40.8 2.1 %exps4.1 = (f32[2048,128]{1,0:T(8,128)S(1)}, f32[8,4096]{1,0:T(8,128)S(1)}, bf16[2048,4096]{1,0:T(8,128)(2,1)S(1)}, bf16[4096,512]{1,0:T(8,128)(2,1)S(1)}) custom-call(s32[4]{0:T(128)S(1)} %pad_add_fusion.refs_0_.info_ref, bf16[512,512]{1,0:T(8,128)(2,1)S(1)} %pad_maximum_fusion.refs_1_, ...), custom_call_target="tpu_custom_call", output_to_operand_aliasing={{0}: (6, {}), {1}: (7, {}), {2}: (8, {}), {3}: (9, {})} | custom-call | tf_op jit(solution)/shard_map/exps4/pallas_call | solution.py:222
  43.0 2.5 %exps5.1 = (f32[2048,128]{1,0:T(8,128)S(1)}, f32[8,4096]{1,0:T(8,128)S(1)}, bf16[2048,4096]{1,0:T(8,128)(2,1)S(1)}, bf16[4096,512]{1,0:T(8,128)(2,1)S(1)}, f32[8,256]{1,0:T(8,128)S(1)}, /*index=5*/f32[24,256]{1,0:T(8,128)S(1)}) custom-call(s32[4]{0:T(128)S(1)} %pad_add_fusion.refs_0_.info_ref, ...), custom_call_target="tpu_custom_call", output_to_operand_aliasing={{0}: (6, {}), {1}: (7, {}), {2}: (8, {}), {3}: (9, {})} | custom-call | tf_op jit(solution)/shard_map/exps5/pallas_call | solution.py:222
  47.2 2.2 %collective-permute-done.17 = f32[24,256]{1,0:T(8,128)S(1)} collective-permute-done((f32[24,256]{1,0:T(8,128)S(1)}, f32[24,256]{1,0:T(8,128)S(1)}, u32[]{:S(2)}, u32[]{:S(2)}) %collective-permute-start.17) | collective-permute-done | bytes 24608 | tf_op jit(solution)/shard_map/ppermute | solution.py:55
  49.4 3.7 %collective-permute-start.18 = (f32[24,256]{1,0:T(8,128)S(1)}, f32[24,256]{1,0:T(8,128)S(1)}, u32[]{:S(2)}, u32[]{:S(2)}) collective-permute-start(f32[24,256]{1,0:T(8,128)S(1)} %add.21), channel_id=1, source_target_pairs={{6,0},{56,32},{70,64},{120,96},{7,1},{57,33},{71,65},{121,97},{14,... | collective-permute-start | bytes 73736 | tf_op jit(solution)/shard_map/ppermute | solution.py:55
  53.0 1.8 %collective-permute-done.18 = f32[24,256]{1,0:T(8,128)S(1)} collective-permute-done((f32[24,256]{1,0:T(8,128)S(1)}, f32[24,256]{1,0:T(8,128)S(1)}, u32[]{:S(2)}, u32[]{:S(2)}) %collective-permute-start.18) | collective-permute-done | bytes 24608 | tf_op jit(solution)/shard_map/ppermute | solution.py:55
  54.9 1.9 %collective-permute-start.15 = (f32[8,256]{1,0:T(8,128)S(1)}, f32[8,256]{1,0:T(8,128)S(1)}, u32[]{:S(2)}, u32[]{:S(2)}) collective-permute-start(f32[8,256]{1,0:T(8,128)S(1)} %add.19), channel_id=1, source_target_pairs={{64,0},{96,32},{0,64},{32,96},{65,1},{97,33},{1,65},{33,97},{72,8}... | collective-permute-start | bytes 24584 | tf_op jit(solution)/shard_map/ppermute | solution.py:55
  56.7 2.0 %collective-permute-done.15 = f32[8,256]{1,0:T(8,128)S(1)} collective-permute-done((f32[8,256]{1,0:T(8,128)S(1)}, f32[8,256]{1,0:T(8,128)S(1)}, u32[]{:S(2)}, u32[]{:S(2)}) %collective-permute-start.15) | collective-permute-done | bytes 8224 | tf_op jit(solution)/shard_map/ppermute | solution.py:55
  58.8 2.6 %collective-permute-start.20 = (f32[24,256]{1,0:T(8,128)S(1)}, f32[24,256]{1,0:T(8,128)S(1)}, u32[]{:S(2)}, u32[]{:S(2)}) collective-permute-start(f32[24,256]{1,0:T(8,128)S(1)} %add.23.refs_2_), channel_id=1, source_target_pairs={{24,0},{38,32},{88,64},{102,96},{25,1},{39,33},{89,65},{103,97},{1... | collective-permute-start | bytes 73736 | tf_op jit(solution)/shard_map/ppermute | solution.py:55
  61.4 1.3 %collective-permute-start.16 = (f32[8,256]{1,0:T(8,128)S(1)}, f32[8,256]{1,0:T(8,128)S(1)}, u32[]{:S(2)}, u32[]{:S(2)}) collective-permute-start(f32[8,256]{1,0:T(8,128)S(1)} %add.20.refs_0_), channel_id=1, source_target_pairs={{65,0},{97,32},{1,64},{33,96},{64,1},{96,33},{0,65},{32,97},{73,8}... | collective-permute-start | bytes 24584 | tf_op jit(solution)/shard_map/ppermute | solution.py:55
  62.7 3.5 %collective-permute-done.16.refs_1_ = f32[8,256]{1,0:T(8,128)S(1)} collective-permute-done((f32[8,256]{1,0:T(8,128)S(1)}, f32[8,256]{1,0:T(8,128)S(1)}, u32[]{:S(2)}, u32[]{:S(2)}) %collective-permute-start.16) | collective-permute-done | bytes 8224 | tf_op jit(solution)/shard_map/ppermute | solution.py:55
  67.1 3.4 %grads_core.1 = bf16[784,512]{1,0:T(8,128)(2,1)S(1)} custom-call(f32[32,128]{1,0:T(8,128)S(1)} %get-tuple-element.86.acol_ref, bf16[2048,128]{1,0:T(8,128)(2,1)S(1)} %get-tuple-element.79.arow_ref, bf16[2048,4096]{1,0:T(8,128)(2,1)S(1)} %get-tuple-element.80.exps_ref, bf16[4096,512]{1,0:T(8,128)(2,1)S(1)} %get-tuple-element.81.unit_ref, ...), custom_call_target="tpu_custom_call" | custom-call | flops 3221225472 | bytes 10485760 | tf_op jit(solution)/shard_map/grads_core/pallas_call | solution.py:312
  73.4 2.3 %grads_near.1 = (bf16[272,512]{1,0:T(8,128)(2,1)S(1)}, f32[256,512]{1,0:T(8,128)S(1)}) custom-call(f32[32,128]{1,0:T(8,128)S(1)} %get-tuple-element.86.acol_ref, bf16[2048,128]{1,0:T(8,128)(2,1)S(1)} %get-tuple-element.79.arow_ref, bf16[2048,4096]{1,0:T(8,128)(2,1)S(1)} %get-tuple-element.80.exps_ref, bf16[4096,512]{1,0:T(8,128)(2,1)S(1)} %get-tuple-element.81.unit_ref, ...), custom_call_target="tpu_custom_call" | custom-call | flops 2147483648 | bytes 8388608 | tf_op jit(solution)/shard_map/grads_near/pallas_call | solution.py:312
  77.8 2.2 %collective-permute-start.24 = (bf16[272,512]{1,0:T(8,128)(2,1)S(1)}, bf16[272,512]{1,0:T(8,128)(2,1)S(1)}, u32[]{:S(2)}, u32[]{:S(2)}) collective-permute-start(bf16[272,512]{1,0:T(8,128)(2,1)S(1)} %get-tuple-element.87), channel_id=1, source_target_pairs={{64,0},{97,32},{1,64},{32,96},{65,1},{96,33},{0,65},{33,97},{72,8}... | collective-permute-start | bytes 835592 | tf_op jit(solution)/shard_map/ppermute | solution.py:42
  82.2 5.1 %collective-permute-done.24.one_ref = bf16[272,512]{1,0:T(8,128)(2,1)S(1)} collective-permute-done((bf16[272,512]{1,0:T(8,128)(2,1)S(1)}, bf16[272,512]{1,0:T(8,128)(2,1)S(1)}, u32[]{:S(2)}, u32[]{:S(2)}) %collective-permute-start.24) | collective-permute-done | bytes 278560 | tf_op jit(solution)/shard_map/ppermute | solution.py:42
  87.2 1.4 %collective-permute-done.25.two_ref = bf16[272,512]{1,0:T(8,128)(2,1)S(1)} collective-permute-done((bf16[272,512]{1,0:T(8,128)(2,1)S(1)}, bf16[272,512]{1,0:T(8,128)(2,1)S(1)}, u32[]{:S(2)}, u32[]{:S(2)}) %collective-permute-start.25) | collective-permute-done | bytes 278560 | tf_op jit(solution)/shard_map/ppermute | solution.py:42
  (56 shorter events, 13.2 us)
Async XLA Ops:
  0.6 1.0 %copy-start = (bf16[256,512]{1,0:T(8,128)(2,1)S(1)}, bf16[256,512]{1,0:T(8,128)(2,1)}, u32[]{:S(2)}) copy-start(bf16[256,512]{1,0:T(8,128)(2,1)} %z_ref.3) | copy-start | bytes 786436
  1.7 9.4 %collective-permute-start = (bf16[256,512]{1,0:T(8,128)(2,1)S(1)}, bf16[256,512]{1,0:T(8,128)(2,1)S(1)}, u32[]{:S(2)}, u32[]{:S(2)}) collective-permute-start(bf16[256,512]{1,0:T(8,128)(2,1)S(1)} %unit.1.unit_ref), channel_id=1, source_target_pairs={{65,0},{96,32},{0,64},{33,96},{64,1},{97,33},{1,65},{32,97},{73,8}... | collective-permute-start | bytes 786440 | tf_op jit(solution)/shard_map/ppermute | solution.py:42
  3.8 7.6 %collective-permute-start.5 = (bf16[256,512]{1,0:T(8,128)(2,1)S(1)}, bf16[256,512]{1,0:T(8,128)(2,1)S(1)}, u32[]{:S(2)}, u32[]{:S(2)}) collective-permute-start(bf16[256,512]{1,0:T(8,128)(2,1)S(1)} %unit.1.unit_ref), channel_id=1, source_target_pairs={{6,0},{56,32},{70,64},{120,96},{7,1},{57,33},{71,65},{121,97},{14,... | collective-permute-start | bytes 786440 | tf_op jit(solution)/shard_map/ppermute | solution.py:42
  5.3 8.5 %collective-permute-start.6 = (bf16[256,512]{1,0:T(8,128)(2,1)S(1)}, bf16[256,512]{1,0:T(8,128)(2,1)S(1)}, u32[]{:S(2)}, u32[]{:S(2)}) collective-permute-start(bf16[256,512]{1,0:T(8,128)(2,1)S(1)} %unit.1.unit_ref), channel_id=1, source_target_pairs={{2,0},{40,32},{66,64},{104,96},{3,1},{41,33},{67,65},{105,97},{10,... | collective-permute-start | bytes 786440 | tf_op jit(solution)/shard_map/ppermute | solution.py:42
  7.0 10.4 %collective-permute-start.7 = (bf16[256,512]{1,0:T(8,128)(2,1)S(1)}, bf16[256,512]{1,0:T(8,128)(2,1)S(1)}, u32[]{:S(2)}, u32[]{:S(2)}) collective-permute-start(bf16[256,512]{1,0:T(8,128)(2,1)S(1)} %unit.1.unit_ref), channel_id=1, source_target_pairs={{4,0},{48,32},{68,64},{112,96},{5,1},{49,33},{69,65},{113,97},{12,... | collective-permute-start | bytes 786440 | tf_op jit(solution)/shard_map/ppermute | solution.py:42
  8.8 10.3 %collective-permute-start.2 = (bf16[256,512]{1,0:T(8,128)(2,1)S(1)}, bf16[256,512]{1,0:T(8,128)(2,1)S(1)}, u32[]{:S(2)}, u32[]{:S(2)}) collective-permute-start(bf16[256,512]{1,0:T(8,128)(2,1)S(1)} %unit.1.unit_ref), channel_id=1, source_target_pairs={{64,0},{97,32},{1,64},{32,96},{65,1},{96,33},{0,65},{33,97},{72,8}... | collective-permute-start | bytes 786440 | tf_op jit(solution)/shard_map/ppermute | solution.py:42
  11.2 11.9 %collective-permute-start.1 = (bf16[512,512]{1,0:T(8,128)(2,1)S(1)}, bf16[512,512]{1,0:T(8,128)(2,1)S(1)}, u32[]{:S(2)}, u32[]{:S(2)}) collective-permute-start(bf16[512,512]{1,0:T(8,128)(2,1)S(1)} %pad_maximum_fusion.refs_1_), channel_id=1, source_target_pairs={{32,0},{0,32},{96,64},{64,96},{33,1},{1,33},{97,65},{65,97},{40,8}... | collective-permute-start | bytes 1572872 | tf_op jit(solution)/shard_map/ppermute | solution.py:42
  13.8 7.7 %collective-permute-start.3 = (bf16[256,512]{1,0:T(8,128)(2,1)S(1)}, bf16[256,512]{1,0:T(8,128)(2,1)S(1)}, u32[]{:S(2)}, u32[]{:S(2)}) collective-permute-start(bf16[256,512]{1,0:T(8,128)(2,1)S(1)} %collective-permute-done), channel_id=1, source_target_pairs={{65,0},{96,32},{0,64},{33,96},{64,1},{97,33},{1,65},{32,97},{73,8}... | collective-permute-start | bytes 786440 | tf_op jit(solution)/shard_map/ppermute | solution.py:42
  15.8 12.7 %collective-permute-start.10 = (bf16[512,512]{1,0:T(8,128)(2,1)S(1)}, bf16[512,512]{1,0:T(8,128)(2,1)S(1)}, u32[]{:S(2)}, u32[]{:S(2)}) collective-permute-start(bf16[512,512]{1,0:T(8,128)(2,1)S(1)} %constant_dynamic-update-slice_fusion.4.refs_3_), channel_id=1, source_target_pairs={{24,0},{38,32},{88,64},{102,96},{25,1},{39,33},{89,65},{103,97},{0... | collective-permute-start | bytes 1572872 | tf_op jit(solution)/shard_map/ppermute | solution.py:42
  17.4 11.0 %collective-permute-start.12 = (bf16[512,512]{1,0:T(8,128)(2,1)S(1)}, bf16[512,512]{1,0:T(8,128)(2,1)S(1)}, u32[]{:S(2)}, u32[]{:S(2)}) collective-permute-start(bf16[512,512]{1,0:T(8,128)(2,1)S(1)} %constant_dynamic-update-slice_fusion.4.refs_3_), channel_id=1, source_target_pairs={{8,0},{34,32},{72,64},{98,96},{9,1},{35,33},{73,65},{99,97},{16,8}... | collective-permute-start | bytes 1572872 | tf_op jit(solution)/shard_map/ppermute | solution.py:42
  19.1 13.1 %collective-permute-start.8 = (bf16[512,512]{1,0:T(8,128)(2,1)S(1)}, bf16[512,512]{1,0:T(8,128)(2,1)S(1)}, u32[]{:S(2)}, u32[]{:S(2)}) collective-permute-start(bf16[512,512]{1,0:T(8,128)(2,1)S(1)} %constant_dynamic-update-slice_fusion.2.refs_4_), channel_id=1, source_target_pairs={{8,0},{34,32},{72,64},{98,96},{9,1},{35,33},{73,65},{99,97},{16,8}... | collective-permute-start | bytes 1572872 | tf_op jit(solution)/shard_map/ppermute | solution.py:42
  21.4 10.8 %collective-permute-start.9 = (bf16[512,512]{1,0:T(8,128)(2,1)S(1)}, bf16[512,512]{1,0:T(8,128)(2,1)S(1)}, u32[]{:S(2)}, u32[]{:S(2)}) collective-permute-start(bf16[512,512]{1,0:T(8,128)(2,1)S(1)} %constant_dynamic-update-slice_fusion.2.refs_4_), channel_id=1, source_target_pairs={{24,0},{38,32},{88,64},{102,96},{25,1},{39,33},{89,65},{103,97},{0... | collective-permute-start | bytes 1572872 | tf_op jit(solution)/shard_map/ppermute | solution.py:42
  23.0 2.8 %collective-permute-start.4 = (bf16[512,512]{1,0:T(8,128)(2,1)S(1)}, bf16[512,512]{1,0:T(8,128)(2,1)S(1)}, u32[]{:S(2)}, u32[]{:S(2)}) collective-permute-start(bf16[512,512]{1,0:T(8,128)(2,1)S(1)} %constant_dynamic-update-slice_fusion.refs_1_.refs_3_), channel_id=1, source_target_pairs={{32,0},{0,32},{96,64},{64,96},{33,1},{1,33},{97,65},{65,97},{40,8}... | collective-permute-start | bytes 1572872 | tf_op jit(solution)/shard_map/ppermute | solution.py:42
  28.4 6.7 %copy-start.2 = (s32[256]{0:T(256)S(1)}, s32[256]{0:T(256)}, u32[]{:S(2)}) copy-start(s32[256]{0:T(256)} %param.3) | copy-start | bytes 3076
  28.5 12.3 %collective-permute-start.13 = (bf16[512,512]{1,0:T(8,128)(2,1)S(1)}, bf16[512,512]{1,0:T(8,128)(2,1)S(1)}, u32[]{:S(2)}, u32[]{:S(2)}) collective-permute-start(bf16[512,512]{1,0:T(8,128)(2,1)S(1)} %collective-permute-done.10.refs_5_), channel_id=1, source_target_pairs={{24,0},{38,32},{88,64},{102,96},{25,1},{39,33},{89,65},{103,97},{0... | collective-permute-start | bytes 1572872 | tf_op jit(solution)/shard_map/ppermute | solution.py:42
  32.3 10.7 %collective-permute-start.11 = (bf16[512,512]{1,0:T(8,128)(2,1)S(1)}, bf16[512,512]{1,0:T(8,128)(2,1)S(1)}, u32[]{:S(2)}, u32[]{:S(2)}) collective-permute-start(bf16[512,512]{1,0:T(8,128)(2,1)S(1)} %collective-permute-done.8.refs_7_), channel_id=1, source_target_pairs={{8,0},{34,32},{72,64},{98,96},{9,1},{35,33},{73,65},{99,97},{16,8}... | collective-permute-start | bytes 1572872 | tf_op jit(solution)/shard_map/ppermute | solution.py:42
  45.5 3.9 %collective-permute-start.17 = (f32[24,256]{1,0:T(8,128)S(1)}, f32[24,256]{1,0:T(8,128)S(1)}, u32[]{:S(2)}, u32[]{:S(2)}) collective-permute-start(f32[24,256]{1,0:T(8,128)S(1)} %get-tuple-element.74), channel_id=1, source_target_pairs={{2,0},{40,32},{66,64},{104,96},{3,1},{41,33},{67,65},{105,97},{10,... | collective-permute-start | bytes 73736 | tf_op jit(solution)/shard_map/ppermute | solution.py:55
  46.0 1.2 %collective-permute-start.14 = (f32[8,256]{1,0:T(8,128)S(1)}, f32[8,256]{1,0:T(8,128)S(1)}, u32[]{:S(2)}, u32[]{:S(2)}) collective-permute-start(f32[8,256]{1,0:T(8,128)S(1)} %get-tuple-element.73), channel_id=1, source_target_pairs={{32,0},{0,32},{96,64},{64,96},{33,1},{1,33},{97,65},{65,97},{40,8}... | collective-permute-start | bytes 24584 | tf_op jit(solution)/shard_map/ppermute | solution.py:42
  49.4 5.5 %collective-permute-start.18 = (f32[24,256]{1,0:T(8,128)S(1)}, f32[24,256]{1,0:T(8,128)S(1)}, u32[]{:S(2)}, u32[]{:S(2)}) collective-permute-start(f32[24,256]{1,0:T(8,128)S(1)} %add.21), channel_id=1, source_target_pairs={{6,0},{56,32},{70,64},{120,96},{7,1},{57,33},{71,65},{121,97},{14,... | collective-permute-start | bytes 73736 | tf_op jit(solution)/shard_map/ppermute | solution.py:55
  54.8 3.9 %collective-permute-start.19 = (f32[24,256]{1,0:T(8,128)S(1)}, f32[24,256]{1,0:T(8,128)S(1)}, u32[]{:S(2)}, u32[]{:S(2)}) collective-permute-start(f32[24,256]{1,0:T(8,128)S(1)} %add.22), channel_id=1, source_target_pairs={{8,0},{34,32},{72,64},{98,96},{9,1},{35,33},{73,65},{99,97},{0,8},... | collective-permute-start | bytes 73736 | tf_op jit(solution)/shard_map/ppermute | solution.py:55
  54.9 3.9 %collective-permute-start.15 = (f32[8,256]{1,0:T(8,128)S(1)}, f32[8,256]{1,0:T(8,128)S(1)}, u32[]{:S(2)}, u32[]{:S(2)}) collective-permute-start(f32[8,256]{1,0:T(8,128)S(1)} %add.19), channel_id=1, source_target_pairs={{64,0},{96,32},{0,64},{32,96},{65,1},{97,33},{1,65},{33,97},{72,8}... | collective-permute-start | bytes 24584 | tf_op jit(solution)/shard_map/ppermute | solution.py:55
  58.8 7.5 %collective-permute-start.20 = (f32[24,256]{1,0:T(8,128)S(1)}, f32[24,256]{1,0:T(8,128)S(1)}, u32[]{:S(2)}, u32[]{:S(2)}) collective-permute-start(f32[24,256]{1,0:T(8,128)S(1)} %add.23.refs_2_), channel_id=1, source_target_pairs={{24,0},{38,32},{88,64},{102,96},{25,1},{39,33},{89,65},{103,97},{1... | collective-permute-start | bytes 73736 | tf_op jit(solution)/shard_map/ppermute | solution.py:55
  61.4 4.9 %collective-permute-start.16 = (f32[8,256]{1,0:T(8,128)S(1)}, f32[8,256]{1,0:T(8,128)S(1)}, u32[]{:S(2)}, u32[]{:S(2)}) collective-permute-start(f32[8,256]{1,0:T(8,128)S(1)} %add.20.refs_0_), channel_id=1, source_target_pairs={{65,0},{97,32},{1,64},{33,96},{64,1},{96,33},{0,65},{32,97},{73,8}... | collective-permute-start | bytes 24584 | tf_op jit(solution)/shard_map/ppermute | solution.py:55
  70.5 2.4 %collective-permute-start.21 = (bf16[784,512]{1,0:T(8,128)(2,1)S(1)}, bf16[784,512]{1,0:T(8,128)(2,1)S(1)}, u32[]{:S(2)}, u32[]{:S(2)}) collective-permute-start(bf16[784,512]{1,0:T(8,128)(2,1)S(1)} %grads_core.1), channel_id=1, source_target_pairs={{32,0},{0,32},{96,64},{64,96},{33,1},{1,33},{97,65},{65,97},{40,8}... | collective-permute-start | bytes 2408456 | tf_op jit(solution)/shard_map/ppermute | solution.py:42
  72.9 7.8 %collective-permute-start.22 = (bf16[272,512]{1,0:T(8,128)(2,1)S(1)}, bf16[272,512]{1,0:T(8,128)(2,1)S(1)}, u32[]{:S(2)}, u32[]{:S(2)}) collective-permute-start(bf16[272,512]{1,0:T(8,128)(2,1)S(1)} %sum_far.1.refs_1_.here_ref), channel_id=1, source_target_pairs={{65,0},{96,32},{0,64},{33,96},{64,1},{97,33},{1,65},{32,97},{73,8}... | collective-permute-start | bytes 835592 | tf_op jit(solution)/shard_map/ppermute | solution.py:42
  77.0 11.6 %copy-start.1 = (bf16[256,512]{1,0:T(8,128)(2,1)S(1)}, bf16[256,512]{1,0:T(8,128)(2,1)}, u32[]{:S(2)}) copy-start(bf16[256,512]{1,0:T(8,128)(2,1)} %z_ref.3) | copy-start | bytes 786436
  77.0 3.9 %collective-permute-start.23 = (bf16[256,512]{1,0:T(8,128)(2,1)S(1)}, bf16[256,512]{1,0:T(8,128)(2,1)S(1)}, u32[]{:S(2)}, u32[]{:S(2)}) collective-permute-start(bf16[256,512]{1,0:T(8,128)(2,1)S(1)} %grads_core_own.1), channel_id=1, source_target_pairs={{32,0},{0,32},{96,64},{64,96},{33,1},{1,33},{97,65},{65,97},{40,8}... | collective-permute-start | bytes 786440 | tf_op jit(solution)/shard_map/ppermute | solution.py:42
  77.8 9.4 %collective-permute-start.24 = (bf16[272,512]{1,0:T(8,128)(2,1)S(1)}, bf16[272,512]{1,0:T(8,128)(2,1)S(1)}, u32[]{:S(2)}, u32[]{:S(2)}) collective-permute-start(bf16[272,512]{1,0:T(8,128)(2,1)S(1)} %get-tuple-element.87), channel_id=1, source_target_pairs={{64,0},{97,32},{1,64},{32,96},{65,1},{96,33},{0,65},{33,97},{72,8}... | collective-permute-start | bytes 835592 | tf_op jit(solution)/shard_map/ppermute | solution.py:42
  80.8 7.8 %collective-permute-start.25 = (bf16[272,512]{1,0:T(8,128)(2,1)S(1)}, bf16[272,512]{1,0:T(8,128)(2,1)S(1)}, u32[]{:S(2)}, u32[]{:S(2)}) collective-permute-start(bf16[272,512]{1,0:T(8,128)(2,1)S(1)} %sum_two.1), channel_id=1, source_target_pairs={{65,0},{96,32},{0,64},{33,96},{64,1},{97,33},{1,65},{32,97},{73,8}... | collective-permute-start | bytes 835592 | tf_op jit(solution)/shard_map/ppermute | solution.py:42

commit v8 on v7

--- a/solution.py
+++ b/solution.py
@@ -113,18 +113,20 @@
     return rows[0:1] + (rows[1:2] + rows[2:3])
 
 
-def unit_kernel(z_ref, unit_ref):
+def unit_kernel(z_ref, unit_ref, scaled_ref):
     zf = z_ref[...].astype(F32)
     recip = lax.rsqrt(jnp.sum(zf * zf, axis=1, keepdims=True) + 1e-06)
-    unit_ref[...] = (zf * recip).astype(BF16)
+    unit = zf * recip
+    unit_ref[...] = unit.astype(BF16)
+    scaled_ref[...] = (unit * EXP_SCALE).astype(BF16)
 
 
 def make_unit(embeds):
     return pl.pallas_call(
         unit_kernel,
-        out_shape=jax.ShapeDtypeStruct((ROWS, E), BF16),
+        out_shape=(jax.ShapeDtypeStruct((ROWS, E), BF16), jax.ShapeDtypeStruct((ROWS, E), BF16)),
         in_specs=[vmem()],
-        out_specs=vmem(),
+        out_specs=(vmem(), vmem()),
         compiler_params=params(4),
         name="unit",
     )(embeds)
@@ -181,8 +183,7 @@
             for k, ref in enumerate(row_refs):
                 start = rows_here[k // 2] * 1024 + (k % 2) * 512
                 part = slice(start, start + 512)
-                s = lax.dot_general(ref[...], cols, NT, preferred_element_type=F32)
-                e = jnp.exp2(s * EXP_SCALE)
+                e = jnp.exp2(lax.dot_general(ref[...], cols, NT, preferred_element_type=F32))
                 if first and n == 0 and k == 0:
                     i = lax.broadcasted_iota(jnp.int32, (ROWS, ROWS), 0)
                     j = lax.broadcasted_iota(jnp.int32, (ROWS, ROWS), 1)
@@ -369,21 +370,21 @@
 
 
 def per_device(embeds, partner):
-    unit = make_unit(embeds)
+    unit, scaled = make_unit(embeds)
     core_id = lax.axis_index("core")
     z = lax.axis_index("zhi") * 2 + lax.axis_index("zlo")
     info = jnp.stack([lax.axis_index("x"), lax.axis_index("y"), z, core_id]).astype(jnp.int32)
 
-    z_one = get(unit, z_own=-1)
+    z_one = get(scaled, z_own=-1)
     before, next_ = get(unit, first=-1), get(unit, first=1)
     before, next_ = lax.optimization_barrier((before, next_))
     far = get(unit, first=2)
-    near = jnp.concatenate([unit, z_one], axis=0)
+    near = jnp.concatenate([scaled, z_one], axis=0)
     line0 = jnp.concatenate([after(unit, near), before], axis=0)
     line1 = jnp.concatenate([next_, far], axis=0)
     before0, after0 = get(line0, second=-1), get(line0, second=1)
     before1, after1 = get(line1, second=-1), get(line1, second=1)
-    z_two = get(unit, z_own=1)
+    z_two = get(scaled, z_own=1)
     z_far = get(z_one, z_own=-1)
     near = [near, get(near, core=1)]
 
@@ -405,9 +406,9 @@
     by_col = col_sums + swap(col_sums, "first", 0)
     by_col = by_col + swap(after(by_col, by_row), "first", 1)
     by_row = by_row + swap(by_row, "z", 0)
-    by_col = by_col + swap(by_col, "second", 0)
-    by_col = after(by_col, by_row)
+    by_col = by_col + swap(after(by_col, by_row), "second", 0)
     by_row = [by_row, swap(by_row, "z", 1)]
+    by_col = after(by_col, by_row[1])
     by_col = [by_col, swap(by_col, "second", 1)]
     arow, acol, loss = make_totals(info, by_row, by_col)
 

time: 90.3 us -> 90.4 us (level)
  transfers between devices with their start and end apart: 26 -> 26, of which waited for: 12 -> 14; matrix products, arithmetic and copies ran while one was open for 0% -> 0% of each run, Pallas kernels for 24% -> 23%
where the time goes in v8:
time: 90.4 us; the launch traced here: 90.2 us
  starting transfers between devices  36.7 us (41%)
  Pallas kernels  29 us (32%)
  waiting for transfers between devices  22.4 us (25%)
  local copies, waits for them, and re-layouts  1.1 us (1%)
    ppermute x20, starting transfers between devices, get(): return lax.ppermute(value, AXES, pairs)  26.5 us
    pallas_call x6, Pallas kernels, make_exps(): pl.pallas_call(functools.partial(exps_kernel, places, rows_here, first, l...  17 us
    ppermute x20, waiting for transfers between devices, get(): return lax.ppermute(value, AXES, pairs)  12.4 us
    ppermute x6, starting transfers between devices, swap(): return lax.ppermute(value, AXES, pairs)  10.3 us
    ppermute x6, waiting for transfers between devices, swap(): return lax.ppermute(value, AXES, pairs)  10 us
    pallas_call x5, Pallas kernels, make_grads(): pl.pallas_call(functools.partial(grads_kernel, pieces, adds, carry is not...  9.47 us
  transfers between devices with their start and end apart: 26, of which 14 were waited for; matrix products, arithmetic and copies ran while one was open for 0% of the time, Pallas kernels for 23%

profile of v8, /device:TPU:0, one launch (start us, length us, event | category | flops | bytes accessed | tf_op | source)
XLA Modules:
  0.0 90.2 jit_solution(5182734704455448735)
XLA Ops:
  1.7 2.1 %collective-permute-start = (bf16[256,512]{1,0:T(8,128)(2,1)S(1)}, bf16[256,512]{1,0:T(8,128)(2,1)S(1)}, u32[]{:S(2)}, u32[]{:S(2)}) collective-permute-start(bf16[256,512]{1,0:T(8,128)(2,1)S(1)} %get-tuple-element.51), channel_id=1, source_target_pairs={{65,0},{96,32},{0,64},{33,96},{64,1},{97,33},{1,65},{32,97},{73,8}... | collective-permute-start | bytes 786440 | tf_op jit(solution)/shard_map/ppermute | solution.py:42
  3.8 1.5 %collective-permute-start.5 = (bf16[256,512]{1,0:T(8,128)(2,1)S(1)}, bf16[256,512]{1,0:T(8,128)(2,1)S(1)}, u32[]{:S(2)}, u32[]{:S(2)}) collective-permute-start(bf16[256,512]{1,0:T(8,128)(2,1)S(1)} %get-tuple-element.53.unit_ref), channel_id=1, source_target_pairs={{6,0},{56,32},{70,64},{120,96},{7,1},{57,33},{71,65},{121,97},{14,... | collective-permute-start | bytes 786440 | tf_op jit(solution)/shard_map/ppermute | solution.py:42
  5.3 1.7 %collective-permute-start.6 = (bf16[256,512]{1,0:T(8,128)(2,1)S(1)}, bf16[256,512]{1,0:T(8,128)(2,1)S(1)}, u32[]{:S(2)}, u32[]{:S(2)}) collective-permute-start(bf16[256,512]{1,0:T(8,128)(2,1)S(1)} %get-tuple-element.53.unit_ref), channel_id=1, source_target_pairs={{2,0},{40,32},{66,64},{104,96},{3,1},{41,33},{67,65},{105,97},{10,... | collective-permute-start | bytes 786440 | tf_op jit(solution)/shard_map/ppermute | solution.py:42
  7.0 1.8 %collective-permute-start.7 = (bf16[256,512]{1,0:T(8,128)(2,1)S(1)}, bf16[256,512]{1,0:T(8,128)(2,1)S(1)}, u32[]{:S(2)}, u32[]{:S(2)}) collective-permute-start(bf16[256,512]{1,0:T(8,128)(2,1)S(1)} %get-tuple-element.53.unit_ref), channel_id=1, source_target_pairs={{4,0},{48,32},{68,64},{112,96},{5,1},{49,33},{69,65},{113,97},{12,... | collective-permute-start | bytes 786440 | tf_op jit(solution)/shard_map/ppermute | solution.py:42
  8.9 2.2 %collective-permute-start.2 = (bf16[256,512]{1,0:T(8,128)(2,1)S(1)}, bf16[256,512]{1,0:T(8,128)(2,1)S(1)}, u32[]{:S(2)}, u32[]{:S(2)}) collective-permute-start(bf16[256,512]{1,0:T(8,128)(2,1)S(1)} %get-tuple-element.51), channel_id=1, source_target_pairs={{64,0},{97,32},{1,64},{32,96},{65,1},{96,33},{0,65},{33,97},{72,8}... | collective-permute-start | bytes 786440 | tf_op jit(solution)/shard_map/ppermute | solution.py:42
  11.4 2.4 %collective-permute-done.6 = bf16[256,512]{1,0:T(8,128)(2,1)S(1)} collective-permute-done((bf16[256,512]{1,0:T(8,128)(2,1)S(1)}, bf16[256,512]{1,0:T(8,128)(2,1)S(1)}, u32[]{:S(2)}, u32[]{:S(2)}) %collective-permute-start.6) | collective-permute-done | bytes 262176 | tf_op jit(solution)/shard_map/ppermute | solution.py:42
  13.8 2.0 %collective-permute-start.3 = (bf16[256,512]{1,0:T(8,128)(2,1)S(1)}, bf16[256,512]{1,0:T(8,128)(2,1)S(1)}, u32[]{:S(2)}, u32[]{:S(2)}) collective-permute-start(bf16[256,512]{1,0:T(8,128)(2,1)S(1)} %collective-permute-done), channel_id=1, source_target_pairs={{65,0},{96,32},{0,64},{33,96},{64,1},{97,33},{1,65},{32,97},{73,8}... | collective-permute-start | bytes 786440 | tf_op jit(solution)/shard_map/ppermute | solution.py:42
  15.8 1.6 %collective-permute-start.10 = (bf16[512,512]{1,0:T(8,128)(2,1)S(1)}, bf16[512,512]{1,0:T(8,128)(2,1)S(1)}, u32[]{:S(2)}, u32[]{:S(2)}) collective-permute-start(bf16[512,512]{1,0:T(8,128)(2,1)S(1)} %constant_dynamic-update-slice_fusion.6.refs_3_), channel_id=1, source_target_pairs={{24,0},{38,32},{88,64},{102,96},{25,1},{39,33},{89,65},{103,97},{0... | collective-permute-start | bytes 1572872 | tf_op jit(solution)/shard_map/ppermute | solution.py:42
  17.4 1.7 %collective-permute-start.12 = (bf16[512,512]{1,0:T(8,128)(2,1)S(1)}, bf16[512,512]{1,0:T(8,128)(2,1)S(1)}, u32[]{:S(2)}, u32[]{:S(2)}) collective-permute-start(bf16[512,512]{1,0:T(8,128)(2,1)S(1)} %constant_dynamic-update-slice_fusion.6.refs_3_), channel_id=1, source_target_pairs={{8,0},{34,32},{72,64},{98,96},{9,1},{35,33},{73,65},{99,97},{16,8}... | collective-permute-start | bytes 1572872 | tf_op jit(solution)/shard_map/ppermute | solution.py:42
  19.1 1.9 %collective-permute-start.8 = (bf16[512,512]{1,0:T(8,128)(2,1)S(1)}, bf16[512,512]{1,0:T(8,128)(2,1)S(1)}, u32[]{:S(2)}, u32[]{:S(2)}) collective-permute-start(bf16[512,512]{1,0:T(8,128)(2,1)S(1)} %constant_dynamic-update-slice_fusion.4.refs_4_), channel_id=1, source_target_pairs={{8,0},{34,32},{72,64},{98,96},{9,1},{35,33},{73,65},{99,97},{16,8}... | collective-permute-start | bytes 1572872 | tf_op jit(solution)/shard_map/ppermute | solution.py:42
  21.4 1.6 %collective-permute-start.9 = (bf16[512,512]{1,0:T(8,128)(2,1)S(1)}, bf16[512,512]{1,0:T(8,128)(2,1)S(1)}, u32[]{:S(2)}, u32[]{:S(2)}) collective-permute-start(bf16[512,512]{1,0:T(8,128)(2,1)S(1)} %constant_dynamic-update-slice_fusion.4.refs_4_), channel_id=1, source_target_pairs={{24,0},{38,32},{88,64},{102,96},{25,1},{39,33},{89,65},{103,97},{0... | collective-permute-start | bytes 1572872 | tf_op jit(solution)/shard_map/ppermute | solution.py:42
  23.1 2.7 %exps0.1 = (f32[2048,128]{1,0:T(8,128)S(1)}, f32[8,4096]{1,0:T(8,128)S(1)}, bf16[2048,4096]{1,0:T(8,128)(2,1)S(1)}, bf16[4096,512]{1,0:T(8,128)(2,1)S(1)}) custom-call(s32[4]{0:T(128)S(1)} %pad_add_fusion.refs_0_.info_ref, bf16[512,512]{1,0:T(8,128)(2,1)S(1)} %constant_dynamic-update-slice_fusion.refs_1_, ...), custom_call_target="tpu_custom_call" | custom-call | flops 8589934592 | bytes 8388608 | tf_op jit(solution)/shard_map/exps0/pallas_call | solution.py:223
  25.8 2.5 %exps1.1 = (f32[2048,128]{1,0:T(8,128)S(1)}, f32[8,4096]{1,0:T(8,128)S(1)}, bf16[2048,4096]{1,0:T(8,128)(2,1)S(1)}, bf16[4096,512]{1,0:T(8,128)(2,1)S(1)}) custom-call(s32[4]{0:T(128)S(1)} %pad_add_fusion.refs_0_.info_ref, ...), custom_call_target="tpu_custom_call", output_to_operand_aliasing={{0}: (5, {}), {1}: (6, {}), {2}: (7, {}), {3}: (8, {})} | custom-call | flops 8589934592 | bytes 8388608 | tf_op jit(solution)/shard_map/exps1/pallas_call | solution.py:223
  28.3 1.6 %collective-permute-start.13 = (bf16[512,512]{1,0:T(8,128)(2,1)S(1)}, bf16[512,512]{1,0:T(8,128)(2,1)S(1)}, u32[]{:S(2)}, u32[]{:S(2)}) collective-permute-start(bf16[512,512]{1,0:T(8,128)(2,1)S(1)} %collective-permute-done.10.refs_5_), channel_id=1, source_target_pairs={{24,0},{38,32},{88,64},{102,96},{25,1},{39,33},{89,65},{103,97},{0... | collective-permute-start | bytes 1572872 | tf_op jit(solution)/shard_map/ppermute | solution.py:42
  29.9 2.1 %exps2.1 = (f32[2048,128]{1,0:T(8,128)S(1)}, f32[8,4096]{1,0:T(8,128)S(1)}, bf16[2048,4096]{1,0:T(8,128)(2,1)S(1)}, bf16[4096,512]{1,0:T(8,128)(2,1)S(1)}) custom-call(s32[4]{0:T(128)S(1)} %pad_add_fusion.refs_0_.info_ref, ...), custom_call_target="tpu_custom_call", output_to_operand_aliasing={{0}: (6, {}), {1}: (7, {}), {2}: (8, {}), {3}: (9, {})} | custom-call | flops 4294967296 | bytes 2097152 | tf_op jit(solution)/shard_map/exps2/pallas_call | solution.py:223
  32.3 2.9 %collective-permute-start.11 = (bf16[512,512]{1,0:T(8,128)(2,1)S(1)}, bf16[512,512]{1,0:T(8,128)(2,1)S(1)}, u32[]{:S(2)}, u32[]{:S(2)}) collective-permute-start(bf16[512,512]{1,0:T(8,128)(2,1)S(1)} %collective-permute-done.8.refs_7_), channel_id=1, source_target_pairs={{8,0},{34,32},{72,64},{98,96},{9,1},{35,33},{73,65},{99,97},{16,8}... | collective-permute-start | bytes 1572872 | tf_op jit(solution)/shard_map/ppermute | solution.py:42
  35.4 5.2 %exps3.1 = (f32[2048,128]{1,0:T(8,128)S(1)}, f32[8,4096]{1,0:T(8,128)S(1)}, bf16[2048,4096]{1,0:T(8,128)(2,1)S(1)}, bf16[4096,512]{1,0:T(8,128)(2,1)S(1)}) custom-call(s32[4]{0:T(128)S(1)} %pad_add_fusion.refs_0_.info_ref, ...), custom_call_target="tpu_custom_call", output_to_operand_aliasing={{0}: (8, {}), {1}: (9, {}), {2}: (10, {}), {3}: (11, {})} | custom-call | tf_op jit(solution)/shard_map/exps3/pallas_call | solution.py:223
  40.7 2.1 %exps4.1 = (f32[2048,128]{1,0:T(8,128)S(1)}, f32[8,4096]{1,0:T(8,128)S(1)}, bf16[2048,4096]{1,0:T(8,128)(2,1)S(1)}, bf16[4096,512]{1,0:T(8,128)(2,1)S(1)}) custom-call(s32[4]{0:T(128)S(1)} %pad_add_fusion.refs_0_.info_ref, ...), custom_call_target="tpu_custom_call", output_to_operand_aliasing={{0}: (6, {}), {1}: (7, {}), {2}: (8, {}), {3}: (9, {})} | custom-call | tf_op jit(solution)/shard_map/exps4/pallas_call | solution.py:223
  42.8 2.5 %exps5.1 = (f32[2048,128]{1,0:T(8,128)S(1)}, f32[8,4096]{1,0:T(8,128)S(1)}, bf16[2048,4096]{1,0:T(8,128)(2,1)S(1)}, bf16[4096,512]{1,0:T(8,128)(2,1)S(1)}, f32[8,256]{1,0:T(8,128)S(1)}, /*index=5*/f32[24,256]{1,0:T(8,128)S(1)}) custom-call(s32[4]{0:T(128)S(1)} %pad_add_fusion.refs_0_.info_ref, ...), custom_call_target="tpu_custom_call", output_to_operand_aliasing={{0}: (6, {}), {1}: (7, {}), {2}: (8, {}), {3}: (9, {})} | custom-call | tf_op jit(solution)/shard_map/exps5/pallas_call | solution.py:223
  47.0 2.1 %collective-permute-done.17 = f32[24,256]{1,0:T(8,128)S(1)} collective-permute-done((f32[24,256]{1,0:T(8,128)S(1)}, f32[24,256]{1,0:T(8,128)S(1)}, u32[]{:S(2)}, u32[]{:S(2)}) %collective-permute-start.17) | collective-permute-done | bytes 24608 | tf_op jit(solution)/shard_map/ppermute | solution.py:55
  49.1 3.7 %collective-permute-start.18 = (f32[24,256]{1,0:T(8,128)S(1)}, f32[24,256]{1,0:T(8,128)S(1)}, u32[]{:S(2)}, u32[]{:S(2)}) collective-permute-start(f32[24,256]{1,0:T(8,128)S(1)} %add.21), channel_id=1, source_target_pairs={{6,0},{56,32},{70,64},{120,96},{7,1},{57,33},{71,65},{121,97},{14,... | collective-permute-start | bytes 73736 | tf_op jit(solution)/shard_map/ppermute | solution.py:55
  52.8 1.6 %collective-permute-start.15 = (f32[8,256]{1,0:T(8,128)S(1)}, f32[8,256]{1,0:T(8,128)S(1)}, u32[]{:S(2)}, u32[]{:S(2)}) collective-permute-start(f32[8,256]{1,0:T(8,128)S(1)} %add.19), channel_id=1, source_target_pairs={{64,0},{96,32},{0,64},{32,96},{65,1},{97,33},{1,65},{33,97},{72,8}... | collective-permute-start | bytes 24584 | tf_op jit(solution)/shard_map/ppermute | solution.py:55
  54.4 2.0 %collective-permute-done.15 = f32[8,256]{1,0:T(8,128)S(1)} collective-permute-done((f32[8,256]{1,0:T(8,128)S(1)}, f32[8,256]{1,0:T(8,128)S(1)}, u32[]{:S(2)}, u32[]{:S(2)}) %collective-permute-start.15) | collective-permute-done | bytes 8224 | tf_op jit(solution)/shard_map/ppermute | solution.py:55
  56.8 1.4 %collective-permute-start.16 = (f32[8,256]{1,0:T(8,128)S(1)}, f32[8,256]{1,0:T(8,128)S(1)}, u32[]{:S(2)}, u32[]{:S(2)}) collective-permute-start(f32[8,256]{1,0:T(8,128)S(1)} %add.20.refs_0_), channel_id=1, source_target_pairs={{65,0},{97,32},{1,64},{33,96},{64,1},{96,33},{0,65},{32,97},{73,8}... | collective-permute-start | bytes 24584 | tf_op jit(solution)/shard_map/ppermute | solution.py:55
  58.1 2.2 %collective-permute-done.19 = f32[24,256]{1,0:T(8,128)S(1)} collective-permute-done((f32[24,256]{1,0:T(8,128)S(1)}, f32[24,256]{1,0:T(8,128)S(1)}, u32[]{:S(2)}, u32[]{:S(2)}) %collective-permute-start.19) | collective-permute-done | bytes 24608 | tf_op jit(solution)/shard_map/ppermute | solution.py:55
  61.7 2.7 %collective-permute-start.20 = (f32[24,256]{1,0:T(8,128)S(1)}, f32[24,256]{1,0:T(8,128)S(1)}, u32[]{:S(2)}, u32[]{:S(2)}) collective-permute-start(f32[24,256]{1,0:T(8,128)S(1)} %add.23.refs_2_), channel_id=1, source_target_pairs={{24,0},{38,32},{88,64},{102,96},{25,1},{39,33},{89,65},{103,97},{1... | collective-permute-start | bytes 73736 | tf_op jit(solution)/shard_map/ppermute | solution.py:55
  64.4 2.3 %collective-permute-done.20.refs_3_ = f32[24,256]{1,0:T(8,128)S(1)} collective-permute-done((f32[24,256]{1,0:T(8,128)S(1)}, f32[24,256]{1,0:T(8,128)S(1)}, u32[]{:S(2)}, u32[]{:S(2)}) %collective-permute-start.20) | collective-permute-done | bytes 24608 | tf_op jit(solution)/shard_map/ppermute | solution.py:55
  67.5 3.4 %grads_core.1 = bf16[784,512]{1,0:T(8,128)(2,1)S(1)} custom-call(f32[32,128]{1,0:T(8,128)S(1)} %get-tuple-element.92.acol_ref, bf16[2048,128]{1,0:T(8,128)(2,1)S(1)} %get-tuple-element.85.arow_ref, bf16[2048,4096]{1,0:T(8,128)(2,1)S(1)} %get-tuple-element.86.exps_ref, bf16[4096,512]{1,0:T(8,128)(2,1)S(1)} %get-tuple-element.87.unit_ref, ...), custom_call_target="tpu_custom_call" | custom-call | flops 3221225472 | bytes 10485760 | tf_op jit(solution)/shard_map/grads_core/pallas_call | solution.py:313
  73.9 2.3 %grads_near.1 = (bf16[272,512]{1,0:T(8,128)(2,1)S(1)}, f32[256,512]{1,0:T(8,128)S(1)}) custom-call(f32[32,128]{1,0:T(8,128)S(1)} %get-tuple-element.92.acol_ref, bf16[2048,128]{1,0:T(8,128)(2,1)S(1)} %get-tuple-element.85.arow_ref, bf16[2048,4096]{1,0:T(8,128)(2,1)S(1)} %get-tuple-element.86.exps_ref, bf16[4096,512]{1,0:T(8,128)(2,1)S(1)} %get-tuple-element.87.unit_ref, ...), custom_call_target="tpu_custom_call" | custom-call | flops 2147483648 | bytes 8388608 | tf_op jit(solution)/shard_map/grads_near/pallas_call | solution.py:313
  78.3 2.1 %collective-permute-start.24 = (bf16[272,512]{1,0:T(8,128)(2,1)S(1)}, bf16[272,512]{1,0:T(8,128)(2,1)S(1)}, u32[]{:S(2)}, u32[]{:S(2)}) collective-permute-start(bf16[272,512]{1,0:T(8,128)(2,1)S(1)} %get-tuple-element.93), channel_id=1, source_target_pairs={{64,0},{97,32},{1,64},{32,96},{65,1},{96,33},{0,65},{33,97},{72,8}... | collective-permute-start | bytes 835592 | tf_op jit(solution)/shard_map/ppermute | solution.py:42
  82.6 5.1 %collective-permute-done.24.one_ref = bf16[272,512]{1,0:T(8,128)(2,1)S(1)} collective-permute-done((bf16[272,512]{1,0:T(8,128)(2,1)S(1)}, bf16[272,512]{1,0:T(8,128)(2,1)S(1)}, u32[]{:S(2)}, u32[]{:S(2)}) %collective-permute-start.24) | collective-permute-done | bytes 278560 | tf_op jit(solution)/shard_map/ppermute | solution.py:42
  87.7 1.4 %collective-permute-done.25.two_ref = bf16[272,512]{1,0:T(8,128)(2,1)S(1)} collective-permute-done((bf16[272,512]{1,0:T(8,128)(2,1)S(1)}, bf16[272,512]{1,0:T(8,128)(2,1)S(1)}, u32[]{:S(2)}, u32[]{:S(2)}) %collective-permute-start.25) | collective-permute-done | bytes 278560 | tf_op jit(solution)/shard_map/ppermute | solution.py:42
  (57 shorter events, 15.0 us)
Async XLA Ops:
  0.6 1.0 %copy-start = (bf16[256,512]{1,0:T(8,128)(2,1)S(1)}, bf16[256,512]{1,0:T(8,128)(2,1)}, u32[]{:S(2)}) copy-start(bf16[256,512]{1,0:T(8,128)(2,1)} %z_ref.3) | copy-start | bytes 786436
  1.7 9.4 %collective-permute-start = (bf16[256,512]{1,0:T(8,128)(2,1)S(1)}, bf16[256,512]{1,0:T(8,128)(2,1)S(1)}, u32[]{:S(2)}, u32[]{:S(2)}) collective-permute-start(bf16[256,512]{1,0:T(8,128)(2,1)S(1)} %get-tuple-element.51), channel_id=1, source_target_pairs={{65,0},{96,32},{0,64},{33,96},{64,1},{97,33},{1,65},{32,97},{73,8}... | collective-permute-start | bytes 786440 | tf_op jit(solution)/shard_map/ppermute | solution.py:42
  3.8 7.6 %collective-permute-start.5 = (bf16[256,512]{1,0:T(8,128)(2,1)S(1)}, bf16[256,512]{1,0:T(8,128)(2,1)S(1)}, u32[]{:S(2)}, u32[]{:S(2)}) collective-permute-start(bf16[256,512]{1,0:T(8,128)(2,1)S(1)} %get-tuple-element.53.unit_ref), channel_id=1, source_target_pairs={{6,0},{56,32},{70,64},{120,96},{7,1},{57,33},{71,65},{121,97},{14,... | collective-permute-start | bytes 786440 | tf_op jit(solution)/shard_map/ppermute | solution.py:42
  5.3 8.5 %collective-permute-start.6 = (bf16[256,512]{1,0:T(8,128)(2,1)S(1)}, bf16[256,512]{1,0:T(8,128)(2,1)S(1)}, u32[]{:S(2)}, u32[]{:S(2)}) collective-permute-start(bf16[256,512]{1,0:T(8,128)(2,1)S(1)} %get-tuple-element.53.unit_ref), channel_id=1, source_target_pairs={{2,0},{40,32},{66,64},{104,96},{3,1},{41,33},{67,65},{105,97},{10,... | collective-permute-start | bytes 786440 | tf_op jit(solution)/shard_map/ppermute | solution.py:42
  7.0 10.4 %collective-permute-start.7 = (bf16[256,512]{1,0:T(8,128)(2,1)S(1)}, bf16[256,512]{1,0:T(8,128)(2,1)S(1)}, u32[]{:S(2)}, u32[]{:S(2)}) collective-permute-start(bf16[256,512]{1,0:T(8,128)(2,1)S(1)} %get-tuple-element.53.unit_ref), channel_id=1, source_target_pairs={{4,0},{48,32},{68,64},{112,96},{5,1},{49,33},{69,65},{113,97},{12,... | collective-permute-start | bytes 786440 | tf_op jit(solution)/shard_map/ppermute | solution.py:42
  8.9 10.3 %collective-permute-start.2 = (bf16[256,512]{1,0:T(8,128)(2,1)S(1)}, bf16[256,512]{1,0:T(8,128)(2,1)S(1)}, u32[]{:S(2)}, u32[]{:S(2)}) collective-permute-start(bf16[256,512]{1,0:T(8,128)(2,1)S(1)} %get-tuple-element.51), channel_id=1, source_target_pairs={{64,0},{97,32},{1,64},{32,96},{65,1},{96,33},{0,65},{33,97},{72,8}... | collective-permute-start | bytes 786440 | tf_op jit(solution)/shard_map/ppermute | solution.py:42
  11.2 11.9 %collective-permute-start.1 = (bf16[512,512]{1,0:T(8,128)(2,1)S(1)}, bf16[512,512]{1,0:T(8,128)(2,1)S(1)}, u32[]{:S(2)}, u32[]{:S(2)}) collective-permute-start(bf16[512,512]{1,0:T(8,128)(2,1)S(1)} %constant_dynamic-update-slice_fusion.refs_1_), channel_id=1, source_target_pairs={{32,0},{0,32},{96,64},{64,96},{33,1},{1,33},{97,65},{65,97},{40,8}... | collective-permute-start | bytes 1572872 | tf_op jit(solution)/shard_map/ppermute | solution.py:42
  13.8 7.7 %collective-permute-start.3 = (bf16[256,512]{1,0:T(8,128)(2,1)S(1)}, bf16[256,512]{1,0:T(8,128)(2,1)S(1)}, u32[]{:S(2)}, u32[]{:S(2)}) collective-permute-start(bf16[256,512]{1,0:T(8,128)(2,1)S(1)} %collective-permute-done), channel_id=1, source_target_pairs={{65,0},{96,32},{0,64},{33,96},{64,1},{97,33},{1,65},{32,97},{73,8}... | collective-permute-start | bytes 786440 | tf_op jit(solution)/shard_map/ppermute | solution.py:42
  15.8 12.5 %collective-permute-start.10 = (bf16[512,512]{1,0:T(8,128)(2,1)S(1)}, bf16[512,512]{1,0:T(8,128)(2,1)S(1)}, u32[]{:S(2)}, u32[]{:S(2)}) collective-permute-start(bf16[512,512]{1,0:T(8,128)(2,1)S(1)} %constant_dynamic-update-slice_fusion.6.refs_3_), channel_id=1, source_target_pairs={{24,0},{38,32},{88,64},{102,96},{25,1},{39,33},{89,65},{103,97},{0... | collective-permute-start | bytes 1572872 | tf_op jit(solution)/shard_map/ppermute | solution.py:42
  17.4 10.9 %collective-permute-start.12 = (bf16[512,512]{1,0:T(8,128)(2,1)S(1)}, bf16[512,512]{1,0:T(8,128)(2,1)S(1)}, u32[]{:S(2)}, u32[]{:S(2)}) collective-permute-start(bf16[512,512]{1,0:T(8,128)(2,1)S(1)} %constant_dynamic-update-slice_fusion.6.refs_3_), channel_id=1, source_target_pairs={{8,0},{34,32},{72,64},{98,96},{9,1},{35,33},{73,65},{99,97},{16,8}... | collective-permute-start | bytes 1572872 | tf_op jit(solution)/shard_map/ppermute | solution.py:42
  19.1 13.1 %collective-permute-start.8 = (bf16[512,512]{1,0:T(8,128)(2,1)S(1)}, bf16[512,512]{1,0:T(8,128)(2,1)S(1)}, u32[]{:S(2)}, u32[]{:S(2)}) collective-permute-start(bf16[512,512]{1,0:T(8,128)(2,1)S(1)} %constant_dynamic-update-slice_fusion.4.refs_4_), channel_id=1, source_target_pairs={{8,0},{34,32},{72,64},{98,96},{9,1},{35,33},{73,65},{99,97},{16,8}... | collective-permute-start | bytes 1572872 | tf_op jit(solution)/shard_map/ppermute | solution.py:42
  21.4 10.8 %collective-permute-start.9 = (bf16[512,512]{1,0:T(8,128)(2,1)S(1)}, bf16[512,512]{1,0:T(8,128)(2,1)S(1)}, u32[]{:S(2)}, u32[]{:S(2)}) collective-permute-start(bf16[512,512]{1,0:T(8,128)(2,1)S(1)} %constant_dynamic-update-slice_fusion.4.refs_4_), channel_id=1, source_target_pairs={{24,0},{38,32},{88,64},{102,96},{25,1},{39,33},{89,65},{103,97},{0... | collective-permute-start | bytes 1572872 | tf_op jit(solution)/shard_map/ppermute | solution.py:42
  23.1 2.8 %collective-permute-start.4 = (bf16[512,512]{1,0:T(8,128)(2,1)S(1)}, bf16[512,512]{1,0:T(8,128)(2,1)S(1)}, u32[]{:S(2)}, u32[]{:S(2)}) collective-permute-start(bf16[512,512]{1,0:T(8,128)(2,1)S(1)} %constant_dynamic-update-slice_fusion.2.refs_1_.refs_3_), channel_id=1, source_target_pairs={{32,0},{0,32},{96,64},{64,96},{33,1},{1,33},{97,65},{65,97},{40,8}... | collective-permute-start | bytes 1572872 | tf_op jit(solution)/shard_map/ppermute | solution.py:42
  28.3 6.8 %copy-start.2 = (s32[256]{0:T(256)S(1)}, s32[256]{0:T(256)}, u32[]{:S(2)}) copy-start(s32[256]{0:T(256)} %param.3) | copy-start | bytes 3076
  28.3 12.3 %collective-permute-start.13 = (bf16[512,512]{1,0:T(8,128)(2,1)S(1)}, bf16[512,512]{1,0:T(8,128)(2,1)S(1)}, u32[]{:S(2)}, u32[]{:S(2)}) collective-permute-start(bf16[512,512]{1,0:T(8,128)(2,1)S(1)} %collective-permute-done.10.refs_5_), channel_id=1, source_target_pairs={{24,0},{38,32},{88,64},{102,96},{25,1},{39,33},{89,65},{103,97},{0... | collective-permute-start | bytes 1572872 | tf_op jit(solution)/shard_map/ppermute | solution.py:42
  32.3 10.5 %collective-permute-start.11 = (bf16[512,512]{1,0:T(8,128)(2,1)S(1)}, bf16[512,512]{1,0:T(8,128)(2,1)S(1)}, u32[]{:S(2)}, u32[]{:S(2)}) collective-permute-start(bf16[512,512]{1,0:T(8,128)(2,1)S(1)} %collective-permute-done.8.refs_7_), channel_id=1, source_target_pairs={{8,0},{34,32},{72,64},{98,96},{9,1},{35,33},{73,65},{99,97},{16,8}... | collective-permute-start | bytes 1572872 | tf_op jit(solution)/shard_map/ppermute | solution.py:42
  45.2 3.9 %collective-permute-start.17 = (f32[24,256]{1,0:T(8,128)S(1)}, f32[24,256]{1,0:T(8,128)S(1)}, u32[]{:S(2)}, u32[]{:S(2)}) collective-permute-start(f32[24,256]{1,0:T(8,128)S(1)} %get-tuple-element.79), channel_id=1, source_target_pairs={{2,0},{40,32},{66,64},{104,96},{3,1},{41,33},{67,65},{105,97},{10,... | collective-permute-start | bytes 73736 | tf_op jit(solution)/shard_map/ppermute | solution.py:55
  45.8 1.2 %collective-permute-start.14 = (f32[8,256]{1,0:T(8,128)S(1)}, f32[8,256]{1,0:T(8,128)S(1)}, u32[]{:S(2)}, u32[]{:S(2)}) collective-permute-start(f32[8,256]{1,0:T(8,128)S(1)} %get-tuple-element.78), channel_id=1, source_target_pairs={{32,0},{0,32},{96,64},{64,96},{33,1},{1,33},{97,65},{65,97},{40,8}... | collective-permute-start | bytes 24584 | tf_op jit(solution)/shard_map/ppermute | solution.py:42
  49.1 7.3 %collective-permute-start.18 = (f32[24,256]{1,0:T(8,128)S(1)}, f32[24,256]{1,0:T(8,128)S(1)}, u32[]{:S(2)}, u32[]{:S(2)}) collective-permute-start(f32[24,256]{1,0:T(8,128)S(1)} %add.21), channel_id=1, source_target_pairs={{6,0},{56,32},{70,64},{120,96},{7,1},{57,33},{71,65},{121,97},{14,... | collective-permute-start | bytes 73736 | tf_op jit(solution)/shard_map/ppermute | solution.py:55
  52.8 3.7 %collective-permute-start.15 = (f32[8,256]{1,0:T(8,128)S(1)}, f32[8,256]{1,0:T(8,128)S(1)}, u32[]{:S(2)}, u32[]{:S(2)}) collective-permute-start(f32[8,256]{1,0:T(8,128)S(1)} %add.19), channel_id=1, source_target_pairs={{64,0},{96,32},{0,64},{32,96},{65,1},{97,33},{1,65},{33,97},{72,8}... | collective-permute-start | bytes 24584 | tf_op jit(solution)/shard_map/ppermute | solution.py:55
  56.5 3.9 %collective-permute-start.19 = (f32[24,256]{1,0:T(8,128)S(1)}, f32[24,256]{1,0:T(8,128)S(1)}, u32[]{:S(2)}, u32[]{:S(2)}) collective-permute-start(f32[24,256]{1,0:T(8,128)S(1)} %add.22), channel_id=1, source_target_pairs={{8,0},{34,32},{72,64},{98,96},{9,1},{35,33},{73,65},{99,97},{0,8},... | collective-permute-start | bytes 73736 | tf_op jit(solution)/shard_map/ppermute | solution.py:55
  56.8 4.9 %collective-permute-start.16 = (f32[8,256]{1,0:T(8,128)S(1)}, f32[8,256]{1,0:T(8,128)S(1)}, u32[]{:S(2)}, u32[]{:S(2)}) collective-permute-start(f32[8,256]{1,0:T(8,128)S(1)} %add.20.refs_0_), channel_id=1, source_target_pairs={{65,0},{97,32},{1,64},{33,96},{64,1},{96,33},{0,65},{32,97},{73,8}... | collective-permute-start | bytes 24584 | tf_op jit(solution)/shard_map/ppermute | solution.py:55
  61.7 5.0 %collective-permute-start.20 = (f32[24,256]{1,0:T(8,128)S(1)}, f32[24,256]{1,0:T(8,128)S(1)}, u32[]{:S(2)}, u32[]{:S(2)}) collective-permute-start(f32[24,256]{1,0:T(8,128)S(1)} %add.23.refs_2_), channel_id=1, source_target_pairs={{24,0},{38,32},{88,64},{102,96},{25,1},{39,33},{89,65},{103,97},{1... | collective-permute-start | bytes 73736 | tf_op jit(solution)/shard_map/ppermute | solution.py:55
  71.0 2.4 %collective-permute-start.21 = (bf16[784,512]{1,0:T(8,128)(2,1)S(1)}, bf16[784,512]{1,0:T(8,128)(2,1)S(1)}, u32[]{:S(2)}, u32[]{:S(2)}) collective-permute-start(bf16[784,512]{1,0:T(8,128)(2,1)S(1)} %grads_core.1), channel_id=1, source_target_pairs={{32,0},{0,32},{96,64},{64,96},{33,1},{1,33},{97,65},{65,97},{40,8}... | collective-permute-start | bytes 2408456 | tf_op jit(solution)/shard_map/ppermute | solution.py:42
  73.4 7.8 %collective-permute-start.22 = (bf16[272,512]{1,0:T(8,128)(2,1)S(1)}, bf16[272,512]{1,0:T(8,128)(2,1)S(1)}, u32[]{:S(2)}, u32[]{:S(2)}) collective-permute-start(bf16[272,512]{1,0:T(8,128)(2,1)S(1)} %sum_far.1.refs_1_.here_ref), channel_id=1, source_target_pairs={{65,0},{96,32},{0,64},{33,96},{64,1},{97,33},{1,65},{32,97},{73,8}... | collective-permute-start | bytes 835592 | tf_op jit(solution)/shard_map/ppermute | solution.py:42
  77.5 11.6 %copy-start.1 = (bf16[256,512]{1,0:T(8,128)(2,1)S(1)}, bf16[256,512]{1,0:T(8,128)(2,1)}, u32[]{:S(2)}) copy-start(bf16[256,512]{1,0:T(8,128)(2,1)} %z_ref.3) | copy-start | bytes 786436
  77.5 3.9 %collective-permute-start.23 = (bf16[256,512]{1,0:T(8,128)(2,1)S(1)}, bf16[256,512]{1,0:T(8,128)(2,1)S(1)}, u32[]{:S(2)}, u32[]{:S(2)}) collective-permute-start(bf16[256,512]{1,0:T(8,128)(2,1)S(1)} %grads_core_own.1), channel_id=1, source_target_pairs={{32,0},{0,32},{96,64},{64,96},{33,1},{1,33},{97,65},{65,97},{40,8}... | collective-permute-start | bytes 786440 | tf_op jit(solution)/shard_map/ppermute | solution.py:42
  78.3 9.4 %collective-permute-start.24 = (bf16[272,512]{1,0:T(8,128)(2,1)S(1)}, bf16[272,512]{1,0:T(8,128)(2,1)S(1)}, u32[]{:S(2)}, u32[]{:S(2)}) collective-permute-start(bf16[272,512]{1,0:T(8,128)(2,1)S(1)} %get-tuple-element.93), channel_id=1, source_target_pairs={{64,0},{97,32},{1,64},{32,96},{65,1},{96,33},{0,65},{33,97},{72,8}... | collective-permute-start | bytes 835592 | tf_op jit(solution)/shard_map/ppermute | solution.py:42
  81.3 7.8 %collective-permute-start.25 = (bf16[272,512]{1,0:T(8,128)(2,1)S(1)}, bf16[272,512]{1,0:T(8,128)(2,1)S(1)}, u32[]{:S(2)}, u32[]{:S(2)}) collective-permute-start(bf16[272,512]{1,0:T(8,128)(2,1)S(1)} %sum_two.1), channel_id=1, source_target_pairs={{65,0},{96,32},{0,64},{33,96},{64,1},{97,33},{1,65},{32,97},{73,8}... | collective-permute-start | bytes 835592 | tf_op jit(solution)/shard_map/ppermute | solution.py:42

commit v9 on v8

--- a/solution.py
+++ b/solution.py
@@ -157,7 +157,7 @@
     )(unit, partner.reshape(1, ROWS))
 
 
-def exps_kernel(places, rows_here, first, last, *refs):
+def exps_kernel(places, rows_here, olds, first, last, *refs):
     count = len(places)
     info_ref, refs = refs[0], refs[1:]
     row_refs, refs = refs[: 2 * len(rows_here)], refs[2 * len(rows_here) :]
@@ -171,7 +171,7 @@
         sums_ref[...] = jnp.zeros_like(sums_ref)
         col_sums_ref[...] = jnp.zeros_like(col_sums_ref)
     for n, col_ref in enumerate(col_refs):
-        if 0 in rows_here:
+        if 0 in rows_here and n not in olds:
             start = places[n] * TILE
             unit_ref[start : start + col_ref.shape[0]] = col_ref[...]
 
@@ -181,6 +181,8 @@
             cols = col_ref[pl.ds(pl.multiple_of(m * ROWS, ROWS), ROWS), :]
             by_col = col_sums_ref[:, here]
             for k, ref in enumerate(row_refs):
+                if n in olds and rows_here[k // 2] == 0:
+                    continue
                 start = rows_here[k // 2] * 1024 + (k % 2) * 512
                 part = slice(start, start + 512)
                 e = jnp.exp2(lax.dot_general(ref[...], cols, NT, preferred_element_type=F32))
@@ -206,7 +208,7 @@
         col_line_ref[16:17, 0:128] = positive_ref[...]
 
 
-def make_exps(info, rows, rows_here, cols, places, chain, positive, weight, name):
+def make_exps(info, rows, rows_here, cols, places, olds, chain, positive, weight, name):
     first, last = chain is None, positive is not None
     count = len(cols)
     tiles = sum(c.shape[0] for c in cols) // TILE
@@ -221,7 +223,7 @@
         out_shape += (jax.ShapeDtypeStruct((8, ROWS), F32), jax.ShapeDtypeStruct((24, ROWS), F32))
     start = 1 + len(rows) + count
     return pl.pallas_call(
-        functools.partial(exps_kernel, places, rows_here, first, last),
+        functools.partial(exps_kernel, places, rows_here, olds, first, last),
         out_shape=out_shape,
         in_specs=[smem()] + [vmem()] * (len(operands) - 1),
         out_specs=(vmem(),) * len(out_shape),
@@ -389,26 +391,27 @@
     near = [near, get(near, core=1)]
 
     mates, positive = make_mates(unit, partner)
-    chain = make_exps(info, near, (0,), [line0, line1], (0, 1), None, None, 8, "exps0")
+    chain = make_exps(info, near, (0,), [line0, line1], (0, 1), (), None, None, 16, "exps0")
     rest = jnp.concatenate([z_two, z_far], axis=0)
-    rest = [rest, get(rest, core=1)]
-    chain = make_exps(info, rest, (1,), [line0, line1], (0, 1), chain, None, 8, "exps1")
+    rest = [rest, get(after(rest, chain[0]), core=1)]
+    chain = make_exps(info, near, (0,), [before0, after0], (2, 4), (), chain, None, 16, "exps1")
     far0 = get(after(before0, after0, chain[0]), second=-1)
+    chain = make_exps(info, rest, (1,), [line0, line1], (0, 1), (), chain, None, 16, "exps2")
+    far1 = get(after(after1, before1, chain[0]), second=1)
     rows = near + rest
-    chain = make_exps(info, rows, (0, 1), [before0], (2,), chain, None, 4, "exps2")
-    far1 = get(after(after1, before1, chain[0]), second=1)
-    chain = make_exps(info, rows, (0, 1), [after0, before1, after1], (4, 3, 5), chain, None, 0, "exps3")
-    chain = make_exps(info, rows, (0, 1), [far0], (6,), chain, None, 0, "exps4")
-    chain = make_exps(info, rows, (0, 1), [far1], (7,), chain, positive, 0, "exps5")
+    cols = [before0, after0, before1, after1]
+    chain = make_exps(info, rows, (0, 1), cols, (2, 4, 3, 5), (0, 1), chain, None, 8, "exps3")
+    chain = make_exps(info, rows, (0, 1), [far0], (6,), (), chain, None, 4, "exps4")
+    chain = make_exps(info, rows, (0, 1), [far1], (7,), (), chain, positive, 4, "exps5")
     _, _, exps, units, sums, col_sums = chain
 
     by_row = sums + get(sums, core=1)
     by_col = col_sums + swap(col_sums, "first", 0)
     by_col = by_col + swap(after(by_col, by_row), "first", 1)
     by_row = by_row + swap(by_row, "z", 0)
-    by_col = by_col + swap(after(by_col, by_row), "second", 0)
+    by_col = by_col + swap(by_col, "second", 0)
+    by_col = after(by_col, by_row)
     by_row = [by_row, swap(by_row, "z", 1)]
-    by_col = after(by_col, by_row[1])
     by_col = [by_col, swap(by_col, "second", 1)]
     arow, acol, loss = make_totals(info, by_row, by_col)
 

time: 90.4 us -> 90.4 us (level)
  waiting for transfers between devices: 22.4 us -> 21.1 us
  transfers between devices with their start and end apart: 26 -> 26, of which waited for: 14 -> 13; matrix products, arithmetic and copies ran while one was open for 0% -> 0% of each run, Pallas kernels for 23% -> 24%
where the time goes in v9:
time: 90.4 us; the launch traced here: 89.8 us
  starting transfers between devices  36.2 us (40%)
  Pallas kernels  29.7 us (33%)
  waiting for transfers between devices  21.1 us (23%)
  local copies, waits for them, and re-layouts  1.78 us (2%)
    ppermute x20, starting transfers between devices, get(): return lax.ppermute(value, AXES, pairs)  25.8 us
    pallas_call x6, Pallas kernels, make_exps(): pl.pallas_call(functools.partial(exps_kernel, places, rows_here, olds, fi...  17.7 us
    ppermute x20, waiting for transfers between devices, get(): return lax.ppermute(value, AXES, pairs)  11.8 us
    ppermute x6, starting transfers between devices, swap(): return lax.ppermute(value, AXES, pairs)  10.4 us
    pallas_call x5, Pallas kernels, make_grads(): pl.pallas_call(functools.partial(grads_kernel, pieces, adds, carry is not...  9.47 us
    ppermute x6, waiting for transfers between devices, swap(): return lax.ppermute(value, AXES, pairs)  9.29 us
  transfers between devices with their start and end apart: 26, of which 13 were waited for; matrix products, arithmetic and copies ran while one was open for 0% of the time, Pallas kernels for 24%

profile of v9, /device:TPU:0, one launch (start us, length us, event | category | flops | bytes accessed | tf_op | source)
XLA Modules:
  0.0 89.8 jit_solution(8999454186295577506)
XLA Ops:
  1.7 2.1 %collective-permute-start = (bf16[256,512]{1,0:T(8,128)(2,1)S(1)}, bf16[256,512]{1,0:T(8,128)(2,1)S(1)}, u32[]{:S(2)}, u32[]{:S(2)}) collective-permute-start(bf16[256,512]{1,0:T(8,128)(2,1)S(1)} %get-tuple-element.51), channel_id=1, source_target_pairs={{65,0},{96,32},{0,64},{33,96},{64,1},{97,33},{1,65},{32,97},{73,8}... | collective-permute-start | bytes 786440 | tf_op jit(solution)/shard_map/ppermute | solution.py:42
  3.8 1.5 %collective-permute-start.4 = (bf16[256,512]{1,0:T(8,128)(2,1)S(1)}, bf16[256,512]{1,0:T(8,128)(2,1)S(1)}, u32[]{:S(2)}, u32[]{:S(2)}) collective-permute-start(bf16[256,512]{1,0:T(8,128)(2,1)S(1)} %get-tuple-element.52.unit_ref), channel_id=1, source_target_pairs={{6,0},{56,32},{70,64},{120,96},{7,1},{57,33},{71,65},{121,97},{14,... | collective-permute-start | bytes 786440 | tf_op jit(solution)/shard_map/ppermute | solution.py:42
  5.3 1.7 %collective-permute-start.5 = (bf16[256,512]{1,0:T(8,128)(2,1)S(1)}, bf16[256,512]{1,0:T(8,128)(2,1)S(1)}, u32[]{:S(2)}, u32[]{:S(2)}) collective-permute-start(bf16[256,512]{1,0:T(8,128)(2,1)S(1)} %get-tuple-element.52.unit_ref), channel_id=1, source_target_pairs={{2,0},{40,32},{66,64},{104,96},{3,1},{41,33},{67,65},{105,97},{10,... | collective-permute-start | bytes 786440 | tf_op jit(solution)/shard_map/ppermute | solution.py:42
  7.0 1.8 %collective-permute-start.6 = (bf16[256,512]{1,0:T(8,128)(2,1)S(1)}, bf16[256,512]{1,0:T(8,128)(2,1)S(1)}, u32[]{:S(2)}, u32[]{:S(2)}) collective-permute-start(bf16[256,512]{1,0:T(8,128)(2,1)S(1)} %get-tuple-element.52.unit_ref), channel_id=1, source_target_pairs={{4,0},{48,32},{68,64},{112,96},{5,1},{49,33},{69,65},{113,97},{12,... | collective-permute-start | bytes 786440 | tf_op jit(solution)/shard_map/ppermute | solution.py:42
  8.9 2.2 %collective-permute-start.2 = (bf16[256,512]{1,0:T(8,128)(2,1)S(1)}, bf16[256,512]{1,0:T(8,128)(2,1)S(1)}, u32[]{:S(2)}, u32[]{:S(2)}) collective-permute-start(bf16[256,512]{1,0:T(8,128)(2,1)S(1)} %get-tuple-element.51), channel_id=1, source_target_pairs={{64,0},{97,32},{1,64},{32,96},{65,1},{96,33},{0,65},{33,97},{72,8}... | collective-permute-start | bytes 786440 | tf_op jit(solution)/shard_map/ppermute | solution.py:42
  12.3 1.4 %collective-permute-done.5 = bf16[256,512]{1,0:T(8,128)(2,1)S(1)} collective-permute-done((bf16[256,512]{1,0:T(8,128)(2,1)S(1)}, bf16[256,512]{1,0:T(8,128)(2,1)S(1)}, u32[]{:S(2)}, u32[]{:S(2)}) %collective-permute-start.5) | collective-permute-done | bytes 262176 | tf_op jit(solution)/shard_map/ppermute | solution.py:42
  13.8 2.0 %collective-permute-start.3 = (bf16[256,512]{1,0:T(8,128)(2,1)S(1)}, bf16[256,512]{1,0:T(8,128)(2,1)S(1)}, u32[]{:S(2)}, u32[]{:S(2)}) collective-permute-start(bf16[256,512]{1,0:T(8,128)(2,1)S(1)} %collective-permute-done), channel_id=1, source_target_pairs={{65,0},{96,32},{0,64},{33,96},{64,1},{97,33},{1,65},{32,97},{73,8}... | collective-permute-start | bytes 786440 | tf_op jit(solution)/shard_map/ppermute | solution.py:42
  15.8 1.6 %collective-permute-start.10 = (bf16[512,512]{1,0:T(8,128)(2,1)S(1)}, bf16[512,512]{1,0:T(8,128)(2,1)S(1)}, u32[]{:S(2)}, u32[]{:S(2)}) collective-permute-start(bf16[512,512]{1,0:T(8,128)(2,1)S(1)} %constant_dynamic-update-slice_fusion.4.refs_3_), channel_id=1, source_target_pairs={{24,0},{38,32},{88,64},{102,96},{25,1},{39,33},{89,65},{103,97},{0... | collective-permute-start | bytes 1572872 | tf_op jit(solution)/shard_map/ppermute | solution.py:42
  17.4 1.7 %collective-permute-start.11 = (bf16[512,512]{1,0:T(8,128)(2,1)S(1)}, bf16[512,512]{1,0:T(8,128)(2,1)S(1)}, u32[]{:S(2)}, u32[]{:S(2)}) collective-permute-start(bf16[512,512]{1,0:T(8,128)(2,1)S(1)} %constant_dynamic-update-slice_fusion.4.refs_3_), channel_id=1, source_target_pairs={{8,0},{34,32},{72,64},{98,96},{9,1},{35,33},{73,65},{99,97},{16,8}... | collective-permute-start | bytes 1572872 | tf_op jit(solution)/shard_map/ppermute | solution.py:42
  19.1 1.9 %collective-permute-start.8 = (bf16[512,512]{1,0:T(8,128)(2,1)S(1)}, bf16[512,512]{1,0:T(8,128)(2,1)S(1)}, u32[]{:S(2)}, u32[]{:S(2)}) collective-permute-start(bf16[512,512]{1,0:T(8,128)(2,1)S(1)} %constant_dynamic-update-slice_fusion.6.refs_4_), channel_id=1, source_target_pairs={{8,0},{34,32},{72,64},{98,96},{9,1},{35,33},{73,65},{99,97},{16,8}... | collective-permute-start | bytes 1572872 | tf_op jit(solution)/shard_map/ppermute | solution.py:42
  21.4 1.6 %collective-permute-start.9 = (bf16[512,512]{1,0:T(8,128)(2,1)S(1)}, bf16[512,512]{1,0:T(8,128)(2,1)S(1)}, u32[]{:S(2)}, u32[]{:S(2)}) collective-permute-start(bf16[512,512]{1,0:T(8,128)(2,1)S(1)} %constant_dynamic-update-slice_fusion.6.refs_4_), channel_id=1, source_target_pairs={{24,0},{38,32},{88,64},{102,96},{25,1},{39,33},{89,65},{103,97},{0... | collective-permute-start | bytes 1572872 | tf_op jit(solution)/shard_map/ppermute | solution.py:42
  23.1 2.6 %exps0.1 = (f32[2048,128]{1,0:T(8,128)S(1)}, f32[8,4096]{1,0:T(8,128)S(1)}, bf16[2048,4096]{1,0:T(8,128)(2,1)S(1)}, bf16[4096,512]{1,0:T(8,128)(2,1)S(1)}) custom-call(s32[4]{0:T(128)S(1)} %pad_add_fusion.refs_0_.info_ref, bf16[512,512]{1,0:T(8,128)(2,1)S(1)} %constant_dynamic-update-slice_fusion.refs_1_, ...), custom_call_target="tpu_custom_call" | custom-call | flops 17179869184 | bytes 16777216 | tf_op jit(solution)/shard_map/exps0/pallas_call | solution.py:225
  26.6 2.5 %exps1.1 = (f32[2048,128]{1,0:T(8,128)S(1)}, f32[8,4096]{1,0:T(8,128)S(1)}, bf16[2048,4096]{1,0:T(8,128)(2,1)S(1)}, bf16[4096,512]{1,0:T(8,128)(2,1)S(1)}) custom-call(s32[4]{0:T(128)S(1)} %pad_add_fusion.refs_0_.info_ref, ...), custom_call_target="tpu_custom_call", output_to_operand_aliasing={{0}: (5, {}), {1}: (6, {}), {2}: (7, {}), {3}: (8, {})} | custom-call | flops 17179869184 | bytes 16777216 | tf_op jit(solution)/shard_map/exps1/pallas_call | solution.py:225
  29.2 1.7 %collective-permute-start.13 = (bf16[512,512]{1,0:T(8,128)(2,1)S(1)}, bf16[512,512]{1,0:T(8,128)(2,1)S(1)}, u32[]{:S(2)}, u32[]{:S(2)}) collective-permute-start(bf16[512,512]{1,0:T(8,128)(2,1)S(1)} %collective-permute-done.10.refs_3_.refs_5_), channel_id=1, source_target_pairs={{24,0},{38,32},{88,64},{102,96},{25,1},{39,33},{89,65},{103,97},{0... | collective-permute-start | bytes 1572872 | tf_op jit(solution)/shard_map/ppermute | solution.py:42
  30.8 2.5 %exps2.1 = (f32[2048,128]{1,0:T(8,128)S(1)}, f32[8,4096]{1,0:T(8,128)S(1)}, bf16[2048,4096]{1,0:T(8,128)(2,1)S(1)}, bf16[4096,512]{1,0:T(8,128)(2,1)S(1)}) custom-call(s32[4]{0:T(128)S(1)} %pad_add_fusion.refs_0_.info_ref, ...), custom_call_target="tpu_custom_call", output_to_operand_aliasing={{0}: (5, {}), {1}: (6, {}), {2}: (7, {}), {3}: (8, {})} | custom-call | flops 17179869184 | bytes 16777216 | tf_op jit(solution)/shard_map/exps2/pallas_call | solution.py:225
  33.3 1.8 %collective-permute-start.12 = (bf16[512,512]{1,0:T(8,128)(2,1)S(1)}, bf16[512,512]{1,0:T(8,128)(2,1)S(1)}, u32[]{:S(2)}, u32[]{:S(2)}) collective-permute-start(bf16[512,512]{1,0:T(8,128)(2,1)S(1)} %collective-permute-done.8.refs_8_), channel_id=1, source_target_pairs={{8,0},{34,32},{72,64},{98,96},{9,1},{35,33},{73,65},{99,97},{16,8}... | collective-permute-start | bytes 1572872 | tf_op jit(solution)/shard_map/ppermute | solution.py:42
  35.1 5.6 %exps3.1 = (f32[2048,128]{1,0:T(8,128)S(1)}, f32[8,4096]{1,0:T(8,128)S(1)}, bf16[2048,4096]{1,0:T(8,128)(2,1)S(1)}, bf16[4096,512]{1,0:T(8,128)(2,1)S(1)}) custom-call(s32[4]{0:T(128)S(1)} %pad_add_fusion.refs_0_.info_ref, ...), custom_call_target="tpu_custom_call", output_to_operand_aliasing={{0}: (9, {}), {1}: (10, {}), {2}: (11, {}), {3}: (12, {})} | custom-call | flops 34359738368 | bytes 16777216 | tf_op jit(solution)/shard_map/exps3/pallas_call | solution.py:225
  40.7 2.1 %exps4.1 = (f32[2048,128]{1,0:T(8,128)S(1)}, f32[8,4096]{1,0:T(8,128)S(1)}, bf16[2048,4096]{1,0:T(8,128)(2,1)S(1)}, bf16[4096,512]{1,0:T(8,128)(2,1)S(1)}) custom-call(s32[4]{0:T(128)S(1)} %pad_add_fusion.refs_0_.info_ref, ...), custom_call_target="tpu_custom_call", output_to_operand_aliasing={{0}: (6, {}), {1}: (7, {}), {2}: (8, {}), {3}: (9, {})} | custom-call | flops 4294967296 | bytes 2097152 | tf_op jit(solution)/shard_map/exps4/pallas_call | solution.py:225
  42.8 2.4 %exps5.1 = (f32[2048,128]{1,0:T(8,128)S(1)}, f32[8,4096]{1,0:T(8,128)S(1)}, bf16[2048,4096]{1,0:T(8,128)(2,1)S(1)}, bf16[4096,512]{1,0:T(8,128)(2,1)S(1)}, f32[8,256]{1,0:T(8,128)S(1)}, /*index=5*/f32[24,256]{1,0:T(8,128)S(1)}) custom-call(s32[4]{0:T(128)S(1)} %pad_add_fusion.refs_0_.info_ref, ...), custom_call_target="tpu_custom_call", output_to_operand_aliasing={{0}: (6, {}), {1}: (7, {}), {2}: (8, {}), {3}: (9, {})} | custom-call | flops 4294967296 | bytes 2097152 | tf_op jit(solution)/shard_map/exps5/pallas_call | solution.py:225
  47.2 2.0 %collective-permute-done.17 = f32[24,256]{1,0:T(8,128)S(1)} collective-permute-done((f32[24,256]{1,0:T(8,128)S(1)}, f32[24,256]{1,0:T(8,128)S(1)}, u32[]{:S(2)}, u32[]{:S(2)}) %collective-permute-start.17) | collective-permute-done | bytes 24608 | tf_op jit(solution)/shard_map/ppermute | solution.py:55
  49.2 3.6 %collective-permute-start.18 = (f32[24,256]{1,0:T(8,128)S(1)}, f32[24,256]{1,0:T(8,128)S(1)}, u32[]{:S(2)}, u32[]{:S(2)}) collective-permute-start(f32[24,256]{1,0:T(8,128)S(1)} %add.21), channel_id=1, source_target_pairs={{6,0},{56,32},{70,64},{120,96},{7,1},{57,33},{71,65},{121,97},{14,... | collective-permute-start | bytes 73736 | tf_op jit(solution)/shard_map/ppermute | solution.py:55
  52.8 1.8 %collective-permute-done.18 = f32[24,256]{1,0:T(8,128)S(1)} collective-permute-done((f32[24,256]{1,0:T(8,128)S(1)}, f32[24,256]{1,0:T(8,128)S(1)}, u32[]{:S(2)}, u32[]{:S(2)}) %collective-permute-start.18) | collective-permute-done | bytes 24608 | tf_op jit(solution)/shard_map/ppermute | solution.py:55
  55.6 1.7 %collective-permute-start.15 = (f32[8,256]{1,0:T(8,128)S(1)}, f32[8,256]{1,0:T(8,128)S(1)}, u32[]{:S(2)}, u32[]{:S(2)}) collective-permute-start(f32[8,256]{1,0:T(8,128)S(1)} %add.19), channel_id=1, source_target_pairs={{64,0},{96,32},{0,64},{32,96},{65,1},{97,33},{1,65},{33,97},{72,8}... | collective-permute-start | bytes 24584 | tf_op jit(solution)/shard_map/ppermute | solution.py:55
  57.3 2.0 %collective-permute-done.15 = f32[8,256]{1,0:T(8,128)S(1)} collective-permute-done((f32[8,256]{1,0:T(8,128)S(1)}, f32[8,256]{1,0:T(8,128)S(1)}, u32[]{:S(2)}, u32[]{:S(2)}) %collective-permute-start.15) | collective-permute-done | bytes 8224 | tf_op jit(solution)/shard_map/ppermute | solution.py:55
  59.3 2.1 %collective-permute-start.20 = (f32[24,256]{1,0:T(8,128)S(1)}, f32[24,256]{1,0:T(8,128)S(1)}, u32[]{:S(2)}, u32[]{:S(2)}) collective-permute-start(f32[24,256]{1,0:T(8,128)S(1)} %add.23.refs_2_), channel_id=1, source_target_pairs={{24,0},{38,32},{88,64},{102,96},{25,1},{39,33},{89,65},{103,97},{1... | collective-permute-start | bytes 73736 | tf_op jit(solution)/shard_map/ppermute | solution.py:55
  61.4 1.4 %collective-permute-start.16 = (f32[8,256]{1,0:T(8,128)S(1)}, f32[8,256]{1,0:T(8,128)S(1)}, u32[]{:S(2)}, u32[]{:S(2)}) collective-permute-start(f32[8,256]{1,0:T(8,128)S(1)} %add.20.refs_0_), channel_id=1, source_target_pairs={{65,0},{97,32},{1,64},{33,96},{64,1},{96,33},{0,65},{32,97},{73,8}... | collective-permute-start | bytes 24584 | tf_op jit(solution)/shard_map/ppermute | solution.py:55
  62.8 3.5 %collective-permute-done.16.refs_1_ = f32[8,256]{1,0:T(8,128)S(1)} collective-permute-done((f32[8,256]{1,0:T(8,128)S(1)}, f32[8,256]{1,0:T(8,128)S(1)}, u32[]{:S(2)}, u32[]{:S(2)}) %collective-permute-start.16) | collective-permute-done | bytes 8224 | tf_op jit(solution)/shard_map/ppermute | solution.py:55
  67.1 3.4 %grads_core.1 = bf16[784,512]{1,0:T(8,128)(2,1)S(1)} custom-call(f32[32,128]{1,0:T(8,128)S(1)} %get-tuple-element.92.acol_ref, bf16[2048,128]{1,0:T(8,128)(2,1)S(1)} %get-tuple-element.85.arow_ref, bf16[2048,4096]{1,0:T(8,128)(2,1)S(1)} %get-tuple-element.86.exps_ref, bf16[4096,512]{1,0:T(8,128)(2,1)S(1)} %get-tuple-element.87.unit_ref, ...), custom_call_target="tpu_custom_call" | custom-call | flops 3221225472 | bytes 10485760 | tf_op jit(solution)/shard_map/grads_core/pallas_call | solution.py:315
  73.5 2.3 %grads_near.1 = (bf16[272,512]{1,0:T(8,128)(2,1)S(1)}, f32[256,512]{1,0:T(8,128)S(1)}) custom-call(f32[32,128]{1,0:T(8,128)S(1)} %get-tuple-element.92.acol_ref, bf16[2048,128]{1,0:T(8,128)(2,1)S(1)} %get-tuple-element.85.arow_ref, bf16[2048,4096]{1,0:T(8,128)(2,1)S(1)} %get-tuple-element.86.exps_ref, bf16[4096,512]{1,0:T(8,128)(2,1)S(1)} %get-tuple-element.87.unit_ref, ...), custom_call_target="tpu_custom_call" | custom-call | flops 2147483648 | bytes 8388608 | tf_op jit(solution)/shard_map/grads_near/pallas_call | solution.py:315
  77.9 2.1 %collective-permute-start.24 = (bf16[272,512]{1,0:T(8,128)(2,1)S(1)}, bf16[272,512]{1,0:T(8,128)(2,1)S(1)}, u32[]{:S(2)}, u32[]{:S(2)}) collective-permute-start(bf16[272,512]{1,0:T(8,128)(2,1)S(1)} %get-tuple-element.93), channel_id=1, source_target_pairs={{64,0},{97,32},{1,64},{32,96},{65,1},{96,33},{0,65},{33,97},{72,8}... | collective-permute-start | bytes 835592 | tf_op jit(solution)/shard_map/ppermute | solution.py:42
  82.2 5.2 %collective-permute-done.24.one_ref = bf16[272,512]{1,0:T(8,128)(2,1)S(1)} collective-permute-done((bf16[272,512]{1,0:T(8,128)(2,1)S(1)}, bf16[272,512]{1,0:T(8,128)(2,1)S(1)}, u32[]{:S(2)}, u32[]{:S(2)}) %collective-permute-start.24) | collective-permute-done | bytes 278560 | tf_op jit(solution)/shard_map/ppermute | solution.py:42
  87.4 1.3 %collective-permute-done.25.two_ref = bf16[272,512]{1,0:T(8,128)(2,1)S(1)} collective-permute-done((bf16[272,512]{1,0:T(8,128)(2,1)S(1)}, bf16[272,512]{1,0:T(8,128)(2,1)S(1)}, u32[]{:S(2)}, u32[]{:S(2)}) %collective-permute-start.25) | collective-permute-done | bytes 278560 | tf_op jit(solution)/shard_map/ppermute | solution.py:42
  (57 shorter events, 15.8 us)
Async XLA Ops:
  0.6 1.0 %copy-start = (bf16[256,512]{1,0:T(8,128)(2,1)S(1)}, bf16[256,512]{1,0:T(8,128)(2,1)}, u32[]{:S(2)}) copy-start(bf16[256,512]{1,0:T(8,128)(2,1)} %z_ref.3) | copy-start | bytes 786436
  1.7 10.4 %collective-permute-start = (bf16[256,512]{1,0:T(8,128)(2,1)S(1)}, bf16[256,512]{1,0:T(8,128)(2,1)S(1)}, u32[]{:S(2)}, u32[]{:S(2)}) collective-permute-start(bf16[256,512]{1,0:T(8,128)(2,1)S(1)} %get-tuple-element.51), channel_id=1, source_target_pairs={{65,0},{96,32},{0,64},{33,96},{64,1},{97,33},{1,65},{32,97},{73,8}... | collective-permute-start | bytes 786440 | tf_op jit(solution)/shard_map/ppermute | solution.py:42
  3.8 8.5 %collective-permute-start.4 = (bf16[256,512]{1,0:T(8,128)(2,1)S(1)}, bf16[256,512]{1,0:T(8,128)(2,1)S(1)}, u32[]{:S(2)}, u32[]{:S(2)}) collective-permute-start(bf16[256,512]{1,0:T(8,128)(2,1)S(1)} %get-tuple-element.52.unit_ref), channel_id=1, source_target_pairs={{6,0},{56,32},{70,64},{120,96},{7,1},{57,33},{71,65},{121,97},{14,... | collective-permute-start | bytes 786440 | tf_op jit(solution)/shard_map/ppermute | solution.py:42
  5.3 8.5 %collective-permute-start.5 = (bf16[256,512]{1,0:T(8,128)(2,1)S(1)}, bf16[256,512]{1,0:T(8,128)(2,1)S(1)}, u32[]{:S(2)}, u32[]{:S(2)}) collective-permute-start(bf16[256,512]{1,0:T(8,128)(2,1)S(1)} %get-tuple-element.52.unit_ref), channel_id=1, source_target_pairs={{2,0},{40,32},{66,64},{104,96},{3,1},{41,33},{67,65},{105,97},{10,... | collective-permute-start | bytes 786440 | tf_op jit(solution)/shard_map/ppermute | solution.py:42
  7.0 10.4 %collective-permute-start.6 = (bf16[256,512]{1,0:T(8,128)(2,1)S(1)}, bf16[256,512]{1,0:T(8,128)(2,1)S(1)}, u32[]{:S(2)}, u32[]{:S(2)}) collective-permute-start(bf16[256,512]{1,0:T(8,128)(2,1)S(1)} %get-tuple-element.52.unit_ref), channel_id=1, source_target_pairs={{4,0},{48,32},{68,64},{112,96},{5,1},{49,33},{69,65},{113,97},{12,... | collective-permute-start | bytes 786440 | tf_op jit(solution)/shard_map/ppermute | solution.py:42
  8.9 10.3 %collective-permute-start.2 = (bf16[256,512]{1,0:T(8,128)(2,1)S(1)}, bf16[256,512]{1,0:T(8,128)(2,1)S(1)}, u32[]{:S(2)}, u32[]{:S(2)}) collective-permute-start(bf16[256,512]{1,0:T(8,128)(2,1)S(1)} %get-tuple-element.51), channel_id=1, source_target_pairs={{64,0},{97,32},{1,64},{32,96},{65,1},{96,33},{0,65},{33,97},{72,8}... | collective-permute-start | bytes 786440 | tf_op jit(solution)/shard_map/ppermute | solution.py:42
  11.2 0.7 copy-start.2
  12.2 10.9 %collective-permute-start.1 = (bf16[512,512]{1,0:T(8,128)(2,1)S(1)}, bf16[512,512]{1,0:T(8,128)(2,1)S(1)}, u32[]{:S(2)}, u32[]{:S(2)}) collective-permute-start(bf16[512,512]{1,0:T(8,128)(2,1)S(1)} %constant_dynamic-update-slice_fusion.refs_1_), channel_id=1, source_target_pairs={{32,0},{0,32},{96,64},{64,96},{33,1},{1,33},{97,65},{65,97},{40,8}... | collective-permute-start | bytes 1572872 | tf_op jit(solution)/shard_map/ppermute | solution.py:42
  13.8 7.7 %collective-permute-start.3 = (bf16[256,512]{1,0:T(8,128)(2,1)S(1)}, bf16[256,512]{1,0:T(8,128)(2,1)S(1)}, u32[]{:S(2)}, u32[]{:S(2)}) collective-permute-start(bf16[256,512]{1,0:T(8,128)(2,1)S(1)} %collective-permute-done), channel_id=1, source_target_pairs={{65,0},{96,32},{0,64},{33,96},{64,1},{97,33},{1,65},{32,97},{73,8}... | collective-permute-start | bytes 786440 | tf_op jit(solution)/shard_map/ppermute | solution.py:42
  15.8 10.5 %collective-permute-start.10 = (bf16[512,512]{1,0:T(8,128)(2,1)S(1)}, bf16[512,512]{1,0:T(8,128)(2,1)S(1)}, u32[]{:S(2)}, u32[]{:S(2)}) collective-permute-start(bf16[512,512]{1,0:T(8,128)(2,1)S(1)} %constant_dynamic-update-slice_fusion.4.refs_3_), channel_id=1, source_target_pairs={{24,0},{38,32},{88,64},{102,96},{25,1},{39,33},{89,65},{103,97},{0... | collective-permute-start | bytes 1572872 | tf_op jit(solution)/shard_map/ppermute | solution.py:42
  17.4 9.2 %collective-permute-start.11 = (bf16[512,512]{1,0:T(8,128)(2,1)S(1)}, bf16[512,512]{1,0:T(8,128)(2,1)S(1)}, u32[]{:S(2)}, u32[]{:S(2)}) collective-permute-start(bf16[512,512]{1,0:T(8,128)(2,1)S(1)} %constant_dynamic-update-slice_fusion.4.refs_3_), channel_id=1, source_target_pairs={{8,0},{34,32},{72,64},{98,96},{9,1},{35,33},{73,65},{99,97},{16,8}... | collective-permute-start | bytes 1572872 | tf_op jit(solution)/shard_map/ppermute | solution.py:42
  19.1 14.2 %collective-permute-start.8 = (bf16[512,512]{1,0:T(8,128)(2,1)S(1)}, bf16[512,512]{1,0:T(8,128)(2,1)S(1)}, u32[]{:S(2)}, u32[]{:S(2)}) collective-permute-start(bf16[512,512]{1,0:T(8,128)(2,1)S(1)} %constant_dynamic-update-slice_fusion.6.refs_4_), channel_id=1, source_target_pairs={{8,0},{34,32},{72,64},{98,96},{9,1},{35,33},{73,65},{99,97},{16,8}... | collective-permute-start | bytes 1572872 | tf_op jit(solution)/shard_map/ppermute | solution.py:42
  21.4 11.9 %collective-permute-start.9 = (bf16[512,512]{1,0:T(8,128)(2,1)S(1)}, bf16[512,512]{1,0:T(8,128)(2,1)S(1)}, u32[]{:S(2)}, u32[]{:S(2)}) collective-permute-start(bf16[512,512]{1,0:T(8,128)(2,1)S(1)} %constant_dynamic-update-slice_fusion.6.refs_4_), channel_id=1, source_target_pairs={{24,0},{38,32},{88,64},{102,96},{25,1},{39,33},{89,65},{103,97},{0... | collective-permute-start | bytes 1572872 | tf_op jit(solution)/shard_map/ppermute | solution.py:42
  25.7 5.1 %collective-permute-start.7 = (bf16[512,512]{1,0:T(8,128)(2,1)S(1)}, bf16[512,512]{1,0:T(8,128)(2,1)S(1)}, u32[]{:S(2)}, u32[]{:S(2)}) collective-permute-start(bf16[512,512]{1,0:T(8,128)(2,1)S(1)} %constant_dynamic-update-slice_fusion.2.refs_1_.refs_3_), channel_id=1, source_target_pairs={{32,0},{0,32},{96,64},{64,96},{33,1},{1,33},{97,65},{65,97},{40,8}... | collective-permute-start | bytes 1572872 | tf_op jit(solution)/shard_map/ppermute | solution.py:42
  29.2 11.6 %collective-permute-start.13 = (bf16[512,512]{1,0:T(8,128)(2,1)S(1)}, bf16[512,512]{1,0:T(8,128)(2,1)S(1)}, u32[]{:S(2)}, u32[]{:S(2)}) collective-permute-start(bf16[512,512]{1,0:T(8,128)(2,1)S(1)} %collective-permute-done.10.refs_3_.refs_5_), channel_id=1, source_target_pairs={{24,0},{38,32},{88,64},{102,96},{25,1},{39,33},{89,65},{103,97},{0... | collective-permute-start | bytes 1572872 | tf_op jit(solution)/shard_map/ppermute | solution.py:42
  33.3 9.5 %collective-permute-start.12 = (bf16[512,512]{1,0:T(8,128)(2,1)S(1)}, bf16[512,512]{1,0:T(8,128)(2,1)S(1)}, u32[]{:S(2)}, u32[]{:S(2)}) collective-permute-start(bf16[512,512]{1,0:T(8,128)(2,1)S(1)} %collective-permute-done.8.refs_8_), channel_id=1, source_target_pairs={{8,0},{34,32},{72,64},{98,96},{9,1},{35,33},{73,65},{99,97},{16,8}... | collective-permute-start | bytes 1572872 | tf_op jit(solution)/shard_map/ppermute | solution.py:42
  45.3 3.9 %collective-permute-start.17 = (f32[24,256]{1,0:T(8,128)S(1)}, f32[24,256]{1,0:T(8,128)S(1)}, u32[]{:S(2)}, u32[]{:S(2)}) collective-permute-start(f32[24,256]{1,0:T(8,128)S(1)} %get-tuple-element.80), channel_id=1, source_target_pairs={{2,0},{40,32},{66,64},{104,96},{3,1},{41,33},{67,65},{105,97},{10,... | collective-permute-start | bytes 73736 | tf_op jit(solution)/shard_map/ppermute | solution.py:55
  45.8 1.3 %collective-permute-start.14 = (f32[8,256]{1,0:T(8,128)S(1)}, f32[8,256]{1,0:T(8,128)S(1)}, u32[]{:S(2)}, u32[]{:S(2)}) collective-permute-start(f32[8,256]{1,0:T(8,128)S(1)} %get-tuple-element.79), channel_id=1, source_target_pairs={{32,0},{0,32},{96,64},{64,96},{33,1},{1,33},{97,65},{65,97},{40,8}... | collective-permute-start | bytes 24584 | tf_op jit(solution)/shard_map/ppermute | solution.py:42
  49.2 5.4 %collective-permute-start.18 = (f32[24,256]{1,0:T(8,128)S(1)}, f32[24,256]{1,0:T(8,128)S(1)}, u32[]{:S(2)}, u32[]{:S(2)}) collective-permute-start(f32[24,256]{1,0:T(8,128)S(1)} %add.21), channel_id=1, source_target_pairs={{6,0},{56,32},{70,64},{120,96},{7,1},{57,33},{71,65},{121,97},{14,... | collective-permute-start | bytes 73736 | tf_op jit(solution)/shard_map/ppermute | solution.py:55
  54.6 4.7 %collective-permute-start.19 = (f32[24,256]{1,0:T(8,128)S(1)}, f32[24,256]{1,0:T(8,128)S(1)}, u32[]{:S(2)}, u32[]{:S(2)}) collective-permute-start(f32[24,256]{1,0:T(8,128)S(1)} %add.22), channel_id=1, source_target_pairs={{8,0},{34,32},{72,64},{98,96},{9,1},{35,33},{73,65},{99,97},{0,8},... | collective-permute-start | bytes 73736 | tf_op jit(solution)/shard_map/ppermute | solution.py:55
  55.6 3.7 %collective-permute-start.15 = (f32[8,256]{1,0:T(8,128)S(1)}, f32[8,256]{1,0:T(8,128)S(1)}, u32[]{:S(2)}, u32[]{:S(2)}) collective-permute-start(f32[8,256]{1,0:T(8,128)S(1)} %add.19), channel_id=1, source_target_pairs={{64,0},{96,32},{0,64},{32,96},{65,1},{97,33},{1,65},{33,97},{72,8}... | collective-permute-start | bytes 24584 | tf_op jit(solution)/shard_map/ppermute | solution.py:55
  59.3 7.0 %collective-permute-start.20 = (f32[24,256]{1,0:T(8,128)S(1)}, f32[24,256]{1,0:T(8,128)S(1)}, u32[]{:S(2)}, u32[]{:S(2)}) collective-permute-start(f32[24,256]{1,0:T(8,128)S(1)} %add.23.refs_2_), channel_id=1, source_target_pairs={{24,0},{38,32},{88,64},{102,96},{25,1},{39,33},{89,65},{103,97},{1... | collective-permute-start | bytes 73736 | tf_op jit(solution)/shard_map/ppermute | solution.py:55
  61.4 4.9 %collective-permute-start.16 = (f32[8,256]{1,0:T(8,128)S(1)}, f32[8,256]{1,0:T(8,128)S(1)}, u32[]{:S(2)}, u32[]{:S(2)}) collective-permute-start(f32[8,256]{1,0:T(8,128)S(1)} %add.20.refs_0_), channel_id=1, source_target_pairs={{65,0},{97,32},{1,64},{33,96},{64,1},{96,33},{0,65},{32,97},{73,8}... | collective-permute-start | bytes 24584 | tf_op jit(solution)/shard_map/ppermute | solution.py:55
  70.5 2.4 %collective-permute-start.21 = (bf16[784,512]{1,0:T(8,128)(2,1)S(1)}, bf16[784,512]{1,0:T(8,128)(2,1)S(1)}, u32[]{:S(2)}, u32[]{:S(2)}) collective-permute-start(bf16[784,512]{1,0:T(8,128)(2,1)S(1)} %grads_core.1), channel_id=1, source_target_pairs={{32,0},{0,32},{96,64},{64,96},{33,1},{1,33},{97,65},{65,97},{40,8}... | collective-permute-start | bytes 2408456 | tf_op jit(solution)/shard_map/ppermute | solution.py:42
  73.0 7.8 %collective-permute-start.22 = (bf16[272,512]{1,0:T(8,128)(2,1)S(1)}, bf16[272,512]{1,0:T(8,128)(2,1)S(1)}, u32[]{:S(2)}, u32[]{:S(2)}) collective-permute-start(bf16[272,512]{1,0:T(8,128)(2,1)S(1)} %sum_far.1.refs_1_.here_ref), channel_id=1, source_target_pairs={{65,0},{96,32},{0,64},{33,96},{64,1},{97,33},{1,65},{32,97},{73,8}... | collective-permute-start | bytes 835592 | tf_op jit(solution)/shard_map/ppermute | solution.py:42
  77.0 11.6 %copy-start.1 = (bf16[256,512]{1,0:T(8,128)(2,1)S(1)}, bf16[256,512]{1,0:T(8,128)(2,1)}, u32[]{:S(2)}) copy-start(bf16[256,512]{1,0:T(8,128)(2,1)} %z_ref.3) | copy-start | bytes 786436
  77.1 3.9 %collective-permute-start.23 = (bf16[256,512]{1,0:T(8,128)(2,1)S(1)}, bf16[256,512]{1,0:T(8,128)(2,1)S(1)}, u32[]{:S(2)}, u32[]{:S(2)}) collective-permute-start(bf16[256,512]{1,0:T(8,128)(2,1)S(1)} %grads_core_own.1), channel_id=1, source_target_pairs={{32,0},{0,32},{96,64},{64,96},{33,1},{1,33},{97,65},{65,97},{40,8}... | collective-permute-start | bytes 786440 | tf_op jit(solution)/shard_map/ppermute | solution.py:42
  77.9 9.4 %collective-permute-start.24 = (bf16[272,512]{1,0:T(8,128)(2,1)S(1)}, bf16[272,512]{1,0:T(8,128)(2,1)S(1)}, u32[]{:S(2)}, u32[]{:S(2)}) collective-permute-start(bf16[272,512]{1,0:T(8,128)(2,1)S(1)} %get-tuple-element.93), channel_id=1, source_target_pairs={{64,0},{97,32},{1,64},{32,96},{65,1},{96,33},{0,65},{33,97},{72,8}... | collective-permute-start | bytes 835592 | tf_op jit(solution)/shard_map/ppermute | solution.py:42
  80.8 7.8 %collective-permute-start.25 = (bf16[272,512]{1,0:T(8,128)(2,1)S(1)}, bf16[272,512]{1,0:T(8,128)(2,1)S(1)}, u32[]{:S(2)}, u32[]{:S(2)}) collective-permute-start(bf16[272,512]{1,0:T(8,128)(2,1)S(1)} %sum_two.1), channel_id=1, source_target_pairs={{65,0},{96,32},{0,64},{33,96},{64,1},{97,33},{1,65},{32,97},{73,8}... | collective-permute-start | bytes 835592 | tf_op jit(solution)/shard_map/ppermute | solution.py:42

commit v10 on v8

--- a/solution.py
+++ b/solution.py
@@ -175,24 +175,20 @@
             start = places[n] * TILE
             unit_ref[start : start + col_ref.shape[0]] = col_ref[...]
 
-        @pl.loop(0, col_ref.shape[0] // ROWS)
-        def _(m):
-            here = pl.ds(pl.multiple_of(places[n] * TILE + m * ROWS, ROWS), ROWS)
-            cols = col_ref[pl.ds(pl.multiple_of(m * ROWS, ROWS), ROWS), :]
-            by_col = col_sums_ref[:, here]
-            for k, ref in enumerate(row_refs):
-                start = rows_here[k // 2] * 1024 + (k % 2) * 512
-                part = slice(start, start + 512)
-                e = jnp.exp2(lax.dot_general(ref[...], cols, NT, preferred_element_type=F32))
-                if first and n == 0 and k == 0:
-                    i = lax.broadcasted_iota(jnp.int32, (ROWS, ROWS), 0)
-                    j = lax.broadcasted_iota(jnp.int32, (ROWS, ROWS), 1)
-                    own = jnp.where(i == j + m * ROWS, 0.0, e[:ROWS])
-                    e = jnp.concatenate([own, e[ROWS:]], axis=0)
-                exps_ref[part, here] = e.astype(BF16)
-                sums_ref[part] += e[:, :128] + e[:, 128:]
-                by_col += jnp.sum(e.reshape(-1, 8, ROWS), axis=0)
-            col_sums_ref[:, here] = by_col
+        here = slice(places[n] * TILE, places[n] * TILE + TILE)
+        by_col = col_sums_ref[:, here]
+        for k, ref in enumerate(row_refs):
+            start = rows_here[k // 2] * 1024 + (k % 2) * 512
+            part = slice(start, start + 512)
+            e = jnp.exp2(lax.dot_general(ref[...], col_ref[...], NT, preferred_element_type=F32))
+            if first and n == 0 and k == 0:
+                i = lax.broadcasted_iota(jnp.int32, (ROWS, TILE), 0)
+                j = lax.broadcasted_iota(jnp.int32, (ROWS, TILE), 1)
+                e = jnp.concatenate([jnp.where(i == j, 0.0, e[:ROWS]), e[ROWS:]], axis=0)
+            exps_ref[part, here] = e.astype(BF16)
+            sums_ref[part] += (e[:, :128] + e[:, 128:256]) + (e[:, 256:384] + e[:, 384:])
+            by_col += jnp.sum(e.reshape(-1, 8, TILE), axis=0)
+        col_sums_ref[:, here] = by_col
 
     if last:
         line_ref, col_line_ref = refs[4:]
@@ -406,9 +402,9 @@
     by_col = col_sums + swap(col_sums, "first", 0)
     by_col = by_col + swap(after(by_col, by_row), "first", 1)
     by_row = by_row + swap(by_row, "z", 0)
-    by_col = by_col + swap(after(by_col, by_row), "second", 0)
+    by_col = by_col + swap(by_col, "second", 0)
+    by_col = after(by_col, by_row)
     by_row = [by_row, swap(by_row, "z", 1)]
-    by_col = after(by_col, by_row[1])
     by_col = [by_col, swap(by_col, "second", 1)]
     arow, acol, loss = make_totals(info, by_row, by_col)
 

time: 90.4 us -> 89.8 us (level)
  Pallas kernels: 29 us -> 25.7 us
  waiting for transfers between devices: 22.4 us -> 23.9 us
    pallas_call x6, Pallas kernels: 17 us -> 13.7 us  [make_exps(): pl.pallas_call(functools.partial(exps_kernel, places, rows_here, first, l...]
    ppermute x20, waiting for transfers between devices: 12.4 us -> 14.3 us  [get(): return lax.ppermute(value, AXES, pairs)]
  transfers between devices with their start and end apart: 26 -> 26, of which waited for: 14 -> 14; matrix products, arithmetic and copies ran while one was open for 0% -> 0% of each run, Pallas kernels for 23% -> 20%
where the time goes in v10:
time: 89.8 us; the launch traced here: 89.3 us
  starting transfers between devices  37.6 us (42%)
  Pallas kernels  25.7 us (29%)
  waiting for transfers between devices  23.9 us (27%)
  local copies, waits for them, and re-layouts  1.1 us (1%)
    ppermute x20, starting transfers between devices, get(): return lax.ppermute(value, AXES, pairs)  26.6 us
    ppermute x20, waiting for transfers between devices, get(): return lax.ppermute(value, AXES, pairs)  14.3 us
    pallas_call x6, Pallas kernels, make_exps(): pl.pallas_call(functools.partial(exps_kernel, places, rows_here, first, l...  13.7 us
    ppermute x6, starting transfers between devices, swap(): return lax.ppermute(value, AXES, pairs)  11 us
    ppermute x6, waiting for transfers between devices, swap(): return lax.ppermute(value, AXES, pairs)  9.54 us
    pallas_call x5, Pallas kernels, make_grads(): pl.pallas_call(functools.partial(grads_kernel, pieces, adds, carry is not...  9.47 us
  transfers between devices with their start and end apart: 26, of which 14 were waited for; matrix products, arithmetic and copies ran while one was open for 0% of the time, Pallas kernels for 20%

profile of v10, /device:TPU:0, one launch (start us, length us, event | category | flops | bytes accessed | tf_op | source)
XLA Modules:
  0.0 89.3 jit_solution(6741754458891838477)
XLA Ops:
  1.7 2.1 %collective-permute-start = (bf16[256,512]{1,0:T(8,128)(2,1)S(1)}, bf16[256,512]{1,0:T(8,128)(2,1)S(1)}, u32[]{:S(2)}, u32[]{:S(2)}) collective-permute-start(bf16[256,512]{1,0:T(8,128)(2,1)S(1)} %get-tuple-element.50), channel_id=1, source_target_pairs={{65,0},{96,32},{0,64},{33,96},{64,1},{97,33},{1,65},{32,97},{73,8}... | collective-permute-start | bytes 786440 | tf_op jit(solution)/shard_map/ppermute | solution.py:42
  3.8 1.5 %collective-permute-start.5 = (bf16[256,512]{1,0:T(8,128)(2,1)S(1)}, bf16[256,512]{1,0:T(8,128)(2,1)S(1)}, u32[]{:S(2)}, u32[]{:S(2)}) collective-permute-start(bf16[256,512]{1,0:T(8,128)(2,1)S(1)} %get-tuple-element.52.unit_ref), channel_id=1, source_target_pairs={{6,0},{56,32},{70,64},{120,96},{7,1},{57,33},{71,65},{121,97},{14,... | collective-permute-start | bytes 786440 | tf_op jit(solution)/shard_map/ppermute | solution.py:42
  5.3 1.7 %collective-permute-start.6 = (bf16[256,512]{1,0:T(8,128)(2,1)S(1)}, bf16[256,512]{1,0:T(8,128)(2,1)S(1)}, u32[]{:S(2)}, u32[]{:S(2)}) collective-permute-start(bf16[256,512]{1,0:T(8,128)(2,1)S(1)} %get-tuple-element.52.unit_ref), channel_id=1, source_target_pairs={{2,0},{40,32},{66,64},{104,96},{3,1},{41,33},{67,65},{105,97},{10,... | collective-permute-start | bytes 786440 | tf_op jit(solution)/shard_map/ppermute | solution.py:42
  7.0 1.8 %collective-permute-start.7 = (bf16[256,512]{1,0:T(8,128)(2,1)S(1)}, bf16[256,512]{1,0:T(8,128)(2,1)S(1)}, u32[]{:S(2)}, u32[]{:S(2)}) collective-permute-start(bf16[256,512]{1,0:T(8,128)(2,1)S(1)} %get-tuple-element.52.unit_ref), channel_id=1, source_target_pairs={{4,0},{48,32},{68,64},{112,96},{5,1},{49,33},{69,65},{113,97},{12,... | collective-permute-start | bytes 786440 | tf_op jit(solution)/shard_map/ppermute | solution.py:42
  8.9 2.2 %collective-permute-start.2 = (bf16[256,512]{1,0:T(8,128)(2,1)S(1)}, bf16[256,512]{1,0:T(8,128)(2,1)S(1)}, u32[]{:S(2)}, u32[]{:S(2)}) collective-permute-start(bf16[256,512]{1,0:T(8,128)(2,1)S(1)} %get-tuple-element.50), channel_id=1, source_target_pairs={{64,0},{97,32},{1,64},{32,96},{65,1},{96,33},{0,65},{33,97},{72,8}... | collective-permute-start | bytes 786440 | tf_op jit(solution)/shard_map/ppermute | solution.py:42
  11.4 2.4 %collective-permute-done.6 = bf16[256,512]{1,0:T(8,128)(2,1)S(1)} collective-permute-done((bf16[256,512]{1,0:T(8,128)(2,1)S(1)}, bf16[256,512]{1,0:T(8,128)(2,1)S(1)}, u32[]{:S(2)}, u32[]{:S(2)}) %collective-permute-start.6) | collective-permute-done | bytes 262176 | tf_op jit(solution)/shard_map/ppermute | solution.py:42
  13.8 2.0 %collective-permute-start.3 = (bf16[256,512]{1,0:T(8,128)(2,1)S(1)}, bf16[256,512]{1,0:T(8,128)(2,1)S(1)}, u32[]{:S(2)}, u32[]{:S(2)}) collective-permute-start(bf16[256,512]{1,0:T(8,128)(2,1)S(1)} %collective-permute-done), channel_id=1, source_target_pairs={{65,0},{96,32},{0,64},{33,96},{64,1},{97,33},{1,65},{32,97},{73,8}... | collective-permute-start | bytes 786440 | tf_op jit(solution)/shard_map/ppermute | solution.py:42
  15.8 1.6 %collective-permute-start.10 = (bf16[512,512]{1,0:T(8,128)(2,1)S(1)}, bf16[512,512]{1,0:T(8,128)(2,1)S(1)}, u32[]{:S(2)}, u32[]{:S(2)}) collective-permute-start(bf16[512,512]{1,0:T(8,128)(2,1)S(1)} %constant_dynamic-update-slice_fusion.6.refs_3_), channel_id=1, source_target_pairs={{24,0},{38,32},{88,64},{102,96},{25,1},{39,33},{89,65},{103,97},{0... | collective-permute-start | bytes 1572872 | tf_op jit(solution)/shard_map/ppermute | solution.py:42
  17.4 1.7 %collective-permute-start.12 = (bf16[512,512]{1,0:T(8,128)(2,1)S(1)}, bf16[512,512]{1,0:T(8,128)(2,1)S(1)}, u32[]{:S(2)}, u32[]{:S(2)}) collective-permute-start(bf16[512,512]{1,0:T(8,128)(2,1)S(1)} %constant_dynamic-update-slice_fusion.6.refs_3_), channel_id=1, source_target_pairs={{8,0},{34,32},{72,64},{98,96},{9,1},{35,33},{73,65},{99,97},{16,8}... | collective-permute-start | bytes 1572872 | tf_op jit(solution)/shard_map/ppermute | solution.py:42
  19.1 1.9 %collective-permute-start.8 = (bf16[512,512]{1,0:T(8,128)(2,1)S(1)}, bf16[512,512]{1,0:T(8,128)(2,1)S(1)}, u32[]{:S(2)}, u32[]{:S(2)}) collective-permute-start(bf16[512,512]{1,0:T(8,128)(2,1)S(1)} %constant_dynamic-update-slice_fusion.4.refs_4_), channel_id=1, source_target_pairs={{8,0},{34,32},{72,64},{98,96},{9,1},{35,33},{73,65},{99,97},{16,8}... | collective-permute-start | bytes 1572872 | tf_op jit(solution)/shard_map/ppermute | solution.py:42
  21.4 1.6 %collective-permute-start.9 = (bf16[512,512]{1,0:T(8,128)(2,1)S(1)}, bf16[512,512]{1,0:T(8,128)(2,1)S(1)}, u32[]{:S(2)}, u32[]{:S(2)}) collective-permute-start(bf16[512,512]{1,0:T(8,128)(2,1)S(1)} %constant_dynamic-update-slice_fusion.4.refs_4_), channel_id=1, source_target_pairs={{24,0},{38,32},{88,64},{102,96},{25,1},{39,33},{89,65},{103,97},{0... | collective-permute-start | bytes 1572872 | tf_op jit(solution)/shard_map/ppermute | solution.py:42
  23.1 1.9 %exps0.1 = (f32[2048,128]{1,0:T(8,128)S(1)}, f32[8,4096]{1,0:T(8,128)S(1)}, bf16[2048,4096]{1,0:T(8,128)(2,1)S(1)}, bf16[4096,512]{1,0:T(8,128)(2,1)S(1)}) custom-call(s32[4]{0:T(128)S(1)} %pad_add_fusion.refs_0_.info_ref, bf16[512,512]{1,0:T(8,128)(2,1)S(1)} %constant_dynamic-update-slice_fusion.refs_1_, ...), custom_call_target="tpu_custom_call" | custom-call | flops 8589934592 | bytes 8388608 | tf_op jit(solution)/shard_map/exps0/pallas_call | solution.py:219
  25.1 1.9 %exps1.1 = (f32[2048,128]{1,0:T(8,128)S(1)}, f32[8,4096]{1,0:T(8,128)S(1)}, bf16[2048,4096]{1,0:T(8,128)(2,1)S(1)}, bf16[4096,512]{1,0:T(8,128)(2,1)S(1)}) custom-call(s32[4]{0:T(128)S(1)} %pad_add_fusion.refs_0_.info_ref, ...), custom_call_target="tpu_custom_call", output_to_operand_aliasing={{0}: (5, {}), {1}: (6, {}), {2}: (7, {}), {3}: (8, {})} | custom-call | flops 8589934592 | bytes 8388608 | tf_op jit(solution)/shard_map/exps1/pallas_call | solution.py:219
  27.0 1.6 %collective-permute-start.13 = (bf16[512,512]{1,0:T(8,128)(2,1)S(1)}, bf16[512,512]{1,0:T(8,128)(2,1)S(1)}, u32[]{:S(2)}, u32[]{:S(2)}) collective-permute-start(bf16[512,512]{1,0:T(8,128)(2,1)S(1)} %collective-permute-done.10.refs_5_), channel_id=1, source_target_pairs={{24,0},{38,32},{88,64},{102,96},{25,1},{39,33},{89,65},{103,97},{0... | collective-permute-start | bytes 1572872 | tf_op jit(solution)/shard_map/ppermute | solution.py:42
  28.6 1.9 %exps2.1 = (f32[2048,128]{1,0:T(8,128)S(1)}, f32[8,4096]{1,0:T(8,128)S(1)}, bf16[2048,4096]{1,0:T(8,128)(2,1)S(1)}, bf16[4096,512]{1,0:T(8,128)(2,1)S(1)}) custom-call(s32[4]{0:T(128)S(1)} %pad_add_fusion.refs_0_.info_ref, ...), custom_call_target="tpu_custom_call", output_to_operand_aliasing={{0}: (6, {}), {1}: (7, {}), {2}: (8, {}), {3}: (9, {})} | custom-call | flops 4294967296 | bytes 2097152 | tf_op jit(solution)/shard_map/exps2/pallas_call | solution.py:219
  30.5 1.7 %collective-permute-done.8.refs_7_ = bf16[512,512]{1,0:T(8,128)(2,1)S(1)} collective-permute-done((bf16[512,512]{1,0:T(8,128)(2,1)S(1)}, bf16[512,512]{1,0:T(8,128)(2,1)S(1)}, u32[]{:S(2)}, u32[]{:S(2)}) %collective-permute-start.8) | collective-permute-done | bytes 524320 | tf_op jit(solution)/shard_map/ppermute | solution.py:42
  32.3 2.9 %collective-permute-start.11 = (bf16[512,512]{1,0:T(8,128)(2,1)S(1)}, bf16[512,512]{1,0:T(8,128)(2,1)S(1)}, u32[]{:S(2)}, u32[]{:S(2)}) collective-permute-start(bf16[512,512]{1,0:T(8,128)(2,1)S(1)} %collective-permute-done.8.refs_7_), channel_id=1, source_target_pairs={{8,0},{34,32},{72,64},{98,96},{9,1},{35,33},{73,65},{99,97},{16,8}... | collective-permute-start | bytes 1572872 | tf_op jit(solution)/shard_map/ppermute | solution.py:42
  35.4 4.2 %exps3.1 = (f32[2048,128]{1,0:T(8,128)S(1)}, f32[8,4096]{1,0:T(8,128)S(1)}, bf16[2048,4096]{1,0:T(8,128)(2,1)S(1)}, bf16[4096,512]{1,0:T(8,128)(2,1)S(1)}) custom-call(s32[4]{0:T(128)S(1)} %pad_add_fusion.refs_0_.info_ref, ...), custom_call_target="tpu_custom_call", output_to_operand_aliasing={{0}: (8, {}), {1}: (9, {}), {2}: (10, {}), {3}: (11, {})} | custom-call | tf_op jit(solution)/shard_map/exps3/pallas_call | solution.py:219
  39.7 1.9 %exps4.1 = (f32[2048,128]{1,0:T(8,128)S(1)}, f32[8,4096]{1,0:T(8,128)S(1)}, bf16[2048,4096]{1,0:T(8,128)(2,1)S(1)}, bf16[4096,512]{1,0:T(8,128)(2,1)S(1)}) custom-call(s32[4]{0:T(128)S(1)} %pad_add_fusion.refs_0_.info_ref, ...), custom_call_target="tpu_custom_call", output_to_operand_aliasing={{0}: (6, {}), {1}: (7, {}), {2}: (8, {}), {3}: (9, {})} | custom-call | tf_op jit(solution)/shard_map/exps4/pallas_call | solution.py:219
  41.8 2.0 %exps5.1 = (f32[2048,128]{1,0:T(8,128)S(1)}, f32[8,4096]{1,0:T(8,128)S(1)}, bf16[2048,4096]{1,0:T(8,128)(2,1)S(1)}, bf16[4096,512]{1,0:T(8,128)(2,1)S(1)}, f32[8,256]{1,0:T(8,128)S(1)}, /*index=5*/f32[24,256]{1,0:T(8,128)S(1)}) custom-call(s32[4]{0:T(128)S(1)} %pad_add_fusion.refs_0_.info_ref, ...), custom_call_target="tpu_custom_call", output_to_operand_aliasing={{0}: (6, {}), {1}: (7, {}), {2}: (8, {}), {3}: (9, {})} | custom-call | tf_op jit(solution)/shard_map/exps5/pallas_call | solution.py:219
  45.6 2.1 %collective-permute-done.17 = f32[24,256]{1,0:T(8,128)S(1)} collective-permute-done((f32[24,256]{1,0:T(8,128)S(1)}, f32[24,256]{1,0:T(8,128)S(1)}, u32[]{:S(2)}, u32[]{:S(2)}) %collective-permute-start.17) | collective-permute-done | bytes 24608 | tf_op jit(solution)/shard_map/ppermute | solution.py:55
  47.7 3.7 %collective-permute-start.18 = (f32[24,256]{1,0:T(8,128)S(1)}, f32[24,256]{1,0:T(8,128)S(1)}, u32[]{:S(2)}, u32[]{:S(2)}) collective-permute-start(f32[24,256]{1,0:T(8,128)S(1)} %add.21), channel_id=1, source_target_pairs={{6,0},{56,32},{70,64},{120,96},{7,1},{57,33},{71,65},{121,97},{14,... | collective-permute-start | bytes 73736 | tf_op jit(solution)/shard_map/ppermute | solution.py:55
  51.4 1.8 %collective-permute-done.18 = f32[24,256]{1,0:T(8,128)S(1)} collective-permute-done((f32[24,256]{1,0:T(8,128)S(1)}, f32[24,256]{1,0:T(8,128)S(1)}, u32[]{:S(2)}, u32[]{:S(2)}) %collective-permute-start.18) | collective-permute-done | bytes 24608 | tf_op jit(solution)/shard_map/ppermute | solution.py:55
  54.4 1.6 %collective-permute-start.15 = (f32[8,256]{1,0:T(8,128)S(1)}, f32[8,256]{1,0:T(8,128)S(1)}, u32[]{:S(2)}, u32[]{:S(2)}) collective-permute-start(f32[8,256]{1,0:T(8,128)S(1)} %add.19), channel_id=1, source_target_pairs={{64,0},{96,32},{0,64},{32,96},{65,1},{97,33},{1,65},{33,97},{72,8}... | collective-permute-start | bytes 24584 | tf_op jit(solution)/shard_map/ppermute | solution.py:55
  56.0 2.0 %collective-permute-done.15 = f32[8,256]{1,0:T(8,128)S(1)} collective-permute-done((f32[8,256]{1,0:T(8,128)S(1)}, f32[8,256]{1,0:T(8,128)S(1)}, u32[]{:S(2)}, u32[]{:S(2)}) %collective-permute-start.15) | collective-permute-done | bytes 8224 | tf_op jit(solution)/shard_map/ppermute | solution.py:55
  58.0 2.7 %collective-permute-start.20 = (f32[24,256]{1,0:T(8,128)S(1)}, f32[24,256]{1,0:T(8,128)S(1)}, u32[]{:S(2)}, u32[]{:S(2)}) collective-permute-start(f32[24,256]{1,0:T(8,128)S(1)} %add.23.refs_2_), channel_id=1, source_target_pairs={{24,0},{38,32},{88,64},{102,96},{25,1},{39,33},{89,65},{103,97},{1... | collective-permute-start | bytes 73736 | tf_op jit(solution)/shard_map/ppermute | solution.py:55
  62.0 3.5 %collective-permute-done.16.refs_1_ = f32[8,256]{1,0:T(8,128)S(1)} collective-permute-done((f32[8,256]{1,0:T(8,128)S(1)}, f32[8,256]{1,0:T(8,128)S(1)}, u32[]{:S(2)}, u32[]{:S(2)}) %collective-permute-start.16) | collective-permute-done | bytes 8224 | tf_op jit(solution)/shard_map/ppermute | solution.py:55
  66.4 3.4 %grads_core.1 = bf16[784,512]{1,0:T(8,128)(2,1)S(1)} custom-call(f32[32,128]{1,0:T(8,128)S(1)} %get-tuple-element.90.acol_ref, bf16[2048,128]{1,0:T(8,128)(2,1)S(1)} %get-tuple-element.83.arow_ref, bf16[2048,4096]{1,0:T(8,128)(2,1)S(1)} %get-tuple-element.84.exps_ref, bf16[4096,512]{1,0:T(8,128)(2,1)S(1)} %get-tuple-element.85.unit_ref, ...), custom_call_target="tpu_custom_call" | custom-call | flops 3221225472 | bytes 10485760 | tf_op jit(solution)/shard_map/grads_core/pallas_call | solution.py:309
  73.0 2.3 %grads_near.1 = (bf16[272,512]{1,0:T(8,128)(2,1)S(1)}, f32[256,512]{1,0:T(8,128)S(1)}) custom-call(f32[32,128]{1,0:T(8,128)S(1)} %get-tuple-element.90.acol_ref, bf16[2048,128]{1,0:T(8,128)(2,1)S(1)} %get-tuple-element.83.arow_ref, bf16[2048,4096]{1,0:T(8,128)(2,1)S(1)} %get-tuple-element.84.exps_ref, bf16[4096,512]{1,0:T(8,128)(2,1)S(1)} %get-tuple-element.85.unit_ref, ...), custom_call_target="tpu_custom_call" | custom-call | flops 2147483648 | bytes 8388608 | tf_op jit(solution)/shard_map/grads_near/pallas_call | solution.py:309
  77.4 2.1 %collective-permute-start.24 = (bf16[272,512]{1,0:T(8,128)(2,1)S(1)}, bf16[272,512]{1,0:T(8,128)(2,1)S(1)}, u32[]{:S(2)}, u32[]{:S(2)}) collective-permute-start(bf16[272,512]{1,0:T(8,128)(2,1)S(1)} %get-tuple-element.91), channel_id=1, source_target_pairs={{64,0},{97,32},{1,64},{32,96},{65,1},{96,33},{0,65},{33,97},{72,8}... | collective-permute-start | bytes 835592 | tf_op jit(solution)/shard_map/ppermute | solution.py:42
  81.7 5.1 %collective-permute-done.24.one_ref = bf16[272,512]{1,0:T(8,128)(2,1)S(1)} collective-permute-done((bf16[272,512]{1,0:T(8,128)(2,1)S(1)}, bf16[272,512]{1,0:T(8,128)(2,1)S(1)}, u32[]{:S(2)}, u32[]{:S(2)}) %collective-permute-start.24) | collective-permute-done | bytes 278560 | tf_op jit(solution)/shard_map/ppermute | solution.py:42
  86.8 1.4 %collective-permute-done.25.two_ref = bf16[272,512]{1,0:T(8,128)(2,1)S(1)} collective-permute-done((bf16[272,512]{1,0:T(8,128)(2,1)S(1)}, bf16[272,512]{1,0:T(8,128)(2,1)S(1)}, u32[]{:S(2)}, u32[]{:S(2)}) %collective-permute-start.25) | collective-permute-done | bytes 278560 | tf_op jit(solution)/shard_map/ppermute | solution.py:42
  (57 shorter events, 16.2 us)
Async XLA Ops:
  0.6 1.0 %copy-start = (bf16[256,512]{1,0:T(8,128)(2,1)S(1)}, bf16[256,512]{1,0:T(8,128)(2,1)}, u32[]{:S(2)}) copy-start(bf16[256,512]{1,0:T(8,128)(2,1)} %z_ref.3) | copy-start | bytes 786436
  1.7 9.4 %collective-permute-start = (bf16[256,512]{1,0:T(8,128)(2,1)S(1)}, bf16[256,512]{1,0:T(8,128)(2,1)S(1)}, u32[]{:S(2)}, u32[]{:S(2)}) collective-permute-start(bf16[256,512]{1,0:T(8,128)(2,1)S(1)} %get-tuple-element.50), channel_id=1, source_target_pairs={{65,0},{96,32},{0,64},{33,96},{64,1},{97,33},{1,65},{32,97},{73,8}... | collective-permute-start | bytes 786440 | tf_op jit(solution)/shard_map/ppermute | solution.py:42
  3.8 7.6 %collective-permute-start.5 = (bf16[256,512]{1,0:T(8,128)(2,1)S(1)}, bf16[256,512]{1,0:T(8,128)(2,1)S(1)}, u32[]{:S(2)}, u32[]{:S(2)}) collective-permute-start(bf16[256,512]{1,0:T(8,128)(2,1)S(1)} %get-tuple-element.52.unit_ref), channel_id=1, source_target_pairs={{6,0},{56,32},{70,64},{120,96},{7,1},{57,33},{71,65},{121,97},{14,... | collective-permute-start | bytes 786440 | tf_op jit(solution)/shard_map/ppermute | solution.py:42
  5.3 8.5 %collective-permute-start.6 = (bf16[256,512]{1,0:T(8,128)(2,1)S(1)}, bf16[256,512]{1,0:T(8,128)(2,1)S(1)}, u32[]{:S(2)}, u32[]{:S(2)}) collective-permute-start(bf16[256,512]{1,0:T(8,128)(2,1)S(1)} %get-tuple-element.52.unit_ref), channel_id=1, source_target_pairs={{2,0},{40,32},{66,64},{104,96},{3,1},{41,33},{67,65},{105,97},{10,... | collective-permute-start | bytes 786440 | tf_op jit(solution)/shard_map/ppermute | solution.py:42
  7.0 10.4 %collective-permute-start.7 = (bf16[256,512]{1,0:T(8,128)(2,1)S(1)}, bf16[256,512]{1,0:T(8,128)(2,1)S(1)}, u32[]{:S(2)}, u32[]{:S(2)}) collective-permute-start(bf16[256,512]{1,0:T(8,128)(2,1)S(1)} %get-tuple-element.52.unit_ref), channel_id=1, source_target_pairs={{4,0},{48,32},{68,64},{112,96},{5,1},{49,33},{69,65},{113,97},{12,... | collective-permute-start | bytes 786440 | tf_op jit(solution)/shard_map/ppermute | solution.py:42
  8.9 10.3 %collective-permute-start.2 = (bf16[256,512]{1,0:T(8,128)(2,1)S(1)}, bf16[256,512]{1,0:T(8,128)(2,1)S(1)}, u32[]{:S(2)}, u32[]{:S(2)}) collective-permute-start(bf16[256,512]{1,0:T(8,128)(2,1)S(1)} %get-tuple-element.50), channel_id=1, source_target_pairs={{64,0},{97,32},{1,64},{32,96},{65,1},{96,33},{0,65},{33,97},{72,8}... | collective-permute-start | bytes 786440 | tf_op jit(solution)/shard_map/ppermute | solution.py:42
  11.2 11.9 %collective-permute-start.1 = (bf16[512,512]{1,0:T(8,128)(2,1)S(1)}, bf16[512,512]{1,0:T(8,128)(2,1)S(1)}, u32[]{:S(2)}, u32[]{:S(2)}) collective-permute-start(bf16[512,512]{1,0:T(8,128)(2,1)S(1)} %constant_dynamic-update-slice_fusion.refs_1_), channel_id=1, source_target_pairs={{32,0},{0,32},{96,64},{64,96},{33,1},{1,33},{97,65},{65,97},{40,8}... | collective-permute-start | bytes 1572872 | tf_op jit(solution)/shard_map/ppermute | solution.py:42
  13.8 7.7 %collective-permute-start.3 = (bf16[256,512]{1,0:T(8,128)(2,1)S(1)}, bf16[256,512]{1,0:T(8,128)(2,1)S(1)}, u32[]{:S(2)}, u32[]{:S(2)}) collective-permute-start(bf16[256,512]{1,0:T(8,128)(2,1)S(1)} %collective-permute-done), channel_id=1, source_target_pairs={{65,0},{96,32},{0,64},{33,96},{64,1},{97,33},{1,65},{32,97},{73,8}... | collective-permute-start | bytes 786440 | tf_op jit(solution)/shard_map/ppermute | solution.py:42
  15.8 11.2 %collective-permute-start.10 = (bf16[512,512]{1,0:T(8,128)(2,1)S(1)}, bf16[512,512]{1,0:T(8,128)(2,1)S(1)}, u32[]{:S(2)}, u32[]{:S(2)}) collective-permute-start(bf16[512,512]{1,0:T(8,128)(2,1)S(1)} %constant_dynamic-update-slice_fusion.6.refs_3_), channel_id=1, source_target_pairs={{24,0},{38,32},{88,64},{102,96},{25,1},{39,33},{89,65},{103,97},{0... | collective-permute-start | bytes 1572872 | tf_op jit(solution)/shard_map/ppermute | solution.py:42
  17.4 9.5 %collective-permute-start.12 = (bf16[512,512]{1,0:T(8,128)(2,1)S(1)}, bf16[512,512]{1,0:T(8,128)(2,1)S(1)}, u32[]{:S(2)}, u32[]{:S(2)}) collective-permute-start(bf16[512,512]{1,0:T(8,128)(2,1)S(1)} %constant_dynamic-update-slice_fusion.6.refs_3_), channel_id=1, source_target_pairs={{8,0},{34,32},{72,64},{98,96},{9,1},{35,33},{73,65},{99,97},{16,8}... | collective-permute-start | bytes 1572872 | tf_op jit(solution)/shard_map/ppermute | solution.py:42
  19.1 13.1 %collective-permute-start.8 = (bf16[512,512]{1,0:T(8,128)(2,1)S(1)}, bf16[512,512]{1,0:T(8,128)(2,1)S(1)}, u32[]{:S(2)}, u32[]{:S(2)}) collective-permute-start(bf16[512,512]{1,0:T(8,128)(2,1)S(1)} %constant_dynamic-update-slice_fusion.4.refs_4_), channel_id=1, source_target_pairs={{8,0},{34,32},{72,64},{98,96},{9,1},{35,33},{73,65},{99,97},{16,8}... | collective-permute-start | bytes 1572872 | tf_op jit(solution)/shard_map/ppermute | solution.py:42
  21.4 10.8 %collective-permute-start.9 = (bf16[512,512]{1,0:T(8,128)(2,1)S(1)}, bf16[512,512]{1,0:T(8,128)(2,1)S(1)}, u32[]{:S(2)}, u32[]{:S(2)}) collective-permute-start(bf16[512,512]{1,0:T(8,128)(2,1)S(1)} %constant_dynamic-update-slice_fusion.4.refs_4_), channel_id=1, source_target_pairs={{24,0},{38,32},{88,64},{102,96},{25,1},{39,33},{89,65},{103,97},{0... | collective-permute-start | bytes 1572872 | tf_op jit(solution)/shard_map/ppermute | solution.py:42
  23.1 2.0 %collective-permute-start.4 = (bf16[512,512]{1,0:T(8,128)(2,1)S(1)}, bf16[512,512]{1,0:T(8,128)(2,1)S(1)}, u32[]{:S(2)}, u32[]{:S(2)}) collective-permute-start(bf16[512,512]{1,0:T(8,128)(2,1)S(1)} %constant_dynamic-update-slice_fusion.2.refs_1_.refs_3_), channel_id=1, source_target_pairs={{32,0},{0,32},{96,64},{64,96},{33,1},{1,33},{97,65},{65,97},{40,8}... | collective-permute-start | bytes 1572872 | tf_op jit(solution)/shard_map/ppermute | solution.py:42
  27.0 8.2 %copy-start.2 = (s32[256]{0:T(256)S(1)}, s32[256]{0:T(256)}, u32[]{:S(2)}) copy-start(s32[256]{0:T(256)} %param.3) | copy-start | bytes 3076
  27.0 12.6 %collective-permute-start.13 = (bf16[512,512]{1,0:T(8,128)(2,1)S(1)}, bf16[512,512]{1,0:T(8,128)(2,1)S(1)}, u32[]{:S(2)}, u32[]{:S(2)}) collective-permute-start(bf16[512,512]{1,0:T(8,128)(2,1)S(1)} %collective-permute-done.10.refs_5_), channel_id=1, source_target_pairs={{24,0},{38,32},{88,64},{102,96},{25,1},{39,33},{89,65},{103,97},{0... | collective-permute-start | bytes 1572872 | tf_op jit(solution)/shard_map/ppermute | solution.py:42
  32.3 9.6 %collective-permute-start.11 = (bf16[512,512]{1,0:T(8,128)(2,1)S(1)}, bf16[512,512]{1,0:T(8,128)(2,1)S(1)}, u32[]{:S(2)}, u32[]{:S(2)}) collective-permute-start(bf16[512,512]{1,0:T(8,128)(2,1)S(1)} %collective-permute-done.8.refs_7_), channel_id=1, source_target_pairs={{8,0},{34,32},{72,64},{98,96},{9,1},{35,33},{73,65},{99,97},{16,8}... | collective-permute-start | bytes 1572872 | tf_op jit(solution)/shard_map/ppermute | solution.py:42
  43.8 3.9 %collective-permute-start.17 = (f32[24,256]{1,0:T(8,128)S(1)}, f32[24,256]{1,0:T(8,128)S(1)}, u32[]{:S(2)}, u32[]{:S(2)}) collective-permute-start(f32[24,256]{1,0:T(8,128)S(1)} %get-tuple-element.78), channel_id=1, source_target_pairs={{2,0},{40,32},{66,64},{104,96},{3,1},{41,33},{67,65},{105,97},{10,... | collective-permute-start | bytes 73736 | tf_op jit(solution)/shard_map/ppermute | solution.py:55
  44.4 1.2 %collective-permute-start.14 = (f32[8,256]{1,0:T(8,128)S(1)}, f32[8,256]{1,0:T(8,128)S(1)}, u32[]{:S(2)}, u32[]{:S(2)}) collective-permute-start(f32[8,256]{1,0:T(8,128)S(1)} %get-tuple-element.77), channel_id=1, source_target_pairs={{32,0},{0,32},{96,64},{64,96},{33,1},{1,33},{97,65},{65,97},{40,8}... | collective-permute-start | bytes 24584 | tf_op jit(solution)/shard_map/ppermute | solution.py:42
  47.7 5.5 %collective-permute-start.18 = (f32[24,256]{1,0:T(8,128)S(1)}, f32[24,256]{1,0:T(8,128)S(1)}, u32[]{:S(2)}, u32[]{:S(2)}) collective-permute-start(f32[24,256]{1,0:T(8,128)S(1)} %add.21), channel_id=1, source_target_pairs={{6,0},{56,32},{70,64},{120,96},{7,1},{57,33},{71,65},{121,97},{14,... | collective-permute-start | bytes 73736 | tf_op jit(solution)/shard_map/ppermute | solution.py:55
  53.2 4.8 %collective-permute-start.19 = (f32[24,256]{1,0:T(8,128)S(1)}, f32[24,256]{1,0:T(8,128)S(1)}, u32[]{:S(2)}, u32[]{:S(2)}) collective-permute-start(f32[24,256]{1,0:T(8,128)S(1)} %add.22), channel_id=1, source_target_pairs={{8,0},{34,32},{72,64},{98,96},{9,1},{35,33},{73,65},{99,97},{0,8},... | collective-permute-start | bytes 73736 | tf_op jit(solution)/shard_map/ppermute | solution.py:55
  54.4 3.7 %collective-permute-start.15 = (f32[8,256]{1,0:T(8,128)S(1)}, f32[8,256]{1,0:T(8,128)S(1)}, u32[]{:S(2)}, u32[]{:S(2)}) collective-permute-start(f32[8,256]{1,0:T(8,128)S(1)} %add.19), channel_id=1, source_target_pairs={{64,0},{96,32},{0,64},{32,96},{65,1},{97,33},{1,65},{33,97},{72,8}... | collective-permute-start | bytes 24584 | tf_op jit(solution)/shard_map/ppermute | solution.py:55
  58.0 7.5 %collective-permute-start.20 = (f32[24,256]{1,0:T(8,128)S(1)}, f32[24,256]{1,0:T(8,128)S(1)}, u32[]{:S(2)}, u32[]{:S(2)}) collective-permute-start(f32[24,256]{1,0:T(8,128)S(1)} %add.23.refs_2_), channel_id=1, source_target_pairs={{24,0},{38,32},{88,64},{102,96},{25,1},{39,33},{89,65},{103,97},{1... | collective-permute-start | bytes 73736 | tf_op jit(solution)/shard_map/ppermute | solution.py:55
  60.7 4.9 %collective-permute-start.16 = (f32[8,256]{1,0:T(8,128)S(1)}, f32[8,256]{1,0:T(8,128)S(1)}, u32[]{:S(2)}, u32[]{:S(2)}) collective-permute-start(f32[8,256]{1,0:T(8,128)S(1)} %add.20.refs_0_), channel_id=1, source_target_pairs={{65,0},{97,32},{1,64},{33,96},{64,1},{96,33},{0,65},{32,97},{73,8}... | collective-permute-start | bytes 24584 | tf_op jit(solution)/shard_map/ppermute | solution.py:55
  69.8 2.6 %collective-permute-start.21 = (bf16[784,512]{1,0:T(8,128)(2,1)S(1)}, bf16[784,512]{1,0:T(8,128)(2,1)S(1)}, u32[]{:S(2)}, u32[]{:S(2)}) collective-permute-start(bf16[784,512]{1,0:T(8,128)(2,1)S(1)} %grads_core.1), channel_id=1, source_target_pairs={{32,0},{0,32},{96,64},{64,96},{33,1},{1,33},{97,65},{65,97},{40,8}... | collective-permute-start | bytes 2408456 | tf_op jit(solution)/shard_map/ppermute | solution.py:42
  72.5 7.8 %collective-permute-start.22 = (bf16[272,512]{1,0:T(8,128)(2,1)S(1)}, bf16[272,512]{1,0:T(8,128)(2,1)S(1)}, u32[]{:S(2)}, u32[]{:S(2)}) collective-permute-start(bf16[272,512]{1,0:T(8,128)(2,1)S(1)} %sum_far.1.refs_1_.here_ref), channel_id=1, source_target_pairs={{65,0},{96,32},{0,64},{33,96},{64,1},{97,33},{1,65},{32,97},{73,8}... | collective-permute-start | bytes 835592 | tf_op jit(solution)/shard_map/ppermute | solution.py:42
  76.5 11.6 %copy-start.1 = (bf16[256,512]{1,0:T(8,128)(2,1)S(1)}, bf16[256,512]{1,0:T(8,128)(2,1)}, u32[]{:S(2)}) copy-start(bf16[256,512]{1,0:T(8,128)(2,1)} %z_ref.3) | copy-start | bytes 786436
  76.6 3.9 %collective-permute-start.23 = (bf16[256,512]{1,0:T(8,128)(2,1)S(1)}, bf16[256,512]{1,0:T(8,128)(2,1)S(1)}, u32[]{:S(2)}, u32[]{:S(2)}) collective-permute-start(bf16[256,512]{1,0:T(8,128)(2,1)S(1)} %grads_core_own.1), channel_id=1, source_target_pairs={{32,0},{0,32},{96,64},{64,96},{33,1},{1,33},{97,65},{65,97},{40,8}... | collective-permute-start | bytes 786440 | tf_op jit(solution)/shard_map/ppermute | solution.py:42
  77.4 9.4 %collective-permute-start.24 = (bf16[272,512]{1,0:T(8,128)(2,1)S(1)}, bf16[272,512]{1,0:T(8,128)(2,1)S(1)}, u32[]{:S(2)}, u32[]{:S(2)}) collective-permute-start(bf16[272,512]{1,0:T(8,128)(2,1)S(1)} %get-tuple-element.91), channel_id=1, source_target_pairs={{64,0},{97,32},{1,64},{32,96},{65,1},{96,33},{0,65},{33,97},{72,8}... | collective-permute-start | bytes 835592 | tf_op jit(solution)/shard_map/ppermute | solution.py:42
  80.4 7.8 %collective-permute-start.25 = (bf16[272,512]{1,0:T(8,128)(2,1)S(1)}, bf16[272,512]{1,0:T(8,128)(2,1)S(1)}, u32[]{:S(2)}, u32[]{:S(2)}) collective-permute-start(bf16[272,512]{1,0:T(8,128)(2,1)S(1)} %sum_two.1), channel_id=1, source_target_pairs={{65,0},{96,32},{0,64},{33,96},{64,1},{97,33},{1,65},{32,97},{73,8}... | collective-permute-start | bytes 835592 | tf_op jit(solution)/shard_map/ppermute | solution.py:42

commit v11 on v10

--- a/solution.py
+++ b/solution.py
@@ -378,7 +378,7 @@
     near = jnp.concatenate([scaled, z_one], axis=0)
     line0 = jnp.concatenate([after(unit, near), before], axis=0)
     line1 = jnp.concatenate([next_, far], axis=0)
-    before0, after0 = get(line0, second=-1), get(line0, second=1)
+    before0 = get(line0, second=-1)
     before1, after1 = get(line1, second=-1), get(line1, second=1)
     z_two = get(scaled, z_own=1)
     z_far = get(z_one, z_own=-1)
@@ -386,14 +386,15 @@
 
     mates, positive = make_mates(unit, partner)
     chain = make_exps(info, near, (0,), [line0, line1], (0, 1), None, None, 8, "exps0")
+    after0 = get(after(line0, line1), second=1)
+    far1 = get(after(after1, chain[0]), second=1)
     rest = jnp.concatenate([z_two, z_far], axis=0)
     rest = [rest, get(rest, core=1)]
     chain = make_exps(info, rest, (1,), [line0, line1], (0, 1), chain, None, 8, "exps1")
-    far0 = get(after(before0, after0, chain[0]), second=-1)
+    far0 = get(after(before0, chain[0]), second=-1)
     rows = near + rest
-    chain = make_exps(info, rows, (0, 1), [before0], (2,), chain, None, 4, "exps2")
-    far1 = get(after(after1, before1, chain[0]), second=1)
-    chain = make_exps(info, rows, (0, 1), [after0, before1, after1], (4, 3, 5), chain, None, 0, "exps3")
+    chain = make_exps(info, rows, (0, 1), [before0, after1], (2, 5), chain, None, 4, "exps2")
+    chain = make_exps(info, rows, (0, 1), [before1, after0], (3, 4), chain, None, 0, "exps3")
     chain = make_exps(info, rows, (0, 1), [far0], (6,), chain, None, 0, "exps4")
     chain = make_exps(info, rows, (0, 1), [far1], (7,), chain, positive, 0, "exps5")
     _, _, exps, units, sums, col_sums = chain

time: 89.8 us -> 88.9 us (0.990)
  starting transfers between devices: 37.6 us -> 33.1 us
  waiting for transfers between devices: 23.9 us -> 26.1 us
    ppermute x6, starting transfers between devices: 11 us -> 7.64 us  [swap(): return lax.ppermute(value, AXES, pairs)]
    ppermute x20, waiting for transfers between devices: 14.3 us -> 16.7 us  [get(): return lax.ppermute(value, AXES, pairs)]
    ppermute x20, starting transfers between devices: 26.6 us -> 25.5 us  [get(): return lax.ppermute(value, AXES, pairs)]
  transfers between devices with their start and end apart: 26 -> 26, of which waited for: 14 -> 15; matrix products, arithmetic and copies ran while one was open for 0% -> 0% of each run, Pallas kernels for 20% -> 21%
where the time goes in v11:
time: 88.9 us; the launch traced here: 87.7 us
  starting transfers between devices  33.1 us (37%)
  waiting for transfers between devices  26.1 us (29%)
  Pallas kernels  25.7 us (29%)
  local copies, waits for them, and re-layouts  1.78 us (2%)
  between operations  0.92 us (1%)
    ppermute x20, starting transfers between devices, get(): return lax.ppermute(value, AXES, pairs)  25.5 us
    ppermute x20, waiting for transfers between devices, get(): return lax.ppermute(value, AXES, pairs)  16.7 us
    pallas_call x6, Pallas kernels, make_exps(): pl.pallas_call(functools.partial(exps_kernel, places, rows_here, first, l...  13.7 us
    pallas_call x5, Pallas kernels, make_grads(): pl.pallas_call(functools.partial(grads_kernel, pieces, adds, carry is not...  9.48 us
    ppermute x6, waiting for transfers between devices, swap(): return lax.ppermute(value, AXES, pairs)  9.4 us
    ppermute x6, starting transfers between devices, swap(): return lax.ppermute(value, AXES, pairs)  7.64 us
  transfers between devices with their start and end apart: 26, of which 15 were waited for; matrix products, arithmetic and copies ran while one was open for 0% of the time, Pallas kernels for 21%

profile of v11, /device:TPU:0, one launch (start us, length us, event | category | flops | bytes accessed | tf_op | source)
XLA Modules:
  0.0 87.7 jit_solution(15735870280734987537)
XLA Ops:
  1.7 2.1 %collective-permute-start = (bf16[256,512]{1,0:T(8,128)(2,1)S(1)}, bf16[256,512]{1,0:T(8,128)(2,1)S(1)}, u32[]{:S(2)}, u32[]{:S(2)}) collective-permute-start(bf16[256,512]{1,0:T(8,128)(2,1)S(1)} %get-tuple-element.51), channel_id=1, source_target_pairs={{65,0},{96,32},{0,64},{33,96},{64,1},{97,33},{1,65},{32,97},{73,8}... | collective-permute-start | bytes 786440 | tf_op jit(solution)/shard_map/ppermute | solution.py:42
  3.8 1.5 %collective-permute-start.5 = (bf16[256,512]{1,0:T(8,128)(2,1)S(1)}, bf16[256,512]{1,0:T(8,128)(2,1)S(1)}, u32[]{:S(2)}, u32[]{:S(2)}) collective-permute-start(bf16[256,512]{1,0:T(8,128)(2,1)S(1)} %get-tuple-element.53.unit_ref), channel_id=1, source_target_pairs={{6,0},{56,32},{70,64},{120,96},{7,1},{57,33},{71,65},{121,97},{14,... | collective-permute-start | bytes 786440 | tf_op jit(solution)/shard_map/ppermute | solution.py:42
  5.3 1.7 %collective-permute-start.6 = (bf16[256,512]{1,0:T(8,128)(2,1)S(1)}, bf16[256,512]{1,0:T(8,128)(2,1)S(1)}, u32[]{:S(2)}, u32[]{:S(2)}) collective-permute-start(bf16[256,512]{1,0:T(8,128)(2,1)S(1)} %get-tuple-element.53.unit_ref), channel_id=1, source_target_pairs={{2,0},{40,32},{66,64},{104,96},{3,1},{41,33},{67,65},{105,97},{10,... | collective-permute-start | bytes 786440 | tf_op jit(solution)/shard_map/ppermute | solution.py:42
  7.0 1.8 %collective-permute-start.7 = (bf16[256,512]{1,0:T(8,128)(2,1)S(1)}, bf16[256,512]{1,0:T(8,128)(2,1)S(1)}, u32[]{:S(2)}, u32[]{:S(2)}) collective-permute-start(bf16[256,512]{1,0:T(8,128)(2,1)S(1)} %get-tuple-element.53.unit_ref), channel_id=1, source_target_pairs={{4,0},{48,32},{68,64},{112,96},{5,1},{49,33},{69,65},{113,97},{12,... | collective-permute-start | bytes 786440 | tf_op jit(solution)/shard_map/ppermute | solution.py:42
  8.9 2.2 %collective-permute-start.2 = (bf16[256,512]{1,0:T(8,128)(2,1)S(1)}, bf16[256,512]{1,0:T(8,128)(2,1)S(1)}, u32[]{:S(2)}, u32[]{:S(2)}) collective-permute-start(bf16[256,512]{1,0:T(8,128)(2,1)S(1)} %get-tuple-element.51), channel_id=1, source_target_pairs={{64,0},{97,32},{1,64},{32,96},{65,1},{96,33},{0,65},{33,97},{72,8}... | collective-permute-start | bytes 786440 | tf_op jit(solution)/shard_map/ppermute | solution.py:42
  12.3 1.5 %collective-permute-done.6 = bf16[256,512]{1,0:T(8,128)(2,1)S(1)} collective-permute-done((bf16[256,512]{1,0:T(8,128)(2,1)S(1)}, bf16[256,512]{1,0:T(8,128)(2,1)S(1)}, u32[]{:S(2)}, u32[]{:S(2)}) %collective-permute-start.6) | collective-permute-done | bytes 262176 | tf_op jit(solution)/shard_map/ppermute | solution.py:42
  13.8 2.0 %collective-permute-start.3 = (bf16[256,512]{1,0:T(8,128)(2,1)S(1)}, bf16[256,512]{1,0:T(8,128)(2,1)S(1)}, u32[]{:S(2)}, u32[]{:S(2)}) collective-permute-start(bf16[256,512]{1,0:T(8,128)(2,1)S(1)} %collective-permute-done), channel_id=1, source_target_pairs={{65,0},{96,32},{0,64},{33,96},{64,1},{97,33},{1,65},{32,97},{73,8}... | collective-permute-start | bytes 786440 | tf_op jit(solution)/shard_map/ppermute | solution.py:42
  15.8 3.1 %collective-permute-start.8 = (bf16[512,512]{1,0:T(8,128)(2,1)S(1)}, bf16[512,512]{1,0:T(8,128)(2,1)S(1)}, u32[]{:S(2)}, u32[]{:S(2)}) collective-permute-start(bf16[512,512]{1,0:T(8,128)(2,1)S(1)} %constant_dynamic-update-slice_fusion.4.refs_4_), channel_id=1, source_target_pairs={{8,0},{34,32},{72,64},{98,96},{9,1},{35,33},{73,65},{99,97},{16,8}... | collective-permute-start | bytes 1572872 | tf_op jit(solution)/shard_map/ppermute | solution.py:42
  19.6 1.9 %collective-permute-done.3 = bf16[256,512]{1,0:T(8,128)(2,1)S(1)} collective-permute-done((bf16[256,512]{1,0:T(8,128)(2,1)S(1)}, bf16[256,512]{1,0:T(8,128)(2,1)S(1)}, u32[]{:S(2)}, u32[]{:S(2)}) %collective-permute-start.3) | collective-permute-done | bytes 262176 | tf_op jit(solution)/shard_map/ppermute | solution.py:42
  21.5 3.0 %collective-permute-start.13 = (bf16[512,512]{1,0:T(8,128)(2,1)S(1)}, bf16[512,512]{1,0:T(8,128)(2,1)S(1)}, u32[]{:S(2)}, u32[]{:S(2)}) collective-permute-start(bf16[512,512]{1,0:T(8,128)(2,1)S(1)} %constant_dynamic-update-slice_fusion.6.refs_3_), channel_id=1, source_target_pairs={{8,0},{34,32},{72,64},{98,96},{9,1},{35,33},{73,65},{99,97},{16,8}... | collective-permute-start | bytes 1572872 | tf_op jit(solution)/shard_map/ppermute | solution.py:42
  24.6 1.9 %exps0.1 = (f32[2048,128]{1,0:T(8,128)S(1)}, f32[8,4096]{1,0:T(8,128)S(1)}, bf16[2048,4096]{1,0:T(8,128)(2,1)S(1)}, bf16[4096,512]{1,0:T(8,128)(2,1)S(1)}) custom-call(s32[4]{0:T(128)S(1)} %pad_add_fusion.refs_0_.info_ref, bf16[512,512]{1,0:T(8,128)(2,1)S(1)} %constant_dynamic-update-slice_fusion.refs_1_, ...), custom_call_target="tpu_custom_call" | custom-call | flops 8589934592 | bytes 8388608 | tf_op jit(solution)/shard_map/exps0/pallas_call | solution.py:219
  26.5 2.8 %collective-permute-start.9 = (bf16[512,512]{1,0:T(8,128)(2,1)S(1)}, bf16[512,512]{1,0:T(8,128)(2,1)S(1)}, u32[]{:S(2)}, u32[]{:S(2)}) collective-permute-start(bf16[512,512]{1,0:T(8,128)(2,1)S(1)} %collective-permute-done.8.refs_6_), channel_id=1, source_target_pairs={{8,0},{34,32},{72,64},{98,96},{9,1},{35,33},{73,65},{99,97},{16,8}... | collective-permute-start | bytes 1572872 | tf_op jit(solution)/shard_map/ppermute | solution.py:42
  29.3 1.9 %exps1.1 = (f32[2048,128]{1,0:T(8,128)S(1)}, f32[8,4096]{1,0:T(8,128)S(1)}, bf16[2048,4096]{1,0:T(8,128)(2,1)S(1)}, bf16[4096,512]{1,0:T(8,128)(2,1)S(1)}) custom-call(s32[4]{0:T(128)S(1)} %pad_add_fusion.refs_0_.info_ref, ...), custom_call_target="tpu_custom_call", output_to_operand_aliasing={{0}: (5, {}), {1}: (6, {}), {2}: (7, {}), {3}: (8, {})} | custom-call | flops 8589934592 | bytes 8388608 | tf_op jit(solution)/shard_map/exps1/pallas_call | solution.py:219
  31.5 3.0 %exps2.1 = (f32[2048,128]{1,0:T(8,128)S(1)}, f32[8,4096]{1,0:T(8,128)S(1)}, bf16[2048,4096]{1,0:T(8,128)(2,1)S(1)}, bf16[4096,512]{1,0:T(8,128)(2,1)S(1)}) custom-call(s32[4]{0:T(128)S(1)} %pad_add_fusion.refs_0_.info_ref, ...), custom_call_target="tpu_custom_call", output_to_operand_aliasing={{0}: (7, {}), {1}: (8, {}), {2}: (9, {}), {3}: (10, {})} | custom-call | flops 8589934592 | bytes 4194304 | tf_op jit(solution)/shard_map/exps2/pallas_call | solution.py:219
  35.0 3.1 %exps3.1 = (f32[2048,128]{1,0:T(8,128)S(1)}, f32[8,4096]{1,0:T(8,128)S(1)}, bf16[2048,4096]{1,0:T(8,128)(2,1)S(1)}, bf16[4096,512]{1,0:T(8,128)(2,1)S(1)}) custom-call(s32[4]{0:T(128)S(1)} %pad_add_fusion.refs_0_.info_ref, ...), custom_call_target="tpu_custom_call", output_to_operand_aliasing={{0}: (7, {}), {1}: (8, {}), {2}: (9, {}), {3}: (10, {})} | custom-call | tf_op jit(solution)/shard_map/exps3/pallas_call | solution.py:219
  38.1 3.8 %collective-permute-done.11.refs_5_ = bf16[512,512]{1,0:T(8,128)(2,1)S(1)} collective-permute-done((bf16[512,512]{1,0:T(8,128)(2,1)S(1)}, bf16[512,512]{1,0:T(8,128)(2,1)S(1)}, u32[]{:S(2)}, u32[]{:S(2)}) %collective-permute-start.11) | collective-permute-done | bytes 524320 | tf_op jit(solution)/shard_map/ppermute | solution.py:42
  41.8 1.9 %exps4.1 = (f32[2048,128]{1,0:T(8,128)S(1)}, f32[8,4096]{1,0:T(8,128)S(1)}, bf16[2048,4096]{1,0:T(8,128)(2,1)S(1)}, bf16[4096,512]{1,0:T(8,128)(2,1)S(1)}) custom-call(s32[4]{0:T(128)S(1)} %pad_add_fusion.refs_0_.info_ref, ...), custom_call_target="tpu_custom_call", output_to_operand_aliasing={{0}: (6, {}), {1}: (7, {}), {2}: (8, {}), {3}: (9, {})} | custom-call | tf_op jit(solution)/shard_map/exps4/pallas_call | solution.py:219
  43.7 2.0 %exps5.1 = (f32[2048,128]{1,0:T(8,128)S(1)}, f32[8,4096]{1,0:T(8,128)S(1)}, bf16[2048,4096]{1,0:T(8,128)(2,1)S(1)}, bf16[4096,512]{1,0:T(8,128)(2,1)S(1)}, f32[8,256]{1,0:T(8,128)S(1)}, /*index=5*/f32[24,256]{1,0:T(8,128)S(1)}) custom-call(s32[4]{0:T(128)S(1)} %pad_add_fusion.refs_0_.info_ref, ...), custom_call_target="tpu_custom_call", output_to_operand_aliasing={{0}: (6, {}), {1}: (7, {}), {2}: (8, {}), {3}: (9, {})} | custom-call | tf_op jit(solution)/shard_map/exps5/pallas_call | solution.py:219
  47.8 1.9 %collective-permute-done.17 = f32[24,256]{1,0:T(8,128)S(1)} collective-permute-done((f32[24,256]{1,0:T(8,128)S(1)}, f32[24,256]{1,0:T(8,128)S(1)}, u32[]{:S(2)}, u32[]{:S(2)}) %collective-permute-start.17) | collective-permute-done | bytes 24608 | tf_op jit(solution)/shard_map/ppermute | solution.py:55
  49.6 3.7 %collective-permute-start.18 = (f32[24,256]{1,0:T(8,128)S(1)}, f32[24,256]{1,0:T(8,128)S(1)}, u32[]{:S(2)}, u32[]{:S(2)}) collective-permute-start(f32[24,256]{1,0:T(8,128)S(1)} %add.21), channel_id=1, source_target_pairs={{6,0},{56,32},{70,64},{120,96},{7,1},{57,33},{71,65},{121,97},{14,... | collective-permute-start | bytes 73736 | tf_op jit(solution)/shard_map/ppermute | solution.py:55
  53.3 1.8 %collective-permute-done.18 = f32[24,256]{1,0:T(8,128)S(1)} collective-permute-done((f32[24,256]{1,0:T(8,128)S(1)}, f32[24,256]{1,0:T(8,128)S(1)}, u32[]{:S(2)}, u32[]{:S(2)}) %collective-permute-start.18) | collective-permute-done | bytes 24608 | tf_op jit(solution)/shard_map/ppermute | solution.py:55
  55.1 1.7 %collective-permute-start.15 = (f32[8,256]{1,0:T(8,128)S(1)}, f32[8,256]{1,0:T(8,128)S(1)}, u32[]{:S(2)}, u32[]{:S(2)}) collective-permute-start(f32[8,256]{1,0:T(8,128)S(1)} %add.19), channel_id=1, source_target_pairs={{64,0},{96,32},{0,64},{32,96},{65,1},{97,33},{1,65},{33,97},{72,8}... | collective-permute-start | bytes 24584 | tf_op jit(solution)/shard_map/ppermute | solution.py:55
  56.8 2.0 %collective-permute-done.15 = f32[8,256]{1,0:T(8,128)S(1)} collective-permute-done((f32[8,256]{1,0:T(8,128)S(1)}, f32[8,256]{1,0:T(8,128)S(1)}, u32[]{:S(2)}, u32[]{:S(2)}) %collective-permute-start.15) | collective-permute-done | bytes 8224 | tf_op jit(solution)/shard_map/ppermute | solution.py:55
  59.0 1.4 %collective-permute-start.16 = (f32[8,256]{1,0:T(8,128)S(1)}, f32[8,256]{1,0:T(8,128)S(1)}, u32[]{:S(2)}, u32[]{:S(2)}) collective-permute-start(f32[8,256]{1,0:T(8,128)S(1)} %add.20.refs_0_), channel_id=1, source_target_pairs={{65,0},{97,32},{1,64},{33,96},{64,1},{96,33},{0,65},{32,97},{73,8}... | collective-permute-start | bytes 24584 | tf_op jit(solution)/shard_map/ppermute | solution.py:55
  60.3 3.5 %collective-permute-done.16.refs_1_ = f32[8,256]{1,0:T(8,128)S(1)} collective-permute-done((f32[8,256]{1,0:T(8,128)S(1)}, f32[8,256]{1,0:T(8,128)S(1)}, u32[]{:S(2)}, u32[]{:S(2)}) %collective-permute-start.16) | collective-permute-done | bytes 8224 | tf_op jit(solution)/shard_map/ppermute | solution.py:55
  64.8 3.4 %grads_core.1 = bf16[784,512]{1,0:T(8,128)(2,1)S(1)} custom-call(f32[32,128]{1,0:T(8,128)S(1)} %get-tuple-element.92.acol_ref, bf16[2048,128]{1,0:T(8,128)(2,1)S(1)} %get-tuple-element.85.arow_ref, bf16[2048,4096]{1,0:T(8,128)(2,1)S(1)} %get-tuple-element.86.exps_ref, bf16[4096,512]{1,0:T(8,128)(2,1)S(1)} %get-tuple-element.87.unit_ref, ...), custom_call_target="tpu_custom_call" | custom-call | flops 3221225472 | bytes 10485760 | tf_op jit(solution)/shard_map/grads_core/pallas_call | solution.py:309
  68.5 1.2 %grads_far.1.raw_ref = f32[256,512]{1,0:T(8,128)S(1)} custom-call(f32[32,128]{1,0:T(8,128)S(1)} %get-tuple-element.92.acol_ref, bf16[2048,128]{1,0:T(8,128)(2,1)S(1)} %get-tuple-element.85.arow_ref, bf16[2048,4096]{1,0:T(8,128)(2,1)S(1)} %get-tuple-element.86.exps_ref, bf16[4096,512]{1,0:T(8,128)(2,1)S(1)} %get-tuple-element.87.unit_ref), custom_call_target="tpu_custom_call" | custom-call | flops 1073741824 | bytes 6291456 | tf_op jit(solution)/shard_map/grads_far/pallas_call | solution.py:309
  70.9 1.7 %collective-permute-start.22 = (bf16[272,512]{1,0:T(8,128)(2,1)S(1)}, bf16[272,512]{1,0:T(8,128)(2,1)S(1)}, u32[]{:S(2)}, u32[]{:S(2)}) collective-permute-start(bf16[272,512]{1,0:T(8,128)(2,1)S(1)} %sum_far.1.refs_1_.here_ref), channel_id=1, source_target_pairs={{65,0},{96,32},{0,64},{33,96},{64,1},{97,33},{1,65},{32,97},{73,8}... | collective-permute-start | bytes 835592 | tf_op jit(solution)/shard_map/ppermute | solution.py:42
  72.6 2.3 %grads_near.1 = (bf16[272,512]{1,0:T(8,128)(2,1)S(1)}, f32[256,512]{1,0:T(8,128)S(1)}) custom-call(f32[32,128]{1,0:T(8,128)S(1)} %get-tuple-element.92.acol_ref, bf16[2048,128]{1,0:T(8,128)(2,1)S(1)} %get-tuple-element.85.arow_ref, bf16[2048,4096]{1,0:T(8,128)(2,1)S(1)} %get-tuple-element.86.exps_ref, bf16[4096,512]{1,0:T(8,128)(2,1)S(1)} %get-tuple-element.87.unit_ref, ...), custom_call_target="tpu_custom_call" | custom-call | flops 2147483648 | bytes 8388608 | tf_op jit(solution)/shard_map/grads_near/pallas_call | solution.py:309
  74.9 1.3 %grads_core_own.1 = bf16[256,512]{1,0:T(8,128)(2,1)S(1)} custom-call(f32[32,128]{1,0:T(8,128)S(1)} %get-tuple-element.92.acol_ref, bf16[2048,128]{1,0:T(8,128)(2,1)S(1)} %get-tuple-element.85.arow_ref, bf16[2048,4096]{1,0:T(8,128)(2,1)S(1)} %get-tuple-element.86.exps_ref, bf16[4096,512]{1,0:T(8,128)(2,1)S(1)} %get-tuple-element.87.unit_ref), custom_call_target="tpu_custom_call" | custom-call | flops 1073741824 | bytes 6291456 | tf_op jit(solution)/shard_map/grads_core_own/pallas_call | solution.py:309
  76.3 1.7 %collective-permute-start.24 = (bf16[272,512]{1,0:T(8,128)(2,1)S(1)}, bf16[272,512]{1,0:T(8,128)(2,1)S(1)}, u32[]{:S(2)}, u32[]{:S(2)}) collective-permute-start(bf16[272,512]{1,0:T(8,128)(2,1)S(1)} %get-tuple-element.93), channel_id=1, source_target_pairs={{64,0},{97,32},{1,64},{32,96},{65,1},{96,33},{0,65},{33,97},{72,8}... | collective-permute-start | bytes 835592 | tf_op jit(solution)/shard_map/ppermute | solution.py:42
  80.5 5.2 %collective-permute-done.24.one_ref = bf16[272,512]{1,0:T(8,128)(2,1)S(1)} collective-permute-done((bf16[272,512]{1,0:T(8,128)(2,1)S(1)}, bf16[272,512]{1,0:T(8,128)(2,1)S(1)}, u32[]{:S(2)}, u32[]{:S(2)}) %collective-permute-start.24) | collective-permute-done | bytes 278560 | tf_op jit(solution)/shard_map/ppermute | solution.py:42
  (57 shorter events, 13.0 us)
Async XLA Ops:
  0.6 1.0 %copy-start = (bf16[256,512]{1,0:T(8,128)(2,1)S(1)}, bf16[256,512]{1,0:T(8,128)(2,1)}, u32[]{:S(2)}) copy-start(bf16[256,512]{1,0:T(8,128)(2,1)} %z_ref.3) | copy-start | bytes 786436
  1.7 10.4 %collective-permute-start = (bf16[256,512]{1,0:T(8,128)(2,1)S(1)}, bf16[256,512]{1,0:T(8,128)(2,1)S(1)}, u32[]{:S(2)}, u32[]{:S(2)}) collective-permute-start(bf16[256,512]{1,0:T(8,128)(2,1)S(1)} %get-tuple-element.51), channel_id=1, source_target_pairs={{65,0},{96,32},{0,64},{33,96},{64,1},{97,33},{1,65},{32,97},{73,8}... | collective-permute-start | bytes 786440 | tf_op jit(solution)/shard_map/ppermute | solution.py:42
  3.8 8.5 %collective-permute-start.5 = (bf16[256,512]{1,0:T(8,128)(2,1)S(1)}, bf16[256,512]{1,0:T(8,128)(2,1)S(1)}, u32[]{:S(2)}, u32[]{:S(2)}) collective-permute-start(bf16[256,512]{1,0:T(8,128)(2,1)S(1)} %get-tuple-element.53.unit_ref), channel_id=1, source_target_pairs={{6,0},{56,32},{70,64},{120,96},{7,1},{57,33},{71,65},{121,97},{14,... | collective-permute-start | bytes 786440 | tf_op jit(solution)/shard_map/ppermute | solution.py:42
  5.3 8.5 %collective-permute-start.6 = (bf16[256,512]{1,0:T(8,128)(2,1)S(1)}, bf16[256,512]{1,0:T(8,128)(2,1)S(1)}, u32[]{:S(2)}, u32[]{:S(2)}) collective-permute-start(bf16[256,512]{1,0:T(8,128)(2,1)S(1)} %get-tuple-element.53.unit_ref), channel_id=1, source_target_pairs={{2,0},{40,32},{66,64},{104,96},{3,1},{41,33},{67,65},{105,97},{10,... | collective-permute-start | bytes 786440 | tf_op jit(solution)/shard_map/ppermute | solution.py:42
  7.0 8.8 %collective-permute-start.7 = (bf16[256,512]{1,0:T(8,128)(2,1)S(1)}, bf16[256,512]{1,0:T(8,128)(2,1)S(1)}, u32[]{:S(2)}, u32[]{:S(2)}) collective-permute-start(bf16[256,512]{1,0:T(8,128)(2,1)S(1)} %get-tuple-element.53.unit_ref), channel_id=1, source_target_pairs={{4,0},{48,32},{68,64},{112,96},{5,1},{49,33},{69,65},{113,97},{12,... | collective-permute-start | bytes 786440 | tf_op jit(solution)/shard_map/ppermute | solution.py:42
  8.9 10.2 %collective-permute-start.2 = (bf16[256,512]{1,0:T(8,128)(2,1)S(1)}, bf16[256,512]{1,0:T(8,128)(2,1)S(1)}, u32[]{:S(2)}, u32[]{:S(2)}) collective-permute-start(bf16[256,512]{1,0:T(8,128)(2,1)S(1)} %get-tuple-element.51), channel_id=1, source_target_pairs={{64,0},{97,32},{1,64},{32,96},{65,1},{96,33},{0,65},{33,97},{72,8}... | collective-permute-start | bytes 786440 | tf_op jit(solution)/shard_map/ppermute | solution.py:42
  11.1 0.7 copy-start.2
  12.2 12.3 %collective-permute-start.1 = (bf16[512,512]{1,0:T(8,128)(2,1)S(1)}, bf16[512,512]{1,0:T(8,128)(2,1)S(1)}, u32[]{:S(2)}, u32[]{:S(2)}) collective-permute-start(bf16[512,512]{1,0:T(8,128)(2,1)S(1)} %constant_dynamic-update-slice_fusion.refs_1_), channel_id=1, source_target_pairs={{32,0},{0,32},{96,64},{64,96},{33,1},{1,33},{97,65},{65,97},{40,8}... | collective-permute-start | bytes 1572872 | tf_op jit(solution)/shard_map/ppermute | solution.py:42
  13.8 7.7 %collective-permute-start.3 = (bf16[256,512]{1,0:T(8,128)(2,1)S(1)}, bf16[256,512]{1,0:T(8,128)(2,1)S(1)}, u32[]{:S(2)}, u32[]{:S(2)}) collective-permute-start(bf16[256,512]{1,0:T(8,128)(2,1)S(1)} %collective-permute-done), channel_id=1, source_target_pairs={{65,0},{96,32},{0,64},{33,96},{64,1},{97,33},{1,65},{32,97},{73,8}... | collective-permute-start | bytes 786440 | tf_op jit(solution)/shard_map/ppermute | solution.py:42
  15.8 10.7 %collective-permute-start.8 = (bf16[512,512]{1,0:T(8,128)(2,1)S(1)}, bf16[512,512]{1,0:T(8,128)(2,1)S(1)}, u32[]{:S(2)}, u32[]{:S(2)}) collective-permute-start(bf16[512,512]{1,0:T(8,128)(2,1)S(1)} %constant_dynamic-update-slice_fusion.4.refs_4_), channel_id=1, source_target_pairs={{8,0},{34,32},{72,64},{98,96},{9,1},{35,33},{73,65},{99,97},{16,8}... | collective-permute-start | bytes 1572872 | tf_op jit(solution)/shard_map/ppermute | solution.py:42
  18.9 12.3 %collective-permute-start.10 = (bf16[512,512]{1,0:T(8,128)(2,1)S(1)}, bf16[512,512]{1,0:T(8,128)(2,1)S(1)}, u32[]{:S(2)}, u32[]{:S(2)}) collective-permute-start(bf16[512,512]{1,0:T(8,128)(2,1)S(1)} %constant_dynamic-update-slice_fusion.6.refs_3_), channel_id=1, source_target_pairs={{24,0},{38,32},{88,64},{102,96},{25,1},{39,33},{89,65},{103,97},{0... | collective-permute-start | bytes 1572872 | tf_op jit(solution)/shard_map/ppermute | solution.py:42
  19.0 16.0 %collective-permute-start.12 = (bf16[512,512]{1,0:T(8,128)(2,1)S(1)}, bf16[512,512]{1,0:T(8,128)(2,1)S(1)}, u32[]{:S(2)}, u32[]{:S(2)}) collective-permute-start(bf16[512,512]{1,0:T(8,128)(2,1)S(1)} %constant_dynamic-update-slice_fusion.4.refs_4_), channel_id=1, source_target_pairs={{24,0},{38,32},{88,64},{102,96},{25,1},{39,33},{89,65},{103,97},{0... | collective-permute-start | bytes 1572872 | tf_op jit(solution)/shard_map/ppermute | solution.py:42
  21.5 13.0 %collective-permute-start.13 = (bf16[512,512]{1,0:T(8,128)(2,1)S(1)}, bf16[512,512]{1,0:T(8,128)(2,1)S(1)}, u32[]{:S(2)}, u32[]{:S(2)}) collective-permute-start(bf16[512,512]{1,0:T(8,128)(2,1)S(1)} %constant_dynamic-update-slice_fusion.6.refs_3_), channel_id=1, source_target_pairs={{8,0},{34,32},{72,64},{98,96},{9,1},{35,33},{73,65},{99,97},{16,8}... | collective-permute-start | bytes 1572872 | tf_op jit(solution)/shard_map/ppermute | solution.py:42
  24.5 4.8 %collective-permute-start.4 = (bf16[512,512]{1,0:T(8,128)(2,1)S(1)}, bf16[512,512]{1,0:T(8,128)(2,1)S(1)}, u32[]{:S(2)}, u32[]{:S(2)}) collective-permute-start(bf16[512,512]{1,0:T(8,128)(2,1)S(1)} %constant_dynamic-update-slice_fusion.2.refs_1_.refs_3_), channel_id=1, source_target_pairs={{32,0},{0,32},{96,64},{64,96},{33,1},{1,33},{97,65},{65,97},{40,8}... | collective-permute-start | bytes 1572872 | tf_op jit(solution)/shard_map/ppermute | solution.py:42
  26.5 17.2 %collective-permute-start.9 = (bf16[512,512]{1,0:T(8,128)(2,1)S(1)}, bf16[512,512]{1,0:T(8,128)(2,1)S(1)}, u32[]{:S(2)}, u32[]{:S(2)}) collective-permute-start(bf16[512,512]{1,0:T(8,128)(2,1)S(1)} %collective-permute-done.8.refs_6_), channel_id=1, source_target_pairs={{8,0},{34,32},{72,64},{98,96},{9,1},{35,33},{73,65},{99,97},{16,8}... | collective-permute-start | bytes 1572872 | tf_op jit(solution)/shard_map/ppermute | solution.py:42
  31.2 10.6 %collective-permute-start.11 = (bf16[512,512]{1,0:T(8,128)(2,1)S(1)}, bf16[512,512]{1,0:T(8,128)(2,1)S(1)}, u32[]{:S(2)}, u32[]{:S(2)}) collective-permute-start(bf16[512,512]{1,0:T(8,128)(2,1)S(1)} %collective-permute-done.10.refs_5_), channel_id=1, source_target_pairs={{24,0},{38,32},{88,64},{102,96},{25,1},{39,33},{89,65},{103,97},{0... | collective-permute-start | bytes 1572872 | tf_op jit(solution)/shard_map/ppermute | solution.py:42
  45.7 3.9 %collective-permute-start.17 = (f32[24,256]{1,0:T(8,128)S(1)}, f32[24,256]{1,0:T(8,128)S(1)}, u32[]{:S(2)}, u32[]{:S(2)}) collective-permute-start(f32[24,256]{1,0:T(8,128)S(1)} %get-tuple-element.80), channel_id=1, source_target_pairs={{2,0},{40,32},{66,64},{104,96},{3,1},{41,33},{67,65},{105,97},{10,... | collective-permute-start | bytes 73736 | tf_op jit(solution)/shard_map/ppermute | solution.py:55
  46.6 1.2 %collective-permute-start.14 = (f32[8,256]{1,0:T(8,128)S(1)}, f32[8,256]{1,0:T(8,128)S(1)}, u32[]{:S(2)}, u32[]{:S(2)}) collective-permute-start(f32[8,256]{1,0:T(8,128)S(1)} %get-tuple-element.79), channel_id=1, source_target_pairs={{32,0},{0,32},{96,64},{64,96},{33,1},{1,33},{97,65},{65,97},{40,8}... | collective-permute-start | bytes 24584 | tf_op jit(solution)/shard_map/ppermute | solution.py:42
  49.6 5.5 %collective-permute-start.18 = (f32[24,256]{1,0:T(8,128)S(1)}, f32[24,256]{1,0:T(8,128)S(1)}, u32[]{:S(2)}, u32[]{:S(2)}) collective-permute-start(f32[24,256]{1,0:T(8,128)S(1)} %add.21), channel_id=1, source_target_pairs={{6,0},{56,32},{70,64},{120,96},{7,1},{57,33},{71,65},{121,97},{14,... | collective-permute-start | bytes 73736 | tf_op jit(solution)/shard_map/ppermute | solution.py:55
  55.1 3.8 %collective-permute-start.19 = (f32[24,256]{1,0:T(8,128)S(1)}, f32[24,256]{1,0:T(8,128)S(1)}, u32[]{:S(2)}, u32[]{:S(2)}) collective-permute-start(f32[24,256]{1,0:T(8,128)S(1)} %add.22), channel_id=1, source_target_pairs={{8,0},{34,32},{72,64},{98,96},{9,1},{35,33},{73,65},{99,97},{0,8},... | collective-permute-start | bytes 73736 | tf_op jit(solution)/shard_map/ppermute | solution.py:55
  55.1 3.7 %collective-permute-start.15 = (f32[8,256]{1,0:T(8,128)S(1)}, f32[8,256]{1,0:T(8,128)S(1)}, u32[]{:S(2)}, u32[]{:S(2)}) collective-permute-start(f32[8,256]{1,0:T(8,128)S(1)} %add.19), channel_id=1, source_target_pairs={{64,0},{96,32},{0,64},{32,96},{65,1},{97,33},{1,65},{33,97},{72,8}... | collective-permute-start | bytes 24584 | tf_op jit(solution)/shard_map/ppermute | solution.py:55
  58.9 5.0 %collective-permute-start.20 = (f32[24,256]{1,0:T(8,128)S(1)}, f32[24,256]{1,0:T(8,128)S(1)}, u32[]{:S(2)}, u32[]{:S(2)}) collective-permute-start(f32[24,256]{1,0:T(8,128)S(1)} %add.23.refs_2_), channel_id=1, source_target_pairs={{24,0},{38,32},{88,64},{102,96},{25,1},{39,33},{89,65},{103,97},{1... | collective-permute-start | bytes 73736 | tf_op jit(solution)/shard_map/ppermute | solution.py:55
  59.0 4.9 %collective-permute-start.16 = (f32[8,256]{1,0:T(8,128)S(1)}, f32[8,256]{1,0:T(8,128)S(1)}, u32[]{:S(2)}, u32[]{:S(2)}) collective-permute-start(f32[8,256]{1,0:T(8,128)S(1)} %add.20.refs_0_), channel_id=1, source_target_pairs={{65,0},{97,32},{1,64},{33,96},{64,1},{96,33},{0,65},{32,97},{73,8}... | collective-permute-start | bytes 24584 | tf_op jit(solution)/shard_map/ppermute | solution.py:55
  68.2 2.6 %collective-permute-start.21 = (bf16[784,512]{1,0:T(8,128)(2,1)S(1)}, bf16[784,512]{1,0:T(8,128)(2,1)S(1)}, u32[]{:S(2)}, u32[]{:S(2)}) collective-permute-start(bf16[784,512]{1,0:T(8,128)(2,1)S(1)} %grads_core.1), channel_id=1, source_target_pairs={{32,0},{0,32},{96,64},{64,96},{33,1},{1,33},{97,65},{65,97},{40,8}... | collective-permute-start | bytes 2408456 | tf_op jit(solution)/shard_map/ppermute | solution.py:42
  70.9 7.8 %collective-permute-start.22 = (bf16[272,512]{1,0:T(8,128)(2,1)S(1)}, bf16[272,512]{1,0:T(8,128)(2,1)S(1)}, u32[]{:S(2)}, u32[]{:S(2)}) collective-permute-start(bf16[272,512]{1,0:T(8,128)(2,1)S(1)} %sum_far.1.refs_1_.here_ref), channel_id=1, source_target_pairs={{65,0},{96,32},{0,64},{33,96},{64,1},{97,33},{1,65},{32,97},{73,8}... | collective-permute-start | bytes 835592 | tf_op jit(solution)/shard_map/ppermute | solution.py:42
  76.2 10.4 %copy-start.1 = (bf16[256,512]{1,0:T(8,128)(2,1)S(1)}, bf16[256,512]{1,0:T(8,128)(2,1)}, u32[]{:S(2)}) copy-start(bf16[256,512]{1,0:T(8,128)(2,1)} %z_ref.3) | copy-start | bytes 786436
  76.2 3.1 %collective-permute-start.23 = (bf16[256,512]{1,0:T(8,128)(2,1)S(1)}, bf16[256,512]{1,0:T(8,128)(2,1)S(1)}, u32[]{:S(2)}, u32[]{:S(2)}) collective-permute-start(bf16[256,512]{1,0:T(8,128)(2,1)S(1)} %grads_core_own.1), channel_id=1, source_target_pairs={{32,0},{0,32},{96,64},{64,96},{33,1},{1,33},{97,65},{65,97},{40,8}... | collective-permute-start | bytes 786440 | tf_op jit(solution)/shard_map/ppermute | solution.py:42
  76.3 9.4 %collective-permute-start.24 = (bf16[272,512]{1,0:T(8,128)(2,1)S(1)}, bf16[272,512]{1,0:T(8,128)(2,1)S(1)}, u32[]{:S(2)}, u32[]{:S(2)}) collective-permute-start(bf16[272,512]{1,0:T(8,128)(2,1)S(1)} %get-tuple-element.93), channel_id=1, source_target_pairs={{64,0},{97,32},{1,64},{32,96},{65,1},{96,33},{0,65},{33,97},{72,8}... | collective-permute-start | bytes 835592 | tf_op jit(solution)/shard_map/ppermute | solution.py:42
  78.8 7.8 %collective-permute-start.25 = (bf16[272,512]{1,0:T(8,128)(2,1)S(1)}, bf16[272,512]{1,0:T(8,128)(2,1)S(1)}, u32[]{:S(2)}, u32[]{:S(2)}) collective-permute-start(bf16[272,512]{1,0:T(8,128)(2,1)S(1)} %sum_two.1), channel_id=1, source_target_pairs={{65,0},{96,32},{0,64},{33,96},{64,1},{97,33},{1,65},{32,97},{73,8}... | collective-permute-start | bytes 835592 | tf_op jit(solution)/shard_map/ppermute | solution.py:42

commit v12 on v11

--- a/solution.py
+++ b/solution.py
@@ -387,11 +387,11 @@
     mates, positive = make_mates(unit, partner)
     chain = make_exps(info, near, (0,), [line0, line1], (0, 1), None, None, 8, "exps0")
     after0 = get(after(line0, line1), second=1)
+    far0 = get(after(before0, chain[0]), second=-1)
     far1 = get(after(after1, chain[0]), second=1)
     rest = jnp.concatenate([z_two, z_far], axis=0)
     rest = [rest, get(rest, core=1)]
     chain = make_exps(info, rest, (1,), [line0, line1], (0, 1), chain, None, 8, "exps1")
-    far0 = get(after(before0, chain[0]), second=-1)
     rows = near + rest
     chain = make_exps(info, rows, (0, 1), [before0, after1], (2, 5), chain, None, 4, "exps2")
     chain = make_exps(info, rows, (0, 1), [before1, after0], (3, 4), chain, None, 0, "exps3")

time: 88.9 us -> 86.2 us (0.970)
  waiting for transfers between devices: 26.1 us -> 22.2 us
  starting transfers between devices: 33.1 us -> 35 us
    ppermute x20, waiting for transfers between devices: 16.7 us -> 12.7 us  [get(): return lax.ppermute(value, AXES, pairs)]
    ppermute x6, starting transfers between devices: 7.64 us -> 9.16 us  [swap(): return lax.ppermute(value, AXES, pairs)]
  transfers between devices with their start and end apart: 26 -> 26, of which waited for: 15 -> 12; matrix products, arithmetic and copies ran while one was open for 0% -> 0% of each run, Pallas kernels for 21% -> 21%
where the time goes in v12:
time: 86.2 us; the launch traced here: 85.6 us
  starting transfers between devices  35 us (41%)
  Pallas kernels  25.7 us (30%)
  waiting for transfers between devices  22.2 us (26%)
  local copies, waits for them, and re-layouts  1.78 us (2%)
  between operations  0.9 us (1%)
    ppermute x20, starting transfers between devices, get(): return lax.ppermute(value, AXES, pairs)  25.8 us
    pallas_call x6, Pallas kernels, make_exps(): pl.pallas_call(functools.partial(exps_kernel, places, rows_here, first, l...  13.7 us
    ppermute x20, waiting for transfers between devices, get(): return lax.ppermute(value, AXES, pairs)  12.7 us
    ppermute x6, waiting for transfers between devices, swap(): return lax.ppermute(value, AXES, pairs)  9.52 us
    pallas_call x5, Pallas kernels, make_grads(): pl.pallas_call(functools.partial(grads_kernel, pieces, adds, carry is not...  9.46 us
    ppermute x6, starting transfers between devices, swap(): return lax.ppermute(value, AXES, pairs)  9.16 us
  transfers between devices with their start and end apart: 26, of which 12 were waited for; matrix products, arithmetic and copies ran while one was open for 0% of the time, Pallas kernels for 21%

profile of v12, /device:TPU:0, one launch (start us, length us, event | category | flops | bytes accessed | tf_op | source)
XLA Modules:
  0.0 85.6 jit_solution(8335437060041446219)
XLA Ops:
  1.7 2.1 %collective-permute-start = (bf16[256,512]{1,0:T(8,128)(2,1)S(1)}, bf16[256,512]{1,0:T(8,128)(2,1)S(1)}, u32[]{:S(2)}, u32[]{:S(2)}) collective-permute-start(bf16[256,512]{1,0:T(8,128)(2,1)S(1)} %get-tuple-element.51), channel_id=1, source_target_pairs={{65,0},{96,32},{0,64},{33,96},{64,1},{97,33},{1,65},{32,97},{73,8}... | collective-permute-start | bytes 786440 | tf_op jit(solution)/shard_map/ppermute | solution.py:42
  3.8 1.5 %collective-permute-start.5 = (bf16[256,512]{1,0:T(8,128)(2,1)S(1)}, bf16[256,512]{1,0:T(8,128)(2,1)S(1)}, u32[]{:S(2)}, u32[]{:S(2)}) collective-permute-start(bf16[256,512]{1,0:T(8,128)(2,1)S(1)} %get-tuple-element.53.unit_ref), channel_id=1, source_target_pairs={{6,0},{56,32},{70,64},{120,96},{7,1},{57,33},{71,65},{121,97},{14,... | collective-permute-start | bytes 786440 | tf_op jit(solution)/shard_map/ppermute | solution.py:42
  5.3 1.7 %collective-permute-start.6 = (bf16[256,512]{1,0:T(8,128)(2,1)S(1)}, bf16[256,512]{1,0:T(8,128)(2,1)S(1)}, u32[]{:S(2)}, u32[]{:S(2)}) collective-permute-start(bf16[256,512]{1,0:T(8,128)(2,1)S(1)} %get-tuple-element.53.unit_ref), channel_id=1, source_target_pairs={{2,0},{40,32},{66,64},{104,96},{3,1},{41,33},{67,65},{105,97},{10,... | collective-permute-start | bytes 786440 | tf_op jit(solution)/shard_map/ppermute | solution.py:42
  7.0 1.8 %collective-permute-start.7 = (bf16[256,512]{1,0:T(8,128)(2,1)S(1)}, bf16[256,512]{1,0:T(8,128)(2,1)S(1)}, u32[]{:S(2)}, u32[]{:S(2)}) collective-permute-start(bf16[256,512]{1,0:T(8,128)(2,1)S(1)} %get-tuple-element.53.unit_ref), channel_id=1, source_target_pairs={{4,0},{48,32},{68,64},{112,96},{5,1},{49,33},{69,65},{113,97},{12,... | collective-permute-start | bytes 786440 | tf_op jit(solution)/shard_map/ppermute | solution.py:42
  8.9 2.2 %collective-permute-start.2 = (bf16[256,512]{1,0:T(8,128)(2,1)S(1)}, bf16[256,512]{1,0:T(8,128)(2,1)S(1)}, u32[]{:S(2)}, u32[]{:S(2)}) collective-permute-start(bf16[256,512]{1,0:T(8,128)(2,1)S(1)} %get-tuple-element.51), channel_id=1, source_target_pairs={{64,0},{97,32},{1,64},{32,96},{65,1},{96,33},{0,65},{33,97},{72,8}... | collective-permute-start | bytes 786440 | tf_op jit(solution)/shard_map/ppermute | solution.py:42
  12.3 1.4 %collective-permute-done.6 = bf16[256,512]{1,0:T(8,128)(2,1)S(1)} collective-permute-done((bf16[256,512]{1,0:T(8,128)(2,1)S(1)}, bf16[256,512]{1,0:T(8,128)(2,1)S(1)}, u32[]{:S(2)}, u32[]{:S(2)}) %collective-permute-start.6) | collective-permute-done | bytes 262176 | tf_op jit(solution)/shard_map/ppermute | solution.py:42
  13.8 2.0 %collective-permute-start.3 = (bf16[256,512]{1,0:T(8,128)(2,1)S(1)}, bf16[256,512]{1,0:T(8,128)(2,1)S(1)}, u32[]{:S(2)}, u32[]{:S(2)}) collective-permute-start(bf16[256,512]{1,0:T(8,128)(2,1)S(1)} %collective-permute-done), channel_id=1, source_target_pairs={{65,0},{96,32},{0,64},{33,96},{64,1},{97,33},{1,65},{32,97},{73,8}... | collective-permute-start | bytes 786440 | tf_op jit(solution)/shard_map/ppermute | solution.py:42
  15.8 1.6 %collective-permute-start.10 = (bf16[512,512]{1,0:T(8,128)(2,1)S(1)}, bf16[512,512]{1,0:T(8,128)(2,1)S(1)}, u32[]{:S(2)}, u32[]{:S(2)}) collective-permute-start(bf16[512,512]{1,0:T(8,128)(2,1)S(1)} %constant_dynamic-update-slice_fusion.6.refs_3_), channel_id=1, source_target_pairs={{24,0},{38,32},{88,64},{102,96},{25,1},{39,33},{89,65},{103,97},{0... | collective-permute-start | bytes 1572872 | tf_op jit(solution)/shard_map/ppermute | solution.py:42
  17.5 1.7 %collective-permute-start.8 = (bf16[512,512]{1,0:T(8,128)(2,1)S(1)}, bf16[512,512]{1,0:T(8,128)(2,1)S(1)}, u32[]{:S(2)}, u32[]{:S(2)}) collective-permute-start(bf16[512,512]{1,0:T(8,128)(2,1)S(1)} %constant_dynamic-update-slice_fusion.4.refs_4_), channel_id=1, source_target_pairs={{8,0},{34,32},{72,64},{98,96},{9,1},{35,33},{73,65},{99,97},{16,8}... | collective-permute-start | bytes 1572872 | tf_op jit(solution)/shard_map/ppermute | solution.py:42
  19.6 1.9 %collective-permute-done.3 = bf16[256,512]{1,0:T(8,128)(2,1)S(1)} collective-permute-done((bf16[256,512]{1,0:T(8,128)(2,1)S(1)}, bf16[256,512]{1,0:T(8,128)(2,1)S(1)}, u32[]{:S(2)}, u32[]{:S(2)}) %collective-permute-start.3) | collective-permute-done | bytes 262176 | tf_op jit(solution)/shard_map/ppermute | solution.py:42
  21.4 3.0 %collective-permute-start.13 = (bf16[512,512]{1,0:T(8,128)(2,1)S(1)}, bf16[512,512]{1,0:T(8,128)(2,1)S(1)}, u32[]{:S(2)}, u32[]{:S(2)}) collective-permute-start(bf16[512,512]{1,0:T(8,128)(2,1)S(1)} %constant_dynamic-update-slice_fusion.6.refs_3_), channel_id=1, source_target_pairs={{8,0},{34,32},{72,64},{98,96},{9,1},{35,33},{73,65},{99,97},{16,8}... | collective-permute-start | bytes 1572872 | tf_op jit(solution)/shard_map/ppermute | solution.py:42
  24.6 1.9 %exps0.1 = (f32[2048,128]{1,0:T(8,128)S(1)}, f32[8,4096]{1,0:T(8,128)S(1)}, bf16[2048,4096]{1,0:T(8,128)(2,1)S(1)}, bf16[4096,512]{1,0:T(8,128)(2,1)S(1)}) custom-call(s32[4]{0:T(128)S(1)} %pad_add_fusion.refs_0_.info_ref, bf16[512,512]{1,0:T(8,128)(2,1)S(1)} %constant_dynamic-update-slice_fusion.refs_1_, ...), custom_call_target="tpu_custom_call" | custom-call | flops 8589934592 | bytes 8388608 | tf_op jit(solution)/shard_map/exps0/pallas_call | solution.py:219
  26.7 1.6 %collective-permute-start.11 = (bf16[512,512]{1,0:T(8,128)(2,1)S(1)}, bf16[512,512]{1,0:T(8,128)(2,1)S(1)}, u32[]{:S(2)}, u32[]{:S(2)}) collective-permute-start(bf16[512,512]{1,0:T(8,128)(2,1)S(1)} %collective-permute-done.10.refs_5_), channel_id=1, source_target_pairs={{24,0},{38,32},{88,64},{102,96},{25,1},{39,33},{89,65},{103,97},{0... | collective-permute-start | bytes 1572872 | tf_op jit(solution)/shard_map/ppermute | solution.py:42
  28.3 1.7 %collective-permute-start.9 = (bf16[512,512]{1,0:T(8,128)(2,1)S(1)}, bf16[512,512]{1,0:T(8,128)(2,1)S(1)}, u32[]{:S(2)}, u32[]{:S(2)}) collective-permute-start(bf16[512,512]{1,0:T(8,128)(2,1)S(1)} %collective-permute-done.8.refs_6_), channel_id=1, source_target_pairs={{8,0},{34,32},{72,64},{98,96},{9,1},{35,33},{73,65},{99,97},{16,8}... | collective-permute-start | bytes 1572872 | tf_op jit(solution)/shard_map/ppermute | solution.py:42
  30.0 1.9 %exps1.1 = (f32[2048,128]{1,0:T(8,128)S(1)}, f32[8,4096]{1,0:T(8,128)S(1)}, bf16[2048,4096]{1,0:T(8,128)(2,1)S(1)}, bf16[4096,512]{1,0:T(8,128)(2,1)S(1)}) custom-call(s32[4]{0:T(128)S(1)} %pad_add_fusion.refs_0_.info_ref, ...), custom_call_target="tpu_custom_call", output_to_operand_aliasing={{0}: (5, {}), {1}: (6, {}), {2}: (7, {}), {3}: (8, {})} | custom-call | flops 8589934592 | bytes 8388608 | tf_op jit(solution)/shard_map/exps1/pallas_call | solution.py:219
  31.9 3.0 %exps2.1 = (f32[2048,128]{1,0:T(8,128)S(1)}, f32[8,4096]{1,0:T(8,128)S(1)}, bf16[2048,4096]{1,0:T(8,128)(2,1)S(1)}, bf16[4096,512]{1,0:T(8,128)(2,1)S(1)}) custom-call(s32[4]{0:T(128)S(1)} %pad_add_fusion.refs_0_.info_ref, ...), custom_call_target="tpu_custom_call", output_to_operand_aliasing={{0}: (7, {}), {1}: (8, {}), {2}: (9, {}), {3}: (10, {})} | custom-call | flops 8589934592 | bytes 4194304 | tf_op jit(solution)/shard_map/exps2/pallas_call | solution.py:219
  34.9 3.1 %exps3.1 = (f32[2048,128]{1,0:T(8,128)S(1)}, f32[8,4096]{1,0:T(8,128)S(1)}, bf16[2048,4096]{1,0:T(8,128)(2,1)S(1)}, bf16[4096,512]{1,0:T(8,128)(2,1)S(1)}) custom-call(s32[4]{0:T(128)S(1)} %pad_add_fusion.refs_0_.info_ref, ...), custom_call_target="tpu_custom_call", output_to_operand_aliasing={{0}: (7, {}), {1}: (8, {}), {2}: (9, {}), {3}: (10, {})} | custom-call | tf_op jit(solution)/shard_map/exps3/pallas_call | solution.py:219
  38.0 1.9 %exps4.1 = (f32[2048,128]{1,0:T(8,128)S(1)}, f32[8,4096]{1,0:T(8,128)S(1)}, bf16[2048,4096]{1,0:T(8,128)(2,1)S(1)}, bf16[4096,512]{1,0:T(8,128)(2,1)S(1)}) custom-call(s32[4]{0:T(128)S(1)} %pad_add_fusion.refs_0_.info_ref, ...), custom_call_target="tpu_custom_call", output_to_operand_aliasing={{0}: (6, {}), {1}: (7, {}), {2}: (8, {}), {3}: (9, {})} | custom-call | tf_op jit(solution)/shard_map/exps4/pallas_call | solution.py:219
  39.9 2.0 %exps5.1 = (f32[2048,128]{1,0:T(8,128)S(1)}, f32[8,4096]{1,0:T(8,128)S(1)}, bf16[2048,4096]{1,0:T(8,128)(2,1)S(1)}, bf16[4096,512]{1,0:T(8,128)(2,1)S(1)}, f32[8,256]{1,0:T(8,128)S(1)}, /*index=5*/f32[24,256]{1,0:T(8,128)S(1)}) custom-call(s32[4]{0:T(128)S(1)} %pad_add_fusion.refs_0_.info_ref, ...), custom_call_target="tpu_custom_call", output_to_operand_aliasing={{0}: (6, {}), {1}: (7, {}), {2}: (8, {}), {3}: (9, {})} | custom-call | tf_op jit(solution)/shard_map/exps5/pallas_call | solution.py:219
  43.6 2.1 %collective-permute-done.17 = f32[24,256]{1,0:T(8,128)S(1)} collective-permute-done((f32[24,256]{1,0:T(8,128)S(1)}, f32[24,256]{1,0:T(8,128)S(1)}, u32[]{:S(2)}, u32[]{:S(2)}) %collective-permute-start.17) | collective-permute-done | bytes 24608 | tf_op jit(solution)/shard_map/ppermute | solution.py:55
  45.8 3.7 %collective-permute-start.18 = (f32[24,256]{1,0:T(8,128)S(1)}, f32[24,256]{1,0:T(8,128)S(1)}, u32[]{:S(2)}, u32[]{:S(2)}) collective-permute-start(f32[24,256]{1,0:T(8,128)S(1)} %add.21), channel_id=1, source_target_pairs={{6,0},{56,32},{70,64},{120,96},{7,1},{57,33},{71,65},{121,97},{14,... | collective-permute-start | bytes 73736 | tf_op jit(solution)/shard_map/ppermute | solution.py:55
  49.4 1.8 %collective-permute-done.18 = f32[24,256]{1,0:T(8,128)S(1)} collective-permute-done((f32[24,256]{1,0:T(8,128)S(1)}, f32[24,256]{1,0:T(8,128)S(1)}, u32[]{:S(2)}, u32[]{:S(2)}) %collective-permute-start.18) | collective-permute-done | bytes 24608 | tf_op jit(solution)/shard_map/ppermute | solution.py:55
  51.6 1.6 %collective-permute-start.15 = (f32[8,256]{1,0:T(8,128)S(1)}, f32[8,256]{1,0:T(8,128)S(1)}, u32[]{:S(2)}, u32[]{:S(2)}) collective-permute-start(f32[8,256]{1,0:T(8,128)S(1)} %add.19), channel_id=1, source_target_pairs={{64,0},{96,32},{0,64},{32,96},{65,1},{97,33},{1,65},{33,97},{72,8}... | collective-permute-start | bytes 24584 | tf_op jit(solution)/shard_map/ppermute | solution.py:55
  53.2 2.0 %collective-permute-done.15 = f32[8,256]{1,0:T(8,128)S(1)} collective-permute-done((f32[8,256]{1,0:T(8,128)S(1)}, f32[8,256]{1,0:T(8,128)S(1)}, u32[]{:S(2)}, u32[]{:S(2)}) %collective-permute-start.15) | collective-permute-done | bytes 8224 | tf_op jit(solution)/shard_map/ppermute | solution.py:55
  55.3 2.0 %collective-permute-start.20 = (f32[24,256]{1,0:T(8,128)S(1)}, f32[24,256]{1,0:T(8,128)S(1)}, u32[]{:S(2)}, u32[]{:S(2)}) collective-permute-start(f32[24,256]{1,0:T(8,128)S(1)} %add.23.refs_2_), channel_id=1, source_target_pairs={{24,0},{38,32},{88,64},{102,96},{25,1},{39,33},{89,65},{103,97},{1... | collective-permute-start | bytes 73736 | tf_op jit(solution)/shard_map/ppermute | solution.py:55
  57.2 1.3 %collective-permute-start.16 = (f32[8,256]{1,0:T(8,128)S(1)}, f32[8,256]{1,0:T(8,128)S(1)}, u32[]{:S(2)}, u32[]{:S(2)}) collective-permute-start(f32[8,256]{1,0:T(8,128)S(1)} %add.20.refs_0_), channel_id=1, source_target_pairs={{65,0},{97,32},{1,64},{33,96},{64,1},{96,33},{0,65},{32,97},{73,8}... | collective-permute-start | bytes 24584 | tf_op jit(solution)/shard_map/ppermute | solution.py:55
  58.6 3.5 %collective-permute-done.16.refs_1_ = f32[8,256]{1,0:T(8,128)S(1)} collective-permute-done((f32[8,256]{1,0:T(8,128)S(1)}, f32[8,256]{1,0:T(8,128)S(1)}, u32[]{:S(2)}, u32[]{:S(2)}) %collective-permute-start.16) | collective-permute-done | bytes 8224 | tf_op jit(solution)/shard_map/ppermute | solution.py:55
  62.9 3.4 %grads_core.1 = bf16[784,512]{1,0:T(8,128)(2,1)S(1)} custom-call(f32[32,128]{1,0:T(8,128)S(1)} %get-tuple-element.92.acol_ref, bf16[2048,128]{1,0:T(8,128)(2,1)S(1)} %get-tuple-element.85.arow_ref, bf16[2048,4096]{1,0:T(8,128)(2,1)S(1)} %get-tuple-element.86.exps_ref, bf16[4096,512]{1,0:T(8,128)(2,1)S(1)} %get-tuple-element.87.unit_ref, ...), custom_call_target="tpu_custom_call" | custom-call | flops 3221225472 | bytes 10485760 | tf_op jit(solution)/shard_map/grads_core/pallas_call | solution.py:309
  69.3 2.3 %grads_near.1 = (bf16[272,512]{1,0:T(8,128)(2,1)S(1)}, f32[256,512]{1,0:T(8,128)S(1)}) custom-call(f32[32,128]{1,0:T(8,128)S(1)} %get-tuple-element.92.acol_ref, bf16[2048,128]{1,0:T(8,128)(2,1)S(1)} %get-tuple-element.85.arow_ref, bf16[2048,4096]{1,0:T(8,128)(2,1)S(1)} %get-tuple-element.86.exps_ref, bf16[4096,512]{1,0:T(8,128)(2,1)S(1)} %get-tuple-element.87.unit_ref, ...), custom_call_target="tpu_custom_call" | custom-call | flops 2147483648 | bytes 8388608 | tf_op jit(solution)/shard_map/grads_near/pallas_call | solution.py:309
  73.7 2.2 %collective-permute-start.24 = (bf16[272,512]{1,0:T(8,128)(2,1)S(1)}, bf16[272,512]{1,0:T(8,128)(2,1)S(1)}, u32[]{:S(2)}, u32[]{:S(2)}) collective-permute-start(bf16[272,512]{1,0:T(8,128)(2,1)S(1)} %get-tuple-element.93), channel_id=1, source_target_pairs={{64,0},{97,32},{1,64},{32,96},{65,1},{96,33},{0,65},{33,97},{72,8}... | collective-permute-start | bytes 835592 | tf_op jit(solution)/shard_map/ppermute | solution.py:42
  78.0 5.1 %collective-permute-done.24.one_ref = bf16[272,512]{1,0:T(8,128)(2,1)S(1)} collective-permute-done((bf16[272,512]{1,0:T(8,128)(2,1)S(1)}, bf16[272,512]{1,0:T(8,128)(2,1)S(1)}, u32[]{:S(2)}, u32[]{:S(2)}) %collective-permute-start.24) | collective-permute-done | bytes 278560 | tf_op jit(solution)/shard_map/ppermute | solution.py:42
  83.1 1.4 %collective-permute-done.25.two_ref = bf16[272,512]{1,0:T(8,128)(2,1)S(1)} collective-permute-done((bf16[272,512]{1,0:T(8,128)(2,1)S(1)}, bf16[272,512]{1,0:T(8,128)(2,1)S(1)}, u32[]{:S(2)}, u32[]{:S(2)}) %collective-permute-start.25) | collective-permute-done | bytes 278560 | tf_op jit(solution)/shard_map/ppermute | solution.py:42
  (57 shorter events, 14.3 us)
Async XLA Ops:
  0.6 1.0 %copy-start = (bf16[256,512]{1,0:T(8,128)(2,1)S(1)}, bf16[256,512]{1,0:T(8,128)(2,1)}, u32[]{:S(2)}) copy-start(bf16[256,512]{1,0:T(8,128)(2,1)} %z_ref.3) | copy-start | bytes 786436
  1.7 10.4 %collective-permute-start = (bf16[256,512]{1,0:T(8,128)(2,1)S(1)}, bf16[256,512]{1,0:T(8,128)(2,1)S(1)}, u32[]{:S(2)}, u32[]{:S(2)}) collective-permute-start(bf16[256,512]{1,0:T(8,128)(2,1)S(1)} %get-tuple-element.51), channel_id=1, source_target_pairs={{65,0},{96,32},{0,64},{33,96},{64,1},{97,33},{1,65},{32,97},{73,8}... | collective-permute-start | bytes 786440 | tf_op jit(solution)/shard_map/ppermute | solution.py:42
  3.8 8.5 %collective-permute-start.5 = (bf16[256,512]{1,0:T(8,128)(2,1)S(1)}, bf16[256,512]{1,0:T(8,128)(2,1)S(1)}, u32[]{:S(2)}, u32[]{:S(2)}) collective-permute-start(bf16[256,512]{1,0:T(8,128)(2,1)S(1)} %get-tuple-element.53.unit_ref), channel_id=1, source_target_pairs={{6,0},{56,32},{70,64},{120,96},{7,1},{57,33},{71,65},{121,97},{14,... | collective-permute-start | bytes 786440 | tf_op jit(solution)/shard_map/ppermute | solution.py:42
  5.3 8.5 %collective-permute-start.6 = (bf16[256,512]{1,0:T(8,128)(2,1)S(1)}, bf16[256,512]{1,0:T(8,128)(2,1)S(1)}, u32[]{:S(2)}, u32[]{:S(2)}) collective-permute-start(bf16[256,512]{1,0:T(8,128)(2,1)S(1)} %get-tuple-element.53.unit_ref), channel_id=1, source_target_pairs={{2,0},{40,32},{66,64},{104,96},{3,1},{41,33},{67,65},{105,97},{10,... | collective-permute-start | bytes 786440 | tf_op jit(solution)/shard_map/ppermute | solution.py:42
  7.0 10.4 %collective-permute-start.7 = (bf16[256,512]{1,0:T(8,128)(2,1)S(1)}, bf16[256,512]{1,0:T(8,128)(2,1)S(1)}, u32[]{:S(2)}, u32[]{:S(2)}) collective-permute-start(bf16[256,512]{1,0:T(8,128)(2,1)S(1)} %get-tuple-element.53.unit_ref), channel_id=1, source_target_pairs={{4,0},{48,32},{68,64},{112,96},{5,1},{49,33},{69,65},{113,97},{12,... | collective-permute-start | bytes 786440 | tf_op jit(solution)/shard_map/ppermute | solution.py:42
  8.9 10.3 %collective-permute-start.2 = (bf16[256,512]{1,0:T(8,128)(2,1)S(1)}, bf16[256,512]{1,0:T(8,128)(2,1)S(1)}, u32[]{:S(2)}, u32[]{:S(2)}) collective-permute-start(bf16[256,512]{1,0:T(8,128)(2,1)S(1)} %get-tuple-element.51), channel_id=1, source_target_pairs={{64,0},{97,32},{1,64},{32,96},{65,1},{96,33},{0,65},{33,97},{72,8}... | collective-permute-start | bytes 786440 | tf_op jit(solution)/shard_map/ppermute | solution.py:42
  11.2 0.7 copy-start.2
  12.2 12.3 %collective-permute-start.1 = (bf16[512,512]{1,0:T(8,128)(2,1)S(1)}, bf16[512,512]{1,0:T(8,128)(2,1)S(1)}, u32[]{:S(2)}, u32[]{:S(2)}) collective-permute-start(bf16[512,512]{1,0:T(8,128)(2,1)S(1)} %constant_dynamic-update-slice_fusion.refs_1_), channel_id=1, source_target_pairs={{32,0},{0,32},{96,64},{64,96},{33,1},{1,33},{97,65},{65,97},{40,8}... | collective-permute-start | bytes 1572872 | tf_op jit(solution)/shard_map/ppermute | solution.py:42
  13.8 7.7 %collective-permute-start.3 = (bf16[256,512]{1,0:T(8,128)(2,1)S(1)}, bf16[256,512]{1,0:T(8,128)(2,1)S(1)}, u32[]{:S(2)}, u32[]{:S(2)}) collective-permute-start(bf16[256,512]{1,0:T(8,128)(2,1)S(1)} %collective-permute-done), channel_id=1, source_target_pairs={{65,0},{96,32},{0,64},{33,96},{64,1},{97,33},{1,65},{32,97},{73,8}... | collective-permute-start | bytes 786440 | tf_op jit(solution)/shard_map/ppermute | solution.py:42
  15.8 10.7 %collective-permute-start.10 = (bf16[512,512]{1,0:T(8,128)(2,1)S(1)}, bf16[512,512]{1,0:T(8,128)(2,1)S(1)}, u32[]{:S(2)}, u32[]{:S(2)}) collective-permute-start(bf16[512,512]{1,0:T(8,128)(2,1)S(1)} %constant_dynamic-update-slice_fusion.6.refs_3_), channel_id=1, source_target_pairs={{24,0},{38,32},{88,64},{102,96},{25,1},{39,33},{89,65},{103,97},{0... | collective-permute-start | bytes 1572872 | tf_op jit(solution)/shard_map/ppermute | solution.py:42
  17.5 9.2 %collective-permute-start.8 = (bf16[512,512]{1,0:T(8,128)(2,1)S(1)}, bf16[512,512]{1,0:T(8,128)(2,1)S(1)}, u32[]{:S(2)}, u32[]{:S(2)}) collective-permute-start(bf16[512,512]{1,0:T(8,128)(2,1)S(1)} %constant_dynamic-update-slice_fusion.4.refs_4_), channel_id=1, source_target_pairs={{8,0},{34,32},{72,64},{98,96},{9,1},{35,33},{73,65},{99,97},{16,8}... | collective-permute-start | bytes 1572872 | tf_op jit(solution)/shard_map/ppermute | solution.py:42
  19.2 15.7 %collective-permute-start.12 = (bf16[512,512]{1,0:T(8,128)(2,1)S(1)}, bf16[512,512]{1,0:T(8,128)(2,1)S(1)}, u32[]{:S(2)}, u32[]{:S(2)}) collective-permute-start(bf16[512,512]{1,0:T(8,128)(2,1)S(1)} %constant_dynamic-update-slice_fusion.4.refs_4_), channel_id=1, source_target_pairs={{24,0},{38,32},{88,64},{102,96},{25,1},{39,33},{89,65},{103,97},{0... | collective-permute-start | bytes 1572872 | tf_op jit(solution)/shard_map/ppermute | solution.py:42
  21.4 13.5 %collective-permute-start.13 = (bf16[512,512]{1,0:T(8,128)(2,1)S(1)}, bf16[512,512]{1,0:T(8,128)(2,1)S(1)}, u32[]{:S(2)}, u32[]{:S(2)}) collective-permute-start(bf16[512,512]{1,0:T(8,128)(2,1)S(1)} %constant_dynamic-update-slice_fusion.6.refs_3_), channel_id=1, source_target_pairs={{8,0},{34,32},{72,64},{98,96},{9,1},{35,33},{73,65},{99,97},{16,8}... | collective-permute-start | bytes 1572872 | tf_op jit(solution)/shard_map/ppermute | solution.py:42
  24.5 5.5 %collective-permute-start.4 = (bf16[512,512]{1,0:T(8,128)(2,1)S(1)}, bf16[512,512]{1,0:T(8,128)(2,1)S(1)}, u32[]{:S(2)}, u32[]{:S(2)}) collective-permute-start(bf16[512,512]{1,0:T(8,128)(2,1)S(1)} %constant_dynamic-update-slice_fusion.2.refs_1_.refs_3_), channel_id=1, source_target_pairs={{32,0},{0,32},{96,64},{64,96},{33,1},{1,33},{97,65},{65,97},{40,8}... | collective-permute-start | bytes 1572872 | tf_op jit(solution)/shard_map/ppermute | solution.py:42
  26.7 11.3 %collective-permute-start.11 = (bf16[512,512]{1,0:T(8,128)(2,1)S(1)}, bf16[512,512]{1,0:T(8,128)(2,1)S(1)}, u32[]{:S(2)}, u32[]{:S(2)}) collective-permute-start(bf16[512,512]{1,0:T(8,128)(2,1)S(1)} %collective-permute-done.10.refs_5_), channel_id=1, source_target_pairs={{24,0},{38,32},{88,64},{102,96},{25,1},{39,33},{89,65},{103,97},{0... | collective-permute-start | bytes 1572872 | tf_op jit(solution)/shard_map/ppermute | solution.py:42
  28.3 11.6 %collective-permute-start.9 = (bf16[512,512]{1,0:T(8,128)(2,1)S(1)}, bf16[512,512]{1,0:T(8,128)(2,1)S(1)}, u32[]{:S(2)}, u32[]{:S(2)}) collective-permute-start(bf16[512,512]{1,0:T(8,128)(2,1)S(1)} %collective-permute-done.8.refs_6_), channel_id=1, source_target_pairs={{8,0},{34,32},{72,64},{98,96},{9,1},{35,33},{73,65},{99,97},{16,8}... | collective-permute-start | bytes 1572872 | tf_op jit(solution)/shard_map/ppermute | solution.py:42
  41.9 3.9 %collective-permute-start.17 = (f32[24,256]{1,0:T(8,128)S(1)}, f32[24,256]{1,0:T(8,128)S(1)}, u32[]{:S(2)}, u32[]{:S(2)}) collective-permute-start(f32[24,256]{1,0:T(8,128)S(1)} %get-tuple-element.80), channel_id=1, source_target_pairs={{2,0},{40,32},{66,64},{104,96},{3,1},{41,33},{67,65},{105,97},{10,... | collective-permute-start | bytes 73736 | tf_op jit(solution)/shard_map/ppermute | solution.py:55
  42.1 1.5 %collective-permute-start.14 = (f32[8,256]{1,0:T(8,128)S(1)}, f32[8,256]{1,0:T(8,128)S(1)}, u32[]{:S(2)}, u32[]{:S(2)}) collective-permute-start(f32[8,256]{1,0:T(8,128)S(1)} %get-tuple-element.79), channel_id=1, source_target_pairs={{32,0},{0,32},{96,64},{64,96},{33,1},{1,33},{97,65},{65,97},{40,8}... | collective-permute-start | bytes 24584 | tf_op jit(solution)/shard_map/ppermute | solution.py:42
  45.8 5.5 %collective-permute-start.18 = (f32[24,256]{1,0:T(8,128)S(1)}, f32[24,256]{1,0:T(8,128)S(1)}, u32[]{:S(2)}, u32[]{:S(2)}) collective-permute-start(f32[24,256]{1,0:T(8,128)S(1)} %add.21), channel_id=1, source_target_pairs={{6,0},{56,32},{70,64},{120,96},{7,1},{57,33},{71,65},{121,97},{14,... | collective-permute-start | bytes 73736 | tf_op jit(solution)/shard_map/ppermute | solution.py:55
  51.2 4.0 %collective-permute-start.19 = (f32[24,256]{1,0:T(8,128)S(1)}, f32[24,256]{1,0:T(8,128)S(1)}, u32[]{:S(2)}, u32[]{:S(2)}) collective-permute-start(f32[24,256]{1,0:T(8,128)S(1)} %add.22), channel_id=1, source_target_pairs={{8,0},{34,32},{72,64},{98,96},{9,1},{35,33},{73,65},{99,97},{0,8},... | collective-permute-start | bytes 73736 | tf_op jit(solution)/shard_map/ppermute | solution.py:55
  51.6 3.7 %collective-permute-start.15 = (f32[8,256]{1,0:T(8,128)S(1)}, f32[8,256]{1,0:T(8,128)S(1)}, u32[]{:S(2)}, u32[]{:S(2)}) collective-permute-start(f32[8,256]{1,0:T(8,128)S(1)} %add.19), channel_id=1, source_target_pairs={{64,0},{96,32},{0,64},{32,96},{65,1},{97,33},{1,65},{33,97},{72,8}... | collective-permute-start | bytes 24584 | tf_op jit(solution)/shard_map/ppermute | solution.py:55
  55.3 6.8 %collective-permute-start.20 = (f32[24,256]{1,0:T(8,128)S(1)}, f32[24,256]{1,0:T(8,128)S(1)}, u32[]{:S(2)}, u32[]{:S(2)}) collective-permute-start(f32[24,256]{1,0:T(8,128)S(1)} %add.23.refs_2_), channel_id=1, source_target_pairs={{24,0},{38,32},{88,64},{102,96},{25,1},{39,33},{89,65},{103,97},{1... | collective-permute-start | bytes 73736 | tf_op jit(solution)/shard_map/ppermute | solution.py:55
  57.2 4.9 %collective-permute-start.16 = (f32[8,256]{1,0:T(8,128)S(1)}, f32[8,256]{1,0:T(8,128)S(1)}, u32[]{:S(2)}, u32[]{:S(2)}) collective-permute-start(f32[8,256]{1,0:T(8,128)S(1)} %add.20.refs_0_), channel_id=1, source_target_pairs={{65,0},{97,32},{1,64},{33,96},{64,1},{96,33},{0,65},{32,97},{73,8}... | collective-permute-start | bytes 24584 | tf_op jit(solution)/shard_map/ppermute | solution.py:55
  66.3 2.4 %collective-permute-start.21 = (bf16[784,512]{1,0:T(8,128)(2,1)S(1)}, bf16[784,512]{1,0:T(8,128)(2,1)S(1)}, u32[]{:S(2)}, u32[]{:S(2)}) collective-permute-start(bf16[784,512]{1,0:T(8,128)(2,1)S(1)} %grads_core.1), channel_id=1, source_target_pairs={{32,0},{0,32},{96,64},{64,96},{33,1},{1,33},{97,65},{65,97},{40,8}... | collective-permute-start | bytes 2408456 | tf_op jit(solution)/shard_map/ppermute | solution.py:42
  68.8 7.8 %collective-permute-start.22 = (bf16[272,512]{1,0:T(8,128)(2,1)S(1)}, bf16[272,512]{1,0:T(8,128)(2,1)S(1)}, u32[]{:S(2)}, u32[]{:S(2)}) collective-permute-start(bf16[272,512]{1,0:T(8,128)(2,1)S(1)} %sum_far.1.refs_1_.here_ref), channel_id=1, source_target_pairs={{65,0},{96,32},{0,64},{33,96},{64,1},{97,33},{1,65},{32,97},{73,8}... | collective-permute-start | bytes 835592 | tf_op jit(solution)/shard_map/ppermute | solution.py:42
  72.9 11.6 %copy-start.1 = (bf16[256,512]{1,0:T(8,128)(2,1)S(1)}, bf16[256,512]{1,0:T(8,128)(2,1)}, u32[]{:S(2)}) copy-start(bf16[256,512]{1,0:T(8,128)(2,1)} %z_ref.3) | copy-start | bytes 786436
  72.9 3.9 %collective-permute-start.23 = (bf16[256,512]{1,0:T(8,128)(2,1)S(1)}, bf16[256,512]{1,0:T(8,128)(2,1)S(1)}, u32[]{:S(2)}, u32[]{:S(2)}) collective-permute-start(bf16[256,512]{1,0:T(8,128)(2,1)S(1)} %grads_core_own.1), channel_id=1, source_target_pairs={{32,0},{0,32},{96,64},{64,96},{33,1},{1,33},{97,65},{65,97},{40,8}... | collective-permute-start | bytes 786440 | tf_op jit(solution)/shard_map/ppermute | solution.py:42
  73.7 9.4 %collective-permute-start.24 = (bf16[272,512]{1,0:T(8,128)(2,1)S(1)}, bf16[272,512]{1,0:T(8,128)(2,1)S(1)}, u32[]{:S(2)}, u32[]{:S(2)}) collective-permute-start(bf16[272,512]{1,0:T(8,128)(2,1)S(1)} %get-tuple-element.93), channel_id=1, source_target_pairs={{64,0},{97,32},{1,64},{32,96},{65,1},{96,33},{0,65},{33,97},{72,8}... | collective-permute-start | bytes 835592 | tf_op jit(solution)/shard_map/ppermute | solution.py:42
  76.7 7.8 %collective-permute-start.25 = (bf16[272,512]{1,0:T(8,128)(2,1)S(1)}, bf16[272,512]{1,0:T(8,128)(2,1)S(1)}, u32[]{:S(2)}, u32[]{:S(2)}) collective-permute-start(bf16[272,512]{1,0:T(8,128)(2,1)S(1)} %sum_two.1), channel_id=1, source_target_pairs={{65,0},{96,32},{0,64},{33,96},{64,1},{97,33},{1,65},{32,97},{73,8}... | collective-permute-start | bytes 835592 | tf_op jit(solution)/shard_map/ppermute | solution.py:42

commit v13 on v12

--- a/solution.py
+++ b/solution.py
@@ -395,8 +395,7 @@
     rows = near + rest
     chain = make_exps(info, rows, (0, 1), [before0, after1], (2, 5), chain, None, 4, "exps2")
     chain = make_exps(info, rows, (0, 1), [before1, after0], (3, 4), chain, None, 0, "exps3")
-    chain = make_exps(info, rows, (0, 1), [far0], (6,), chain, None, 0, "exps4")
-    chain = make_exps(info, rows, (0, 1), [far1], (7,), chain, positive, 0, "exps5")
+    chain = make_exps(info, rows, (0, 1), [far0, far1], (6, 7), chain, positive, 0, "exps4")
     _, _, exps, units, sums, col_sums = chain
 
     by_row = sums + get(sums, core=1)

time: 86.2 us -> 86.6 us (level)
  starting transfers between devices: 35 us -> 36.1 us
    ppermute x6, starting transfers between devices: 9.16 us -> 10.4 us  [swap(): return lax.ppermute(value, AXES, pairs)]
    pallas_call x6 -> x5, Pallas kernels: 13.7 us -> 12.9 us  [make_exps(): pl.pallas_call(functools.partial(exps_kernel, places, rows_here, first, l...]
  transfers between devices with their start and end apart: 26 -> 26, of which waited for: 12 -> 12; matrix products, arithmetic and copies ran while one was open for 0% -> 0% of each run, Pallas kernels for 21% -> 19%
where the time goes in v13:
time: 86.6 us; the launch traced here: 86.1 us
  starting transfers between devices  36.1 us (42%)
  Pallas kernels  24.9 us (29%)
  waiting for transfers between devices  22.2 us (26%)
  local copies, waits for them, and re-layouts  1.78 us (2%)
  between operations  0.88 us (1%)
    ppermute x20, starting transfers between devices, get(): return lax.ppermute(value, AXES, pairs)  25.8 us
    pallas_call x5, Pallas kernels, make_exps(): pl.pallas_call(functools.partial(exps_kernel, places, rows_here, first, l...  12.9 us
    ppermute x20, waiting for transfers between devices, get(): return lax.ppermute(value, AXES, pairs)  12.7 us
    ppermute x6, starting transfers between devices, swap(): return lax.ppermute(value, AXES, pairs)  10.4 us
    ppermute x6, waiting for transfers between devices, swap(): return lax.ppermute(value, AXES, pairs)  9.54 us
    pallas_call x5, Pallas kernels, make_grads(): pl.pallas_call(functools.partial(grads_kernel, pieces, adds, carry is not...  9.48 us
  transfers between devices with their start and end apart: 26, of which 12 were waited for; matrix products, arithmetic and copies ran while one was open for 0% of the time, Pallas kernels for 19%

profile of v13, /device:TPU:0, one launch (start us, length us, event | category | flops | bytes accessed | tf_op | source)
XLA Modules:
  0.0 86.1 jit_solution(5610382580329940391)
XLA Ops:
  1.7 2.1 %collective-permute-start = (bf16[256,512]{1,0:T(8,128)(2,1)S(1)}, bf16[256,512]{1,0:T(8,128)(2,1)S(1)}, u32[]{:S(2)}, u32[]{:S(2)}) collective-permute-start(bf16[256,512]{1,0:T(8,128)(2,1)S(1)} %get-tuple-element.47), channel_id=1, source_target_pairs={{65,0},{96,32},{0,64},{33,96},{64,1},{97,33},{1,65},{32,97},{73,8}... | collective-permute-start | bytes 786440 | tf_op jit(solution)/shard_map/ppermute | solution.py:42
  3.8 1.5 %collective-permute-start.5 = (bf16[256,512]{1,0:T(8,128)(2,1)S(1)}, bf16[256,512]{1,0:T(8,128)(2,1)S(1)}, u32[]{:S(2)}, u32[]{:S(2)}) collective-permute-start(bf16[256,512]{1,0:T(8,128)(2,1)S(1)} %get-tuple-element.48.unit_ref), channel_id=1, source_target_pairs={{6,0},{56,32},{70,64},{120,96},{7,1},{57,33},{71,65},{121,97},{14,... | collective-permute-start | bytes 786440 | tf_op jit(solution)/shard_map/ppermute | solution.py:42
  5.3 1.7 %collective-permute-start.6 = (bf16[256,512]{1,0:T(8,128)(2,1)S(1)}, bf16[256,512]{1,0:T(8,128)(2,1)S(1)}, u32[]{:S(2)}, u32[]{:S(2)}) collective-permute-start(bf16[256,512]{1,0:T(8,128)(2,1)S(1)} %get-tuple-element.48.unit_ref), channel_id=1, source_target_pairs={{2,0},{40,32},{66,64},{104,96},{3,1},{41,33},{67,65},{105,97},{10,... | collective-permute-start | bytes 786440 | tf_op jit(solution)/shard_map/ppermute | solution.py:42
  7.0 1.8 %collective-permute-start.8 = (bf16[256,512]{1,0:T(8,128)(2,1)S(1)}, bf16[256,512]{1,0:T(8,128)(2,1)S(1)}, u32[]{:S(2)}, u32[]{:S(2)}) collective-permute-start(bf16[256,512]{1,0:T(8,128)(2,1)S(1)} %get-tuple-element.48.unit_ref), channel_id=1, source_target_pairs={{4,0},{48,32},{68,64},{112,96},{5,1},{49,33},{69,65},{113,97},{12,... | collective-permute-start | bytes 786440 | tf_op jit(solution)/shard_map/ppermute | solution.py:42
  8.9 2.2 %collective-permute-start.2 = (bf16[256,512]{1,0:T(8,128)(2,1)S(1)}, bf16[256,512]{1,0:T(8,128)(2,1)S(1)}, u32[]{:S(2)}, u32[]{:S(2)}) collective-permute-start(bf16[256,512]{1,0:T(8,128)(2,1)S(1)} %get-tuple-element.47), channel_id=1, source_target_pairs={{64,0},{97,32},{1,64},{32,96},{65,1},{96,33},{0,65},{33,97},{72,8}... | collective-permute-start | bytes 786440 | tf_op jit(solution)/shard_map/ppermute | solution.py:42
  12.3 1.4 %collective-permute-done.6 = bf16[256,512]{1,0:T(8,128)(2,1)S(1)} collective-permute-done((bf16[256,512]{1,0:T(8,128)(2,1)S(1)}, bf16[256,512]{1,0:T(8,128)(2,1)S(1)}, u32[]{:S(2)}, u32[]{:S(2)}) %collective-permute-start.6) | collective-permute-done | bytes 262176 | tf_op jit(solution)/shard_map/ppermute | solution.py:42
  13.8 2.0 %collective-permute-start.3 = (bf16[256,512]{1,0:T(8,128)(2,1)S(1)}, bf16[256,512]{1,0:T(8,128)(2,1)S(1)}, u32[]{:S(2)}, u32[]{:S(2)}) collective-permute-start(bf16[256,512]{1,0:T(8,128)(2,1)S(1)} %collective-permute-done), channel_id=1, source_target_pairs={{65,0},{96,32},{0,64},{33,96},{64,1},{97,33},{1,65},{32,97},{73,8}... | collective-permute-start | bytes 786440 | tf_op jit(solution)/shard_map/ppermute | solution.py:42
  15.8 1.6 %collective-permute-start.7 = (bf16[512,512]{1,0:T(8,128)(2,1)S(1)}, bf16[512,512]{1,0:T(8,128)(2,1)S(1)}, u32[]{:S(2)}, u32[]{:S(2)}) collective-permute-start(bf16[512,512]{1,0:T(8,128)(2,1)S(1)} %constant_dynamic-update-slice_fusion.4.refs_3_), channel_id=1, source_target_pairs={{24,0},{38,32},{88,64},{102,96},{25,1},{39,33},{89,65},{103,97},{0... | collective-permute-start | bytes 1572872 | tf_op jit(solution)/shard_map/ppermute | solution.py:42
  17.5 1.7 %collective-permute-start.10 = (bf16[512,512]{1,0:T(8,128)(2,1)S(1)}, bf16[512,512]{1,0:T(8,128)(2,1)S(1)}, u32[]{:S(2)}, u32[]{:S(2)}) collective-permute-start(bf16[512,512]{1,0:T(8,128)(2,1)S(1)} %constant_dynamic-update-slice_fusion.6.refs_4_), channel_id=1, source_target_pairs={{8,0},{34,32},{72,64},{98,96},{9,1},{35,33},{73,65},{99,97},{16,8}... | collective-permute-start | bytes 1572872 | tf_op jit(solution)/shard_map/ppermute | solution.py:42
  19.6 1.9 %collective-permute-done.3 = bf16[256,512]{1,0:T(8,128)(2,1)S(1)} collective-permute-done((bf16[256,512]{1,0:T(8,128)(2,1)S(1)}, bf16[256,512]{1,0:T(8,128)(2,1)S(1)}, u32[]{:S(2)}, u32[]{:S(2)}) %collective-permute-start.3) | collective-permute-done | bytes 262176 | tf_op jit(solution)/shard_map/ppermute | solution.py:42
  21.4 3.0 %collective-permute-start.13 = (bf16[512,512]{1,0:T(8,128)(2,1)S(1)}, bf16[512,512]{1,0:T(8,128)(2,1)S(1)}, u32[]{:S(2)}, u32[]{:S(2)}) collective-permute-start(bf16[512,512]{1,0:T(8,128)(2,1)S(1)} %constant_dynamic-update-slice_fusion.4.refs_3_), channel_id=1, source_target_pairs={{8,0},{34,32},{72,64},{98,96},{9,1},{35,33},{73,65},{99,97},{16,8}... | collective-permute-start | bytes 1572872 | tf_op jit(solution)/shard_map/ppermute | solution.py:42
  24.6 1.9 %exps0.1 = (f32[2048,128]{1,0:T(8,128)S(1)}, f32[8,4096]{1,0:T(8,128)S(1)}, bf16[2048,4096]{1,0:T(8,128)(2,1)S(1)}, bf16[4096,512]{1,0:T(8,128)(2,1)S(1)}) custom-call(s32[4]{0:T(128)S(1)} %pad_add_fusion.refs_0_.info_ref, bf16[512,512]{1,0:T(8,128)(2,1)S(1)} %constant_dynamic-update-slice_fusion.refs_1_, ...), custom_call_target="tpu_custom_call" | custom-call | flops 8589934592 | bytes 8388608 | tf_op jit(solution)/shard_map/exps0/pallas_call | solution.py:219
  26.7 1.6 %collective-permute-start.9 = (bf16[512,512]{1,0:T(8,128)(2,1)S(1)}, bf16[512,512]{1,0:T(8,128)(2,1)S(1)}, u32[]{:S(2)}, u32[]{:S(2)}) collective-permute-start(bf16[512,512]{1,0:T(8,128)(2,1)S(1)} %collective-permute-done.7.refs_5_), channel_id=1, source_target_pairs={{24,0},{38,32},{88,64},{102,96},{25,1},{39,33},{89,65},{103,97},{0... | collective-permute-start | bytes 1572872 | tf_op jit(solution)/shard_map/ppermute | solution.py:42
  28.3 1.7 %collective-permute-start.11 = (bf16[512,512]{1,0:T(8,128)(2,1)S(1)}, bf16[512,512]{1,0:T(8,128)(2,1)S(1)}, u32[]{:S(2)}, u32[]{:S(2)}) collective-permute-start(bf16[512,512]{1,0:T(8,128)(2,1)S(1)} %collective-permute-done.10.refs_6_), channel_id=1, source_target_pairs={{8,0},{34,32},{72,64},{98,96},{9,1},{35,33},{73,65},{99,97},{16,8}... | collective-permute-start | bytes 1572872 | tf_op jit(solution)/shard_map/ppermute | solution.py:42
  30.0 1.9 %exps1.1 = (f32[2048,128]{1,0:T(8,128)S(1)}, f32[8,4096]{1,0:T(8,128)S(1)}, bf16[2048,4096]{1,0:T(8,128)(2,1)S(1)}, bf16[4096,512]{1,0:T(8,128)(2,1)S(1)}) custom-call(s32[4]{0:T(128)S(1)} %pad_add_fusion.refs_0_.info_ref, ...), custom_call_target="tpu_custom_call", output_to_operand_aliasing={{0}: (5, {}), {1}: (6, {}), {2}: (7, {}), {3}: (8, {})} | custom-call | flops 8589934592 | bytes 8388608 | tf_op jit(solution)/shard_map/exps1/pallas_call | solution.py:219
  31.8 3.0 %exps2.1 = (f32[2048,128]{1,0:T(8,128)S(1)}, f32[8,4096]{1,0:T(8,128)S(1)}, bf16[2048,4096]{1,0:T(8,128)(2,1)S(1)}, bf16[4096,512]{1,0:T(8,128)(2,1)S(1)}) custom-call(s32[4]{0:T(128)S(1)} %pad_add_fusion.refs_0_.info_ref, ...), custom_call_target="tpu_custom_call", output_to_operand_aliasing={{0}: (7, {}), {1}: (8, {}), {2}: (9, {}), {3}: (10, {})} | custom-call | flops 8589934592 | bytes 4194304 | tf_op jit(solution)/shard_map/exps2/pallas_call | solution.py:219
  34.9 3.0 %exps3.1 = (f32[2048,128]{1,0:T(8,128)S(1)}, f32[8,4096]{1,0:T(8,128)S(1)}, bf16[2048,4096]{1,0:T(8,128)(2,1)S(1)}, bf16[4096,512]{1,0:T(8,128)(2,1)S(1)}) custom-call(s32[4]{0:T(128)S(1)} %pad_add_fusion.refs_0_.info_ref, ...), custom_call_target="tpu_custom_call", output_to_operand_aliasing={{0}: (7, {}), {1}: (8, {}), {2}: (9, {}), {3}: (10, {})} | custom-call | tf_op jit(solution)/shard_map/exps3/pallas_call | solution.py:219
  38.0 3.1 %exps4.1 = (f32[2048,128]{1,0:T(8,128)S(1)}, f32[8,4096]{1,0:T(8,128)S(1)}, bf16[2048,4096]{1,0:T(8,128)(2,1)S(1)}, bf16[4096,512]{1,0:T(8,128)(2,1)S(1)}, f32[8,256]{1,0:T(8,128)S(1)}, /*index=5*/f32[24,256]{1,0:T(8,128)S(1)}) custom-call(s32[4]{0:T(128)S(1)} %pad_add_fusion.refs_0_.info_ref, ...), custom_call_target="tpu_custom_call", output_to_operand_aliasing={{0}: (7, {}), {1}: (8, {}), {2}: (9, {}), {3}: (10, {})} | custom-call | tf_op jit(solution)/shard_map/exps4/pallas_call | solution.py:219
  42.8 2.2 %collective-permute-done.17 = f32[24,256]{1,0:T(8,128)S(1)} collective-permute-done((f32[24,256]{1,0:T(8,128)S(1)}, f32[24,256]{1,0:T(8,128)S(1)}, u32[]{:S(2)}, u32[]{:S(2)}) %collective-permute-start.17) | collective-permute-done | bytes 24608 | tf_op jit(solution)/shard_map/ppermute | solution.py:55
  45.0 3.7 %collective-permute-start.18 = (f32[24,256]{1,0:T(8,128)S(1)}, f32[24,256]{1,0:T(8,128)S(1)}, u32[]{:S(2)}, u32[]{:S(2)}) collective-permute-start(f32[24,256]{1,0:T(8,128)S(1)} %add.21), channel_id=1, source_target_pairs={{6,0},{56,32},{70,64},{120,96},{7,1},{57,33},{71,65},{121,97},{14,... | collective-permute-start | bytes 73736 | tf_op jit(solution)/shard_map/ppermute | solution.py:55
  48.7 1.8 %collective-permute-done.18 = f32[24,256]{1,0:T(8,128)S(1)} collective-permute-done((f32[24,256]{1,0:T(8,128)S(1)}, f32[24,256]{1,0:T(8,128)S(1)}, u32[]{:S(2)}, u32[]{:S(2)}) %collective-permute-start.18) | collective-permute-done | bytes 24608 | tf_op jit(solution)/shard_map/ppermute | solution.py:55
  50.5 1.6 %collective-permute-start.19 = (f32[24,256]{1,0:T(8,128)S(1)}, f32[24,256]{1,0:T(8,128)S(1)}, u32[]{:S(2)}, u32[]{:S(2)}) collective-permute-start(f32[24,256]{1,0:T(8,128)S(1)} %add.22), channel_id=1, source_target_pairs={{8,0},{34,32},{72,64},{98,96},{9,1},{35,33},{73,65},{99,97},{0,8},... | collective-permute-start | bytes 73736 | tf_op jit(solution)/shard_map/ppermute | solution.py:55
  52.1 1.6 %collective-permute-start.15 = (f32[8,256]{1,0:T(8,128)S(1)}, f32[8,256]{1,0:T(8,128)S(1)}, u32[]{:S(2)}, u32[]{:S(2)}) collective-permute-start(f32[8,256]{1,0:T(8,128)S(1)} %add.19), channel_id=1, source_target_pairs={{64,0},{96,32},{0,64},{32,96},{65,1},{97,33},{1,65},{33,97},{72,8}... | collective-permute-start | bytes 24584 | tf_op jit(solution)/shard_map/ppermute | solution.py:55
  53.7 2.0 %collective-permute-done.15 = f32[8,256]{1,0:T(8,128)S(1)} collective-permute-done((f32[8,256]{1,0:T(8,128)S(1)}, f32[8,256]{1,0:T(8,128)S(1)}, u32[]{:S(2)}, u32[]{:S(2)}) %collective-permute-start.15) | collective-permute-done | bytes 8224 | tf_op jit(solution)/shard_map/ppermute | solution.py:55
  55.7 2.0 %collective-permute-start.20 = (f32[24,256]{1,0:T(8,128)S(1)}, f32[24,256]{1,0:T(8,128)S(1)}, u32[]{:S(2)}, u32[]{:S(2)}) collective-permute-start(f32[24,256]{1,0:T(8,128)S(1)} %add.23.refs_2_), channel_id=1, source_target_pairs={{24,0},{38,32},{88,64},{102,96},{25,1},{39,33},{89,65},{103,97},{1... | collective-permute-start | bytes 73736 | tf_op jit(solution)/shard_map/ppermute | solution.py:55
  57.7 1.3 %collective-permute-start.16 = (f32[8,256]{1,0:T(8,128)S(1)}, f32[8,256]{1,0:T(8,128)S(1)}, u32[]{:S(2)}, u32[]{:S(2)}) collective-permute-start(f32[8,256]{1,0:T(8,128)S(1)} %add.20.refs_0_), channel_id=1, source_target_pairs={{65,0},{97,32},{1,64},{33,96},{64,1},{96,33},{0,65},{32,97},{73,8}... | collective-permute-start | bytes 24584 | tf_op jit(solution)/shard_map/ppermute | solution.py:55
  59.0 3.5 %collective-permute-done.16.refs_1_ = f32[8,256]{1,0:T(8,128)S(1)} collective-permute-done((f32[8,256]{1,0:T(8,128)S(1)}, f32[8,256]{1,0:T(8,128)S(1)}, u32[]{:S(2)}, u32[]{:S(2)}) %collective-permute-start.16) | collective-permute-done | bytes 8224 | tf_op jit(solution)/shard_map/ppermute | solution.py:55
  63.4 3.4 %grads_core.1 = bf16[784,512]{1,0:T(8,128)(2,1)S(1)} custom-call(f32[32,128]{1,0:T(8,128)S(1)} %get-tuple-element.84.acol_ref, bf16[2048,128]{1,0:T(8,128)(2,1)S(1)} %get-tuple-element.77.arow_ref, bf16[2048,4096]{1,0:T(8,128)(2,1)S(1)} %get-tuple-element.78.exps_ref, bf16[4096,512]{1,0:T(8,128)(2,1)S(1)} %get-tuple-element.79.unit_ref, ...), custom_call_target="tpu_custom_call" | custom-call | flops 3221225472 | bytes 10485760 | tf_op jit(solution)/shard_map/grads_core/pallas_call | solution.py:309
  69.7 2.3 %grads_near.1 = (bf16[272,512]{1,0:T(8,128)(2,1)S(1)}, f32[256,512]{1,0:T(8,128)S(1)}) custom-call(f32[32,128]{1,0:T(8,128)S(1)} %get-tuple-element.84.acol_ref, bf16[2048,128]{1,0:T(8,128)(2,1)S(1)} %get-tuple-element.77.arow_ref, bf16[2048,4096]{1,0:T(8,128)(2,1)S(1)} %get-tuple-element.78.exps_ref, bf16[4096,512]{1,0:T(8,128)(2,1)S(1)} %get-tuple-element.79.unit_ref, ...), custom_call_target="tpu_custom_call" | custom-call | flops 2147483648 | bytes 8388608 | tf_op jit(solution)/shard_map/grads_near/pallas_call | solution.py:309
  74.2 2.1 %collective-permute-start.24 = (bf16[272,512]{1,0:T(8,128)(2,1)S(1)}, bf16[272,512]{1,0:T(8,128)(2,1)S(1)}, u32[]{:S(2)}, u32[]{:S(2)}) collective-permute-start(bf16[272,512]{1,0:T(8,128)(2,1)S(1)} %get-tuple-element.85), channel_id=1, source_target_pairs={{64,0},{97,32},{1,64},{32,96},{65,1},{96,33},{0,65},{33,97},{72,8}... | collective-permute-start | bytes 835592 | tf_op jit(solution)/shard_map/ppermute | solution.py:42
  78.5 5.1 %collective-permute-done.24.one_ref = bf16[272,512]{1,0:T(8,128)(2,1)S(1)} collective-permute-done((bf16[272,512]{1,0:T(8,128)(2,1)S(1)}, bf16[272,512]{1,0:T(8,128)(2,1)S(1)}, u32[]{:S(2)}, u32[]{:S(2)}) %collective-permute-start.24) | collective-permute-done | bytes 278560 | tf_op jit(solution)/shard_map/ppermute | solution.py:42
  83.6 1.4 %collective-permute-done.25.two_ref = bf16[272,512]{1,0:T(8,128)(2,1)S(1)} collective-permute-done((bf16[272,512]{1,0:T(8,128)(2,1)S(1)}, bf16[272,512]{1,0:T(8,128)(2,1)S(1)}, u32[]{:S(2)}, u32[]{:S(2)}) %collective-permute-start.25) | collective-permute-done | bytes 278560 | tf_op jit(solution)/shard_map/ppermute | solution.py:42
  (56 shorter events, 14.0 us)
Async XLA Ops:
  0.6 1.0 %copy-start = (bf16[256,512]{1,0:T(8,128)(2,1)S(1)}, bf16[256,512]{1,0:T(8,128)(2,1)}, u32[]{:S(2)}) copy-start(bf16[256,512]{1,0:T(8,128)(2,1)} %z_ref.3) | copy-start | bytes 786436
  1.7 10.4 %collective-permute-start = (bf16[256,512]{1,0:T(8,128)(2,1)S(1)}, bf16[256,512]{1,0:T(8,128)(2,1)S(1)}, u32[]{:S(2)}, u32[]{:S(2)}) collective-permute-start(bf16[256,512]{1,0:T(8,128)(2,1)S(1)} %get-tuple-element.47), channel_id=1, source_target_pairs={{65,0},{96,32},{0,64},{33,96},{64,1},{97,33},{1,65},{32,97},{73,8}... | collective-permute-start | bytes 786440 | tf_op jit(solution)/shard_map/ppermute | solution.py:42
  3.8 8.5 %collective-permute-start.5 = (bf16[256,512]{1,0:T(8,128)(2,1)S(1)}, bf16[256,512]{1,0:T(8,128)(2,1)S(1)}, u32[]{:S(2)}, u32[]{:S(2)}) collective-permute-start(bf16[256,512]{1,0:T(8,128)(2,1)S(1)} %get-tuple-element.48.unit_ref), channel_id=1, source_target_pairs={{6,0},{56,32},{70,64},{120,96},{7,1},{57,33},{71,65},{121,97},{14,... | collective-permute-start | bytes 786440 | tf_op jit(solution)/shard_map/ppermute | solution.py:42
  5.3 8.5 %collective-permute-start.6 = (bf16[256,512]{1,0:T(8,128)(2,1)S(1)}, bf16[256,512]{1,0:T(8,128)(2,1)S(1)}, u32[]{:S(2)}, u32[]{:S(2)}) collective-permute-start(bf16[256,512]{1,0:T(8,128)(2,1)S(1)} %get-tuple-element.48.unit_ref), channel_id=1, source_target_pairs={{2,0},{40,32},{66,64},{104,96},{3,1},{41,33},{67,65},{105,97},{10,... | collective-permute-start | bytes 786440 | tf_op jit(solution)/shard_map/ppermute | solution.py:42
  7.0 10.4 %collective-permute-start.8 = (bf16[256,512]{1,0:T(8,128)(2,1)S(1)}, bf16[256,512]{1,0:T(8,128)(2,1)S(1)}, u32[]{:S(2)}, u32[]{:S(2)}) collective-permute-start(bf16[256,512]{1,0:T(8,128)(2,1)S(1)} %get-tuple-element.48.unit_ref), channel_id=1, source_target_pairs={{4,0},{48,32},{68,64},{112,96},{5,1},{49,33},{69,65},{113,97},{12,... | collective-permute-start | bytes 786440 | tf_op jit(solution)/shard_map/ppermute | solution.py:42
  8.9 10.3 %collective-permute-start.2 = (bf16[256,512]{1,0:T(8,128)(2,1)S(1)}, bf16[256,512]{1,0:T(8,128)(2,1)S(1)}, u32[]{:S(2)}, u32[]{:S(2)}) collective-permute-start(bf16[256,512]{1,0:T(8,128)(2,1)S(1)} %get-tuple-element.47), channel_id=1, source_target_pairs={{64,0},{97,32},{1,64},{32,96},{65,1},{96,33},{0,65},{33,97},{72,8}... | collective-permute-start | bytes 786440 | tf_op jit(solution)/shard_map/ppermute | solution.py:42
  11.2 0.7 copy-start.2
  12.2 12.3 %collective-permute-start.1 = (bf16[512,512]{1,0:T(8,128)(2,1)S(1)}, bf16[512,512]{1,0:T(8,128)(2,1)S(1)}, u32[]{:S(2)}, u32[]{:S(2)}) collective-permute-start(bf16[512,512]{1,0:T(8,128)(2,1)S(1)} %constant_dynamic-update-slice_fusion.refs_1_), channel_id=1, source_target_pairs={{32,0},{0,32},{96,64},{64,96},{33,1},{1,33},{97,65},{65,97},{40,8}... | collective-permute-start | bytes 1572872 | tf_op jit(solution)/shard_map/ppermute | solution.py:42
  13.8 7.7 %collective-permute-start.3 = (bf16[256,512]{1,0:T(8,128)(2,1)S(1)}, bf16[256,512]{1,0:T(8,128)(2,1)S(1)}, u32[]{:S(2)}, u32[]{:S(2)}) collective-permute-start(bf16[256,512]{1,0:T(8,128)(2,1)S(1)} %collective-permute-done), channel_id=1, source_target_pairs={{65,0},{96,32},{0,64},{33,96},{64,1},{97,33},{1,65},{32,97},{73,8}... | collective-permute-start | bytes 786440 | tf_op jit(solution)/shard_map/ppermute | solution.py:42
  15.8 10.7 %collective-permute-start.7 = (bf16[512,512]{1,0:T(8,128)(2,1)S(1)}, bf16[512,512]{1,0:T(8,128)(2,1)S(1)}, u32[]{:S(2)}, u32[]{:S(2)}) collective-permute-start(bf16[512,512]{1,0:T(8,128)(2,1)S(1)} %constant_dynamic-update-slice_fusion.4.refs_3_), channel_id=1, source_target_pairs={{24,0},{38,32},{88,64},{102,96},{25,1},{39,33},{89,65},{103,97},{0... | collective-permute-start | bytes 1572872 | tf_op jit(solution)/shard_map/ppermute | solution.py:42
  17.5 9.2 %collective-permute-start.10 = (bf16[512,512]{1,0:T(8,128)(2,1)S(1)}, bf16[512,512]{1,0:T(8,128)(2,1)S(1)}, u32[]{:S(2)}, u32[]{:S(2)}) collective-permute-start(bf16[512,512]{1,0:T(8,128)(2,1)S(1)} %constant_dynamic-update-slice_fusion.6.refs_4_), channel_id=1, source_target_pairs={{8,0},{34,32},{72,64},{98,96},{9,1},{35,33},{73,65},{99,97},{16,8}... | collective-permute-start | bytes 1572872 | tf_op jit(solution)/shard_map/ppermute | solution.py:42
  19.2 15.7 %collective-permute-start.12 = (bf16[512,512]{1,0:T(8,128)(2,1)S(1)}, bf16[512,512]{1,0:T(8,128)(2,1)S(1)}, u32[]{:S(2)}, u32[]{:S(2)}) collective-permute-start(bf16[512,512]{1,0:T(8,128)(2,1)S(1)} %constant_dynamic-update-slice_fusion.6.refs_4_), channel_id=1, source_target_pairs={{24,0},{38,32},{88,64},{102,96},{25,1},{39,33},{89,65},{103,97},{0... | collective-permute-start | bytes 1572872 | tf_op jit(solution)/shard_map/ppermute | solution.py:42
  21.4 13.4 %collective-permute-start.13 = (bf16[512,512]{1,0:T(8,128)(2,1)S(1)}, bf16[512,512]{1,0:T(8,128)(2,1)S(1)}, u32[]{:S(2)}, u32[]{:S(2)}) collective-permute-start(bf16[512,512]{1,0:T(8,128)(2,1)S(1)} %constant_dynamic-update-slice_fusion.4.refs_3_), channel_id=1, source_target_pairs={{8,0},{34,32},{72,64},{98,96},{9,1},{35,33},{73,65},{99,97},{16,8}... | collective-permute-start | bytes 1572872 | tf_op jit(solution)/shard_map/ppermute | solution.py:42
  24.5 5.5 %collective-permute-start.4 = (bf16[512,512]{1,0:T(8,128)(2,1)S(1)}, bf16[512,512]{1,0:T(8,128)(2,1)S(1)}, u32[]{:S(2)}, u32[]{:S(2)}) collective-permute-start(bf16[512,512]{1,0:T(8,128)(2,1)S(1)} %constant_dynamic-update-slice_fusion.2.refs_1_.refs_3_), channel_id=1, source_target_pairs={{32,0},{0,32},{96,64},{64,96},{33,1},{1,33},{97,65},{65,97},{40,8}... | collective-permute-start | bytes 1572872 | tf_op jit(solution)/shard_map/ppermute | solution.py:42
  26.7 11.2 %collective-permute-start.9 = (bf16[512,512]{1,0:T(8,128)(2,1)S(1)}, bf16[512,512]{1,0:T(8,128)(2,1)S(1)}, u32[]{:S(2)}, u32[]{:S(2)}) collective-permute-start(bf16[512,512]{1,0:T(8,128)(2,1)S(1)} %collective-permute-done.7.refs_5_), channel_id=1, source_target_pairs={{24,0},{38,32},{88,64},{102,96},{25,1},{39,33},{89,65},{103,97},{0... | collective-permute-start | bytes 1572872 | tf_op jit(solution)/shard_map/ppermute | solution.py:42
  28.3 9.7 %collective-permute-start.11 = (bf16[512,512]{1,0:T(8,128)(2,1)S(1)}, bf16[512,512]{1,0:T(8,128)(2,1)S(1)}, u32[]{:S(2)}, u32[]{:S(2)}) collective-permute-start(bf16[512,512]{1,0:T(8,128)(2,1)S(1)} %collective-permute-done.10.refs_6_), channel_id=1, source_target_pairs={{8,0},{34,32},{72,64},{98,96},{9,1},{35,33},{73,65},{99,97},{16,8}... | collective-permute-start | bytes 1572872 | tf_op jit(solution)/shard_map/ppermute | solution.py:42
  41.1 3.9 %collective-permute-start.17 = (f32[24,256]{1,0:T(8,128)S(1)}, f32[24,256]{1,0:T(8,128)S(1)}, u32[]{:S(2)}, u32[]{:S(2)}) collective-permute-start(f32[24,256]{1,0:T(8,128)S(1)} %get-tuple-element.72), channel_id=1, source_target_pairs={{2,0},{40,32},{66,64},{104,96},{3,1},{41,33},{67,65},{105,97},{10,... | collective-permute-start | bytes 73736 | tf_op jit(solution)/shard_map/ppermute | solution.py:55
  41.3 1.5 %collective-permute-start.14 = (f32[8,256]{1,0:T(8,128)S(1)}, f32[8,256]{1,0:T(8,128)S(1)}, u32[]{:S(2)}, u32[]{:S(2)}) collective-permute-start(f32[8,256]{1,0:T(8,128)S(1)} %get-tuple-element.71), channel_id=1, source_target_pairs={{32,0},{0,32},{96,64},{64,96},{33,1},{1,33},{97,65},{65,97},{40,8}... | collective-permute-start | bytes 24584 | tf_op jit(solution)/shard_map/ppermute | solution.py:42
  45.0 5.5 %collective-permute-start.18 = (f32[24,256]{1,0:T(8,128)S(1)}, f32[24,256]{1,0:T(8,128)S(1)}, u32[]{:S(2)}, u32[]{:S(2)}) collective-permute-start(f32[24,256]{1,0:T(8,128)S(1)} %add.21), channel_id=1, source_target_pairs={{6,0},{56,32},{70,64},{120,96},{7,1},{57,33},{71,65},{121,97},{14,... | collective-permute-start | bytes 73736 | tf_op jit(solution)/shard_map/ppermute | solution.py:55
  50.5 5.2 %collective-permute-start.19 = (f32[24,256]{1,0:T(8,128)S(1)}, f32[24,256]{1,0:T(8,128)S(1)}, u32[]{:S(2)}, u32[]{:S(2)}) collective-permute-start(f32[24,256]{1,0:T(8,128)S(1)} %add.22), channel_id=1, source_target_pairs={{8,0},{34,32},{72,64},{98,96},{9,1},{35,33},{73,65},{99,97},{0,8},... | collective-permute-start | bytes 73736 | tf_op jit(solution)/shard_map/ppermute | solution.py:55
  52.1 3.7 %collective-permute-start.15 = (f32[8,256]{1,0:T(8,128)S(1)}, f32[8,256]{1,0:T(8,128)S(1)}, u32[]{:S(2)}, u32[]{:S(2)}) collective-permute-start(f32[8,256]{1,0:T(8,128)S(1)} %add.19), channel_id=1, source_target_pairs={{64,0},{96,32},{0,64},{32,96},{65,1},{97,33},{1,65},{33,97},{72,8}... | collective-permute-start | bytes 24584 | tf_op jit(solution)/shard_map/ppermute | solution.py:55
  55.7 6.8 %collective-permute-start.20 = (f32[24,256]{1,0:T(8,128)S(1)}, f32[24,256]{1,0:T(8,128)S(1)}, u32[]{:S(2)}, u32[]{:S(2)}) collective-permute-start(f32[24,256]{1,0:T(8,128)S(1)} %add.23.refs_2_), channel_id=1, source_target_pairs={{24,0},{38,32},{88,64},{102,96},{25,1},{39,33},{89,65},{103,97},{1... | collective-permute-start | bytes 73736 | tf_op jit(solution)/shard_map/ppermute | solution.py:55
  57.7 4.9 %collective-permute-start.16 = (f32[8,256]{1,0:T(8,128)S(1)}, f32[8,256]{1,0:T(8,128)S(1)}, u32[]{:S(2)}, u32[]{:S(2)}) collective-permute-start(f32[8,256]{1,0:T(8,128)S(1)} %add.20.refs_0_), channel_id=1, source_target_pairs={{65,0},{97,32},{1,64},{33,96},{64,1},{96,33},{0,65},{32,97},{73,8}... | collective-permute-start | bytes 24584 | tf_op jit(solution)/shard_map/ppermute | solution.py:55
  66.8 2.4 %collective-permute-start.21 = (bf16[784,512]{1,0:T(8,128)(2,1)S(1)}, bf16[784,512]{1,0:T(8,128)(2,1)S(1)}, u32[]{:S(2)}, u32[]{:S(2)}) collective-permute-start(bf16[784,512]{1,0:T(8,128)(2,1)S(1)} %grads_core.1), channel_id=1, source_target_pairs={{32,0},{0,32},{96,64},{64,96},{33,1},{1,33},{97,65},{65,97},{40,8}... | collective-permute-start | bytes 2408456 | tf_op jit(solution)/shard_map/ppermute | solution.py:42
  69.2 7.8 %collective-permute-start.22 = (bf16[272,512]{1,0:T(8,128)(2,1)S(1)}, bf16[272,512]{1,0:T(8,128)(2,1)S(1)}, u32[]{:S(2)}, u32[]{:S(2)}) collective-permute-start(bf16[272,512]{1,0:T(8,128)(2,1)S(1)} %sum_far.1.refs_1_.here_ref), channel_id=1, source_target_pairs={{65,0},{96,32},{0,64},{33,96},{64,1},{97,33},{1,65},{32,97},{73,8}... | collective-permute-start | bytes 835592 | tf_op jit(solution)/shard_map/ppermute | solution.py:42
  73.3 11.6 %copy-start.1 = (bf16[256,512]{1,0:T(8,128)(2,1)S(1)}, bf16[256,512]{1,0:T(8,128)(2,1)}, u32[]{:S(2)}) copy-start(bf16[256,512]{1,0:T(8,128)(2,1)} %z_ref.3) | copy-start | bytes 786436
  73.3 3.9 %collective-permute-start.23 = (bf16[256,512]{1,0:T(8,128)(2,1)S(1)}, bf16[256,512]{1,0:T(8,128)(2,1)S(1)}, u32[]{:S(2)}, u32[]{:S(2)}) collective-permute-start(bf16[256,512]{1,0:T(8,128)(2,1)S(1)} %grads_core_own.1), channel_id=1, source_target_pairs={{32,0},{0,32},{96,64},{64,96},{33,1},{1,33},{97,65},{65,97},{40,8}... | collective-permute-start | bytes 786440 | tf_op jit(solution)/shard_map/ppermute | solution.py:42
  74.2 9.4 %collective-permute-start.24 = (bf16[272,512]{1,0:T(8,128)(2,1)S(1)}, bf16[272,512]{1,0:T(8,128)(2,1)S(1)}, u32[]{:S(2)}, u32[]{:S(2)}) collective-permute-start(bf16[272,512]{1,0:T(8,128)(2,1)S(1)} %get-tuple-element.85), channel_id=1, source_target_pairs={{64,0},{97,32},{1,64},{32,96},{65,1},{96,33},{0,65},{33,97},{72,8}... | collective-permute-start | bytes 835592 | tf_op jit(solution)/shard_map/ppermute | solution.py:42
  77.1 7.8 %collective-permute-start.25 = (bf16[272,512]{1,0:T(8,128)(2,1)S(1)}, bf16[272,512]{1,0:T(8,128)(2,1)S(1)}, u32[]{:S(2)}, u32[]{:S(2)}) collective-permute-start(bf16[272,512]{1,0:T(8,128)(2,1)S(1)} %sum_two.1), channel_id=1, source_target_pairs={{65,0},{96,32},{0,64},{33,96},{64,1},{97,33},{1,65},{32,97},{73,8}... | collective-permute-start | bytes 835592 | tf_op jit(solution)/shard_map/ppermute | solution.py:42
